TPU v7x, 32 devices: a whole 2x2x4 slice. The times are simulated.
32 devices in a mesh: expert: 4 (over z), dp: 8 (over y, x, core).
Axes of the slice: x: 2, y: 2, z: 4, core: 2. Of those that a mesh axis runs over, the one named last changes fastest.
Arguments:
- act_attn: bfloat16 [8192, 32], P(('expert', 'dp')), may hold values from -10 to 10
- dy_attn: bfloat16 [8192, 6144], P(('expert', 'dp')), may hold values from -10 to 10
- act_exp: bfloat16 [4, 1024, 16], P('expert', 'dp'), may hold values from -10 to 10
- dy_exp: bfloat16 [4, 1024, 6144], P('expert', 'dp'), may hold values from -10 to 10
- w_attn: float32 [32, 6144], P(('expert', 'dp')), may hold values from -0.3 to 0.3
- m_attn: float32 [32, 6144], P(('expert', 'dp')), may hold values from -1.5 to 1.5
- v_attn: float32 [32, 6144], P(('expert', 'dp')), may hold values from 0.05 to 1
- w_exp: float32 [4, 16, 6144], P('expert', 'dp'), may hold values from -0.3 to 0.3
- m_exp: float32 [4, 16, 6144], P('expert', 'dp'), may hold values from -1.5 to 1.5
- v_exp: float32 [4, 16, 6144], P('expert', 'dp'), may hold values from 0.05 to 1
Outputs:
- w_attn_new: float32 [32, 6144], P(('expert', 'dp'))
- m_attn_new: float32 [32, 6144], P(('expert', 'dp'))
- v_attn_new: float32 [32, 6144], P(('expert', 'dp'))
- w_exp_new: float32 [4, 16, 6144], P('expert', 'dp')
- m_exp_new: float32 [4, 16, 6144], P('expert', 'dp')
- v_exp_new: float32 [4, 16, 6144], P('expert', 'dp')
- attn_weights: bfloat16 [32, 6144], replicated
- expert_weights: bfloat16 [4, 16, 6144], P('expert')
All inputs are finite; a program needn't handle non-finite values.
Results may differ from a plain program's by a relative error of at most 0.0075.
Values may be sent and summed in bfloat16 or wider, within the bound.
No kernel may reach another device: no remote copies, remote signals or barrier semaphores. Data moves between devices by JAX's collectives and lax.ppermute only.
A program may use at most 64 MiB of HBM per device.

v0:
```python
import math

import jax
import jax.numpy as jnp
from jax import lax
from jax.sharding import PartitionSpec as P

beta_first = 0.9
beta_second = 0.95
bias_first = 1.0 - 0.9**10
bias_second = 1.0 - 0.95**10
learn_rate = 0.01
decay_rate = 0.1
adam_eps = 1e-08


def contract_rows(left, right):
    return lax.dot_general(
        left, right, (((0,), (0,)), ((), ())), preferred_element_type=jnp.float32
    )


def adamw(grad, weight, moment, second, factor):
    scaled = factor * grad
    moment_new = beta_first * moment + (1.0 - beta_first) * scaled
    second_new = beta_second * second + (1.0 - beta_second) * scaled * scaled
    update = moment_new / bias_first / (jnp.sqrt(second_new / bias_second) + adam_eps)
    weight_new = weight - learn_rate * (update + decay_rate * weight)
    return (weight_new, moment_new, second_new)


def body(act_attn, dy_attn, act_exp, dy_exp, w_attn, m_attn, v_attn, w_exp, m_exp, v_exp):
    width = w_attn.shape[1]
    n_expert = lax.axis_size("expert")
    total_params = width * (act_attn.shape[1] + n_expert * act_exp.shape[2])
    limit = 0.5 * math.sqrt(total_params)
    g_attn = lax.psum_scatter(
        contract_rows(act_attn, dy_attn), ("expert", "dp"), scatter_dimension=0, tiled=True
    )
    sq_attn = jnp.sum(g_attn * g_attn)
    local_act = act_exp[0]
    local_dy = dy_exp[0]
    g_exp = lax.psum_scatter(
        contract_rows(local_act, local_dy), "dp", scatter_dimension=0, tiled=True
    )
    sq_exp = jnp.sum(g_exp * g_exp)
    summed = lax.psum((sq_attn, sq_exp), ("expert", "dp"))
    total = summed[0] + summed[1]
    norm = jnp.sqrt(total)
    factor = jnp.minimum(1.0, limit / (norm + 1e-06))
    wa_new, ma_new, va_new = adamw(g_attn, w_attn, m_attn, v_attn, factor)
    we_new, me_new, ve_new = adamw(g_exp[None], w_exp, m_exp, v_exp, factor)
    attn_half = wa_new.astype(jnp.bfloat16)
    attn_full = lax.all_gather(attn_half, ("expert", "dp"), axis=0, tiled=True)
    expert_full = lax.all_gather(we_new.astype(jnp.bfloat16), "dp", axis=1, tiled=True)
    return (wa_new, ma_new, va_new, we_new, me_new, ve_new, attn_full, expert_full)


def solution(mesh):
    return jax.shard_map(
        body,
        mesh=mesh,
        in_specs=(
            P(("expert", "dp"), None),
            P(("expert", "dp"), None),
            P("expert", "dp", None),
            P("expert", "dp", None),
            P(("expert", "dp"), None),
            P(("expert", "dp"), None),
            P(("expert", "dp"), None),
            P("expert", "dp", None),
            P("expert", "dp", None),
            P("expert", "dp", None),
        ),
        out_specs=(
            P(("expert", "dp"), None),
            P(("expert", "dp"), None),
            P(("expert", "dp"), None),
            P("expert", "dp", None),
            P("expert", "dp", None),
            P("expert", "dp", None),
            P(),
            P("expert", None, None),
        ),
        check_vma=False,
    )
```

profile of v0, /device:TPU:0, one launch (start us, length us, event | category | flops | bytes accessed | tf_op | source)
XLA Modules:
  0.0 308.3 jit_solution(8928084795869120509)
XLA Ops:
  7.2 0.0 copy-start
  7.2 0.0 copy-start.7
  7.2 0.0 copy-start.4
  7.2 0.0 copy-start.5
  7.2 0.0 copy-start.6
  7.2 0.0 all-reduce.7.cloned.1.call-start
  7.3 2.6 fusion
  9.9 0.0 all-reduce.7.cloned.1.call-update
  9.9 0.0 copy-start.1
  10.0 0.0 copy-start.2
  10.0 0.0 copy-start.3
  10.0 0.0 all-reduce.5.cloned.1.call-start
  10.0 0.0 copy-done
  10.0 2.3 fusion.9
  12.3 0.0 all-reduce.5.cloned.1.call-update
  12.3 0.0 copy-done.7
  12.3 0.6 dynamic-slice.1
  13.6 55.0 %all-reduce.7.cloned.1.call-done = f32[16,6144]{1,0:T(8,128)} async-done(((f32[16,6144]{1,0:T(8,128)}), f32[16,6144]{1,0:T(8,128)}) %all-reduce.7.cloned.1.call-update) | async-done | bytes 393232
  68.6 1.6 multiply_reduce_fusion
  70.2 132.0 %all-reduce.5.cloned.1.call-done = f32[32,6144]{1,0:T(8,128)} async-done(((f32[32,6144]{1,0:T(8,128)}), f32[32,6144]{1,0:T(8,128)}) %all-reduce.5.cloned.1.call-update) | async-done | bytes 786448
  202.1 1.6 multiply_reduce_fusion.1
  205.0 39.2 %psum.16 = f32[]{:T(128)} all-reduce(f32[]{:T(128)S(6)} %add.44), channel_id=1, replica_groups=mesh['expert'=4,'dp'=8] {'expert','dp'}, use_global_device_ids=true, to_apply=%region_2.0 | all-reduce | flops 1 | bytes 8 | tf_op jit(solution)/shard_map/psum | solution.py:47
  244.9 0.0 copy-done.4
  244.9 0.0 copy-done.5
  244.9 0.0 copy-done.6
  244.9 1.7 convert_bitcast_fusion
  246.7 42.8 %all-gather = bf16[32,1,6144]{2,1,0:T(2,128)(2,1)S(1)} all-gather(bf16[1,1,6144]{2,1,0:T(2,128)(2,1)S(1)} %get-tuple-element.28), channel_id=1, replica_groups=mesh['expert'=4,'dp'=8] {'expert','dp'}, dimensions={0}, use_global_device_ids=true | all-gather | bytes 405504 | tf_op jit(solution)/shard_map/all_gather | solution.py:54
  289.5 1.0 copy.24
  290.5 0.0 copy-done.1
  290.5 1.8 fusion.6
  292.3 8.4 %all_gather.7 = bf16[1,16,6144]{2,0,1:T(2,128)(2,1)S(1)} all-gather(bf16[1,2,6144]{2,0,1:T(2,128)(2,1)S(1)} %copy.20), channel_id=1, replica_groups=mesh['expert'=4,'dp'=8] {'dp'}, dimensions={1}, use_global_device_ids=true | all-gather | bytes 221184 | tf_op jit(solution)/shard_map/all_gather | solution.py:55
  300.7 0.8 copy.21
  (3 shorter events, 0.0 us)
Async XLA Ops:
  7.2 2.9 copy-start
  7.2 5.1 %copy-start.7 = (u32[32]{0:T(128)S(1)}, u32[32]{0:T(128)}, u32[]{:S(2)}) copy-start(u32[32]{0:T(128)} %constant.49) | copy-start | bytes 388
  7.2 237.7 %copy-start.4 = (f32[1,6144]{1,0:T(1,128)S(1)}, f32[1,6144]{1,0:T(1,128)}, u32[]{:S(2)}) copy-start(f32[1,6144]{1,0:T(1,128)} %param.14) | copy-start | bytes 73732
  7.2 237.7 %copy-start.5 = (f32[1,6144]{1,0:T(1,128)S(1)}, f32[1,6144]{1,0:T(1,128)}, u32[]{:S(2)}) copy-start(f32[1,6144]{1,0:T(1,128)} %param.15) | copy-start | bytes 73732
  7.2 237.7 %copy-start.6 = (f32[1,6144]{1,0:T(1,128)S(1)}, f32[1,6144]{1,0:T(1,128)}, u32[]{:S(2)}) copy-start(f32[1,6144]{1,0:T(1,128)} %param.16) | copy-start | bytes 73732
  7.2 61.3 %all-reduce.7.cloned.1.call-start = ((), (), s32[]{:S(2)}) async-start(), calls=%async_computation.1 | async-start | bytes 786432
  9.9 280.5 %copy-start.1 = (f32[1,2,6144]{2,1,0:T(2,128)S(1)}, f32[1,2,6144]{2,1,0:T(2,128)}, u32[]{:S(2)}) copy-start(f32[1,2,6144]{2,1,0:T(2,128)} %param.17) | copy-start | bytes 147460
  10.0 280.5 %copy-start.2 = (f32[1,2,6144]{2,1,0:T(2,128)S(1)}, f32[1,2,6144]{2,1,0:T(2,128)}, u32[]{:S(2)}) copy-start(f32[1,2,6144]{2,1,0:T(2,128)} %param.18) | copy-start | bytes 147460
  10.0 280.5 %copy-start.3 = (f32[1,2,6144]{2,1,0:T(2,128)S(1)}, f32[1,2,6144]{2,1,0:T(2,128)}, u32[]{:S(2)}) copy-start(f32[1,2,6144]{2,1,0:T(2,128)} %param.19) | copy-start | bytes 147460
  10.0 192.1 %all-reduce.5.cloned.1.call-start = ((), (), s32[]{:S(2)}) async-start(), calls=%async_computation | async-start | bytes 1572864
Sparse Core Ops, SparseCore 0:
  11.7 56.8 all-reduce.6
  73.8 128.3 all-reduce.4
where the time goes:
time: 309 us; the launch traced here: 308 us
  waiting for transfers between devices  187 us (61%)
  blocking collectives  90.4 us (29%)
  between operations  16.8 us (5%)
  other arithmetic  6.67 us (2%)
  matrix products  4.91 us (2%)
    unnamed x4, waiting for transfers between devices  187 us
    all_gather x1, blocking collectives, body(): attn_full = lax.all_gather(attn_half, ('expert', 'dp'), axis=0, tiled=True)  42.8 us
    psum x1, blocking collectives, body(): summed = lax.psum((sq_attn, sq_exp), ('expert', 'dp'))  39.2 us
    all_gather x1, blocking collectives, body(): lax.all_gather(we_new.astype(jnp.bfloat16), 'dp', axis=1, tiled=True)  8.39 us
  transfers between devices with their start and end apart: 2, of which 2 were waited for; matrix products, arithmetic and copies ran while one was open for 1% of the time, Pallas kernels for 0%

commit v1 on v0

--- a/solution.py
+++ b/solution.py
@@ -29,30 +29,49 @@
     return (weight_new, moment_new, second_new)
 
 
+def doubling_sum(value, axis):
+    size = lax.axis_size(axis)
+    step = 1
+    while step < size:
+        value = value + lax.ppermute(value, axis, [(i, i ^ step) for i in range(size)])
+        step *= 2
+    return value
+
+
 def body(act_attn, dy_attn, act_exp, dy_exp, w_attn, m_attn, v_attn, w_exp, m_exp, v_exp):
     width = w_attn.shape[1]
     n_expert = lax.axis_size("expert")
+    n_dp = lax.axis_size("dp")
+    rows_a = w_attn.shape[0]
+    rows_e = w_exp.shape[1]
     total_params = width * (act_attn.shape[1] + n_expert * act_exp.shape[2])
     limit = 0.5 * math.sqrt(total_params)
-    g_attn = lax.psum_scatter(
-        contract_rows(act_attn, dy_attn), ("expert", "dp"), scatter_dimension=0, tiled=True
+    terms_a = contract_rows(act_attn, dy_attn).astype(jnp.bfloat16)
+    terms_e = contract_rows(act_exp[0], dy_exp[0]).astype(jnp.bfloat16)
+    terms_a = terms_a.reshape(n_expert, n_dp, rows_a, width).transpose(1, 0, 2, 3)
+    terms = jnp.concatenate(
+        [terms_a.reshape(n_dp, n_expert * rows_a, width), terms_e.reshape(n_dp, rows_e, width)], axis=1
     )
-    sq_attn = jnp.sum(g_attn * g_attn)
-    local_act = act_exp[0]
-    local_dy = dy_exp[0]
-    g_exp = lax.psum_scatter(
-        contract_rows(local_act, local_dy), "dp", scatter_dimension=0, tiled=True
-    )
-    sq_exp = jnp.sum(g_exp * g_exp)
-    summed = lax.psum((sq_attn, sq_exp), ("expert", "dp"))
-    total = summed[0] + summed[1]
-    norm = jnp.sqrt(total)
+    got = lax.all_to_all(terms, "dp", split_axis=0, concat_axis=0, tiled=True)
+    part = jnp.sum(got.astype(jnp.float32), axis=0)
+    g_exp = part[n_expert * rows_a :]
+    part_a = part[: n_expert * rows_a].reshape(n_expert, rows_a, width).astype(jnp.bfloat16)
+    got_a = lax.all_to_all(part_a, "expert", split_axis=0, concat_axis=0, tiled=True)
+    g_attn = jnp.sum(got_a.astype(jnp.float32), axis=0)
+    square = jnp.sum(g_attn * g_attn) + jnp.sum(g_exp * g_exp)
+    square = doubling_sum(doubling_sum(jnp.full((1, 128), square), "dp"), "expert")
+    norm = jnp.sqrt(square[0, 0])
     factor = jnp.minimum(1.0, limit / (norm + 1e-06))
     wa_new, ma_new, va_new = adamw(g_attn, w_attn, m_attn, v_attn, factor)
     we_new, me_new, ve_new = adamw(g_exp[None], w_exp, m_exp, v_exp, factor)
-    attn_half = wa_new.astype(jnp.bfloat16)
-    attn_full = lax.all_gather(attn_half, ("expert", "dp"), axis=0, tiled=True)
-    expert_full = lax.all_gather(we_new.astype(jnp.bfloat16), "dp", axis=1, tiled=True)
+    half_a = lax.all_gather(wa_new.astype(jnp.bfloat16), "expert", axis=0, tiled=False)
+    both = jnp.concatenate(
+        [half_a.reshape(n_expert * rows_a, width), we_new[0].astype(jnp.bfloat16)], axis=0
+    )
+    full = lax.all_gather(both, "dp", axis=0, tiled=False)
+    attn_full = full[:, : n_expert * rows_a].reshape(n_dp, n_expert, rows_a, width)
+    attn_full = attn_full.transpose(1, 0, 2, 3).reshape(-1, width)
+    expert_full = full[:, n_expert * rows_a :].reshape(1, n_dp * rows_e, width)
     return (wa_new, ma_new, va_new, we_new, me_new, ve_new, attn_full, expert_full)
 
 

time: 309 us -> 81.9 us (0.27)
  waiting for transfers between devices: 187 us -> 18.6 us
  blocking collectives: 90.4 us -> 40.5 us
  between operations: 16.8 us -> 2.19 us
  starting transfers between devices: 0.08 us -> 7.59 us
    unnamed x4 -> x0, waiting for transfers between devices: 187 us -> none
    psum x1 -> x0, blocking collectives: 39.2 us -> none  [body(): summed = lax.psum((sq_attn, sq_exp), ('expert', 'dp'))]
    all_gather x2, blocking collectives: 51.2 us -> 22.8 us  [the longest x1 13.4 us: body(): lax.all_gather(wa_new.astype(jnp.bfloat16), 'expert', axis=0, tiled=False)]
    all_to_all x0 -> x1, blocking collectives: none -> 17.7 us  [body(): got = lax.all_to_all(terms, 'dp', split_axis=0, concat_axis=0, tiled=True)]
    ppermute x0 -> x5, waiting for transfers between devices: none -> 13.5 us  [doubling_sum(): lax.ppermute(value, axis, [(i, i ^ step) for i in range(size)])]
    all_to_all x0 -> x1, waiting for transfers between devices: none -> 5.05 us  [body(): lax.all_to_all(part_a, 'expert', split_axis=0, concat_axis=0, tiled=True)]
    all_to_all x0 -> x1, starting transfers between devices: none -> 4.87 us  [body(): lax.all_to_all(part_a, 'expert', split_axis=0, concat_axis=0, tiled=True)]
  transfers between devices with their start and end apart: 2 -> 6, of which waited for: 2 -> 6; matrix products, arithmetic and copies ran while one was open for 1% -> 1% of each run, Pallas kernels for 0% -> 0%
where the time goes in v1:
time: 81.9 us; the launch traced here: 81.4 us
  blocking collectives  40.5 us (49%)
  waiting for transfers between devices  18.6 us (23%)
  starting transfers between devices  7.59 us (9%)
  other arithmetic  5.91 us (7%)
  local copies, waits for them, and re-layouts  4.14 us (5%)
  matrix products  2.53 us (3%)
  between operations  2.19 us (3%)
    all_to_all x1, blocking collectives, body(): got = lax.all_to_all(terms, 'dp', split_axis=0, concat_axis=0, tiled=True)  17.7 us
    ppermute x5, waiting for transfers between devices, doubling_sum(): lax.ppermute(value, axis, [(i, i ^ step) for i in range(size)])  13.5 us
    all_gather x1, blocking collectives, body(): lax.all_gather(wa_new.astype(jnp.bfloat16), 'expert', axis=0, tiled=False)  13.4 us
    all_gather x1, blocking collectives, body(): full = lax.all_gather(both, 'dp', axis=0, tiled=False)  9.46 us
    all_to_all x1, waiting for transfers between devices, body(): lax.all_to_all(part_a, 'expert', split_axis=0, concat_axis=0, tiled=True)  5.05 us
    all_to_all x1, starting transfers between devices, body(): lax.all_to_all(part_a, 'expert', split_axis=0, concat_axis=0, tiled=True)  4.87 us
    ppermute x5, starting transfers between devices, doubling_sum(): lax.ppermute(value, axis, [(i, i ^ step) for i in range(size)])  2.72 us
    dot_general x2, matrix products, contract_rows(): lax.dot_general(left, right, (((0,), (0,)), ((), ())), preferred_element_...  2.53 us
  transfers between devices with their start and end apart: 6, of which 6 were waited for; matrix products, arithmetic and copies ran while one was open for 1% of the time, Pallas kernels for 0%

profile of v1, /device:TPU:0, one launch (start us, length us, event | category | flops | bytes accessed | tf_op | source)
XLA Modules:
  0.0 81.4 jit_solution(2172755429221396493)
XLA Ops:
  0.7 1.9 %convolution_convert_fusion.1 = bf16[16,6144]{1,0:T(8,128)(2,1)S(1)} fusion(bf16[1,128,6144]{2,1,0:T(8,128)(2,1)} %param.13, bf16[1,128,16]{1,2,0:T(8,128)(2,1)} %param.12), kind=kOutput, calls=%fused_computation.2 | convolution fusion | flops 25264128 | bytes 1773568 | tf_op jit(solution)/shard_map/dot_general | solution.py:18
  2.5 0.2 reshape.83
  2.7 0.3 copy-done
  3.0 0.6 fusion
  3.7 0.3 copy.30
  4.0 0.4 pad_maximum_fusion
  4.4 17.7 %all_to_all.10 = bf16[8,6,6144]{2,1,0:T(8,128)(2,1)S(1)} all-to-all(bf16[8,6,6144]{2,1,0:T(8,128)(2,1)S(1)} %pad_maximum_fusion), channel_id=1, replica_groups=mesh['expert'=4,'dp'=8] {'dp'}, dimensions={0} | all-to-all | bytes 1179648 | tf_op jit(solution)/shard_map/all_to_all | solution.py:55
  22.0 0.2 convert_reduce_fusion
  22.2 0.5 broadcast.56
  22.7 0.7 reduce.2
  23.4 0.7 reshape.96
  24.1 4.9 %all-to-all-start.1 = ((bf16[4,2,3072]{2,1,0:T(2,128)(2,1)}), bf16[4,2,3072]{2,1,0:T(2,128)(2,1)S(1)}, u32[]{:S(2)}, u32[]{:S(2)}) async-start(bf16[4,2,3072]{2,1,0:T(2,128)(2,1)} %reshape.96), calls=%async_computation.1 | async-start | bytes 98304 | tf_op jit(solution)/shard_map/all_to_all | solution.py:59
  29.0 0.7 multiply_reduce_fusion
  29.6 5.0 %all-to-all-done.1 = bf16[4,2,3072]{2,1,0:T(2,128)(2,1)S(1)} async-done(((bf16[4,2,3072]{2,1,0:T(2,128)(2,1)}), bf16[4,2,3072]{2,1,0:T(2,128)(2,1)S(1)}, u32[]{:S(2)}, u32[]{:S(2)}) %all-to-all-start.1) | async-done | bytes 49184 | tf_op jit(solution)/shard_map/all_to_all | solution.py:59
  34.8 0.6 multiply_reduce_fusion.1
  36.8 1.1 %collective-permute-done = f32[1,128]{1,0:T(1,128)S(1)} collective-permute-done((f32[1,128]{1,0:T(1,128)S(1)}, f32[1,128]{1,0:T(1,128)S(1)}, u32[]{:S(2)}, u32[]{:S(2)}) %collective-permute-start) | collective-permute-done | bytes 544 | tf_op jit(solution)/shard_map/ppermute | solution.py:36
  37.9 0.6 collective-permute-start.1
  38.5 3.0 %collective-permute-done.1 = f32[1,128]{1,0:T(1,128)S(1)} collective-permute-done((f32[1,128]{1,0:T(1,128)S(1)}, f32[1,128]{1,0:T(1,128)S(1)}, u32[]{:S(2)}, u32[]{:S(2)}) %collective-permute-start.1) | collective-permute-done | bytes 544 | tf_op jit(solution)/shard_map/ppermute | solution.py:36
  41.5 0.6 collective-permute-start.2
  42.0 3.0 %collective-permute-done.2 = f32[1,128]{1,0:T(1,128)S(1)} collective-permute-done((f32[1,128]{1,0:T(1,128)S(1)}, f32[1,128]{1,0:T(1,128)S(1)}, u32[]{:S(2)}, u32[]{:S(2)}) %collective-permute-start.2) | collective-permute-done | bytes 544 | tf_op jit(solution)/shard_map/ppermute | solution.py:36
  45.0 0.8 %collective-permute-start.3 = (f32[1,128]{1,0:T(1,128)S(1)}, f32[1,128]{1,0:T(1,128)S(1)}, u32[]{:S(2)}, u32[]{:S(2)}) collective-permute-start(f32[1,128]{1,0:T(1,128)S(1)} %add.55), channel_id=1, source_target_pairs={{0,8},{8,0},{16,24},{24,16},{1,9},{9,1},{17,25},{25,17},{2,10},{10... | collective-permute-start | bytes 1544 | tf_op jit(solution)/shard_map/ppermute | solution.py:36
  45.9 2.7 %collective-permute-done.3 = f32[1,128]{1,0:T(1,128)S(1)} collective-permute-done((f32[1,128]{1,0:T(1,128)S(1)}, f32[1,128]{1,0:T(1,128)S(1)}, u32[]{:S(2)}, u32[]{:S(2)}) %collective-permute-start.3) | collective-permute-done | bytes 544 | tf_op jit(solution)/shard_map/ppermute | solution.py:36
  48.6 0.7 collective-permute-start.4
  49.3 3.7 %collective-permute-done.4 = f32[1,128]{1,0:T(1,128)S(1)} collective-permute-done((f32[1,128]{1,0:T(1,128)S(1)}, f32[1,128]{1,0:T(1,128)S(1)}, u32[]{:S(2)}, u32[]{:S(2)}) %collective-permute-start.4) | collective-permute-done | bytes 544 | tf_op jit(solution)/shard_map/ppermute | solution.py:36
  53.2 1.6 %convert_bitcast_fusion.1 = (bf16[1,1,6144]{2,1,0:T(2,128)(2,1)S(1)}, f32[1,6144]{1,0:T(1,128)}, f32[1,6144]{1,0:T(1,128)}, f32[1,6144]{1,0:T(1,128)}) fusion(f32[1,6144]{1,0:T(1,128)} %param.14, f32[1,6144]{1,0:T(1,128)S(1)} %bitcast.47, f32[1,6144]{1,0:T(1,128)} %param.15, f32[1,6144]{1,0:T(1,128)} %param.16), kind=kLoop, calls=%fused_computation.23 | loop fusion | flops 98304 | bytes 184320
  54.7 13.4 %all-gather.2 = bf16[4,1,6144]{2,1,0:T(2,128)(2,1)S(1)} all-gather(bf16[1,1,6144]{2,1,0:T(2,128)(2,1)S(1)} %get-tuple-element.8), channel_id=2, replica_groups=mesh['expert'=4,'dp'=8] {'expert'}, dimensions={0}, use_global_device_ids=true | all-gather | bytes 61440 | tf_op jit(solution)/shard_map/all_gather | solution.py:67
  68.2 1.7 %convert_bitcast_fusion = (bf16[2,6144]{1,0:T(2,128)(2,1)S(1)}, f32[1,2,6144]{2,1,0:T(2,128)}, f32[1,2,6144]{2,1,0:T(2,128)}, f32[1,2,6144]{2,1,0:T(2,128)}) fusion(f32[1,2,6144]{2,1,0:T(2,128)S(1)} %copy-done.1, f32[6,6144]{1,0:T(8,128)S(1)} %convert_reduce_fusion, f32[]{:T(128)} %bitcast.6, f32[1,2,6144]{2,1,0:T(2,128)} %param.18, f32[1,2,6144]{2,1,0:T(2,128)} %param.19), kind=kLoop, calls=%fused_computation.22 | loop fusion | flops 208896 | bytes 368644 | tf_op jit(solution)/shard_map/convert_element_type | solution.py:69
  69.9 9.5 %all-gather.3 = bf16[8,6,6144]{2,1,0:T(8,128)(2,1)S(1)} all-gather(bf16[1,6,6144]{2,1,0:T(8,128)(2,1)S(1)} %maximum_bitcast_fusion), channel_id=3, replica_groups=mesh['expert'=4,'dp'=8] {'dp'}, dimensions={0}, use_global_device_ids=true | all-gather | bytes 663552 | tf_op jit(solution)/shard_map/all_gather | solution.py:71
  79.3 0.2 slice.24
  79.6 0.1 slice.23
  79.7 1.0 %copy.29 = bf16[8,4,6144]{2,0,1:T(8,128)(2,1)} copy(bf16[8,4,6144]{2,1,0:T(4,128)(2,1)S(1)} %slice.23) | data formatting | bytes 786432
  80.7 0.8 reshape.87
  (18 shorter events, 0.4 us)
Async XLA Ops:
  0.6 2.4 %copy-start = (bf16[256,6144]{1,0:T(8,128)(2,1)S(1)}, bf16[256,6144]{1,0:T(8,128)(2,1)}, u32[]{:S(2)}) copy-start(bf16[256,6144]{1,0:T(8,128)(2,1)} %param.11) | copy-start | bytes 9437188
  0.6 2.4 %copy-start.2 = (bf16[256,32]{0,1:T(8,128)(2,1)S(1)}, bf16[256,32]{0,1:T(8,128)(2,1)}, u32[]{:S(2)}) copy-start(bf16[256,32]{0,1:T(8,128)(2,1)} %param.10) | copy-start | bytes 49156
  4.4 63.8 %copy-start.1 = (f32[1,2,6144]{2,1,0:T(2,128)S(1)}, f32[1,2,6144]{2,1,0:T(2,128)}, u32[]{:S(2)}) copy-start(f32[1,2,6144]{2,1,0:T(2,128)} %param.17) | copy-start | bytes 147460
  24.1 10.6 %all-to-all-start.1 = ((bf16[4,2,3072]{2,1,0:T(2,128)(2,1)}), bf16[4,2,3072]{2,1,0:T(2,128)(2,1)S(1)}, u32[]{:S(2)}, u32[]{:S(2)}) async-start(bf16[4,2,3072]{2,1,0:T(2,128)(2,1)} %reshape.96), calls=%async_computation.1 | async-start | bytes 98304 | tf_op jit(solution)/shard_map/all_to_all | solution.py:59
  36.7 1.2 %collective-permute-start = (f32[1,128]{1,0:T(1,128)S(1)}, f32[1,128]{1,0:T(1,128)S(1)}, u32[]{:S(2)}, u32[]{:S(2)}) collective-permute-start(f32[1,128]{1,0:T(1,128)S(1)} %broadcast_in_dim.4), channel_id=1, source_target_pairs={{0,1},{1,0},{2,3},{3,2},{4,5},{5,4},{6,7},{7,6},{8,9},{9,8},{10,11... | collective-permute-start | bytes 1544 | tf_op jit(solution)/shard_map/ppermute | solution.py:36
  37.9 3.5 %collective-permute-start.1 = (f32[1,128]{1,0:T(1,128)S(1)}, f32[1,128]{1,0:T(1,128)S(1)}, u32[]{:S(2)}, u32[]{:S(2)}) collective-permute-start(f32[1,128]{1,0:T(1,128)S(1)} %broadcast_add_fusion), channel_id=1, source_target_pairs={{0,2},{1,3},{2,0},{3,1},{4,6},{5,7},{6,4},{7,5},{8,10},{9,11},{10,... | collective-permute-start | bytes 1544 | tf_op jit(solution)/shard_map/ppermute | solution.py:36
  41.5 3.5 %collective-permute-start.2 = (f32[1,128]{1,0:T(1,128)S(1)}, f32[1,128]{1,0:T(1,128)S(1)}, u32[]{:S(2)}, u32[]{:S(2)}) collective-permute-start(f32[1,128]{1,0:T(1,128)S(1)} %fusion.11), channel_id=1, source_target_pairs={{0,4},{1,5},{2,6},{3,7},{4,0},{5,1},{6,2},{7,3},{8,12},{9,13},{10,... | collective-permute-start | bytes 1544 | tf_op jit(solution)/shard_map/ppermute | solution.py:36
  45.0 3.5 %collective-permute-start.3 = (f32[1,128]{1,0:T(1,128)S(1)}, f32[1,128]{1,0:T(1,128)S(1)}, u32[]{:S(2)}, u32[]{:S(2)}) collective-permute-start(f32[1,128]{1,0:T(1,128)S(1)} %add.55), channel_id=1, source_target_pairs={{0,8},{8,0},{16,24},{24,16},{1,9},{9,1},{17,25},{25,17},{2,10},{10... | collective-permute-start | bytes 1544 | tf_op jit(solution)/shard_map/ppermute | solution.py:36
  48.6 4.4 %collective-permute-start.4 = (f32[1,128]{1,0:T(1,128)S(1)}, f32[1,128]{1,0:T(1,128)S(1)}, u32[]{:S(2)}, u32[]{:S(2)}) collective-permute-start(f32[1,128]{1,0:T(1,128)S(1)} %add.56), channel_id=1, source_target_pairs={{0,16},{8,24},{16,0},{24,8},{1,17},{9,25},{17,1},{25,9},{2,18},{10... | collective-permute-start | bytes 1544 | tf_op jit(solution)/shard_map/ppermute | solution.py:36

commit v2 on v0

--- a/solution.py
+++ b/solution.py
@@ -3,6 +3,8 @@
 import jax
 import jax.numpy as jnp
 from jax import lax
+from jax.experimental import pallas as pl
+from jax.experimental.pallas import tpu as pltpu
 from jax.sharding import PartitionSpec as P
 
 beta_first = 0.9
@@ -14,12 +16,6 @@
 adam_eps = 1e-08
 
 
-def contract_rows(left, right):
-    return lax.dot_general(
-        left, right, (((0,), (0,)), ((), ())), preferred_element_type=jnp.float32
-    )
-
-
 def adamw(grad, weight, moment, second, factor):
     scaled = factor * grad
     moment_new = beta_first * moment + (1.0 - beta_first) * scaled
@@ -29,30 +25,162 @@
     return (weight_new, moment_new, second_new)
 
 
+class Plan:
+    def __init__(self, n_expert, n_dp, rows_a, rows_e):
+        self.n_expert, self.n_dp, self.rows_a, self.rows_e = n_expert, n_dp, rows_a, rows_e
+        self.chips = n_dp // 2
+        self.split = n_expert * rows_a
+        self.chunk = -(-(self.split + rows_e) // 8) * 8
+        self.rows = n_dp * self.chunk
+
+    def columns(self, place, me_dp, me_ex):
+        half = place // (self.chips * self.chunk)
+        chip = (place // self.chunk) % self.chips
+        row = place % self.chunk
+        owner = (2 * chip + half) ^ me_dp
+        expert = (row // self.rows_a) ^ me_ex
+        attn = (expert * self.n_dp + owner) * self.rows_a + row % self.rows_a
+        exp = owner * self.rows_e + row - self.split
+        attn = jnp.where(row < self.split, attn, -1)
+        exp = jnp.where((row >= self.split) & (row < self.split + self.rows_e), exp, -1)
+        return attn, exp
+
+
+def select(place, index):
+    return (place == index).astype(jnp.bfloat16)
+
+
+def dot(left, right):
+    return lax.dot_general(left, right, (((1,), (0,)), ((), ())), preferred_element_type=jnp.float32)
+
+
+def terms_kernel(plan, act_a, dy_a, act_e, dy_e, keep, send, left_a, left_e):
+    @pl.when(pl.program_id(0) == 0)
+    def _():
+        me_dp, me_ex = lax.axis_index("dp"), lax.axis_index("expert")
+        count_a, count_e = act_a.shape[0], act_e.shape[0]
+        place = lax.broadcasted_iota(jnp.int32, (plan.rows, count_a), 0)
+        want, _unused = plan.columns(place, me_dp, me_ex)
+        pick = select(want, lax.broadcasted_iota(jnp.int32, (plan.rows, count_a), 1))
+        left_a[...] = dot(pick, act_a[...]).astype(jnp.bfloat16)
+        place = lax.broadcasted_iota(jnp.int32, (plan.rows, count_e), 0)
+        _unused, want = plan.columns(place, me_dp, me_ex)
+        pick = select(want, lax.broadcasted_iota(jnp.int32, (plan.rows, count_e), 1))
+        left_e[...] = dot(pick, act_e[...]).astype(jnp.bfloat16)
+
+    terms = dot(left_a[...], dy_a[...]) + dot(left_e[...], dy_e[...])
+    half = plan.rows // 2
+    keep[...] = terms[:half]
+    send[...] = terms[half:].astype(jnp.bfloat16)
+
+
+def make_terms(plan, act_a, dy_a, act_e, dy_e):
+    width = dy_a.shape[1]
+    tile = width // 4
+    half = plan.rows // 2
+    return pl.pallas_call(
+        lambda *refs: terms_kernel(plan, *refs),
+        grid=(width // tile,),
+        in_specs=[
+            pl.BlockSpec(act_a.shape, lambda i: (0, 0)),
+            pl.BlockSpec((dy_a.shape[0], tile), lambda i: (0, i)),
+            pl.BlockSpec(act_e.shape, lambda i: (0, 0)),
+            pl.BlockSpec((dy_e.shape[0], tile), lambda i: (0, i)),
+        ],
+        out_specs=[pl.BlockSpec((half, tile), lambda i: (0, i))] * 2,
+        out_shape=[
+            jax.ShapeDtypeStruct((half, width), jnp.float32),
+            jax.ShapeDtypeStruct((half, width), jnp.bfloat16),
+        ],
+        scratch_shapes=[
+            pltpu.VMEM((plan.rows, act_a.shape[1]), jnp.bfloat16),
+            pltpu.VMEM((plan.rows, act_e.shape[1]), jnp.bfloat16),
+        ],
+        compiler_params=pltpu.CompilerParams(vmem_limit_bytes=48 * 1024 * 1024),
+    )(act_a, dy_a, act_e, dy_e)
+
+
+def order_kernel(plan, n_parts, *refs):
+    parts, (attn, exp) = refs[:n_parts], refs[n_parts:]
+    me_dp, me_ex = lax.axis_index("dp"), lax.axis_index("expert")
+    rows = jnp.concatenate([part[...].astype(jnp.float32) for part in parts], axis=0).astype(jnp.bfloat16)
+    count_a, count_e = attn.shape[0], exp.shape[1]
+    place = lax.broadcasted_iota(jnp.int32, (count_a, plan.rows), 1)
+    want, _unused = plan.columns(place, me_dp, me_ex)
+    attn[...] = dot(select(want, lax.broadcasted_iota(jnp.int32, (count_a, plan.rows), 0)), rows).astype(jnp.bfloat16)
+    place = lax.broadcasted_iota(jnp.int32, (count_e, plan.rows), 1)
+    _unused, want = plan.columns(place, me_dp, me_ex)
+    exp[0] = dot(select(want, lax.broadcasted_iota(jnp.int32, (count_e, plan.rows), 0)), rows).astype(jnp.bfloat16)
+
+
+def put_in_order(plan, parts):
+    width = parts[0].shape[1]
+    tile = width // 4
+    count_a = plan.n_expert * plan.n_dp * plan.rows_a
+    count_e = plan.n_dp * plan.rows_e
+    return pl.pallas_call(
+        lambda *refs: order_kernel(plan, len(parts), *refs),
+        grid=(width // tile,),
+        in_specs=[pl.BlockSpec((part.shape[0], tile), lambda i: (0, i)) for part in parts],
+        out_specs=[
+            pl.BlockSpec((count_a, tile), lambda i: (0, i)),
+            pl.BlockSpec((1, count_e, tile), lambda i: (0, 0, i)),
+        ],
+        out_shape=[
+            jax.ShapeDtypeStruct((count_a, width), jnp.bfloat16),
+            jax.ShapeDtypeStruct((1, count_e, width), jnp.bfloat16),
+        ],
+        compiler_params=pltpu.CompilerParams(vmem_limit_bytes=48 * 1024 * 1024),
+    )(*parts)
+
+
+def swap(value, axis, distance):
+    size = lax.axis_size(axis)
+    return lax.ppermute(value, axis, [(i, i ^ distance) for i in range(size)])
+
+
 def body(act_attn, dy_attn, act_exp, dy_exp, w_attn, m_attn, v_attn, w_exp, m_exp, v_exp):
     width = w_attn.shape[1]
     n_expert = lax.axis_size("expert")
+    n_dp = lax.axis_size("dp")
+    rows_a, rows_e = w_attn.shape[0], w_exp.shape[1]
+    plan = Plan(n_expert, n_dp, rows_a, rows_e)
     total_params = width * (act_attn.shape[1] + n_expert * act_exp.shape[2])
     limit = 0.5 * math.sqrt(total_params)
-    g_attn = lax.psum_scatter(
-        contract_rows(act_attn, dy_attn), ("expert", "dp"), scatter_dimension=0, tiled=True
-    )
-    sq_attn = jnp.sum(g_attn * g_attn)
-    local_act = act_exp[0]
-    local_dy = dy_exp[0]
-    g_exp = lax.psum_scatter(
-        contract_rows(local_act, local_dy), "dp", scatter_dimension=0, tiled=True
-    )
-    sq_exp = jnp.sum(g_exp * g_exp)
-    summed = lax.psum((sq_attn, sq_exp), ("expert", "dp"))
-    total = summed[0] + summed[1]
-    norm = jnp.sqrt(total)
+    chips, chunk, split = plan.chips, plan.chunk, plan.split
+
+    keep, send = make_terms(plan, act_attn.T, dy_attn, act_exp[0].T, dy_exp[0])
+    got = swap(send, "dp", 1)
+    sums = [
+        keep[c * chunk : (c + 1) * chunk] + got[c * chunk : (c + 1) * chunk].astype(jnp.float32)
+        for c in range(chips)
+    ]
+    got = [swap(sums[c].astype(jnp.bfloat16), "dp", 2 * c) for c in range(1, chips)]
+    part = sums[0] + sum(piece.astype(jnp.float32) for piece in got)
+    g_exp = part[split : split + rows_e]
+    got = [
+        swap(part[q * rows_a : (q + 1) * rows_a].astype(jnp.bfloat16), "expert", q) for q in range(1, n_expert)
+    ]
+    g_attn = part[:rows_a] + sum(piece.astype(jnp.float32) for piece in got)
+    square = jnp.sum(g_attn * g_attn) + jnp.sum(g_exp * g_exp)
+    square = jnp.full((1, 128), square)
+    square = square + swap(square, "dp", 1)
+    square = square + sum([swap(square, "dp", 2 * c) for c in range(1, chips)])
+    square = square + sum([swap(square, "expert", q) for q in range(1, n_expert)])
+    norm = jnp.sqrt(square[0, 0])
     factor = jnp.minimum(1.0, limit / (norm + 1e-06))
     wa_new, ma_new, va_new = adamw(g_attn, w_attn, m_attn, v_attn, factor)
     we_new, me_new, ve_new = adamw(g_exp[None], w_exp, m_exp, v_exp, factor)
-    attn_half = wa_new.astype(jnp.bfloat16)
-    attn_full = lax.all_gather(attn_half, ("expert", "dp"), axis=0, tiled=True)
-    expert_full = lax.all_gather(we_new.astype(jnp.bfloat16), "dp", axis=1, tiled=True)
+
+    half_a = wa_new.astype(jnp.bfloat16)
+    mine = [half_a] + [swap(half_a, "expert", q) for q in range(1, n_expert)]
+    mine.append(we_new[0].astype(jnp.bfloat16))
+    if chunk > split + rows_e:
+        mine.append(jnp.zeros((chunk - split - rows_e, width), jnp.bfloat16))
+    mine = jnp.concatenate(mine, axis=0)
+    near = [mine] + [swap(mine, "dp", 2 * c) for c in range(1, chips)]
+    far = [swap(piece, "dp", 1) for piece in near]
+    attn_full, expert_full = put_in_order(plan, near + far)
     return (wa_new, ma_new, va_new, we_new, me_new, ve_new, attn_full, expert_full)
 
 

time: 309 us -> 66.4 us (0.21)
  waiting for transfers between devices: 187 us -> 26.7 us
  blocking collectives: 90.4 us -> 0 us
  starting transfers between devices: 0.08 us -> 25.3 us
  between operations: 16.8 us -> 2.21 us
  matrix products: 4.91 us -> 0 us
  Pallas kernels: 0 us -> 3.77 us
  other arithmetic: 6.67 us -> 3.07 us
    unnamed x4 -> x0, waiting for transfers between devices: 187 us -> none
    all_gather x2 -> x0, blocking collectives: 51.2 us -> none  [the longest x1 42.8 us: body(): attn_full = lax.all_gather(attn_half, ('expert', 'dp'), axis=0, tiled=True)]
    psum x1 -> x0, blocking collectives: 39.2 us -> none  [body(): summed = lax.psum((sq_attn, sq_exp), ('expert', 'dp'))]
    ppermute x0 -> x24, waiting for transfers between devices: none -> 26.7 us  [swap(): return lax.ppermute(value, axis, [(i, i ^ distance) for i in range(size)])]
    ppermute x0 -> x24, starting transfers between devices: none -> 25.3 us  [swap(): return lax.ppermute(value, axis, [(i, i ^ distance) for i in range(size)])]
    dot_general x2 -> x0, matrix products: 4.91 us -> none  [contract_rows(): lax.dot_general(left, right, (((0,), (0,)), ((), ())), preferred_element_...]
    pallas_call x0 -> x2, Pallas kernels: none -> 3.77 us  [the longest x1 1.92 us: make_terms(): pl.pallas_call(lambda *refs: terms_kernel(plan, *refs), grid=(width // ti...]
  transfers between devices with their start and end apart: 2 -> 24, of which waited for: 2 -> 18; matrix products, arithmetic and copies ran while one was open for 1% -> 2% of each run, Pallas kernels for 0% -> 0%
where the time goes in v2:
time: 66.4 us; the launch traced here: 66.1 us
  waiting for transfers between devices  26.7 us (40%)
  starting transfers between devices  25.3 us (38%)
  local copies, waits for them, and re-layouts  5.02 us (8%)
  Pallas kernels  3.77 us (6%)
  other arithmetic  3.07 us (5%)
  between operations  2.21 us (3%)
    ppermute x24, waiting for transfers between devices, swap(): return lax.ppermute(value, axis, [(i, i ^ distance) for i in range(size)])  26.7 us
    ppermute x24, starting transfers between devices, swap(): return lax.ppermute(value, axis, [(i, i ^ distance) for i in range(size)])  25.3 us
    unnamed x20, local copies, waits for them, and re-layouts  4.72 us
    pallas_call x1, Pallas kernels, make_terms(): pl.pallas_call(lambda *refs: terms_kernel(plan, *refs), grid=(width // ti...  1.92 us
    pallas_call x1, Pallas kernels, put_in_order(): pl.pallas_call(lambda *refs: order_kernel(plan, len(parts), *refs), grid=...  1.85 us
  transfers between devices with their start and end apart: 24, of which 18 were waited for; matrix products, arithmetic and copies ran while one was open for 2% of the time, Pallas kernels for 0%

profile of v2, /device:TPU:0, one launch (start us, length us, event | category | flops | bytes accessed | tf_op | source)
XLA Modules:
  0.0 66.1 jit_solution(15345783952088183645)
XLA Ops:
  0.6 1.9 %copy-done = bf16[256,6144]{1,0:T(8,128)(2,1)S(1)} copy-done((bf16[256,6144]{1,0:T(8,128)(2,1)S(1)}, bf16[256,6144]{1,0:T(8,128)(2,1)}, u32[]{:S(2)}) %copy-start) | copy-done | bytes 3145752
  2.5 1.4 %copy-done.1 = bf16[1,128,6144]{2,1,0:T(8,128)(2,1)S(1)} copy-done((bf16[1,128,6144]{2,1,0:T(8,128)(2,1)S(1)}, bf16[1,128,6144]{2,1,0:T(8,128)(2,1)}, u32[]{:S(2)}) %copy-start.1) | copy-done | bytes 1572888
  5.4 1.9 %shard_map.161 = (f32[32,6144]{1,0:T(8,128)S(1)}, bf16[32,6144]{1,0:T(8,128)(2,1)S(1)}) custom-call(bf16[32,256]{1,0:T(8,128)(2,1)S(1)} %bitcast.18, bf16[256,6144]{1,0:T(8,128)(2,1)S(1)} %copy-done, bf16[16,128]{1,0:T(8,128)(2,1)S(1)} %bitcast.19, bf16[128,6144]{1,0:T(8,128)(2,1)S(1)} %bitcast.17), custom_call_target="tpu_custom_call" | custom-call | tf_op jit(solution)/shard_map/pallas_call | solution.py:81
  7.8 1.3 %collective-permute-done = bf16[32,6144]{1,0:T(8,128)(2,1)S(1)} collective-permute-done((bf16[32,6144]{1,0:T(8,128)(2,1)S(1)}, bf16[32,6144]{1,0:T(8,128)(2,1)S(1)}, u32[]{:S(2)}, u32[]{:S(2)}) %collective-permute-start) | collective-permute-done | bytes 393248 | tf_op jit(solution)/shard_map/ppermute | solution.py:139
  9.2 2.9 %collective-permute-start.1 = (bf16[8,6144]{1,0:T(8,128)(2,1)S(1)}, bf16[8,6144]{1,0:T(8,128)(2,1)S(1)}, u32[]{:S(2)}, u32[]{:S(2)}) collective-permute-start(bf16[8,6144]{1,0:T(8,128)(2,1)S(1)} %get-tuple-element.28), channel_id=1, source_target_pairs={{0,2},{1,3},{2,0},{3,1},{4,6},{5,7},{6,4},{7,5},{8,10},{9,11},{10,... | collective-permute-start | bytes 294920 | tf_op jit(solution)/shard_map/ppermute | solution.py:139
  12.2 1.5 %collective-permute-start.2 = (bf16[8,6144]{1,0:T(8,128)(2,1)S(1)}, bf16[8,6144]{1,0:T(8,128)(2,1)S(1)}, u32[]{:S(2)}, u32[]{:S(2)}) collective-permute-start(bf16[8,6144]{1,0:T(8,128)(2,1)S(1)} %get-tuple-element.30), channel_id=1, source_target_pairs={{0,4},{1,5},{2,6},{3,7},{4,0},{5,1},{6,2},{7,3},{8,12},{9,13},{10,... | collective-permute-start | bytes 294920 | tf_op jit(solution)/shard_map/ppermute | solution.py:139
  13.7 1.6 %collective-permute-done.1 = bf16[8,6144]{1,0:T(8,128)(2,1)S(1)} collective-permute-done((bf16[8,6144]{1,0:T(8,128)(2,1)S(1)}, bf16[8,6144]{1,0:T(8,128)(2,1)S(1)}, u32[]{:S(2)}, u32[]{:S(2)}) %collective-permute-start.1) | collective-permute-done | bytes 98336 | tf_op jit(solution)/shard_map/ppermute | solution.py:139
  15.3 2.6 %collective-permute-done.2 = bf16[8,6144]{1,0:T(8,128)(2,1)S(1)} collective-permute-done((bf16[8,6144]{1,0:T(8,128)(2,1)S(1)}, bf16[8,6144]{1,0:T(8,128)(2,1)S(1)}, u32[]{:S(2)}, u32[]{:S(2)}) %collective-permute-start.2) | collective-permute-done | bytes 98336 | tf_op jit(solution)/shard_map/ppermute | solution.py:139
  17.9 1.3 %collective-permute-done.3 = bf16[8,6144]{1,0:T(8,128)(2,1)S(1)} collective-permute-done((bf16[8,6144]{1,0:T(8,128)(2,1)S(1)}, bf16[8,6144]{1,0:T(8,128)(2,1)S(1)}, u32[]{:S(2)}, u32[]{:S(2)}) %collective-permute-start.3) | collective-permute-done | bytes 98336 | tf_op jit(solution)/shard_map/ppermute | solution.py:139
  19.3 1.6 %collective-permute-start.4 = (bf16[1,6144]{1,0:T(2,128)(2,1)S(1)}, bf16[1,6144]{1,0:T(2,128)(2,1)S(1)}, u32[]{:S(2)}, u32[]{:S(2)}) collective-permute-start(bf16[1,6144]{1,0:T(2,128)(2,1)S(1)} %get-tuple-element.31), channel_id=1, source_target_pairs={{0,8},{8,0},{16,24},{24,16},{1,9},{9,1},{17,25},{25,17},{2,10},{10... | collective-permute-start | bytes 36872 | tf_op jit(solution)/shard_map/ppermute | solution.py:139
  21.0 2.6 %collective-permute-start.5 = (bf16[1,6144]{1,0:T(2,128)(2,1)S(1)}, bf16[1,6144]{1,0:T(2,128)(2,1)S(1)}, u32[]{:S(2)}, u32[]{:S(2)}) collective-permute-start(bf16[1,6144]{1,0:T(2,128)(2,1)S(1)} %get-tuple-element.33), channel_id=1, source_target_pairs={{0,16},{8,24},{16,0},{24,8},{1,17},{9,25},{17,1},{25,9},{2,18},{10... | collective-permute-start | bytes 36872 | tf_op jit(solution)/shard_map/ppermute | solution.py:139
  24.4 1.4 %collective-permute-done.5 = bf16[1,6144]{1,0:T(2,128)(2,1)S(1)} collective-permute-done((bf16[1,6144]{1,0:T(2,128)(2,1)S(1)}, bf16[1,6144]{1,0:T(2,128)(2,1)S(1)}, u32[]{:S(2)}, u32[]{:S(2)}) %collective-permute-start.5) | collective-permute-done | bytes 12320 | tf_op jit(solution)/shard_map/ppermute | solution.py:139
  25.8 3.3 %collective-permute-done.6 = bf16[1,6144]{1,0:T(2,128)(2,1)S(1)} collective-permute-done((bf16[1,6144]{1,0:T(2,128)(2,1)S(1)}, bf16[1,6144]{1,0:T(2,128)(2,1)S(1)}, u32[]{:S(2)}, u32[]{:S(2)}) %collective-permute-start.6) | collective-permute-done | bytes 12320 | tf_op jit(solution)/shard_map/ppermute | solution.py:139
  31.2 1.1 %collective-permute-done.7 = f32[1,128]{1,0:T(1,128)S(1)} collective-permute-done((f32[1,128]{1,0:T(1,128)S(1)}, f32[1,128]{1,0:T(1,128)S(1)}, u32[]{:S(2)}, u32[]{:S(2)}) %collective-permute-start.7) | collective-permute-done | bytes 544 | tf_op jit(solution)/shard_map/ppermute | solution.py:139
  32.4 1.2 %collective-permute-start.10 = (f32[1,128]{1,0:T(1,128)S(1)}, f32[1,128]{1,0:T(1,128)S(1)}, u32[]{:S(2)}, u32[]{:S(2)}) collective-permute-start(f32[1,128]{1,0:T(1,128)S(1)} %broadcast_add_fusion), channel_id=1, source_target_pairs={{0,6},{1,7},{2,4},{3,5},{4,2},{5,3},{6,0},{7,1},{8,14},{9,15},{10,... | collective-permute-start | bytes 1544 | tf_op jit(solution)/shard_map/ppermute | solution.py:139
  33.5 1.5 %collective-permute-start.8 = (f32[1,128]{1,0:T(1,128)S(1)}, f32[1,128]{1,0:T(1,128)S(1)}, u32[]{:S(2)}, u32[]{:S(2)}) collective-permute-start(f32[1,128]{1,0:T(1,128)S(1)} %broadcast_add_fusion), channel_id=1, source_target_pairs={{0,2},{1,3},{2,0},{3,1},{4,6},{5,7},{6,4},{7,5},{8,10},{9,11},{10,... | collective-permute-start | bytes 1544 | tf_op jit(solution)/shard_map/ppermute | solution.py:139
  35.0 0.8 %collective-permute-start.9 = (f32[1,128]{1,0:T(1,128)S(1)}, f32[1,128]{1,0:T(1,128)S(1)}, u32[]{:S(2)}, u32[]{:S(2)}) collective-permute-start(f32[1,128]{1,0:T(1,128)S(1)} %broadcast_add_fusion), channel_id=1, source_target_pairs={{0,4},{1,5},{2,6},{3,7},{4,0},{5,1},{6,2},{7,3},{8,12},{9,13},{10,... | collective-permute-start | bytes 1544 | tf_op jit(solution)/shard_map/ppermute | solution.py:139
  35.8 0.9 %collective-permute-done.10 = f32[1,128]{1,0:T(1,128)S(1)} collective-permute-done((f32[1,128]{1,0:T(1,128)S(1)}, f32[1,128]{1,0:T(1,128)S(1)}, u32[]{:S(2)}, u32[]{:S(2)}) %collective-permute-start.10) | collective-permute-done | bytes 544 | tf_op jit(solution)/shard_map/ppermute | solution.py:139
  37.1 1.5 %collective-permute-done.9 = f32[1,128]{1,0:T(1,128)S(1)} collective-permute-done((f32[1,128]{1,0:T(1,128)S(1)}, f32[1,128]{1,0:T(1,128)S(1)}, u32[]{:S(2)}, u32[]{:S(2)}) %collective-permute-start.9) | collective-permute-done | bytes 544 | tf_op jit(solution)/shard_map/ppermute | solution.py:139
  38.6 0.8 %collective-permute-start.12 = (f32[1,128]{1,0:T(1,128)S(1)}, f32[1,128]{1,0:T(1,128)S(1)}, u32[]{:S(2)}, u32[]{:S(2)}) collective-permute-start(f32[1,128]{1,0:T(1,128)S(1)} %add_add_fusion.2), channel_id=1, source_target_pairs={{0,16},{8,24},{16,0},{24,8},{1,17},{9,25},{17,1},{25,9},{2,18},{10... | collective-permute-start | bytes 1544 | tf_op jit(solution)/shard_map/ppermute | solution.py:139
  39.4 3.6 %collective-permute-start.13 = (f32[1,128]{1,0:T(1,128)S(1)}, f32[1,128]{1,0:T(1,128)S(1)}, u32[]{:S(2)}, u32[]{:S(2)}) collective-permute-start(f32[1,128]{1,0:T(1,128)S(1)} %add_add_fusion.2), channel_id=1, source_target_pairs={{0,24},{8,16},{16,8},{24,0},{1,25},{9,17},{17,9},{25,1},{2,26},{10... | collective-permute-start | bytes 1544 | tf_op jit(solution)/shard_map/ppermute | solution.py:139
  43.1 1.7 %collective-permute-done.13 = f32[1,128]{1,0:T(1,128)S(1)} collective-permute-done((f32[1,128]{1,0:T(1,128)S(1)}, f32[1,128]{1,0:T(1,128)S(1)}, u32[]{:S(2)}, u32[]{:S(2)}) %collective-permute-start.13) | collective-permute-done | bytes 544 | tf_op jit(solution)/shard_map/ppermute | solution.py:139
  44.9 0.8 %fusion.4 = (bf16[1,6144]{1,0:T(2,128)(2,1)S(1)}, f32[1,6144]{1,0:T(1,128)}, f32[1,6144]{1,0:T(1,128)}, f32[1,6144]{1,0:T(1,128)}) fusion(f32[1,6144]{1,0:T(1,128)S(1)} %copy-done.7, f32[1,6144]{1,0:T(1,128)S(1)} %get-tuple-element.25, f32[]{:T(128)} %bitcast.4, f32[1,6144]{1,0:T(1,128)S(1)} %copy-done.8, f32[1,6144]{1,0:T(1,128)S(1)} %copy-done.9), kind=kLoop, calls=%fused_computation.21 | loop fusion | flops 104448 | bytes 184324 | tf_op jit(solution)/shard_map/convert_element_type | solution.py:175
  46.0 3.8 %collective-permute-start.15 = (bf16[1,6144]{1,0:T(2,128)(2,1)S(1)}, bf16[1,6144]{1,0:T(2,128)(2,1)S(1)}, u32[]{:S(2)}, u32[]{:S(2)}) collective-permute-start(bf16[1,6144]{1,0:T(2,128)(2,1)S(1)} %get-tuple-element.20), channel_id=1, source_target_pairs={{0,16},{8,24},{16,0},{24,8},{1,17},{9,25},{17,1},{25,9},{2,18},{10... | collective-permute-start | bytes 36872 | tf_op jit(solution)/shard_map/ppermute | solution.py:139
  50.1 0.8 %convert_bitcast_fusion = (bf16[2,6144]{1,0:T(2,128)(2,1)S(1)}, f32[1,2,6144]{2,1,0:T(2,128)}, f32[1,2,6144]{2,1,0:T(2,128)}, f32[1,2,6144]{2,1,0:T(2,128)}) fusion(f32[1,2,6144]{2,1,0:T(2,128)S(1)} %copy-done.4, f32[8,6144]{1,0:T(8,128)S(1)} %get-tuple-element.27, f32[]{:T(128)} %bitcast.4, f32[1,2,6144]{2,1,0:T(2,128)S(1)} %copy-done.5, ...), kind=kLoop, calls=%fused_computation.14 | loop fusion | flops 208896 | bytes 368644 | tf_op jit(solution)/shard_map/convert_element_type | solution.py:177
  51.6 3.8 %collective-permute-done.16 = bf16[1,6144]{1,0:T(2,128)(2,1)S(1)} collective-permute-done((bf16[1,6144]{1,0:T(2,128)(2,1)S(1)}, bf16[1,6144]{1,0:T(2,128)(2,1)S(1)}, u32[]{:S(2)}, u32[]{:S(2)}) %collective-permute-start.16) | collective-permute-done | bytes 12320 | tf_op jit(solution)/shard_map/ppermute | solution.py:139
  56.3 1.1 %collective-permute-start.18 = (bf16[8,6144]{1,0:T(8,128)(2,1)S(1)}, bf16[8,6144]{1,0:T(8,128)(2,1)S(1)}, u32[]{:S(2)}, u32[]{:S(2)}) collective-permute-start(bf16[8,6144]{1,0:T(8,128)(2,1)S(1)} %concatenate.3.refs_0_), channel_id=1, source_target_pairs={{0,4},{1,5},{2,6},{3,7},{4,0},{5,1},{6,2},{7,3},{8,12},{9,13},{10,... | collective-permute-start | bytes 294920 | tf_op jit(solution)/shard_map/ppermute | solution.py:139
  57.5 1.8 %collective-permute-start.19 = (bf16[8,6144]{1,0:T(8,128)(2,1)S(1)}, bf16[8,6144]{1,0:T(8,128)(2,1)S(1)}, u32[]{:S(2)}, u32[]{:S(2)}) collective-permute-start(bf16[8,6144]{1,0:T(8,128)(2,1)S(1)} %concatenate.3.refs_0_), channel_id=1, source_target_pairs={{0,6},{1,7},{2,4},{3,5},{4,2},{5,3},{6,0},{7,1},{8,14},{9,15},{10,... | collective-permute-start | bytes 294920 | tf_op jit(solution)/shard_map/ppermute | solution.py:139
  59.3 1.1 %collective-permute-done.17.refs_1_ = bf16[8,6144]{1,0:T(8,128)(2,1)S(1)} collective-permute-done((bf16[8,6144]{1,0:T(8,128)(2,1)S(1)}, bf16[8,6144]{1,0:T(8,128)(2,1)S(1)}, u32[]{:S(2)}, u32[]{:S(2)}) %collective-permute-start.17) | collective-permute-done | bytes 98336 | tf_op jit(solution)/shard_map/ppermute | solution.py:139
  60.9 2.0 %collective-permute-done.19.refs_3_ = bf16[8,6144]{1,0:T(8,128)(2,1)S(1)} collective-permute-done((bf16[8,6144]{1,0:T(8,128)(2,1)S(1)}, bf16[8,6144]{1,0:T(8,128)(2,1)S(1)}, u32[]{:S(2)}, u32[]{:S(2)}) %collective-permute-start.19) | collective-permute-done | bytes 98336 | tf_op jit(solution)/shard_map/ppermute | solution.py:139
  63.0 1.3 %collective-permute-done.23.refs_7_ = bf16[8,6144]{1,0:T(8,128)(2,1)S(1)} collective-permute-done((bf16[8,6144]{1,0:T(8,128)(2,1)S(1)}, bf16[8,6144]{1,0:T(8,128)(2,1)S(1)}, u32[]{:S(2)}, u32[]{:S(2)}) %collective-permute-start.23) | collective-permute-done | bytes 98336 | tf_op jit(solution)/shard_map/ppermute | solution.py:139
  64.3 1.8 %shard_map.162 = (bf16[32,6144]{1,0:T(8,128)(2,1)}, bf16[1,16,6144]{2,1,0:T(8,128)(2,1)}) custom-call(bf16[8,6144]{1,0:T(8,128)(2,1)S(1)} %concatenate.3.refs_0_, bf16[8,6144]{1,0:T(8,128)(2,1)S(1)} %collective-permute-done.17.refs_1_, bf16[8,6144]{1,0:T(8,128)(2,1)S(1)} %collective-permute-done.18.refs_2_, ...), custom_call_target="tpu_custom_call" | custom-call | tf_op jit(solution)/shard_map/pallas_call | solution.py:121
  (51 shorter events, 6.8 us)
Async XLA Ops:
  0.6 1.9 %copy-start = (bf16[256,6144]{1,0:T(8,128)(2,1)S(1)}, bf16[256,6144]{1,0:T(8,128)(2,1)}, u32[]{:S(2)}) copy-start(bf16[256,6144]{1,0:T(8,128)(2,1)} %refs_1_.1) | copy-start | bytes 9437188
  2.5 1.4 %copy-start.1 = (bf16[1,128,6144]{2,1,0:T(8,128)(2,1)S(1)}, bf16[1,128,6144]{2,1,0:T(8,128)(2,1)}, u32[]{:S(2)}) copy-start(bf16[1,128,6144]{2,1,0:T(8,128)(2,1)} %param.13) | copy-start | bytes 4718596
  5.3 39.5 %copy-start.7 = (f32[1,6144]{1,0:T(1,128)S(1)}, f32[1,6144]{1,0:T(1,128)}, u32[]{:S(2)}) copy-start(f32[1,6144]{1,0:T(1,128)} %param.14) | copy-start | bytes 73732
  5.3 39.5 %copy-start.8 = (f32[1,6144]{1,0:T(1,128)S(1)}, f32[1,6144]{1,0:T(1,128)}, u32[]{:S(2)}) copy-start(f32[1,6144]{1,0:T(1,128)} %param.15) | copy-start | bytes 73732
  5.3 39.6 %copy-start.9 = (f32[1,6144]{1,0:T(1,128)S(1)}, f32[1,6144]{1,0:T(1,128)}, u32[]{:S(2)}) copy-start(f32[1,6144]{1,0:T(1,128)} %param.16) | copy-start | bytes 73732
  5.3 44.8 %copy-start.4 = (f32[1,2,6144]{2,1,0:T(2,128)S(1)}, f32[1,2,6144]{2,1,0:T(2,128)}, u32[]{:S(2)}) copy-start(f32[1,2,6144]{2,1,0:T(2,128)} %param.17) | copy-start | bytes 147460
  5.4 44.8 %copy-start.5 = (f32[1,2,6144]{2,1,0:T(2,128)S(1)}, f32[1,2,6144]{2,1,0:T(2,128)}, u32[]{:S(2)}) copy-start(f32[1,2,6144]{2,1,0:T(2,128)} %param.18) | copy-start | bytes 147460
  5.4 44.7 %copy-start.6 = (f32[1,2,6144]{2,1,0:T(2,128)S(1)}, f32[1,2,6144]{2,1,0:T(2,128)}, u32[]{:S(2)}) copy-start(f32[1,2,6144]{2,1,0:T(2,128)} %param.19) | copy-start | bytes 147460
  7.3 1.9 %collective-permute-start = (bf16[32,6144]{1,0:T(8,128)(2,1)S(1)}, bf16[32,6144]{1,0:T(8,128)(2,1)S(1)}, u32[]{:S(2)}, u32[]{:S(2)}) collective-permute-start(bf16[32,6144]{1,0:T(8,128)(2,1)S(1)} %get-tuple-element.13), channel_id=1, source_target_pairs={{0,1},{1,0},{2,3},{3,2},{4,5},{5,4},{6,7},{7,6},{8,9},{9,8},{10,11... | collective-permute-start | bytes 1179656 | tf_op jit(solution)/shard_map/ppermute | solution.py:139
  9.2 6.1 %collective-permute-start.1 = (bf16[8,6144]{1,0:T(8,128)(2,1)S(1)}, bf16[8,6144]{1,0:T(8,128)(2,1)S(1)}, u32[]{:S(2)}, u32[]{:S(2)}) collective-permute-start(bf16[8,6144]{1,0:T(8,128)(2,1)S(1)} %get-tuple-element.28), channel_id=1, source_target_pairs={{0,2},{1,3},{2,0},{3,1},{4,6},{5,7},{6,4},{7,5},{8,10},{9,11},{10,... | collective-permute-start | bytes 294920 | tf_op jit(solution)/shard_map/ppermute | solution.py:139
  12.2 5.8 %collective-permute-start.2 = (bf16[8,6144]{1,0:T(8,128)(2,1)S(1)}, bf16[8,6144]{1,0:T(8,128)(2,1)S(1)}, u32[]{:S(2)}, u32[]{:S(2)}) collective-permute-start(bf16[8,6144]{1,0:T(8,128)(2,1)S(1)} %get-tuple-element.30), channel_id=1, source_target_pairs={{0,4},{1,5},{2,6},{3,7},{4,0},{5,1},{6,2},{7,3},{8,12},{9,13},{10,... | collective-permute-start | bytes 294920 | tf_op jit(solution)/shard_map/ppermute | solution.py:139
  13.7 5.5 %collective-permute-start.3 = (bf16[8,6144]{1,0:T(8,128)(2,1)S(1)}, bf16[8,6144]{1,0:T(8,128)(2,1)S(1)}, u32[]{:S(2)}, u32[]{:S(2)}) collective-permute-start(bf16[8,6144]{1,0:T(8,128)(2,1)S(1)} %get-tuple-element.29), channel_id=1, source_target_pairs={{0,6},{1,7},{2,4},{3,5},{4,2},{5,3},{6,0},{7,1},{8,14},{9,15},{10,... | collective-permute-start | bytes 294920 | tf_op jit(solution)/shard_map/ppermute | solution.py:139
  19.3 5.1 %collective-permute-start.4 = (bf16[1,6144]{1,0:T(2,128)(2,1)S(1)}, bf16[1,6144]{1,0:T(2,128)(2,1)S(1)}, u32[]{:S(2)}, u32[]{:S(2)}) collective-permute-start(bf16[1,6144]{1,0:T(2,128)(2,1)S(1)} %get-tuple-element.31), channel_id=1, source_target_pairs={{0,8},{8,0},{16,24},{24,16},{1,9},{9,1},{17,25},{25,17},{2,10},{10... | collective-permute-start | bytes 36872 | tf_op jit(solution)/shard_map/ppermute | solution.py:139
  21.0 4.9 %collective-permute-start.5 = (bf16[1,6144]{1,0:T(2,128)(2,1)S(1)}, bf16[1,6144]{1,0:T(2,128)(2,1)S(1)}, u32[]{:S(2)}, u32[]{:S(2)}) collective-permute-start(bf16[1,6144]{1,0:T(2,128)(2,1)S(1)} %get-tuple-element.33), channel_id=1, source_target_pairs={{0,16},{8,24},{16,0},{24,8},{1,17},{9,25},{17,1},{25,9},{2,18},{10... | collective-permute-start | bytes 36872 | tf_op jit(solution)/shard_map/ppermute | solution.py:139
  23.6 5.6 %collective-permute-start.6 = (bf16[1,6144]{1,0:T(2,128)(2,1)S(1)}, bf16[1,6144]{1,0:T(2,128)(2,1)S(1)}, u32[]{:S(2)}, u32[]{:S(2)}) collective-permute-start(bf16[1,6144]{1,0:T(2,128)(2,1)S(1)} %get-tuple-element.32), channel_id=1, source_target_pairs={{0,24},{8,16},{16,8},{24,0},{1,25},{9,17},{17,9},{25,1},{2,26},{10... | collective-permute-start | bytes 36872 | tf_op jit(solution)/shard_map/ppermute | solution.py:139
  31.2 1.2 %collective-permute-start.7 = (f32[1,128]{1,0:T(1,128)S(1)}, f32[1,128]{1,0:T(1,128)S(1)}, u32[]{:S(2)}, u32[]{:S(2)}) collective-permute-start(f32[1,128]{1,0:T(1,128)S(1)} %broadcast_in_dim.7), channel_id=1, source_target_pairs={{0,1},{1,0},{2,3},{3,2},{4,5},{5,4},{6,7},{7,6},{8,9},{9,8},{10,11... | collective-permute-start | bytes 1544 | tf_op jit(solution)/shard_map/ppermute | solution.py:139
  32.4 4.4 %collective-permute-start.10 = (f32[1,128]{1,0:T(1,128)S(1)}, f32[1,128]{1,0:T(1,128)S(1)}, u32[]{:S(2)}, u32[]{:S(2)}) collective-permute-start(f32[1,128]{1,0:T(1,128)S(1)} %broadcast_add_fusion), channel_id=1, source_target_pairs={{0,6},{1,7},{2,4},{3,5},{4,2},{5,3},{6,0},{7,1},{8,14},{9,15},{10,... | collective-permute-start | bytes 1544 | tf_op jit(solution)/shard_map/ppermute | solution.py:139
  33.5 3.5 %collective-permute-start.8 = (f32[1,128]{1,0:T(1,128)S(1)}, f32[1,128]{1,0:T(1,128)S(1)}, u32[]{:S(2)}, u32[]{:S(2)}) collective-permute-start(f32[1,128]{1,0:T(1,128)S(1)} %broadcast_add_fusion), channel_id=1, source_target_pairs={{0,2},{1,3},{2,0},{3,1},{4,6},{5,7},{6,4},{7,5},{8,10},{9,11},{10,... | collective-permute-start | bytes 1544 | tf_op jit(solution)/shard_map/ppermute | solution.py:139
  35.0 3.5 %collective-permute-start.9 = (f32[1,128]{1,0:T(1,128)S(1)}, f32[1,128]{1,0:T(1,128)S(1)}, u32[]{:S(2)}, u32[]{:S(2)}) collective-permute-start(f32[1,128]{1,0:T(1,128)S(1)} %broadcast_add_fusion), channel_id=1, source_target_pairs={{0,4},{1,5},{2,6},{3,7},{4,0},{5,1},{6,2},{7,3},{8,12},{9,13},{10,... | collective-permute-start | bytes 1544 | tf_op jit(solution)/shard_map/ppermute | solution.py:139
  38.6 4.4 %collective-permute-start.11 = (f32[1,128]{1,0:T(1,128)S(1)}, f32[1,128]{1,0:T(1,128)S(1)}, u32[]{:S(2)}, u32[]{:S(2)}) collective-permute-start(f32[1,128]{1,0:T(1,128)S(1)} %add_add_fusion.2), channel_id=1, source_target_pairs={{0,8},{8,0},{16,24},{24,16},{1,9},{9,1},{17,25},{25,17},{2,10},{10... | collective-permute-start | bytes 1544 | tf_op jit(solution)/shard_map/ppermute | solution.py:139
  38.6 4.5 %collective-permute-start.12 = (f32[1,128]{1,0:T(1,128)S(1)}, f32[1,128]{1,0:T(1,128)S(1)}, u32[]{:S(2)}, u32[]{:S(2)}) collective-permute-start(f32[1,128]{1,0:T(1,128)S(1)} %add_add_fusion.2), channel_id=1, source_target_pairs={{0,16},{8,24},{16,0},{24,8},{1,17},{9,25},{17,1},{25,9},{2,18},{10... | collective-permute-start | bytes 1544 | tf_op jit(solution)/shard_map/ppermute | solution.py:139
  39.4 5.3 %collective-permute-start.13 = (f32[1,128]{1,0:T(1,128)S(1)}, f32[1,128]{1,0:T(1,128)S(1)}, u32[]{:S(2)}, u32[]{:S(2)}) collective-permute-start(f32[1,128]{1,0:T(1,128)S(1)} %add_add_fusion.2), channel_id=1, source_target_pairs={{0,24},{8,16},{16,8},{24,0},{1,25},{9,17},{17,9},{25,1},{2,26},{10... | collective-permute-start | bytes 1544 | tf_op jit(solution)/shard_map/ppermute | solution.py:139
  45.7 5.2 %collective-permute-start.14 = (bf16[1,6144]{1,0:T(2,128)(2,1)S(1)}, bf16[1,6144]{1,0:T(2,128)(2,1)S(1)}, u32[]{:S(2)}, u32[]{:S(2)}) collective-permute-start(bf16[1,6144]{1,0:T(2,128)(2,1)S(1)} %get-tuple-element.20), channel_id=1, source_target_pairs={{0,8},{8,0},{16,24},{24,16},{1,9},{9,1},{17,25},{25,17},{2,10},{10... | collective-permute-start | bytes 36872 | tf_op jit(solution)/shard_map/ppermute | solution.py:139
  46.0 5.6 %collective-permute-start.15 = (bf16[1,6144]{1,0:T(2,128)(2,1)S(1)}, bf16[1,6144]{1,0:T(2,128)(2,1)S(1)}, u32[]{:S(2)}, u32[]{:S(2)}) collective-permute-start(bf16[1,6144]{1,0:T(2,128)(2,1)S(1)} %get-tuple-element.20), channel_id=1, source_target_pairs={{0,16},{8,24},{16,0},{24,8},{1,17},{9,25},{17,1},{25,9},{2,18},{10... | collective-permute-start | bytes 36872 | tf_op jit(solution)/shard_map/ppermute | solution.py:139
  49.8 5.6 %collective-permute-start.16 = (bf16[1,6144]{1,0:T(2,128)(2,1)S(1)}, bf16[1,6144]{1,0:T(2,128)(2,1)S(1)}, u32[]{:S(2)}, u32[]{:S(2)}) collective-permute-start(bf16[1,6144]{1,0:T(2,128)(2,1)S(1)} %get-tuple-element.20), channel_id=1, source_target_pairs={{0,24},{8,16},{16,8},{24,0},{1,25},{9,17},{17,9},{25,1},{2,26},{10... | collective-permute-start | bytes 36872 | tf_op jit(solution)/shard_map/ppermute | solution.py:139
  55.7 4.7 %collective-permute-start.17 = (bf16[8,6144]{1,0:T(8,128)(2,1)S(1)}, bf16[8,6144]{1,0:T(8,128)(2,1)S(1)}, u32[]{:S(2)}, u32[]{:S(2)}) collective-permute-start(bf16[8,6144]{1,0:T(8,128)(2,1)S(1)} %concatenate.3.refs_0_), channel_id=1, source_target_pairs={{0,2},{1,3},{2,0},{3,1},{4,6},{5,7},{6,4},{7,5},{8,10},{9,11},{10,... | collective-permute-start | bytes 294920 | tf_op jit(solution)/shard_map/ppermute | solution.py:139
  56.3 4.6 %collective-permute-start.18 = (bf16[8,6144]{1,0:T(8,128)(2,1)S(1)}, bf16[8,6144]{1,0:T(8,128)(2,1)S(1)}, u32[]{:S(2)}, u32[]{:S(2)}) collective-permute-start(bf16[8,6144]{1,0:T(8,128)(2,1)S(1)} %concatenate.3.refs_0_), channel_id=1, source_target_pairs={{0,4},{1,5},{2,6},{3,7},{4,0},{5,1},{6,2},{7,3},{8,12},{9,13},{10,... | collective-permute-start | bytes 294920 | tf_op jit(solution)/shard_map/ppermute | solution.py:139
  57.5 5.5 %collective-permute-start.19 = (bf16[8,6144]{1,0:T(8,128)(2,1)S(1)}, bf16[8,6144]{1,0:T(8,128)(2,1)S(1)}, u32[]{:S(2)}, u32[]{:S(2)}) collective-permute-start(bf16[8,6144]{1,0:T(8,128)(2,1)S(1)} %concatenate.3.refs_0_), channel_id=1, source_target_pairs={{0,6},{1,7},{2,4},{3,5},{4,2},{5,3},{6,0},{7,1},{8,14},{9,15},{10,... | collective-permute-start | bytes 294920 | tf_op jit(solution)/shard_map/ppermute | solution.py:139
  59.3 3.7 %collective-permute-start.20 = (bf16[8,6144]{1,0:T(8,128)(2,1)S(1)}, bf16[8,6144]{1,0:T(8,128)(2,1)S(1)}, u32[]{:S(2)}, u32[]{:S(2)}) collective-permute-start(bf16[8,6144]{1,0:T(8,128)(2,1)S(1)} %concatenate.3.refs_0_), channel_id=1, source_target_pairs={{0,1},{1,0},{2,3},{3,2},{4,5},{5,4},{6,7},{7,6},{8,9},{9,8},{10,11... | collective-permute-start | bytes 294920 | tf_op jit(solution)/shard_map/ppermute | solution.py:139
  60.4 2.6 %collective-permute-start.21 = (bf16[8,6144]{1,0:T(8,128)(2,1)S(1)}, bf16[8,6144]{1,0:T(8,128)(2,1)S(1)}, u32[]{:S(2)}, u32[]{:S(2)}) collective-permute-start(bf16[8,6144]{1,0:T(8,128)(2,1)S(1)} %collective-permute-done.17.refs_1_), channel_id=1, source_target_pairs={{0,1},{1,0},{2,3},{3,2},{4,5},{5,4},{6,7},{7,6},{8,9},{9,8},{10,11... | collective-permute-start | bytes 294920 | tf_op jit(solution)/shard_map/ppermute | solution.py:139
  60.9 2.1 %collective-permute-start.22 = (bf16[8,6144]{1,0:T(8,128)(2,1)S(1)}, bf16[8,6144]{1,0:T(8,128)(2,1)S(1)}, u32[]{:S(2)}, u32[]{:S(2)}) collective-permute-start(bf16[8,6144]{1,0:T(8,128)(2,1)S(1)} %collective-permute-done.18.refs_2_), channel_id=1, source_target_pairs={{0,1},{1,0},{2,3},{3,2},{4,5},{5,4},{6,7},{7,6},{8,9},{9,8},{10,11... | collective-permute-start | bytes 294920 | tf_op jit(solution)/shard_map/ppermute | solution.py:139
  63.0 1.3 %collective-permute-start.23 = (bf16[8,6144]{1,0:T(8,128)(2,1)S(1)}, bf16[8,6144]{1,0:T(8,128)(2,1)S(1)}, u32[]{:S(2)}, u32[]{:S(2)}) collective-permute-start(bf16[8,6144]{1,0:T(8,128)(2,1)S(1)} %collective-permute-done.19.refs_3_), channel_id=1, source_target_pairs={{0,1},{1,0},{2,3},{3,2},{4,5},{5,4},{6,7},{7,6},{8,9},{9,8},{10,11... | collective-permute-start | bytes 294920 | tf_op jit(solution)/shard_map/ppermute | solution.py:139
  (2 other events, 1.4 us)

commit v3 on v0

v3 whole, which is shorter than its diff:
```python
import math

import jax
import jax.numpy as jnp
from jax import lax
from jax.experimental import pallas as pl
from jax.experimental.pallas import tpu as pltpu
from jax.sharding import PartitionSpec as P

beta_first = 0.9
beta_second = 0.95
bias_first = 1.0 - 0.9**10
bias_second = 1.0 - 0.95**10
learn_rate = 0.01
decay_rate = 0.1
adam_eps = 1e-08

LANES = 128
f32, bf16 = jnp.float32, jnp.bfloat16


def adamw(grad, weight, moment, second, factor):
    scaled = factor * grad
    moment_new = beta_first * moment + (1.0 - beta_first) * scaled
    second_new = beta_second * second + (1.0 - beta_second) * scaled * scaled
    update = moment_new / bias_first / (jnp.sqrt(second_new / bias_second) + adam_eps)
    weight_new = weight - learn_rate * (update + decay_rate * weight)
    return (weight_new, moment_new, second_new)


class Plan:
    def __init__(self, n_expert, n_dp, rows_a, rows_e, width):
        self.n_expert, self.n_dp, self.rows_a, self.rows_e = n_expert, n_dp, rows_a, rows_e
        self.width = width
        self.chips = n_dp // 2
        self.blocks = width // LANES
        self.size_a = self.blocks * rows_a
        self.size_e = self.blocks * rows_e
        self.all_a = n_expert * self.size_a
        self.chunk = self.all_a + self.size_e

    def places(self, block):
        attn = [
            (e * self.rows_a + r, e * self.size_a + block * self.rows_a + r)
            for e in range(self.n_expert)
            for r in range(self.rows_a)
        ]
        exp = [(r, self.all_a + block * self.rows_e + r) for r in range(self.rows_e)]
        return attn, exp


def dot(left, right):
    return lax.dot_general(left, right, (((1,), (0,)), ((), ())), preferred_element_type=f32)


def call(kernel, args, outs, scratch=(), specs=None):
    whole = pl.BlockSpec(memory_space=pltpu.VMEM)
    return pl.pallas_call(
        kernel,
        in_specs=specs or [whole] * len(args),
        out_specs=[whole] * len(outs),
        out_shape=[jax.ShapeDtypeStruct(shape, dtype) for shape, dtype in outs],
        scratch_shapes=list(scratch),
        compiler_params=pltpu.CompilerParams(vmem_limit_bytes=48 * 1024 * 1024),
    )(*args)


def two_pieces(value):
    high = value.astype(bf16).astype(f32)
    return high, (value - high).astype(bf16).astype(f32)


def by_eights(value):
    return jnp.sum(value.reshape(-1, 8, LANES), axis=0)


STEPS = 4


def terms_kernel(plan, act_a, dy_a, act_e, dy_e, w, m, v, full, send, pack, act_a_v, dy_a_v, act_e_v, dy_e_v, state, sems):
    tile = plan.width // STEPS
    small = [
        pltpu.make_async_copy(act_a, act_a_v, sems.at[0]),
        pltpu.make_async_copy(act_e, act_e_v, sems.at[1]),
    ]
    big = []
    for t in range(STEPS):
        cols = pl.ds(t * tile, tile)
        big.append(pltpu.make_async_copy(dy_a.at[:, cols], dy_a_v.at[:, cols], sems.at[2 + 2 * t]))
        big.append(pltpu.make_async_copy(dy_e.at[:, cols], dy_e_v.at[:, cols], sems.at[3 + 2 * t]))
    extra = [pltpu.make_async_copy(ref, state.at[i], sems.at[2 + 2 * STEPS + i]) for i, ref in enumerate((w, m, v))]
    for copy in small + big + extra:
        copy.start()

    me = lax.axis_index("dp")

    def pick(groups, per_owner, count):
        shape = (groups * plan.n_dp, count)
        row = lax.broadcasted_iota(jnp.int32, shape, 0)
        col = lax.broadcasted_iota(jnp.int32, shape, 1)
        group, place = row // plan.n_dp, row % plan.n_dp
        owner = (2 * (place % plan.chips) + place // plan.chips) ^ me
        want = ((group // per_owner) * plan.n_dp + owner) * per_owner + group % per_owner
        return (want == col).astype(bf16)

    for copy in small:
        copy.wait()
    left_a = dot(pick(plan.n_expert * plan.rows_a, plan.rows_a, act_a.shape[0]), act_a_v[...]).astype(bf16)
    left_e = dot(pick(plan.rows_e, plan.rows_e, act_e.shape[0]), act_e_v[...]).astype(bf16)
    n_dp = plan.n_dp
    for t in range(STEPS):
        cols = pl.ds(t * tile, tile)
        big[2 * t].wait()
        terms_a = dot(left_a, dy_a_v[:, cols])
        big[2 * t + 1].wait()
        terms_e = dot(left_e, dy_e_v[:, cols])
        for b in range(tile // LANES):
            attn, exp = plan.places(t * (tile // LANES) + b)
            span = slice(b * LANES, (b + 1) * LANES)
            for terms, places in ((terms_a, attn), (terms_e, exp)):
                for group, start in places:
                    full[pl.ds(start, n_dp, stride=plan.chunk), :] = terms[group * n_dp : (group + 1) * n_dp, span]
    for c in range(plan.chips):
        send[pl.ds(c * plan.chunk, plan.chunk), :] = full[
            pl.ds((plan.chips + c) * plan.chunk, plan.chunk), :
        ].astype(bf16)
    for copy in extra:
        copy.wait()
    size = plan.size_a
    high, low = two_pieces(state[0])
    for i, value in enumerate((high, low, state[1], state[2])):
        pack[pl.ds(i * size, size), :] = value.astype(bf16)


def make_terms(plan, act_a, dy_a, act_e, dy_e, w, m, v):
    args = (act_a, dy_a, act_e, dy_e, w, m, v)
    half = plan.chips * plan.chunk
    return call(
        lambda *refs: terms_kernel(plan, *refs),
        args,
        [((2 * half, LANES), f32), ((half, LANES), bf16), ((4 * plan.size_a, LANES), bf16)],
        [
            pltpu.VMEM(act_a.shape, bf16),
            pltpu.VMEM(dy_a.shape, bf16),
            pltpu.VMEM(act_e.shape, bf16),
            pltpu.VMEM(dy_e.shape, bf16),
            pltpu.VMEM((3,) + w.shape, f32),
            pltpu.SemaphoreType.DMA((5 + 2 * STEPS,)),
        ],
        [pl.BlockSpec(memory_space=pltpu.HBM)] * len(args),
    )


def share_kernel(plan, *refs):
    own, got, (payload, g_exp) = refs[0], refs[1:-2], refs[-2:]
    total = own[...]
    for ref in got:
        total = total + ref[...].astype(f32)
    a = plan.all_a
    exp = total[a:]
    g_exp[...] = exp
    payload[:a, :] = total[:a].astype(bf16)
    payload[a:, :] = jnp.concatenate(two_pieces(by_eights(exp * exp)), axis=0).astype(bf16)


def pair_sum(plan, mine, other):
    a = plan.all_a
    attn = mine[:a, :].astype(f32) + other[:a, :].astype(f32)
    one, two = mine[a:, :].astype(f32), other[a:, :].astype(f32)
    return attn, (one[:8] + one[8:]) + (two[:8] + two[8:])


def again_kernel(plan, mine, other, payload):
    attn, square = pair_sum(plan, mine, other)
    a = plan.all_a
    payload[:a, :] = attn.astype(bf16)
    payload[a:, :] = jnp.concatenate(two_pieces(square), axis=0).astype(bf16)


def last_kernel(plan, mine, other, g_attn, square):
    attn, partial = pair_sum(plan, mine, other)
    g_attn[...] = attn
    square[...] = partial + by_eights(attn * attn)


def update_kernel(plan, limit, *refs):
    square, g_attn, g_exp, wa, ma, va, we, me, ve = refs[:9]
    packs = refs[9 : 9 + plan.n_expert]
    wa_new, ma_new, va_new, we_new, me_new, ve_new, mine = refs[9 + plan.n_expert :]
    norm = jnp.sqrt(jnp.sum(square[...], keepdims=True))
    factor = jnp.minimum(1.0, limit / (norm + 1e-06))
    place = lax.axis_index("expert")
    size = plan.size_a

    def rows(expert):
        return pl.ds(pl.multiple_of(expert * size, 16), size)

    wa_new[...], ma_new[...], va_new[...] = adamw(g_attn[rows(place), :], wa[...], ma[...], va[...], factor)
    for q, pack in enumerate(packs):
        high, low, moment, second = [pack[pl.ds(i * size, size), :].astype(f32) for i in range(4)]
        weight, _, _ = adamw(g_attn[rows(place ^ q), :], high + low, moment, second, factor)
        mine[rows(place ^ q), :] = weight.astype(bf16)
    weight, moment, second = adamw(g_exp[...], we[...], me[...], ve[...], factor)
    we_new[...], me_new[...], ve_new[...] = weight, moment, second
    mine[plan.all_a :, :] = weight.astype(bf16)


def order_kernel(plan, *refs):
    n_dp = plan.n_dp
    parts, (attn, exp, rows, rows_a, rows_e) = refs[:n_dp], refs[n_dp:]
    me = lax.axis_index("dp")
    for i, part in enumerate(parts):
        owner = (2 * (i % plan.chips) + i // plan.chips) ^ me
        rows[pl.ds(pl.multiple_of(owner * plan.chunk, 16), plan.chunk), :] = part[...].astype(f32)
    count_a, count_e = attn.shape[0], exp.shape[1]
    for b in range(plan.blocks):
        places_a, places_e = plan.places(b)
        span = pl.ds(b * LANES, LANES)
        values = [rows[pl.ds(start, n_dp, stride=plan.chunk), :] for _, start in places_a]
        if plan.rows_a == 1:
            attn[:, span] = jnp.concatenate(values, axis=0).astype(bf16)
        else:
            for (group, _), value in zip(places_a, values):
                start = (group // plan.rows_a) * n_dp * plan.rows_a + group % plan.rows_a
                rows_a[pl.ds(start, n_dp, stride=plan.rows_a), :] = value
            attn[:, span] = rows_a[...].astype(bf16)
        for r, start in places_e:
            rows_e[pl.ds(b * count_e + r, n_dp, stride=plan.rows_e), :] = rows[
                pl.ds(start, n_dp, stride=plan.chunk), :
            ]
    for b in range(plan.blocks):
        exp[0, :, pl.ds(b * LANES, LANES)] = rows_e[pl.ds(b * count_e, count_e), :].astype(bf16)


def put_in_order(plan, parts):
    count_a = plan.n_expert * plan.n_dp * plan.rows_a
    count_e = plan.n_dp * plan.rows_e
    return call(
        lambda *refs: order_kernel(plan, *refs),
        parts,
        [((count_a, plan.width), bf16), ((1, count_e, plan.width), bf16)],
        [
            pltpu.VMEM((plan.n_dp * plan.chunk, LANES), f32),
            pltpu.VMEM((count_a, LANES), f32),
            pltpu.VMEM((plan.blocks * count_e, LANES), f32),
        ],
    )


def swap(value, axis, distance):
    size = lax.axis_size(axis)
    return lax.ppermute(value, axis, [(i, i ^ distance) for i in range(size)])


def to_blocks(value):
    rows, width = value.shape
    return value.reshape(rows, width // LANES, LANES).transpose(1, 0, 2).reshape(-1, LANES)


def from_blocks(value, rows):
    return value.reshape(-1, rows, LANES).transpose(1, 0, 2).reshape(rows, -1)


def body(act_attn, dy_attn, act_exp, dy_exp, w_attn, m_attn, v_attn, w_exp, m_exp, v_exp):
    width = w_attn.shape[1]
    n_expert = lax.axis_size("expert")
    n_dp = lax.axis_size("dp")
    rows_a, rows_e = w_attn.shape[0], w_exp.shape[1]
    plan = Plan(n_expert, n_dp, rows_a, rows_e, width)
    total_params = width * (act_attn.shape[1] + n_expert * act_exp.shape[2])
    limit = 0.5 * math.sqrt(total_params)
    chips, chunk = plan.chips, plan.chunk
    state_a = [to_blocks(value) for value in (w_attn, m_attn, v_attn)]
    state_e = [to_blocks(value[0]) for value in (w_exp, m_exp, v_exp)]

    full, send, pack = make_terms(plan, act_attn.T, dy_attn, act_exp[0].T, dy_exp[0], *state_a)
    got = swap(send, "dp", 1)
    packs = [pack] + [swap(pack, "expert", q) for q in range(1, n_expert)]
    sums = [
        full[c * chunk : (c + 1) * chunk] + got[c * chunk : (c + 1) * chunk].astype(f32) for c in range(chips)
    ]
    got = [swap(sums[c].astype(bf16), "dp", 2 * c) for c in range(1, chips)]
    shared = ((plan.all_a + 16, LANES), bf16)
    payload, g_exp = call(
        lambda *refs: share_kernel(plan, *refs), [sums[0]] + got, [shared, ((plan.size_e, LANES), f32)]
    )
    distance = 1
    while 2 * distance < n_expert:
        other = swap(payload, "expert", distance)
        (payload,) = call(lambda *refs: again_kernel(plan, *refs), [payload, other], [shared])
        distance *= 2
    other = swap(payload, "expert", distance)
    g_attn, square = call(
        lambda *refs: last_kernel(plan, *refs), [payload, other], [((plan.all_a, LANES), f32), ((8, LANES), f32)]
    )
    distance = 1
    while distance < n_dp:
        square = square + swap(square, "dp", distance)
        distance *= 2
    block_a, block_e = ((plan.size_a, LANES), f32), ((plan.size_e, LANES), f32)
    wa, ma, va, we, me, ve, mine = call(
        lambda *refs: update_kernel(plan, limit, *refs),
        [square, g_attn, g_exp, *state_a, *state_e, *packs],
        [block_a] * 3 + [block_e] * 3 + [((chunk, LANES), bf16)],
    )
    near = [mine] + [swap(mine, "dp", 2 * c) for c in range(1, chips)]
    far = [swap(piece, "dp", 1) for piece in near]
    attn_full, expert_full = put_in_order(plan, near + far)
    new_a = [from_blocks(value, rows_a) for value in (wa, ma, va)]
    new_e = [from_blocks(value, rows_e)[None] for value in (we, me, ve)]
    return (*new_a, *new_e, attn_full, expert_full)


def solution(mesh):
    return jax.shard_map(
        body,
        mesh=mesh,
        in_specs=(
            P(("expert", "dp"), None),
            P(("expert", "dp"), None),
            P("expert", "dp", None),
            P("expert", "dp", None),
            P(("expert", "dp"), None),
            P(("expert", "dp"), None),
            P(("expert", "dp"), None),
            P("expert", "dp", None),
            P("expert", "dp", None),
            P("expert", "dp", None),
        ),
        out_specs=(
            P(("expert", "dp"), None),
            P(("expert", "dp"), None),
            P(("expert", "dp"), None),
            P("expert", "dp", None),
            P("expert", "dp", None),
            P("expert", "dp", None),
            P(),
            P("expert", None, None),
        ),
        check_vma=False,
    )
```

time: 309 us -> 50.8 us (0.16)
  waiting for transfers between devices: 187 us -> 20.3 us
  blocking collectives: 90.4 us -> 0 us
  starting transfers between devices: 0.08 us -> 18.1 us
  between operations: 16.8 us -> 0.76 us
  other arithmetic: 6.67 us -> 0.07 us
  Pallas kernels: 0 us -> 6.12 us
  matrix products: 4.91 us -> 0 us
    unnamed x4 -> x0, waiting for transfers between devices: 187 us -> none
    all_gather x2 -> x0, blocking collectives: 51.2 us -> none  [the longest x1 42.8 us: body(): attn_full = lax.all_gather(attn_half, ('expert', 'dp'), axis=0, tiled=True)]
    psum x1 -> x0, blocking collectives: 39.2 us -> none  [body(): summed = lax.psum((sq_attn, sq_exp), ('expert', 'dp'))]
    ppermute x0 -> x19, waiting for transfers between devices: none -> 20.3 us  [swap(): return lax.ppermute(value, axis, [(i, i ^ distance) for i in range(size)])]
    ppermute x0 -> x19, starting transfers between devices: none -> 18.1 us  [swap(): return lax.ppermute(value, axis, [(i, i ^ distance) for i in range(size)])]
    pallas_call x0 -> x6, Pallas kernels: none -> 6.12 us  [call(): pl.pallas_call(kernel, in_specs=specs or [whole] * len(args), out_specs=[...]
    dot_general x2 -> x0, matrix products: 4.91 us -> none  [contract_rows(): lax.dot_general(left, right, (((0,), (0,)), ((), ())), preferred_element_...]
    reduce_sum x2 -> x0, other arithmetic: 3.17 us -> none  [the longest x1 1.58 us: body(): sq_attn = jnp.sum(g_attn * g_attn)]
  transfers between devices with their start and end apart: 2 -> 19, of which waited for: 2 -> 12; matrix products, arithmetic and copies ran while one was open for 1% -> 0% of each run, Pallas kernels for 0% -> 0%
where the time goes in v3:
time: 50.8 us; the launch traced here: 50.4 us
  waiting for transfers between devices  20.3 us (40%)
  starting transfers between devices  18.1 us (36%)
  Pallas kernels  6.12 us (12%)
  local copies, waits for them, and re-layouts  5.03 us (10%)
  between operations  0.76 us (1%)
    ppermute x19, waiting for transfers between devices, swap(): return lax.ppermute(value, axis, [(i, i ^ distance) for i in range(size)])  20.3 us
    ppermute x19, starting transfers between devices, swap(): return lax.ppermute(value, axis, [(i, i ^ distance) for i in range(size)])  18.1 us
    pallas_call x6, Pallas kernels, call(): pl.pallas_call(kernel, in_specs=specs or [whole] * len(args), out_specs=[...  6.12 us
    unnamed x18, local copies, waits for them, and re-layouts  5.03 us
  transfers between devices with their start and end apart: 19, of which 12 were waited for; matrix products, arithmetic and copies ran while one was open for 0% of the time, Pallas kernels for 0%

profile of v3, /device:TPU:0, one launch (start us, length us, event | category | flops | bytes accessed | tf_op | source)
XLA Modules:
  0.0 50.4 jit_solution(4938433254772653362)
XLA Ops:
  0.6 1.4 %copy-done = bf16[1,128,6144]{2,1,0:T(8,128)(2,1)S(1)} copy-done((bf16[1,128,6144]{2,1,0:T(8,128)(2,1)S(1)}, bf16[1,128,6144]{2,1,0:T(8,128)(2,1)}, u32[]{:S(2)}) %copy-start) | copy-done | bytes 1572888
  2.0 0.7 %copy-done.1 = f32[1,6144]{1,0:T(1,128)S(1)} copy-done((f32[1,6144]{1,0:T(1,128)S(1)}, f32[1,6144]{1,0:T(1,128)}, u32[]{:S(2)}) %copy-start.1) | copy-done | bytes 24600
  2.8 0.7 %copy-done.2 = f32[1,6144]{1,0:T(1,128)S(1)} copy-done((f32[1,6144]{1,0:T(1,128)S(1)}, f32[1,6144]{1,0:T(1,128)}, u32[]{:S(2)}) %copy-start.2) | copy-done | bytes 24600
  3.5 0.7 %copy-done.3 = f32[1,6144]{1,0:T(1,128)S(1)} copy-done((f32[1,6144]{1,0:T(1,128)S(1)}, f32[1,6144]{1,0:T(1,128)}, u32[]{:S(2)}) %copy-start.3) | copy-done | bytes 24600
  4.3 0.7 %copy-done.7 = bf16[256,32]{0,1:T(8,128)(2,1)S(1)} copy-done((bf16[256,32]{0,1:T(8,128)(2,1)S(1)}, bf16[256,32]{0,1:T(8,128)(2,1)}, u32[]{:S(2)}) %copy-start.7) | copy-done | bytes 16408
  5.0 0.7 %copy-done.8 = bf16[1,128,16]{1,2,0:T(8,128)(2,1)S(1)} copy-done((bf16[1,128,16]{1,2,0:T(8,128)(2,1)S(1)}, bf16[1,128,16]{1,2,0:T(8,128)(2,1)}, u32[]{:S(2)}) %copy-start.8) | copy-done | bytes 4120
  5.7 3.6 %shard_map.161 = (f32[2304,128]{1,0:T(8,128)S(1)}, bf16[1152,128]{1,0:T(8,128)(2,1)S(1)}, bf16[192,128]{1,0:T(8,128)(2,1)S(1)}) custom-call(bf16[32,256]{1,0:T(8,128)(2,1)S(1)} %bitcast.51, bf16[256,6144]{1,0:T(8,128)(2,1)} %refs_1_.1, bf16[16,128]{1,0:T(8,128)(2,1)S(1)} %bitcast.52, bf16[128,6144]{1,0:T(8,128)(2,1)S(1)} %bitcast.41, ...), custom_call_target="tpu_custom_call" | custom-call | tf_op jit(solution)/shard_map/pallas_call | solution.py:58
  9.3 0.5 %collective-permute-start = (bf16[1152,128]{1,0:T(8,128)(2,1)S(1)}, bf16[1152,128]{1,0:T(8,128)(2,1)S(1)}, u32[]{:S(2)}, u32[]{:S(2)}) collective-permute-start(bf16[1152,128]{1,0:T(8,128)(2,1)S(1)} %get-tuple-element.25), channel_id=1, source_target_pairs={{0,1},{1,0},{2,3},{3,2},{4,5},{5,4},{6,7},{7,6},{8,9},{9,8},{10,11... | collective-permute-start | bytes 884744 | tf_op jit(solution)/shard_map/ppermute | solution.py:252
  9.8 1.2 %collective-permute-done = bf16[1152,128]{1,0:T(8,128)(2,1)S(1)} collective-permute-done((bf16[1152,128]{1,0:T(8,128)(2,1)S(1)}, bf16[1152,128]{1,0:T(8,128)(2,1)S(1)}, u32[]{:S(2)}, u32[]{:S(2)}) %collective-permute-start) | collective-permute-done | bytes 294944 | tf_op jit(solution)/shard_map/ppermute | solution.py:252
  11.1 2.9 %collective-permute-start.1 = (bf16[288,128]{1,0:T(8,128)(2,1)S(1)}, bf16[288,128]{1,0:T(8,128)(2,1)S(1)}, u32[]{:S(2)}, u32[]{:S(2)}) collective-permute-start(bf16[288,128]{1,0:T(8,128)(2,1)S(1)} %get-tuple-element.42), channel_id=1, source_target_pairs={{0,2},{1,3},{2,0},{3,1},{4,6},{5,7},{6,4},{7,5},{8,10},{9,11},{10,... | collective-permute-start | bytes 221192 | tf_op jit(solution)/shard_map/ppermute | solution.py:252
  14.0 1.5 %collective-permute-start.2 = (bf16[288,128]{1,0:T(8,128)(2,1)S(1)}, bf16[288,128]{1,0:T(8,128)(2,1)S(1)}, u32[]{:S(2)}, u32[]{:S(2)}) collective-permute-start(bf16[288,128]{1,0:T(8,128)(2,1)S(1)} %get-tuple-element.41), channel_id=1, source_target_pairs={{0,4},{1,5},{2,6},{3,7},{4,0},{5,1},{6,2},{7,3},{8,12},{9,13},{10,... | collective-permute-start | bytes 221192 | tf_op jit(solution)/shard_map/ppermute | solution.py:252
  15.5 1.0 %collective-permute-done.1.refs_1_ = bf16[288,128]{1,0:T(8,128)(2,1)S(1)} collective-permute-done((bf16[288,128]{1,0:T(8,128)(2,1)S(1)}, bf16[288,128]{1,0:T(8,128)(2,1)S(1)}, u32[]{:S(2)}, u32[]{:S(2)}) %collective-permute-start.1) | collective-permute-done | bytes 73760 | tf_op jit(solution)/shard_map/ppermute | solution.py:252
  16.6 1.8 %collective-permute-done.2.refs_2_ = bf16[288,128]{1,0:T(8,128)(2,1)S(1)} collective-permute-done((bf16[288,128]{1,0:T(8,128)(2,1)S(1)}, bf16[288,128]{1,0:T(8,128)(2,1)S(1)}, u32[]{:S(2)}, u32[]{:S(2)}) %collective-permute-start.2) | collective-permute-done | bytes 73760 | tf_op jit(solution)/shard_map/ppermute | solution.py:252
  18.3 2.4 %collective-permute-done.3.refs_3_ = bf16[288,128]{1,0:T(8,128)(2,1)S(1)} collective-permute-done((bf16[288,128]{1,0:T(8,128)(2,1)S(1)}, bf16[288,128]{1,0:T(8,128)(2,1)S(1)}, u32[]{:S(2)}, u32[]{:S(2)}) %collective-permute-start.3) | collective-permute-done | bytes 73760 | tf_op jit(solution)/shard_map/ppermute | solution.py:252
  20.8 1.6 %collective-permute-start.4 = (bf16[208,128]{1,0:T(8,128)(2,1)S(1)}, bf16[208,128]{1,0:T(8,128)(2,1)S(1)}, u32[]{:S(2)}, u32[]{:S(2)}) collective-permute-start(bf16[208,128]{1,0:T(8,128)(2,1)S(1)} %get-tuple-element.26.refs_0_), channel_id=1, source_target_pairs={{0,8},{8,0},{16,24},{24,16},{1,9},{9,1},{17,25},{25,17},{2,10},{10... | collective-permute-start | bytes 159752 | tf_op jit(solution)/shard_map/ppermute | solution.py:252
  22.5 2.6 %collective-permute-done.4.refs_1_ = bf16[208,128]{1,0:T(8,128)(2,1)S(1)} collective-permute-done((bf16[208,128]{1,0:T(8,128)(2,1)S(1)}, bf16[208,128]{1,0:T(8,128)(2,1)S(1)}, u32[]{:S(2)}, u32[]{:S(2)}) %collective-permute-start.4) | collective-permute-done | bytes 53280 | tf_op jit(solution)/shard_map/ppermute | solution.py:252
  25.0 2.9 %collective-permute-start.5 = (bf16[208,128]{1,0:T(8,128)(2,1)S(1)}, bf16[208,128]{1,0:T(8,128)(2,1)S(1)}, u32[]{:S(2)}, u32[]{:S(2)}) collective-permute-start(bf16[208,128]{1,0:T(8,128)(2,1)S(1)} %shard_map.163.refs_0_), channel_id=1, source_target_pairs={{0,16},{8,24},{16,0},{24,8},{1,17},{9,25},{17,1},{25,9},{2,18},{10... | collective-permute-start | bytes 159752 | tf_op jit(solution)/shard_map/ppermute | solution.py:252
  28.0 3.6 %collective-permute-start.11 = (bf16[192,128]{1,0:T(8,128)(2,1)S(1)}, bf16[192,128]{1,0:T(8,128)(2,1)S(1)}, u32[]{:S(2)}, u32[]{:S(2)}) collective-permute-start(bf16[192,128]{1,0:T(8,128)(2,1)S(1)} %get-tuple-element.30.refs_9_), channel_id=1, source_target_pairs={{0,24},{8,16},{16,8},{24,0},{1,25},{9,17},{17,9},{25,1},{2,26},{10... | collective-permute-start | bytes 147464 | tf_op jit(solution)/shard_map/ppermute | solution.py:252
  31.7 1.2 %collective-permute-done.6 = f32[8,128]{1,0:T(8,128)S(1)} collective-permute-done((f32[8,128]{1,0:T(8,128)S(1)}, f32[8,128]{1,0:T(8,128)S(1)}, u32[]{:S(2)}, u32[]{:S(2)}) %collective-permute-start.6) | collective-permute-done | bytes 4128 | tf_op jit(solution)/shard_map/ppermute | solution.py:252
  32.9 0.6 %collective-permute-start.7 = (f32[8,128]{1,0:T(8,128)S(1)}, f32[8,128]{1,0:T(8,128)S(1)}, u32[]{:S(2)}, u32[]{:S(2)}) collective-permute-start(f32[8,128]{1,0:T(8,128)S(1)} %add.25), channel_id=1, source_target_pairs={{0,2},{1,3},{2,0},{3,1},{4,6},{5,7},{6,4},{7,5},{8,10},{9,11},{10,... | collective-permute-start | bytes 12296 | tf_op jit(solution)/shard_map/ppermute | solution.py:252
  33.5 3.0 %collective-permute-done.7 = f32[8,128]{1,0:T(8,128)S(1)} collective-permute-done((f32[8,128]{1,0:T(8,128)S(1)}, f32[8,128]{1,0:T(8,128)S(1)}, u32[]{:S(2)}, u32[]{:S(2)}) %collective-permute-start.7) | collective-permute-done | bytes 4128 | tf_op jit(solution)/shard_map/ppermute | solution.py:252
  36.5 0.7 %collective-permute-start.8 = (f32[8,128]{1,0:T(8,128)S(1)}, f32[8,128]{1,0:T(8,128)S(1)}, u32[]{:S(2)}, u32[]{:S(2)}) collective-permute-start(f32[8,128]{1,0:T(8,128)S(1)} %add.26), channel_id=1, source_target_pairs={{0,4},{1,5},{2,6},{3,7},{4,0},{5,1},{6,2},{7,3},{8,12},{9,13},{10,... | collective-permute-start | bytes 12296 | tf_op jit(solution)/shard_map/ppermute | solution.py:252
  37.2 2.9 %collective-permute-done.8 = f32[8,128]{1,0:T(8,128)S(1)} collective-permute-done((f32[8,128]{1,0:T(8,128)S(1)}, f32[8,128]{1,0:T(8,128)S(1)}, u32[]{:S(2)}, u32[]{:S(2)}) %collective-permute-start.8) | collective-permute-done | bytes 4128 | tf_op jit(solution)/shard_map/ppermute | solution.py:252
  40.2 0.9 %shard_map.165 = (f32[48,128]{1,0:T(8,128)}, f32[48,128]{1,0:T(8,128)}, f32[48,128]{1,0:T(8,128)}, f32[96,128]{1,0:T(8,128)}, f32[96,128]{1,0:T(8,128)}, /*index...) custom-call(f32[8,128]{1,0:T(8,128)S(1)} %add.27.refs_0_, f32[192,128]{1,0:T(8,128)S(1)} %get-tuple-element.28.refs_1_, ...), custom_call_target="tpu_custom_call" | custom-call | tf_op jit(solution)/shard_map/pallas_call | solution.py:58
  41.0 0.6 %collective-permute-start.12 = (bf16[288,128]{1,0:T(8,128)(2,1)S(1)}, bf16[288,128]{1,0:T(8,128)(2,1)S(1)}, u32[]{:S(2)}, u32[]{:S(2)}) collective-permute-start(bf16[288,128]{1,0:T(8,128)(2,1)S(1)} %get-tuple-element.37.refs_0_), channel_id=1, source_target_pairs={{0,2},{1,3},{2,0},{3,1},{4,6},{5,7},{6,4},{7,5},{8,10},{9,11},{10,... | collective-permute-start | bytes 221192 | tf_op jit(solution)/shard_map/ppermute | solution.py:252
  41.6 0.6 %collective-permute-start.13 = (bf16[288,128]{1,0:T(8,128)(2,1)S(1)}, bf16[288,128]{1,0:T(8,128)(2,1)S(1)}, u32[]{:S(2)}, u32[]{:S(2)}) collective-permute-start(bf16[288,128]{1,0:T(8,128)(2,1)S(1)} %get-tuple-element.37.refs_0_), channel_id=1, source_target_pairs={{0,4},{1,5},{2,6},{3,7},{4,0},{5,1},{6,2},{7,3},{8,12},{9,13},{10,... | collective-permute-start | bytes 221192 | tf_op jit(solution)/shard_map/ppermute | solution.py:252
  42.3 2.3 %collective-permute-start.14 = (bf16[288,128]{1,0:T(8,128)(2,1)S(1)}, bf16[288,128]{1,0:T(8,128)(2,1)S(1)}, u32[]{:S(2)}, u32[]{:S(2)}) collective-permute-start(bf16[288,128]{1,0:T(8,128)(2,1)S(1)} %get-tuple-element.37.refs_0_), channel_id=1, source_target_pairs={{0,6},{1,7},{2,4},{3,5},{4,2},{5,3},{6,0},{7,1},{8,14},{9,15},{10,... | collective-permute-start | bytes 221192 | tf_op jit(solution)/shard_map/ppermute | solution.py:252
  44.5 0.9 %collective-permute-done.12.refs_1_ = bf16[288,128]{1,0:T(8,128)(2,1)S(1)} collective-permute-done((bf16[288,128]{1,0:T(8,128)(2,1)S(1)}, bf16[288,128]{1,0:T(8,128)(2,1)S(1)}, u32[]{:S(2)}, u32[]{:S(2)}) %collective-permute-start.12) | collective-permute-done | bytes 73760 | tf_op jit(solution)/shard_map/ppermute | solution.py:252
  45.4 0.6 %collective-permute-done.13.refs_2_ = bf16[288,128]{1,0:T(8,128)(2,1)S(1)} collective-permute-done((bf16[288,128]{1,0:T(8,128)(2,1)S(1)}, bf16[288,128]{1,0:T(8,128)(2,1)S(1)}, u32[]{:S(2)}, u32[]{:S(2)}) %collective-permute-start.13) | collective-permute-done | bytes 73760 | tf_op jit(solution)/shard_map/ppermute | solution.py:252
  46.0 1.5 %collective-permute-done.14.refs_3_ = bf16[288,128]{1,0:T(8,128)(2,1)S(1)} collective-permute-done((bf16[288,128]{1,0:T(8,128)(2,1)S(1)}, bf16[288,128]{1,0:T(8,128)(2,1)S(1)}, u32[]{:S(2)}, u32[]{:S(2)}) %collective-permute-start.14) | collective-permute-done | bytes 73760 | tf_op jit(solution)/shard_map/ppermute | solution.py:252
  47.5 1.2 %collective-permute-done.18.refs_7_ = bf16[288,128]{1,0:T(8,128)(2,1)S(1)} collective-permute-done((bf16[288,128]{1,0:T(8,128)(2,1)S(1)}, bf16[288,128]{1,0:T(8,128)(2,1)S(1)}, u32[]{:S(2)}, u32[]{:S(2)}) %collective-permute-start.18) | collective-permute-done | bytes 73760 | tf_op jit(solution)/shard_map/ppermute | solution.py:252
  48.8 1.6 %shard_map.166 = (bf16[32,6144]{1,0:T(8,128)(2,1)}, bf16[1,16,6144]{2,1,0:T(8,128)(2,1)}) custom-call(bf16[288,128]{1,0:T(8,128)(2,1)S(1)} %get-tuple-element.37.refs_0_, bf16[288,128]{1,0:T(8,128)(2,1)S(1)} %collective-permute-done.12.refs_1_, bf16[288,128]{1,0:T(8,128)(2,1)S(1)} %collective-permute-done.13.refs_2_, ...), custom_call_target="tpu_custom_call" | custom-call | tf_op jit(solution)/shard_map/pallas_call | solution.py:58
  (34 shorter events, 0.4 us)
Async XLA Ops:
  0.6 1.4 %copy-start = (bf16[1,128,6144]{2,1,0:T(8,128)(2,1)S(1)}, bf16[1,128,6144]{2,1,0:T(8,128)(2,1)}, u32[]{:S(2)}) copy-start(bf16[1,128,6144]{2,1,0:T(8,128)(2,1)} %param.13) | copy-start | bytes 4718596
  2.0 0.7 %copy-start.1 = (f32[1,6144]{1,0:T(1,128)S(1)}, f32[1,6144]{1,0:T(1,128)}, u32[]{:S(2)}) copy-start(f32[1,6144]{1,0:T(1,128)} %param.14) | copy-start | bytes 73732
  2.8 0.7 %copy-start.2 = (f32[1,6144]{1,0:T(1,128)S(1)}, f32[1,6144]{1,0:T(1,128)}, u32[]{:S(2)}) copy-start(f32[1,6144]{1,0:T(1,128)} %param.15) | copy-start | bytes 73732
  3.5 0.7 %copy-start.3 = (f32[1,6144]{1,0:T(1,128)S(1)}, f32[1,6144]{1,0:T(1,128)}, u32[]{:S(2)}) copy-start(f32[1,6144]{1,0:T(1,128)} %param.16) | copy-start | bytes 73732
  4.3 0.7 %copy-start.7 = (bf16[256,32]{0,1:T(8,128)(2,1)S(1)}, bf16[256,32]{0,1:T(8,128)(2,1)}, u32[]{:S(2)}) copy-start(bf16[256,32]{0,1:T(8,128)(2,1)} %param.10) | copy-start | bytes 49156
  5.0 0.7 %copy-start.8 = (bf16[1,128,16]{1,2,0:T(8,128)(2,1)S(1)}, bf16[1,128,16]{1,2,0:T(8,128)(2,1)}, u32[]{:S(2)}) copy-start(bf16[1,128,16]{1,2,0:T(8,128)(2,1)} %param.12) | copy-start | bytes 12292
  9.2 30.9 %copy-start.4 = (f32[1,2,6144]{2,1,0:T(2,128)S(1)}, f32[1,2,6144]{2,1,0:T(2,128)}, u32[]{:S(2)}) copy-start(f32[1,2,6144]{2,1,0:T(2,128)} %param.17) | copy-start | bytes 147460
  9.3 30.9 %copy-start.5 = (f32[1,2,6144]{2,1,0:T(2,128)S(1)}, f32[1,2,6144]{2,1,0:T(2,128)}, u32[]{:S(2)}) copy-start(f32[1,2,6144]{2,1,0:T(2,128)} %param.18) | copy-start | bytes 147460
  9.3 30.9 %copy-start.6 = (f32[1,2,6144]{2,1,0:T(2,128)S(1)}, f32[1,2,6144]{2,1,0:T(2,128)}, u32[]{:S(2)}) copy-start(f32[1,2,6144]{2,1,0:T(2,128)} %param.19) | copy-start | bytes 147460
  9.3 1.7 %collective-permute-start = (bf16[1152,128]{1,0:T(8,128)(2,1)S(1)}, bf16[1152,128]{1,0:T(8,128)(2,1)S(1)}, u32[]{:S(2)}, u32[]{:S(2)}) collective-permute-start(bf16[1152,128]{1,0:T(8,128)(2,1)S(1)} %get-tuple-element.25), channel_id=1, source_target_pairs={{0,1},{1,0},{2,3},{3,2},{4,5},{5,4},{6,7},{7,6},{8,9},{9,8},{10,11... | collective-permute-start | bytes 884744 | tf_op jit(solution)/shard_map/ppermute | solution.py:252
  11.1 5.5 %collective-permute-start.1 = (bf16[288,128]{1,0:T(8,128)(2,1)S(1)}, bf16[288,128]{1,0:T(8,128)(2,1)S(1)}, u32[]{:S(2)}, u32[]{:S(2)}) collective-permute-start(bf16[288,128]{1,0:T(8,128)(2,1)S(1)} %get-tuple-element.42), channel_id=1, source_target_pairs={{0,2},{1,3},{2,0},{3,1},{4,6},{5,7},{6,4},{7,5},{8,10},{9,11},{10,... | collective-permute-start | bytes 221192 | tf_op jit(solution)/shard_map/ppermute | solution.py:252
  14.0 4.4 %collective-permute-start.2 = (bf16[288,128]{1,0:T(8,128)(2,1)S(1)}, bf16[288,128]{1,0:T(8,128)(2,1)S(1)}, u32[]{:S(2)}, u32[]{:S(2)}) collective-permute-start(bf16[288,128]{1,0:T(8,128)(2,1)S(1)} %get-tuple-element.41), channel_id=1, source_target_pairs={{0,4},{1,5},{2,6},{3,7},{4,0},{5,1},{6,2},{7,3},{8,12},{9,13},{10,... | collective-permute-start | bytes 221192 | tf_op jit(solution)/shard_map/ppermute | solution.py:252
  15.5 5.3 %collective-permute-start.3 = (bf16[288,128]{1,0:T(8,128)(2,1)S(1)}, bf16[288,128]{1,0:T(8,128)(2,1)S(1)}, u32[]{:S(2)}, u32[]{:S(2)}) collective-permute-start(bf16[288,128]{1,0:T(8,128)(2,1)S(1)} %get-tuple-element.40), channel_id=1, source_target_pairs={{0,6},{1,7},{2,4},{3,5},{4,2},{5,3},{6,0},{7,1},{8,14},{9,15},{10,... | collective-permute-start | bytes 221192 | tf_op jit(solution)/shard_map/ppermute | solution.py:252
  20.8 4.2 %collective-permute-start.4 = (bf16[208,128]{1,0:T(8,128)(2,1)S(1)}, bf16[208,128]{1,0:T(8,128)(2,1)S(1)}, u32[]{:S(2)}, u32[]{:S(2)}) collective-permute-start(bf16[208,128]{1,0:T(8,128)(2,1)S(1)} %get-tuple-element.26.refs_0_), channel_id=1, source_target_pairs={{0,8},{8,0},{16,24},{24,16},{1,9},{9,1},{17,25},{25,17},{2,10},{10... | collective-permute-start | bytes 159752 | tf_op jit(solution)/shard_map/ppermute | solution.py:252
  25.0 6.6 %collective-permute-start.5 = (bf16[208,128]{1,0:T(8,128)(2,1)S(1)}, bf16[208,128]{1,0:T(8,128)(2,1)S(1)}, u32[]{:S(2)}, u32[]{:S(2)}) collective-permute-start(bf16[208,128]{1,0:T(8,128)(2,1)S(1)} %shard_map.163.refs_0_), channel_id=1, source_target_pairs={{0,16},{8,24},{16,0},{24,8},{1,17},{9,25},{17,1},{25,9},{2,18},{10... | collective-permute-start | bytes 159752 | tf_op jit(solution)/shard_map/ppermute | solution.py:252
  27.9 12.2 %collective-permute-start.10 = (bf16[192,128]{1,0:T(8,128)(2,1)S(1)}, bf16[192,128]{1,0:T(8,128)(2,1)S(1)}, u32[]{:S(2)}, u32[]{:S(2)}) collective-permute-start(bf16[192,128]{1,0:T(8,128)(2,1)S(1)} %get-tuple-element.30.refs_9_), channel_id=1, source_target_pairs={{0,16},{8,24},{16,0},{24,8},{1,17},{9,25},{17,1},{25,9},{2,18},{10... | collective-permute-start | bytes 147464 | tf_op jit(solution)/shard_map/ppermute | solution.py:252
  28.0 12.1 %collective-permute-start.11 = (bf16[192,128]{1,0:T(8,128)(2,1)S(1)}, bf16[192,128]{1,0:T(8,128)(2,1)S(1)}, u32[]{:S(2)}, u32[]{:S(2)}) collective-permute-start(bf16[192,128]{1,0:T(8,128)(2,1)S(1)} %get-tuple-element.30.refs_9_), channel_id=1, source_target_pairs={{0,24},{8,16},{16,8},{24,0},{1,25},{9,17},{17,9},{25,1},{2,26},{10... | collective-permute-start | bytes 147464 | tf_op jit(solution)/shard_map/ppermute | solution.py:252
  31.6 8.5 %collective-permute-start.9 = (bf16[192,128]{1,0:T(8,128)(2,1)S(1)}, bf16[192,128]{1,0:T(8,128)(2,1)S(1)}, u32[]{:S(2)}, u32[]{:S(2)}) collective-permute-start(bf16[192,128]{1,0:T(8,128)(2,1)S(1)} %get-tuple-element.30.refs_9_), channel_id=1, source_target_pairs={{0,8},{8,0},{16,24},{24,16},{1,9},{9,1},{17,25},{25,17},{2,10},{10... | collective-permute-start | bytes 147464 | tf_op jit(solution)/shard_map/ppermute | solution.py:252
  31.7 1.2 %collective-permute-start.6 = (f32[8,128]{1,0:T(8,128)S(1)}, f32[8,128]{1,0:T(8,128)S(1)}, u32[]{:S(2)}, u32[]{:S(2)}) collective-permute-start(f32[8,128]{1,0:T(8,128)S(1)} %get-tuple-element.27), channel_id=1, source_target_pairs={{0,1},{1,0},{2,3},{3,2},{4,5},{5,4},{6,7},{7,6},{8,9},{9,8},{10,11... | collective-permute-start | bytes 12296 | tf_op jit(solution)/shard_map/ppermute | solution.py:252
  32.9 3.6 %collective-permute-start.7 = (f32[8,128]{1,0:T(8,128)S(1)}, f32[8,128]{1,0:T(8,128)S(1)}, u32[]{:S(2)}, u32[]{:S(2)}) collective-permute-start(f32[8,128]{1,0:T(8,128)S(1)} %add.25), channel_id=1, source_target_pairs={{0,2},{1,3},{2,0},{3,1},{4,6},{5,7},{6,4},{7,5},{8,10},{9,11},{10,... | collective-permute-start | bytes 12296 | tf_op jit(solution)/shard_map/ppermute | solution.py:252
  36.5 3.6 %collective-permute-start.8 = (f32[8,128]{1,0:T(8,128)S(1)}, f32[8,128]{1,0:T(8,128)S(1)}, u32[]{:S(2)}, u32[]{:S(2)}) collective-permute-start(f32[8,128]{1,0:T(8,128)S(1)} %add.26), channel_id=1, source_target_pairs={{0,4},{1,5},{2,6},{3,7},{4,0},{5,1},{6,2},{7,3},{8,12},{9,13},{10,... | collective-permute-start | bytes 12296 | tf_op jit(solution)/shard_map/ppermute | solution.py:252
  41.0 4.4 %collective-permute-start.12 = (bf16[288,128]{1,0:T(8,128)(2,1)S(1)}, bf16[288,128]{1,0:T(8,128)(2,1)S(1)}, u32[]{:S(2)}, u32[]{:S(2)}) collective-permute-start(bf16[288,128]{1,0:T(8,128)(2,1)S(1)} %get-tuple-element.37.refs_0_), channel_id=1, source_target_pairs={{0,2},{1,3},{2,0},{3,1},{4,6},{5,7},{6,4},{7,5},{8,10},{9,11},{10,... | collective-permute-start | bytes 221192 | tf_op jit(solution)/shard_map/ppermute | solution.py:252
  41.6 4.4 %collective-permute-start.13 = (bf16[288,128]{1,0:T(8,128)(2,1)S(1)}, bf16[288,128]{1,0:T(8,128)(2,1)S(1)}, u32[]{:S(2)}, u32[]{:S(2)}) collective-permute-start(bf16[288,128]{1,0:T(8,128)(2,1)S(1)} %get-tuple-element.37.refs_0_), channel_id=1, source_target_pairs={{0,4},{1,5},{2,6},{3,7},{4,0},{5,1},{6,2},{7,3},{8,12},{9,13},{10,... | collective-permute-start | bytes 221192 | tf_op jit(solution)/shard_map/ppermute | solution.py:252
  42.3 5.3 %collective-permute-start.14 = (bf16[288,128]{1,0:T(8,128)(2,1)S(1)}, bf16[288,128]{1,0:T(8,128)(2,1)S(1)}, u32[]{:S(2)}, u32[]{:S(2)}) collective-permute-start(bf16[288,128]{1,0:T(8,128)(2,1)S(1)} %get-tuple-element.37.refs_0_), channel_id=1, source_target_pairs={{0,6},{1,7},{2,4},{3,5},{4,2},{5,3},{6,0},{7,1},{8,14},{9,15},{10,... | collective-permute-start | bytes 221192 | tf_op jit(solution)/shard_map/ppermute | solution.py:252
  44.5 3.0 %collective-permute-start.15 = (bf16[288,128]{1,0:T(8,128)(2,1)S(1)}, bf16[288,128]{1,0:T(8,128)(2,1)S(1)}, u32[]{:S(2)}, u32[]{:S(2)}) collective-permute-start(bf16[288,128]{1,0:T(8,128)(2,1)S(1)} %get-tuple-element.37.refs_0_), channel_id=1, source_target_pairs={{0,1},{1,0},{2,3},{3,2},{4,5},{5,4},{6,7},{7,6},{8,9},{9,8},{10,11... | collective-permute-start | bytes 221192 | tf_op jit(solution)/shard_map/ppermute | solution.py:252
  45.4 2.1 %collective-permute-start.16 = (bf16[288,128]{1,0:T(8,128)(2,1)S(1)}, bf16[288,128]{1,0:T(8,128)(2,1)S(1)}, u32[]{:S(2)}, u32[]{:S(2)}) collective-permute-start(bf16[288,128]{1,0:T(8,128)(2,1)S(1)} %collective-permute-done.12.refs_1_), channel_id=1, source_target_pairs={{0,1},{1,0},{2,3},{3,2},{4,5},{5,4},{6,7},{7,6},{8,9},{9,8},{10,11... | collective-permute-start | bytes 221192 | tf_op jit(solution)/shard_map/ppermute | solution.py:252
  46.0 1.5 %collective-permute-start.17 = (bf16[288,128]{1,0:T(8,128)(2,1)S(1)}, bf16[288,128]{1,0:T(8,128)(2,1)S(1)}, u32[]{:S(2)}, u32[]{:S(2)}) collective-permute-start(bf16[288,128]{1,0:T(8,128)(2,1)S(1)} %collective-permute-done.13.refs_2_), channel_id=1, source_target_pairs={{0,1},{1,0},{2,3},{3,2},{4,5},{5,4},{6,7},{7,6},{8,9},{9,8},{10,11... | collective-permute-start | bytes 221192 | tf_op jit(solution)/shard_map/ppermute | solution.py:252
  47.5 1.3 %collective-permute-start.18 = (bf16[288,128]{1,0:T(8,128)(2,1)S(1)}, bf16[288,128]{1,0:T(8,128)(2,1)S(1)}, u32[]{:S(2)}, u32[]{:S(2)}) collective-permute-start(bf16[288,128]{1,0:T(8,128)(2,1)S(1)} %collective-permute-done.14.refs_3_), channel_id=1, source_target_pairs={{0,1},{1,0},{2,3},{3,2},{4,5},{5,4},{6,7},{7,6},{8,9},{9,8},{10,11... | collective-permute-start | bytes 221192 | tf_op jit(solution)/shard_map/ppermute | solution.py:252

commit v4 on v3

--- a/solution.py
+++ b/solution.py
@@ -75,6 +75,14 @@
 
 
 STEPS = 4
+
+
+def each(count, step, unrolled):
+    if unrolled:
+        for i in range(count):
+            step(i)
+    else:
+        pl.loop(0, count)(step)
 
 
 def terms_kernel(plan, act_a, dy_a, act_e, dy_e, w, m, v, full, send, pack, act_a_v, dy_a_v, act_e_v, dy_e_v, state, sems):
@@ -152,7 +160,11 @@
 
 
 def share_kernel(plan, *refs):
-    own, got, (payload, g_exp) = refs[0], refs[1:-2], refs[-2:]
+    packs, refs = refs[: plan.n_expert], refs[plan.n_expert :]
+    own, got, (payload, g_exp, states) = refs[0], refs[1:-3], refs[-3:]
+    place = lax.axis_index("expert")
+    for q, pack in enumerate(packs):
+        states[place ^ q] = pack[...]
     total = own[...]
     for ref in got:
         total = total + ref[...].astype(f32)
@@ -185,8 +197,7 @@
 
 def update_kernel(plan, limit, *refs):
     square, g_attn, g_exp, wa, ma, va, we, me, ve = refs[:9]
-    packs = refs[9 : 9 + plan.n_expert]
-    wa_new, ma_new, va_new, we_new, me_new, ve_new, mine = refs[9 + plan.n_expert :]
+    states, wa_new, ma_new, va_new, we_new, me_new, ve_new, mine = refs[9:]
     norm = jnp.sqrt(jnp.sum(square[...], keepdims=True))
     factor = jnp.minimum(1.0, limit / (norm + 1e-06))
     place = lax.axis_index("expert")
@@ -196,10 +207,10 @@
         return pl.ds(pl.multiple_of(expert * size, 16), size)
 
     wa_new[...], ma_new[...], va_new[...] = adamw(g_attn[rows(place), :], wa[...], ma[...], va[...], factor)
-    for q, pack in enumerate(packs):
-        high, low, moment, second = [pack[pl.ds(i * size, size), :].astype(f32) for i in range(4)]
-        weight, _, _ = adamw(g_attn[rows(place ^ q), :], high + low, moment, second, factor)
-        mine[rows(place ^ q), :] = weight.astype(bf16)
+    for e in range(plan.n_expert):
+        high, low, moment, second = [states[e, pl.ds(i * size, size), :].astype(f32) for i in range(4)]
+        weight, _, _ = adamw(g_attn[pl.ds(e * size, size), :], high + low, moment, second, factor)
+        mine[pl.ds(e * size, size), :] = weight.astype(bf16)
     weight, moment, second = adamw(g_exp[...], we[...], me[...], ve[...], factor)
     we_new[...], me_new[...], ve_new[...] = weight, moment, second
     mine[plan.all_a :, :] = weight.astype(bf16)
@@ -213,9 +224,10 @@
         owner = (2 * (i % plan.chips) + i // plan.chips) ^ me
         rows[pl.ds(pl.multiple_of(owner * plan.chunk, 16), plan.chunk), :] = part[...].astype(f32)
     count_a, count_e = attn.shape[0], exp.shape[1]
-    for b in range(plan.blocks):
+
+    def one(b):
         places_a, places_e = plan.places(b)
-        span = pl.ds(b * LANES, LANES)
+        span = pl.ds(b * LANES if isinstance(b, int) else pl.multiple_of(b * LANES, LANES), LANES)
         values = [rows[pl.ds(start, n_dp, stride=plan.chunk), :] for _, start in places_a]
         if plan.rows_a == 1:
             attn[:, span] = jnp.concatenate(values, axis=0).astype(bf16)
@@ -228,6 +240,8 @@
             rows_e[pl.ds(b * count_e + r, n_dp, stride=plan.rows_e), :] = rows[
                 pl.ds(start, n_dp, stride=plan.chunk), :
             ]
+
+    each(plan.blocks, one, n_dp <= 8)
     for b in range(plan.blocks):
         exp[0, :, pl.ds(b * LANES, LANES)] = rows_e[pl.ds(b * count_e, count_e), :].astype(bf16)
 
@@ -273,7 +287,8 @@
     state_a = [to_blocks(value) for value in (w_attn, m_attn, v_attn)]
     state_e = [to_blocks(value[0]) for value in (w_exp, m_exp, v_exp)]
 
-    full, send, pack = make_terms(plan, act_attn.T, dy_attn, act_exp[0].T, dy_exp[0], *state_a)
+    held = [pltpu.with_memory_space_constraint(x, pltpu.HBM) for x in (act_attn.T, dy_attn, act_exp[0].T, dy_exp[0])]
+    full, send, pack = make_terms(plan, *held, *[pltpu.with_memory_space_constraint(x, pltpu.HBM) for x in state_a])
     got = swap(send, "dp", 1)
     packs = [pack] + [swap(pack, "expert", q) for q in range(1, n_expert)]
     sums = [
@@ -281,8 +296,10 @@
     ]
     got = [swap(sums[c].astype(bf16), "dp", 2 * c) for c in range(1, chips)]
     shared = ((plan.all_a + 16, LANES), bf16)
-    payload, g_exp = call(
-        lambda *refs: share_kernel(plan, *refs), [sums[0]] + got, [shared, ((plan.size_e, LANES), f32)]
+    payload, g_exp, states = call(
+        lambda *refs: share_kernel(plan, *refs),
+        packs + [sums[0]] + got,
+        [shared, ((plan.size_e, LANES), f32), ((n_expert, 4 * plan.size_a, LANES), bf16)],
     )
     distance = 1
     while 2 * distance < n_expert:
@@ -300,7 +317,7 @@
     block_a, block_e = ((plan.size_a, LANES), f32), ((plan.size_e, LANES), f32)
     wa, ma, va, we, me, ve, mine = call(
         lambda *refs: update_kernel(plan, limit, *refs),
-        [square, g_attn, g_exp, *state_a, *state_e, *packs],
+        [square, g_attn, g_exp, *state_a, *state_e, states],
         [block_a] * 3 + [block_e] * 3 + [((chunk, LANES), bf16)],
     )
     near = [mine] + [swap(mine, "dp", 2 * c) for c in range(1, chips)]

time: 50.8 us -> 49.8 us (0.980)
  local copies, waits for them, and re-layouts: 5.03 us -> 0.04 us
  waiting for transfers between devices: 20.3 us -> 23.9 us
    unnamed x18 -> x12, local copies, waits for them, and re-layouts: 5.03 us -> 0.04 us
    ppermute x19, waiting for transfers between devices: 20.3 us -> 23.9 us  [swap(): return lax.ppermute(value, axis, [(i, i ^ distance) for i in range(size)])]
    ppermute x19, starting transfers between devices: 18.1 us -> 18.6 us  [swap(): return lax.ppermute(value, axis, [(i, i ^ distance) for i in range(size)])]
  transfers between devices with their start and end apart: 19 -> 19, of which waited for: 12 -> 11; matrix products, arithmetic and copies ran while one was open for 0% -> 0% of each run, Pallas kernels for 0% -> 0%
where the time goes in v4:
time: 49.8 us; the launch traced here: 49.5 us
  waiting for transfers between devices  23.9 us (48%)
  starting transfers between devices  18.6 us (37%)
  Pallas kernels  6.16 us (12%)
  between operations  0.78 us (2%)
    ppermute x19, waiting for transfers between devices, swap(): return lax.ppermute(value, axis, [(i, i ^ distance) for i in range(size)])  23.9 us
    ppermute x19, starting transfers between devices, swap(): return lax.ppermute(value, axis, [(i, i ^ distance) for i in range(size)])  18.6 us
    pallas_call x6, Pallas kernels, call(): pl.pallas_call(kernel, in_specs=specs or [whole] * len(args), out_specs=[...  6.16 us
  transfers between devices with their start and end apart: 19, of which 11 were waited for; matrix products, arithmetic and copies ran while one was open for 0% of the time, Pallas kernels for 0%

profile of v4, /device:TPU:0, one launch (start us, length us, event | category | flops | bytes accessed | tf_op | source)
XLA Modules:
  0.0 49.5 jit_solution(4976305566217521306)
XLA Ops:
  0.6 3.6 %shard_map.161 = (f32[2304,128]{1,0:T(8,128)S(1)}, bf16[1152,128]{1,0:T(8,128)(2,1)S(1)}, bf16[192,128]{1,0:T(8,128)(2,1)S(1)}) custom-call(bf16[32,256]{1,0:T(8,128)(2,1)} %bitcast.51, bf16[256,6144]{1,0:T(8,128)(2,1)} %refs_1_.1, bf16[16,128]{1,0:T(8,128)(2,1)} %bitcast.52, bf16[128,6144]{1,0:T(8,128)(2,1)} %bitcast.50, f32[48,128]{1,0:T(8,128)} %bitcast.41, ...), custom_call_target="tpu_custom_call" | custom-call | tf_op jit(solution)/shard_map/pallas_call | solution.py:58
  4.3 0.0 copy-start.2
  4.3 0.5 %collective-permute-start.3 = (bf16[1152,128]{1,0:T(8,128)(2,1)S(1)}, bf16[1152,128]{1,0:T(8,128)(2,1)S(1)}, u32[]{:S(2)}, u32[]{:S(2)}) collective-permute-start(bf16[1152,128]{1,0:T(8,128)(2,1)S(1)} %get-tuple-element.27), channel_id=1, source_target_pairs={{0,1},{1,0},{2,3},{3,2},{4,5},{5,4},{6,7},{7,6},{8,9},{9,8},{10,11... | collective-permute-start | bytes 884744 | tf_op jit(solution)/shard_map/ppermute | solution.py:266
  4.8 2.6 %collective-permute-start = (bf16[192,128]{1,0:T(8,128)(2,1)S(1)}, bf16[192,128]{1,0:T(8,128)(2,1)S(1)}, u32[]{:S(2)}, u32[]{:S(2)}) collective-permute-start(bf16[192,128]{1,0:T(8,128)(2,1)S(1)} %get-tuple-element.25.refs_0_), channel_id=1, source_target_pairs={{0,8},{8,0},{16,24},{24,16},{1,9},{9,1},{17,25},{25,17},{2,10},{10... | collective-permute-start | bytes 147464 | tf_op jit(solution)/shard_map/ppermute | solution.py:266
  7.5 0.1 add_convert_fusion
  7.5 1.6 %collective-permute-start.4 = (bf16[288,128]{1,0:T(8,128)(2,1)S(1)}, bf16[288,128]{1,0:T(8,128)(2,1)S(1)}, u32[]{:S(2)}, u32[]{:S(2)}) collective-permute-start(bf16[288,128]{1,0:T(8,128)(2,1)S(1)} %get-tuple-element.44), channel_id=1, source_target_pairs={{0,2},{1,3},{2,0},{3,1},{4,6},{5,7},{6,4},{7,5},{8,10},{9,11},{10,... | collective-permute-start | bytes 221192 | tf_op jit(solution)/shard_map/ppermute | solution.py:266
  9.1 1.5 %collective-permute-start.5 = (bf16[288,128]{1,0:T(8,128)(2,1)S(1)}, bf16[288,128]{1,0:T(8,128)(2,1)S(1)}, u32[]{:S(2)}, u32[]{:S(2)}) collective-permute-start(bf16[288,128]{1,0:T(8,128)(2,1)S(1)} %get-tuple-element.43), channel_id=1, source_target_pairs={{0,4},{1,5},{2,6},{3,7},{4,0},{5,1},{6,2},{7,3},{8,12},{9,13},{10,... | collective-permute-start | bytes 221192 | tf_op jit(solution)/shard_map/ppermute | solution.py:266
  10.6 0.5 collective-permute-start.6
  11.1 2.6 %collective-permute-start.1 = (bf16[192,128]{1,0:T(8,128)(2,1)S(1)}, bf16[192,128]{1,0:T(8,128)(2,1)S(1)}, u32[]{:S(2)}, u32[]{:S(2)}) collective-permute-start(bf16[192,128]{1,0:T(8,128)(2,1)S(1)} %get-tuple-element.25.refs_0_), channel_id=1, source_target_pairs={{0,16},{8,24},{16,0},{24,8},{1,17},{9,25},{17,1},{25,9},{2,18},{10... | collective-permute-start | bytes 147464 | tf_op jit(solution)/shard_map/ppermute | solution.py:266
  13.7 1.3 %collective-permute-start.2 = (bf16[192,128]{1,0:T(8,128)(2,1)S(1)}, bf16[192,128]{1,0:T(8,128)(2,1)S(1)}, u32[]{:S(2)}, u32[]{:S(2)}) collective-permute-start(bf16[192,128]{1,0:T(8,128)(2,1)S(1)} %get-tuple-element.25.refs_0_), channel_id=1, source_target_pairs={{0,24},{8,16},{16,8},{24,0},{1,25},{9,17},{17,9},{25,1},{2,26},{10... | collective-permute-start | bytes 147464 | tf_op jit(solution)/shard_map/ppermute | solution.py:266
  15.0 1.1 %collective-permute-done.1.refs_2_ = bf16[192,128]{1,0:T(8,128)(2,1)S(1)} collective-permute-done((bf16[192,128]{1,0:T(8,128)(2,1)S(1)}, bf16[192,128]{1,0:T(8,128)(2,1)S(1)}, u32[]{:S(2)}, u32[]{:S(2)}) %collective-permute-start.1) | collective-permute-done | bytes 49184 | tf_op jit(solution)/shard_map/ppermute | solution.py:266
  16.1 3.5 %collective-permute-done.2.refs_3_ = bf16[192,128]{1,0:T(8,128)(2,1)S(1)} collective-permute-done((bf16[192,128]{1,0:T(8,128)(2,1)S(1)}, bf16[192,128]{1,0:T(8,128)(2,1)S(1)}, u32[]{:S(2)}, u32[]{:S(2)}) %collective-permute-start.2) | collective-permute-done | bytes 49184 | tf_op jit(solution)/shard_map/ppermute | solution.py:266
  19.6 0.1 shard_map.162
  19.7 0.1 collective-permute-start.7
  19.7 4.1 %collective-permute-done.7.refs_1_ = bf16[208,128]{1,0:T(8,128)(2,1)S(1)} collective-permute-done((bf16[208,128]{1,0:T(8,128)(2,1)S(1)}, bf16[208,128]{1,0:T(8,128)(2,1)S(1)}, u32[]{:S(2)}, u32[]{:S(2)}) %collective-permute-start.7) | collective-permute-done | bytes 53280 | tf_op jit(solution)/shard_map/ppermute | solution.py:266
  23.9 1.4 %collective-permute-start.8 = (bf16[208,128]{1,0:T(8,128)(2,1)S(1)}, bf16[208,128]{1,0:T(8,128)(2,1)S(1)}, u32[]{:S(2)}, u32[]{:S(2)}) collective-permute-start(bf16[208,128]{1,0:T(8,128)(2,1)S(1)} %shard_map.163.refs_0_), channel_id=1, source_target_pairs={{0,16},{8,24},{16,0},{24,8},{1,17},{9,25},{17,1},{25,9},{2,18},{10... | collective-permute-start | bytes 159752 | tf_op jit(solution)/shard_map/ppermute | solution.py:266
  25.3 3.7 %collective-permute-done.8.refs_1_ = bf16[208,128]{1,0:T(8,128)(2,1)S(1)} collective-permute-done((bf16[208,128]{1,0:T(8,128)(2,1)S(1)}, bf16[208,128]{1,0:T(8,128)(2,1)S(1)}, u32[]{:S(2)}, u32[]{:S(2)}) %collective-permute-start.8) | collective-permute-done | bytes 53280 | tf_op jit(solution)/shard_map/ppermute | solution.py:266
  29.0 0.1 collective-permute-start.9
  29.1 1.2 %collective-permute-done.9 = f32[8,128]{1,0:T(8,128)S(1)} collective-permute-done((f32[8,128]{1,0:T(8,128)S(1)}, f32[8,128]{1,0:T(8,128)S(1)}, u32[]{:S(2)}, u32[]{:S(2)}) %collective-permute-start.9) | collective-permute-done | bytes 4128 | tf_op jit(solution)/shard_map/ppermute | solution.py:266
  30.3 1.5 %collective-permute-start.10 = (f32[8,128]{1,0:T(8,128)S(1)}, f32[8,128]{1,0:T(8,128)S(1)}, u32[]{:S(2)}, u32[]{:S(2)}) collective-permute-start(f32[8,128]{1,0:T(8,128)S(1)} %add.25), channel_id=1, source_target_pairs={{0,2},{1,3},{2,0},{3,1},{4,6},{5,7},{6,4},{7,5},{8,10},{9,11},{10,... | collective-permute-start | bytes 12296 | tf_op jit(solution)/shard_map/ppermute | solution.py:266
  31.8 2.1 %collective-permute-done.10 = f32[8,128]{1,0:T(8,128)S(1)} collective-permute-done((f32[8,128]{1,0:T(8,128)S(1)}, f32[8,128]{1,0:T(8,128)S(1)}, u32[]{:S(2)}, u32[]{:S(2)}) %collective-permute-start.10) | collective-permute-done | bytes 4128 | tf_op jit(solution)/shard_map/ppermute | solution.py:266
  33.9 1.5 %collective-permute-start.11 = (f32[8,128]{1,0:T(8,128)S(1)}, f32[8,128]{1,0:T(8,128)S(1)}, u32[]{:S(2)}, u32[]{:S(2)}) collective-permute-start(f32[8,128]{1,0:T(8,128)S(1)} %add.26), channel_id=1, source_target_pairs={{0,4},{1,5},{2,6},{3,7},{4,0},{5,1},{6,2},{7,3},{8,12},{9,13},{10,... | collective-permute-start | bytes 12296 | tf_op jit(solution)/shard_map/ppermute | solution.py:266
  35.4 2.1 %collective-permute-done.11 = f32[8,128]{1,0:T(8,128)S(1)} collective-permute-done((f32[8,128]{1,0:T(8,128)S(1)}, f32[8,128]{1,0:T(8,128)S(1)}, u32[]{:S(2)}, u32[]{:S(2)}) %collective-permute-start.11) | collective-permute-done | bytes 4128 | tf_op jit(solution)/shard_map/ppermute | solution.py:266
  37.5 0.9 %shard_map.165 = (f32[48,128]{1,0:T(8,128)}, f32[48,128]{1,0:T(8,128)}, f32[48,128]{1,0:T(8,128)}, f32[96,128]{1,0:T(8,128)}, f32[96,128]{1,0:T(8,128)}, /*index...) custom-call(f32[8,128]{1,0:T(8,128)S(1)} %add.27.refs_0_, f32[192,128]{1,0:T(8,128)S(1)} %get-tuple-element.30.refs_1_, ...), custom_call_target="tpu_custom_call" | custom-call | tf_op jit(solution)/shard_map/pallas_call | solution.py:58
  38.4 1.5 %collective-permute-start.12 = (bf16[288,128]{1,0:T(8,128)(2,1)S(1)}, bf16[288,128]{1,0:T(8,128)(2,1)S(1)}, u32[]{:S(2)}, u32[]{:S(2)}) collective-permute-start(bf16[288,128]{1,0:T(8,128)(2,1)S(1)} %get-tuple-element.39.refs_0_), channel_id=1, source_target_pairs={{0,2},{1,3},{2,0},{3,1},{4,6},{5,7},{6,4},{7,5},{8,10},{9,11},{10,... | collective-permute-start | bytes 221192 | tf_op jit(solution)/shard_map/ppermute | solution.py:266
  39.9 1.5 %collective-permute-start.13 = (bf16[288,128]{1,0:T(8,128)(2,1)S(1)}, bf16[288,128]{1,0:T(8,128)(2,1)S(1)}, u32[]{:S(2)}, u32[]{:S(2)}) collective-permute-start(bf16[288,128]{1,0:T(8,128)(2,1)S(1)} %get-tuple-element.39.refs_0_), channel_id=1, source_target_pairs={{0,4},{1,5},{2,6},{3,7},{4,0},{5,1},{6,2},{7,3},{8,12},{9,13},{10,... | collective-permute-start | bytes 221192 | tf_op jit(solution)/shard_map/ppermute | solution.py:266
  41.4 0.5 collective-permute-start.14
  41.9 0.9 %collective-permute-done.12.refs_1_ = bf16[288,128]{1,0:T(8,128)(2,1)S(1)} collective-permute-done((bf16[288,128]{1,0:T(8,128)(2,1)S(1)}, bf16[288,128]{1,0:T(8,128)(2,1)S(1)}, u32[]{:S(2)}, u32[]{:S(2)}) %collective-permute-start.12) | collective-permute-done | bytes 73760 | tf_op jit(solution)/shard_map/ppermute | solution.py:266
  42.8 1.4 %collective-permute-done.13.refs_2_ = bf16[288,128]{1,0:T(8,128)(2,1)S(1)} collective-permute-done((bf16[288,128]{1,0:T(8,128)(2,1)S(1)}, bf16[288,128]{1,0:T(8,128)(2,1)S(1)}, u32[]{:S(2)}, u32[]{:S(2)}) %collective-permute-start.13) | collective-permute-done | bytes 73760 | tf_op jit(solution)/shard_map/ppermute | solution.py:266
  44.3 2.4 %collective-permute-done.14.refs_3_ = bf16[288,128]{1,0:T(8,128)(2,1)S(1)} collective-permute-done((bf16[288,128]{1,0:T(8,128)(2,1)S(1)}, bf16[288,128]{1,0:T(8,128)(2,1)S(1)}, u32[]{:S(2)}, u32[]{:S(2)}) %collective-permute-start.14) | collective-permute-done | bytes 73760 | tf_op jit(solution)/shard_map/ppermute | solution.py:266
  46.7 1.2 %collective-permute-done.18.refs_7_ = bf16[288,128]{1,0:T(8,128)(2,1)S(1)} collective-permute-done((bf16[288,128]{1,0:T(8,128)(2,1)S(1)}, bf16[288,128]{1,0:T(8,128)(2,1)S(1)}, u32[]{:S(2)}, u32[]{:S(2)}) %collective-permute-start.18) | collective-permute-done | bytes 73760 | tf_op jit(solution)/shard_map/ppermute | solution.py:266
  47.9 1.6 %shard_map.166 = (bf16[32,6144]{1,0:T(8,128)(2,1)}, bf16[1,16,6144]{2,1,0:T(8,128)(2,1)}) custom-call(bf16[288,128]{1,0:T(8,128)(2,1)S(1)} %get-tuple-element.39.refs_0_, bf16[288,128]{1,0:T(8,128)(2,1)S(1)} %collective-permute-done.12.refs_1_, bf16[288,128]{1,0:T(8,128)(2,1)S(1)} %collective-permute-done.13.refs_2_, ...), custom_call_target="tpu_custom_call" | custom-call | tf_op jit(solution)/shard_map/pallas_call | solution.py:58
  (28 shorter events, 0.1 us)
Async XLA Ops:
  4.2 33.2 %copy-start = (f32[1,6144]{1,0:T(1,128)S(1)}, f32[1,6144]{1,0:T(1,128)}, u32[]{:S(2)}) copy-start(f32[1,6144]{1,0:T(1,128)} %param.14) | copy-start | bytes 73732
  4.3 33.2 %copy-start.1 = (f32[1,6144]{1,0:T(1,128)S(1)}, f32[1,6144]{1,0:T(1,128)}, u32[]{:S(2)}) copy-start(f32[1,6144]{1,0:T(1,128)} %param.15) | copy-start | bytes 73732
  4.3 33.2 %copy-start.2 = (f32[1,6144]{1,0:T(1,128)S(1)}, f32[1,6144]{1,0:T(1,128)}, u32[]{:S(2)}) copy-start(f32[1,6144]{1,0:T(1,128)} %param.16) | copy-start | bytes 73732
  4.3 33.2 %copy-start.3 = (f32[1,2,6144]{2,1,0:T(2,128)S(1)}, f32[1,2,6144]{2,1,0:T(2,128)}, u32[]{:S(2)}) copy-start(f32[1,2,6144]{2,1,0:T(2,128)} %param.17) | copy-start | bytes 147460
  4.3 33.2 %copy-start.4 = (f32[1,2,6144]{2,1,0:T(2,128)S(1)}, f32[1,2,6144]{2,1,0:T(2,128)}, u32[]{:S(2)}) copy-start(f32[1,2,6144]{2,1,0:T(2,128)} %param.18) | copy-start | bytes 147460
  4.3 33.2 %copy-start.5 = (f32[1,2,6144]{2,1,0:T(2,128)S(1)}, f32[1,2,6144]{2,1,0:T(2,128)}, u32[]{:S(2)}) copy-start(f32[1,2,6144]{2,1,0:T(2,128)} %param.19) | copy-start | bytes 147460
  4.3 3.2 %collective-permute-start.3 = (bf16[1152,128]{1,0:T(8,128)(2,1)S(1)}, bf16[1152,128]{1,0:T(8,128)(2,1)S(1)}, u32[]{:S(2)}, u32[]{:S(2)}) collective-permute-start(bf16[1152,128]{1,0:T(8,128)(2,1)S(1)} %get-tuple-element.27), channel_id=1, source_target_pairs={{0,1},{1,0},{2,3},{3,2},{4,5},{5,4},{6,7},{7,6},{8,9},{9,8},{10,11... | collective-permute-start | bytes 884744 | tf_op jit(solution)/shard_map/ppermute | solution.py:266
  4.8 8.9 %collective-permute-start = (bf16[192,128]{1,0:T(8,128)(2,1)S(1)}, bf16[192,128]{1,0:T(8,128)(2,1)S(1)}, u32[]{:S(2)}, u32[]{:S(2)}) collective-permute-start(bf16[192,128]{1,0:T(8,128)(2,1)S(1)} %get-tuple-element.25.refs_0_), channel_id=1, source_target_pairs={{0,8},{8,0},{16,24},{24,16},{1,9},{9,1},{17,25},{25,17},{2,10},{10... | collective-permute-start | bytes 147464 | tf_op jit(solution)/shard_map/ppermute | solution.py:266
  7.5 12.0 %collective-permute-start.4 = (bf16[288,128]{1,0:T(8,128)(2,1)S(1)}, bf16[288,128]{1,0:T(8,128)(2,1)S(1)}, u32[]{:S(2)}, u32[]{:S(2)}) collective-permute-start(bf16[288,128]{1,0:T(8,128)(2,1)S(1)} %get-tuple-element.44), channel_id=1, source_target_pairs={{0,2},{1,3},{2,0},{3,1},{4,6},{5,7},{6,4},{7,5},{8,10},{9,11},{10,... | collective-permute-start | bytes 221192 | tf_op jit(solution)/shard_map/ppermute | solution.py:266
  9.1 10.5 %collective-permute-start.5 = (bf16[288,128]{1,0:T(8,128)(2,1)S(1)}, bf16[288,128]{1,0:T(8,128)(2,1)S(1)}, u32[]{:S(2)}, u32[]{:S(2)}) collective-permute-start(bf16[288,128]{1,0:T(8,128)(2,1)S(1)} %get-tuple-element.43), channel_id=1, source_target_pairs={{0,4},{1,5},{2,6},{3,7},{4,0},{5,1},{6,2},{7,3},{8,12},{9,13},{10,... | collective-permute-start | bytes 221192 | tf_op jit(solution)/shard_map/ppermute | solution.py:266
  10.6 9.0 %collective-permute-start.6 = (bf16[288,128]{1,0:T(8,128)(2,1)S(1)}, bf16[288,128]{1,0:T(8,128)(2,1)S(1)}, u32[]{:S(2)}, u32[]{:S(2)}) collective-permute-start(bf16[288,128]{1,0:T(8,128)(2,1)S(1)} %get-tuple-element.42), channel_id=1, source_target_pairs={{0,6},{1,7},{2,4},{3,5},{4,2},{5,3},{6,0},{7,1},{8,14},{9,15},{10,... | collective-permute-start | bytes 221192 | tf_op jit(solution)/shard_map/ppermute | solution.py:266
  11.1 5.0 %collective-permute-start.1 = (bf16[192,128]{1,0:T(8,128)(2,1)S(1)}, bf16[192,128]{1,0:T(8,128)(2,1)S(1)}, u32[]{:S(2)}, u32[]{:S(2)}) collective-permute-start(bf16[192,128]{1,0:T(8,128)(2,1)S(1)} %get-tuple-element.25.refs_0_), channel_id=1, source_target_pairs={{0,16},{8,24},{16,0},{24,8},{1,17},{9,25},{17,1},{25,9},{2,18},{10... | collective-permute-start | bytes 147464 | tf_op jit(solution)/shard_map/ppermute | solution.py:266
  13.7 5.9 %collective-permute-start.2 = (bf16[192,128]{1,0:T(8,128)(2,1)S(1)}, bf16[192,128]{1,0:T(8,128)(2,1)S(1)}, u32[]{:S(2)}, u32[]{:S(2)}) collective-permute-start(bf16[192,128]{1,0:T(8,128)(2,1)S(1)} %get-tuple-element.25.refs_0_), channel_id=1, source_target_pairs={{0,24},{8,16},{16,8},{24,0},{1,25},{9,17},{17,9},{25,1},{2,26},{10... | collective-permute-start | bytes 147464 | tf_op jit(solution)/shard_map/ppermute | solution.py:266
  19.7 4.2 %collective-permute-start.7 = (bf16[208,128]{1,0:T(8,128)(2,1)S(1)}, bf16[208,128]{1,0:T(8,128)(2,1)S(1)}, u32[]{:S(2)}, u32[]{:S(2)}) collective-permute-start(bf16[208,128]{1,0:T(8,128)(2,1)S(1)} %get-tuple-element.28.refs_0_), channel_id=1, source_target_pairs={{0,8},{8,0},{16,24},{24,16},{1,9},{9,1},{17,25},{25,17},{2,10},{10... | collective-permute-start | bytes 159752 | tf_op jit(solution)/shard_map/ppermute | solution.py:266
  23.9 5.1 %collective-permute-start.8 = (bf16[208,128]{1,0:T(8,128)(2,1)S(1)}, bf16[208,128]{1,0:T(8,128)(2,1)S(1)}, u32[]{:S(2)}, u32[]{:S(2)}) collective-permute-start(bf16[208,128]{1,0:T(8,128)(2,1)S(1)} %shard_map.163.refs_0_), channel_id=1, source_target_pairs={{0,16},{8,24},{16,0},{24,8},{1,17},{9,25},{17,1},{25,9},{2,18},{10... | collective-permute-start | bytes 159752 | tf_op jit(solution)/shard_map/ppermute | solution.py:266
  29.0 1.2 %collective-permute-start.9 = (f32[8,128]{1,0:T(8,128)S(1)}, f32[8,128]{1,0:T(8,128)S(1)}, u32[]{:S(2)}, u32[]{:S(2)}) collective-permute-start(f32[8,128]{1,0:T(8,128)S(1)} %get-tuple-element.29), channel_id=1, source_target_pairs={{0,1},{1,0},{2,3},{3,2},{4,5},{5,4},{6,7},{7,6},{8,9},{9,8},{10,11... | collective-permute-start | bytes 12296 | tf_op jit(solution)/shard_map/ppermute | solution.py:266
  30.3 3.6 %collective-permute-start.10 = (f32[8,128]{1,0:T(8,128)S(1)}, f32[8,128]{1,0:T(8,128)S(1)}, u32[]{:S(2)}, u32[]{:S(2)}) collective-permute-start(f32[8,128]{1,0:T(8,128)S(1)} %add.25), channel_id=1, source_target_pairs={{0,2},{1,3},{2,0},{3,1},{4,6},{5,7},{6,4},{7,5},{8,10},{9,11},{10,... | collective-permute-start | bytes 12296 | tf_op jit(solution)/shard_map/ppermute | solution.py:266
  33.9 3.6 %collective-permute-start.11 = (f32[8,128]{1,0:T(8,128)S(1)}, f32[8,128]{1,0:T(8,128)S(1)}, u32[]{:S(2)}, u32[]{:S(2)}) collective-permute-start(f32[8,128]{1,0:T(8,128)S(1)} %add.26), channel_id=1, source_target_pairs={{0,4},{1,5},{2,6},{3,7},{4,0},{5,1},{6,2},{7,3},{8,12},{9,13},{10,... | collective-permute-start | bytes 12296 | tf_op jit(solution)/shard_map/ppermute | solution.py:266
  38.4 4.4 %collective-permute-start.12 = (bf16[288,128]{1,0:T(8,128)(2,1)S(1)}, bf16[288,128]{1,0:T(8,128)(2,1)S(1)}, u32[]{:S(2)}, u32[]{:S(2)}) collective-permute-start(bf16[288,128]{1,0:T(8,128)(2,1)S(1)} %get-tuple-element.39.refs_0_), channel_id=1, source_target_pairs={{0,2},{1,3},{2,0},{3,1},{4,6},{5,7},{6,4},{7,5},{8,10},{9,11},{10,... | collective-permute-start | bytes 221192 | tf_op jit(solution)/shard_map/ppermute | solution.py:266
  39.9 4.4 %collective-permute-start.13 = (bf16[288,128]{1,0:T(8,128)(2,1)S(1)}, bf16[288,128]{1,0:T(8,128)(2,1)S(1)}, u32[]{:S(2)}, u32[]{:S(2)}) collective-permute-start(bf16[288,128]{1,0:T(8,128)(2,1)S(1)} %get-tuple-element.39.refs_0_), channel_id=1, source_target_pairs={{0,4},{1,5},{2,6},{3,7},{4,0},{5,1},{6,2},{7,3},{8,12},{9,13},{10,... | collective-permute-start | bytes 221192 | tf_op jit(solution)/shard_map/ppermute | solution.py:266
  41.4 5.3 %collective-permute-start.14 = (bf16[288,128]{1,0:T(8,128)(2,1)S(1)}, bf16[288,128]{1,0:T(8,128)(2,1)S(1)}, u32[]{:S(2)}, u32[]{:S(2)}) collective-permute-start(bf16[288,128]{1,0:T(8,128)(2,1)S(1)} %get-tuple-element.39.refs_0_), channel_id=1, source_target_pairs={{0,6},{1,7},{2,4},{3,5},{4,2},{5,3},{6,0},{7,1},{8,14},{9,15},{10,... | collective-permute-start | bytes 221192 | tf_op jit(solution)/shard_map/ppermute | solution.py:266
  41.9 4.8 %collective-permute-start.15 = (bf16[288,128]{1,0:T(8,128)(2,1)S(1)}, bf16[288,128]{1,0:T(8,128)(2,1)S(1)}, u32[]{:S(2)}, u32[]{:S(2)}) collective-permute-start(bf16[288,128]{1,0:T(8,128)(2,1)S(1)} %get-tuple-element.39.refs_0_), channel_id=1, source_target_pairs={{0,1},{1,0},{2,3},{3,2},{4,5},{5,4},{6,7},{7,6},{8,9},{9,8},{10,11... | collective-permute-start | bytes 221192 | tf_op jit(solution)/shard_map/ppermute | solution.py:266
  42.8 3.8 %collective-permute-start.16 = (bf16[288,128]{1,0:T(8,128)(2,1)S(1)}, bf16[288,128]{1,0:T(8,128)(2,1)S(1)}, u32[]{:S(2)}, u32[]{:S(2)}) collective-permute-start(bf16[288,128]{1,0:T(8,128)(2,1)S(1)} %collective-permute-done.12.refs_1_), channel_id=1, source_target_pairs={{0,1},{1,0},{2,3},{3,2},{4,5},{5,4},{6,7},{7,6},{8,9},{9,8},{10,11... | collective-permute-start | bytes 221192 | tf_op jit(solution)/shard_map/ppermute | solution.py:266
  44.2 2.4 %collective-permute-start.17 = (bf16[288,128]{1,0:T(8,128)(2,1)S(1)}, bf16[288,128]{1,0:T(8,128)(2,1)S(1)}, u32[]{:S(2)}, u32[]{:S(2)}) collective-permute-start(bf16[288,128]{1,0:T(8,128)(2,1)S(1)} %collective-permute-done.13.refs_2_), channel_id=1, source_target_pairs={{0,1},{1,0},{2,3},{3,2},{4,5},{5,4},{6,7},{7,6},{8,9},{9,8},{10,11... | collective-permute-start | bytes 221192 | tf_op jit(solution)/shard_map/ppermute | solution.py:266
  46.7 1.3 %collective-permute-start.18 = (bf16[288,128]{1,0:T(8,128)(2,1)S(1)}, bf16[288,128]{1,0:T(8,128)(2,1)S(1)}, u32[]{:S(2)}, u32[]{:S(2)}) collective-permute-start(bf16[288,128]{1,0:T(8,128)(2,1)S(1)} %collective-permute-done.14.refs_3_), channel_id=1, source_target_pairs={{0,1},{1,0},{2,3},{3,2},{4,5},{5,4},{6,7},{7,6},{8,9},{9,8},{10,11... | collective-permute-start | bytes 221192 | tf_op jit(solution)/shard_map/ppermute | solution.py:266

commit v5 on v4

--- a/solution.py
+++ b/solution.py
@@ -107,7 +107,7 @@
         row = lax.broadcasted_iota(jnp.int32, shape, 0)
         col = lax.broadcasted_iota(jnp.int32, shape, 1)
         group, place = row // plan.n_dp, row % plan.n_dp
-        owner = (2 * (place % plan.chips) + place // plan.chips) ^ me
+        owner = 2 * (place % plan.chips) + ((place // plan.chips) ^ (me % 2))
         want = ((group // per_owner) * plan.n_dp + owner) * per_owner + group % per_owner
         return (want == col).astype(bf16)
 
@@ -159,15 +159,8 @@
     )
 
 
-def share_kernel(plan, *refs):
-    packs, refs = refs[: plan.n_expert], refs[plan.n_expert :]
-    own, got, (payload, g_exp, states) = refs[0], refs[1:-3], refs[-3:]
-    place = lax.axis_index("expert")
-    for q, pack in enumerate(packs):
-        states[place ^ q] = pack[...]
-    total = own[...]
-    for ref in got:
-        total = total + ref[...].astype(f32)
+def share_kernel(plan, got, payload, g_exp):
+    total = jnp.sum(got[...].astype(f32), axis=0)
     a = plan.all_a
     exp = total[a:]
     g_exp[...] = exp
@@ -182,23 +175,27 @@
     return attn, (one[:8] + one[8:]) + (two[:8] + two[8:])
 
 
-def again_kernel(plan, mine, other, payload):
+def again_kernel(plan, mine, other, *refs):
+    packs, (payload, states) = refs[:-2], refs[-2:]
     attn, square = pair_sum(plan, mine, other)
     a = plan.all_a
     payload[:a, :] = attn.astype(bf16)
     payload[a:, :] = jnp.concatenate(two_pieces(square), axis=0).astype(bf16)
+    place = lax.axis_index("expert")
+    for q, pack in enumerate(packs):
+        states[place ^ q] = pack[...]
 
 
 def last_kernel(plan, mine, other, g_attn, square):
     attn, partial = pair_sum(plan, mine, other)
     g_attn[...] = attn
-    square[...] = partial + by_eights(attn * attn)
+    square[...] = jnp.broadcast_to((partial + by_eights(attn * attn))[None], square.shape)
 
 
 def update_kernel(plan, limit, *refs):
     square, g_attn, g_exp, wa, ma, va, we, me, ve = refs[:9]
     states, wa_new, ma_new, va_new, we_new, me_new, ve_new, mine = refs[9:]
-    norm = jnp.sqrt(jnp.sum(square[...], keepdims=True))
+    norm = jnp.sqrt(jnp.sum(jnp.sum(square[...], axis=0), keepdims=True))
     factor = jnp.minimum(1.0, limit / (norm + 1e-06))
     place = lax.axis_index("expert")
     size = plan.size_a
@@ -210,19 +207,22 @@
     for e in range(plan.n_expert):
         high, low, moment, second = [states[e, pl.ds(i * size, size), :].astype(f32) for i in range(4)]
         weight, _, _ = adamw(g_attn[pl.ds(e * size, size), :], high + low, moment, second, factor)
-        mine[pl.ds(e * size, size), :] = weight.astype(bf16)
+        for c in range(plan.chips):
+            mine[c, pl.ds(e * size, size), :] = weight.astype(bf16)
     weight, moment, second = adamw(g_exp[...], we[...], me[...], ve[...], factor)
     we_new[...], me_new[...], ve_new[...] = weight, moment, second
-    mine[plan.all_a :, :] = weight.astype(bf16)
+    for c in range(plan.chips):
+        mine[c, plan.all_a :, :] = weight.astype(bf16)
 
 
 def order_kernel(plan, *refs):
     n_dp = plan.n_dp
-    parts, (attn, exp, rows, rows_a, rows_e) = refs[:n_dp], refs[n_dp:]
-    me = lax.axis_index("dp")
-    for i, part in enumerate(parts):
-        owner = (2 * (i % plan.chips) + i // plan.chips) ^ me
-        rows[pl.ds(pl.multiple_of(owner * plan.chunk, 16), plan.chunk), :] = part[...].astype(f32)
+    near, far, attn, exp, rows, rows_a, rows_e = refs
+    core = lax.axis_index("dp") % 2
+    for part, bit in ((near, core), (far, 1 - core)):
+        for c in range(plan.chips):
+            start = pl.multiple_of((2 * c + bit) * plan.chunk, 16)
+            rows[pl.ds(start, plan.chunk), :] = part[c].astype(f32)
     count_a, count_e = attn.shape[0], exp.shape[1]
 
     def one(b):
@@ -266,6 +266,12 @@
     return lax.ppermute(value, axis, [(i, i ^ distance) for i in range(size)])
 
 
+def between_chips(value):
+    size = lax.axis_size("dp")
+    groups = [list(range(core, size, 2)) for core in range(2)]
+    return lax.all_to_all(value, "dp", 0, 0, axis_index_groups=groups, tiled=True)
+
+
 def to_blocks(value):
     rows, width = value.shape
     return value.reshape(rows, width // LANES, LANES).transpose(1, 0, 2).reshape(-1, LANES)
@@ -291,38 +297,32 @@
     full, send, pack = make_terms(plan, *held, *[pltpu.with_memory_space_constraint(x, pltpu.HBM) for x in state_a])
     got = swap(send, "dp", 1)
     packs = [pack] + [swap(pack, "expert", q) for q in range(1, n_expert)]
-    sums = [
-        full[c * chunk : (c + 1) * chunk] + got[c * chunk : (c + 1) * chunk].astype(f32) for c in range(chips)
-    ]
-    got = [swap(sums[c].astype(bf16), "dp", 2 * c) for c in range(1, chips)]
+    sums = (full[: chips * chunk] + got.astype(f32)).astype(bf16).reshape(chips, chunk, LANES)
+    got = between_chips(sums)
     shared = ((plan.all_a + 16, LANES), bf16)
-    payload, g_exp, states = call(
-        lambda *refs: share_kernel(plan, *refs),
-        packs + [sums[0]] + got,
-        [shared, ((plan.size_e, LANES), f32), ((n_expert, 4 * plan.size_a, LANES), bf16)],
-    )
-    distance = 1
-    while 2 * distance < n_expert:
-        other = swap(payload, "expert", distance)
-        (payload,) = call(lambda *refs: again_kernel(plan, *refs), [payload, other], [shared])
-        distance *= 2
-    other = swap(payload, "expert", distance)
+    payload, g_exp = call(
+        lambda *refs: share_kernel(plan, *refs), [got], [shared, ((plan.size_e, LANES), f32)]
+    )
+    other = swap(payload, "expert", 1)
+    payload, states = call(
+        lambda *refs: again_kernel(plan, *refs),
+        [payload, other, *packs],
+        [shared, ((n_expert, 4 * plan.size_a, LANES), bf16)],
+    )
+    other = swap(payload, "expert", 2)
     g_attn, square = call(
-        lambda *refs: last_kernel(plan, *refs), [payload, other], [((plan.all_a, LANES), f32), ((8, LANES), f32)]
-    )
-    distance = 1
-    while distance < n_dp:
-        square = square + swap(square, "dp", distance)
-        distance *= 2
+        lambda *refs: last_kernel(plan, *refs), [payload, other], [((plan.all_a, LANES), f32), ((n_dp, 8, LANES), f32)]
+    )
+    square = lax.all_to_all(square, "dp", 0, 0, tiled=True)
     block_a, block_e = ((plan.size_a, LANES), f32), ((plan.size_e, LANES), f32)
     wa, ma, va, we, me, ve, mine = call(
         lambda *refs: update_kernel(plan, limit, *refs),
         [square, g_attn, g_exp, *state_a, *state_e, states],
-        [block_a] * 3 + [block_e] * 3 + [((chunk, LANES), bf16)],
-    )
-    near = [mine] + [swap(mine, "dp", 2 * c) for c in range(1, chips)]
-    far = [swap(piece, "dp", 1) for piece in near]
-    attn_full, expert_full = put_in_order(plan, near + far)
+        [block_a] * 3 + [block_e] * 3 + [((chips, chunk, LANES), bf16)],
+    )
+    near = between_chips(mine)
+    far = swap(near, "dp", 1)
+    attn_full, expert_full = put_in_order(plan, [near, far])
     new_a = [from_blocks(value, rows_a) for value in (wa, ma, va)]
     new_e = [from_blocks(value, rows_e)[None] for value in (we, me, ve)]
     return (*new_a, *new_e, attn_full, expert_full)

time: 49.8 us -> 54 us (1.084)
  blocking collectives: 0 us -> 27.6 us
  waiting for transfers between devices: 23.9 us -> 11.8 us
  starting transfers between devices: 18.6 us -> 7.21 us
    all_to_all x0 -> x3, blocking collectives: none -> 27.6 us  [the longest x2 20.4 us: between_chips(): lax.all_to_all(value, 'dp', 0, 0, axis_index_groups=groups, tiled=True)]
    ppermute x19 -> x7, waiting for transfers between devices: 23.9 us -> 11.8 us  [swap(): return lax.ppermute(value, axis, [(i, i ^ distance) for i in range(size)])]
    ppermute x19 -> x7, starting transfers between devices: 18.6 us -> 7.21 us  [swap(): return lax.ppermute(value, axis, [(i, i ^ distance) for i in range(size)])]
  transfers between devices with their start and end apart: 19 -> 7, of which waited for: 11 -> 5; matrix products, arithmetic and copies ran while one was open for 0% -> 0% of each run, Pallas kernels for 0% -> 0%
where the time goes in v5:
time: 54 us; the launch traced here: 53.6 us
  blocking collectives  27.6 us (51%)
  waiting for transfers between devices  11.8 us (22%)
  starting transfers between devices  7.21 us (13%)
  Pallas kernels  6.15 us (11%)
  between operations  0.74 us (1%)
    all_to_all x2, blocking collectives, between_chips(): lax.all_to_all(value, 'dp', 0, 0, axis_index_groups=groups, tiled=True)  20.4 us
    ppermute x7, waiting for transfers between devices, swap(): return lax.ppermute(value, axis, [(i, i ^ distance) for i in range(size)])  11.8 us
    all_to_all x1, blocking collectives, body(): square = lax.all_to_all(square, 'dp', 0, 0, tiled=True)  7.21 us
    ppermute x7, starting transfers between devices, swap(): return lax.ppermute(value, axis, [(i, i ^ distance) for i in range(size)])  7.21 us
    pallas_call x6, Pallas kernels, call(): pl.pallas_call(kernel, in_specs=specs or [whole] * len(args), out_specs=[...  6.15 us
  transfers between devices with their start and end apart: 7, of which 5 were waited for; matrix products, arithmetic and copies ran while one was open for 0% of the time, Pallas kernels for 0%

profile of v5, /device:TPU:0, one launch (start us, length us, event | category | flops | bytes accessed | tf_op | source)
XLA Modules:
  0.0 53.6 jit_solution(2078492730551868346)
XLA Ops:
  0.6 3.6 %shard_map.161 = (f32[2304,128]{1,0:T(8,128)S(1)}, bf16[1152,128]{1,0:T(8,128)(2,1)S(1)}, bf16[192,128]{1,0:T(8,128)(2,1)S(1)}) custom-call(bf16[32,256]{1,0:T(8,128)(2,1)} %bitcast.53, bf16[256,6144]{1,0:T(8,128)(2,1)} %refs_1_.1, bf16[16,128]{1,0:T(8,128)(2,1)} %bitcast.54, bf16[128,6144]{1,0:T(8,128)(2,1)} %bitcast.51, f32[48,128]{1,0:T(8,128)} %bitcast.42, ...), custom_call_target="tpu_custom_call" | custom-call | tf_op jit(solution)/shard_map/pallas_call | solution.py:58
  4.2 0.0 copy-start
  4.3 0.0 copy-start.1
  4.3 0.0 copy-start.2
  4.3 0.0 copy-start.3
  4.3 0.0 copy-start.4
  4.3 0.0 copy-start.5
  4.3 0.5 collective-permute-start
  4.8 1.2 %collective-permute-done = bf16[1152,128]{1,0:T(8,128)(2,1)S(1)} collective-permute-done((bf16[1152,128]{1,0:T(8,128)(2,1)S(1)}, bf16[1152,128]{1,0:T(8,128)(2,1)S(1)}, u32[]{:S(2)}, u32[]{:S(2)}) %collective-permute-start) | collective-permute-done | bytes 294944 | tf_op jit(solution)/shard_map/ppermute | solution.py:266
  6.0 0.1 add_convert_fusion
  6.1 11.5 %all_to_all.15.refs_0_ = bf16[4,288,128]{2,1,0:T(8,128)(2,1)S(1)} all-to-all(bf16[4,288,128]{2,1,0:T(8,128)(2,1)S(1)} %bitcast.52), channel_id=1, replica_groups={{0,2,4,6},{1,3,5,7},{8,10,12,14},{9,11,13,15},{16,18,20,22},{17,19,21,2..., dimensions={0} | all-to-all | bytes 589824 | tf_op jit(solution)/shard_map/all_to_all | solution.py:272
  17.7 1.6 %collective-permute-start.1 = (bf16[208,128]{1,0:T(8,128)(2,1)S(1)}, bf16[208,128]{1,0:T(8,128)(2,1)S(1)}, u32[]{:S(2)}, u32[]{:S(2)}) collective-permute-start(bf16[208,128]{1,0:T(8,128)(2,1)S(1)} %get-tuple-element.28.refs_0_), channel_id=1, source_target_pairs={{0,8},{8,0},{16,24},{24,16},{1,9},{9,1},{17,25},{25,17},{2,10},{10... | collective-permute-start | bytes 159752 | tf_op jit(solution)/shard_map/ppermute | solution.py:266
  19.3 0.4 collective-permute-start.2
  19.8 2.6 %collective-permute-start.3 = (bf16[192,128]{1,0:T(8,128)(2,1)S(1)}, bf16[192,128]{1,0:T(8,128)(2,1)S(1)}, u32[]{:S(2)}, u32[]{:S(2)}) collective-permute-start(bf16[192,128]{1,0:T(8,128)(2,1)S(1)} %get-tuple-element.29.refs_2_), channel_id=1, source_target_pairs={{0,16},{8,24},{16,0},{24,8},{1,17},{9,25},{17,1},{25,9},{2,18},{10... | collective-permute-start | bytes 147464 | tf_op jit(solution)/shard_map/ppermute | solution.py:266
  22.4 1.3 %collective-permute-start.4 = (bf16[192,128]{1,0:T(8,128)(2,1)S(1)}, bf16[192,128]{1,0:T(8,128)(2,1)S(1)}, u32[]{:S(2)}, u32[]{:S(2)}) collective-permute-start(bf16[192,128]{1,0:T(8,128)(2,1)S(1)} %get-tuple-element.29.refs_2_), channel_id=1, source_target_pairs={{0,24},{8,16},{16,8},{24,0},{1,25},{9,17},{17,9},{25,1},{2,26},{10... | collective-permute-start | bytes 147464 | tf_op jit(solution)/shard_map/ppermute | solution.py:266
  23.7 0.0 collective-permute-done.2.refs_3_
  23.7 1.7 %collective-permute-done.3.refs_4_ = bf16[192,128]{1,0:T(8,128)(2,1)S(1)} collective-permute-done((bf16[192,128]{1,0:T(8,128)(2,1)S(1)}, bf16[192,128]{1,0:T(8,128)(2,1)S(1)}, u32[]{:S(2)}, u32[]{:S(2)}) %collective-permute-start.3) | collective-permute-done | bytes 49184 | tf_op jit(solution)/shard_map/ppermute | solution.py:266
  25.4 2.9 %collective-permute-done.4.refs_5_ = bf16[192,128]{1,0:T(8,128)(2,1)S(1)} collective-permute-done((bf16[192,128]{1,0:T(8,128)(2,1)S(1)}, bf16[192,128]{1,0:T(8,128)(2,1)S(1)}, u32[]{:S(2)}, u32[]{:S(2)}) %collective-permute-start.4) | collective-permute-done | bytes 49184 | tf_op jit(solution)/shard_map/ppermute | solution.py:266
  28.3 0.0 collective-permute-done.1.refs_1_
  28.4 0.7 %collective-permute-start.5 = (bf16[208,128]{1,0:T(8,128)(2,1)S(1)}, bf16[208,128]{1,0:T(8,128)(2,1)S(1)}, u32[]{:S(2)}, u32[]{:S(2)}) collective-permute-start(bf16[208,128]{1,0:T(8,128)(2,1)S(1)} %get-tuple-element.30.refs_0_), channel_id=1, source_target_pairs={{0,16},{8,24},{16,0},{24,8},{1,17},{9,25},{17,1},{25,9},{2,18},{10... | collective-permute-start | bytes 159752 | tf_op jit(solution)/shard_map/ppermute | solution.py:266
  29.0 4.4 %collective-permute-done.5.refs_1_ = bf16[208,128]{1,0:T(8,128)(2,1)S(1)} collective-permute-done((bf16[208,128]{1,0:T(8,128)(2,1)S(1)}, bf16[208,128]{1,0:T(8,128)(2,1)S(1)}, u32[]{:S(2)}, u32[]{:S(2)}) %collective-permute-start.5) | collective-permute-done | bytes 53280 | tf_op jit(solution)/shard_map/ppermute | solution.py:266
  33.5 7.2 %all_to_all.16.refs_0_ = f32[8,8,128]{2,1,0:T(8,128)S(1)} all-to-all(f32[8,8,128]{2,1,0:T(8,128)S(1)} %get-tuple-element.31), channel_id=1, replica_groups=mesh['expert'=4,'dp'=8] {'dp'}, dimensions={0} | all-to-all | bytes 65536 | tf_op jit(solution)/shard_map/all_to_all | solution.py:316
  40.7 0.0 copy-done
  40.7 0.0 copy-done.1
  40.7 0.0 copy-done.2
  40.7 0.0 copy-done.3
  40.7 0.0 copy-done.4
  40.8 0.9 %shard_map.165 = (f32[48,128]{1,0:T(8,128)}, f32[48,128]{1,0:T(8,128)}, f32[48,128]{1,0:T(8,128)}, f32[96,128]{1,0:T(8,128)}, f32[96,128]{1,0:T(8,128)}, /*index...) custom-call(f32[8,8,128]{2,1,0:T(8,128)S(1)} %all_to_all.16.refs_0_, f32[192,128]{1,0:T(8,128)S(1)} %get-tuple-element.32.refs_1_, ...), custom_call_target="tpu_custom_call" | custom-call | tf_op jit(solution)/shard_map/pallas_call | solution.py:58
  41.6 8.9 %all_to_all.17.refs_0_ = bf16[4,288,128]{2,1,0:T(8,128)(2,1)S(1)} all-to-all(bf16[4,288,128]{2,1,0:T(8,128)(2,1)S(1)} %get-tuple-element.41), channel_id=1, replica_groups={{0,2,4,6},{1,3,5,7},{8,10,12,14},{9,11,13,15},{16,18,20,22},{17,19,21,2..., dimensions={0} | all-to-all | bytes 589824 | tf_op jit(solution)/shard_map/all_to_all | solution.py:272
  50.5 0.0 collective-permute-start.6
  50.5 1.6 %collective-permute-done.6.refs_1_ = bf16[4,288,128]{2,1,0:T(8,128)(2,1)S(1)} collective-permute-done((bf16[4,288,128]{2,1,0:T(8,128)(2,1)S(1)}, bf16[4,288,128]{2,1,0:T(8,128)(2,1)S(1)}, u32[]{:S(2)}, u32[]{:S(2)}) %collective-permute-start.6) | collective-permute-done | bytes 294944 | tf_op jit(solution)/shard_map/ppermute | solution.py:266
  52.1 1.6 %shard_map.166 = (bf16[32,6144]{1,0:T(8,128)(2,1)}, bf16[1,16,6144]{2,1,0:T(8,128)(2,1)}) custom-call(bf16[4,288,128]{2,1,0:T(8,128)(2,1)S(1)} %all_to_all.17.refs_0_, bf16[4,288,128]{2,1,0:T(8,128)(2,1)S(1)} %collective-permute-done.6.refs_1_), custom_call_target="tpu_custom_call" | custom-call | tf_op jit(solution)/shard_map/pallas_call | solution.py:58
  (4 shorter events, 0.1 us)
Async XLA Ops:
  4.2 36.5 %copy-start = (f32[1,6144]{1,0:T(1,128)S(1)}, f32[1,6144]{1,0:T(1,128)}, u32[]{:S(2)}) copy-start(f32[1,6144]{1,0:T(1,128)} %param.14) | copy-start | bytes 73732
  4.3 36.5 %copy-start.1 = (f32[1,6144]{1,0:T(1,128)S(1)}, f32[1,6144]{1,0:T(1,128)}, u32[]{:S(2)}) copy-start(f32[1,6144]{1,0:T(1,128)} %param.15) | copy-start | bytes 73732
  4.3 36.5 %copy-start.2 = (f32[1,6144]{1,0:T(1,128)S(1)}, f32[1,6144]{1,0:T(1,128)}, u32[]{:S(2)}) copy-start(f32[1,6144]{1,0:T(1,128)} %param.16) | copy-start | bytes 73732
  4.3 36.5 %copy-start.3 = (f32[1,2,6144]{2,1,0:T(2,128)S(1)}, f32[1,2,6144]{2,1,0:T(2,128)}, u32[]{:S(2)}) copy-start(f32[1,2,6144]{2,1,0:T(2,128)} %param.17) | copy-start | bytes 147460
  4.3 36.4 %copy-start.4 = (f32[1,2,6144]{2,1,0:T(2,128)S(1)}, f32[1,2,6144]{2,1,0:T(2,128)}, u32[]{:S(2)}) copy-start(f32[1,2,6144]{2,1,0:T(2,128)} %param.18) | copy-start | bytes 147460
  4.3 36.4 %copy-start.5 = (f32[1,2,6144]{2,1,0:T(2,128)S(1)}, f32[1,2,6144]{2,1,0:T(2,128)}, u32[]{:S(2)}) copy-start(f32[1,2,6144]{2,1,0:T(2,128)} %param.19) | copy-start | bytes 147460
  4.3 1.7 %collective-permute-start = (bf16[1152,128]{1,0:T(8,128)(2,1)S(1)}, bf16[1152,128]{1,0:T(8,128)(2,1)S(1)}, u32[]{:S(2)}, u32[]{:S(2)}) collective-permute-start(bf16[1152,128]{1,0:T(8,128)(2,1)S(1)} %get-tuple-element.27), channel_id=1, source_target_pairs={{0,1},{1,0},{2,3},{3,2},{4,5},{5,4},{6,7},{7,6},{8,9},{9,8},{10,11... | collective-permute-start | bytes 884744 | tf_op jit(solution)/shard_map/ppermute | solution.py:266
  17.7 10.7 %collective-permute-start.1 = (bf16[208,128]{1,0:T(8,128)(2,1)S(1)}, bf16[208,128]{1,0:T(8,128)(2,1)S(1)}, u32[]{:S(2)}, u32[]{:S(2)}) collective-permute-start(bf16[208,128]{1,0:T(8,128)(2,1)S(1)} %get-tuple-element.28.refs_0_), channel_id=1, source_target_pairs={{0,8},{8,0},{16,24},{24,16},{1,9},{9,1},{17,25},{25,17},{2,10},{10... | collective-permute-start | bytes 159752 | tf_op jit(solution)/shard_map/ppermute | solution.py:266
  19.3 4.4 %collective-permute-start.2 = (bf16[192,128]{1,0:T(8,128)(2,1)S(1)}, bf16[192,128]{1,0:T(8,128)(2,1)S(1)}, u32[]{:S(2)}, u32[]{:S(2)}) collective-permute-start(bf16[192,128]{1,0:T(8,128)(2,1)S(1)} %get-tuple-element.29.refs_2_), channel_id=1, source_target_pairs={{0,8},{8,0},{16,24},{24,16},{1,9},{9,1},{17,25},{25,17},{2,10},{10... | collective-permute-start | bytes 147464 | tf_op jit(solution)/shard_map/ppermute | solution.py:266
  19.8 5.7 %collective-permute-start.3 = (bf16[192,128]{1,0:T(8,128)(2,1)S(1)}, bf16[192,128]{1,0:T(8,128)(2,1)S(1)}, u32[]{:S(2)}, u32[]{:S(2)}) collective-permute-start(bf16[192,128]{1,0:T(8,128)(2,1)S(1)} %get-tuple-element.29.refs_2_), channel_id=1, source_target_pairs={{0,16},{8,24},{16,0},{24,8},{1,17},{9,25},{17,1},{25,9},{2,18},{10... | collective-permute-start | bytes 147464 | tf_op jit(solution)/shard_map/ppermute | solution.py:266
  22.4 6.0 %collective-permute-start.4 = (bf16[192,128]{1,0:T(8,128)(2,1)S(1)}, bf16[192,128]{1,0:T(8,128)(2,1)S(1)}, u32[]{:S(2)}, u32[]{:S(2)}) collective-permute-start(bf16[192,128]{1,0:T(8,128)(2,1)S(1)} %get-tuple-element.29.refs_2_), channel_id=1, source_target_pairs={{0,24},{8,16},{16,8},{24,0},{1,25},{9,17},{17,9},{25,1},{2,26},{10... | collective-permute-start | bytes 147464 | tf_op jit(solution)/shard_map/ppermute | solution.py:266
  28.4 5.1 %collective-permute-start.5 = (bf16[208,128]{1,0:T(8,128)(2,1)S(1)}, bf16[208,128]{1,0:T(8,128)(2,1)S(1)}, u32[]{:S(2)}, u32[]{:S(2)}) collective-permute-start(bf16[208,128]{1,0:T(8,128)(2,1)S(1)} %get-tuple-element.30.refs_0_), channel_id=1, source_target_pairs={{0,16},{8,24},{16,0},{24,8},{1,17},{9,25},{17,1},{25,9},{2,18},{10... | collective-permute-start | bytes 159752 | tf_op jit(solution)/shard_map/ppermute | solution.py:266
  50.5 1.6 %collective-permute-start.6 = (bf16[4,288,128]{2,1,0:T(8,128)(2,1)S(1)}, bf16[4,288,128]{2,1,0:T(8,128)(2,1)S(1)}, u32[]{:S(2)}, u32[]{:S(2)}) collective-permute-start(bf16[4,288,128]{2,1,0:T(8,128)(2,1)S(1)} %all_to_all.17.refs_0_), channel_id=1, source_target_pairs={{0,1},{1,0},{2,3},{3,2},{4,5},{5,4},{6,7},{7,6},{8,9},{9,8},{10,11... | collective-permute-start | bytes 884744 | tf_op jit(solution)/shard_map/ppermute | solution.py:266

commit v6 on v4

--- a/solution.py
+++ b/solution.py
@@ -85,7 +85,7 @@
         pl.loop(0, count)(step)
 
 
-def terms_kernel(plan, act_a, dy_a, act_e, dy_e, w, m, v, full, send, pack, act_a_v, dy_a_v, act_e_v, dy_e_v, state, sems):
+def terms_kernel(plan, act_a, dy_a, act_e, dy_e, full, send, act_a_v, dy_a_v, act_e_v, dy_e_v, sems):
     tile = plan.width // STEPS
     small = [
         pltpu.make_async_copy(act_a, act_a_v, sems.at[0]),
@@ -96,8 +96,7 @@
         cols = pl.ds(t * tile, tile)
         big.append(pltpu.make_async_copy(dy_a.at[:, cols], dy_a_v.at[:, cols], sems.at[2 + 2 * t]))
         big.append(pltpu.make_async_copy(dy_e.at[:, cols], dy_e_v.at[:, cols], sems.at[3 + 2 * t]))
-    extra = [pltpu.make_async_copy(ref, state.at[i], sems.at[2 + 2 * STEPS + i]) for i, ref in enumerate((w, m, v))]
-    for copy in small + big + extra:
+    for copy in small + big:
         copy.start()
 
     me = lax.axis_index("dp")
@@ -132,39 +131,28 @@
         send[pl.ds(c * plan.chunk, plan.chunk), :] = full[
             pl.ds((plan.chips + c) * plan.chunk, plan.chunk), :
         ].astype(bf16)
-    for copy in extra:
-        copy.wait()
-    size = plan.size_a
-    high, low = two_pieces(state[0])
-    for i, value in enumerate((high, low, state[1], state[2])):
-        pack[pl.ds(i * size, size), :] = value.astype(bf16)
-
-
-def make_terms(plan, act_a, dy_a, act_e, dy_e, w, m, v):
-    args = (act_a, dy_a, act_e, dy_e, w, m, v)
+
+
+def make_terms(plan, *args):
+    act_a, dy_a, act_e, dy_e = args
     half = plan.chips * plan.chunk
     return call(
         lambda *refs: terms_kernel(plan, *refs),
         args,
-        [((2 * half, LANES), f32), ((half, LANES), bf16), ((4 * plan.size_a, LANES), bf16)],
+        [((2 * half, LANES), f32), ((half, LANES), bf16)],
         [
             pltpu.VMEM(act_a.shape, bf16),
             pltpu.VMEM(dy_a.shape, bf16),
             pltpu.VMEM(act_e.shape, bf16),
             pltpu.VMEM(dy_e.shape, bf16),
-            pltpu.VMEM((3,) + w.shape, f32),
-            pltpu.SemaphoreType.DMA((5 + 2 * STEPS,)),
+            pltpu.SemaphoreType.DMA((2 + 2 * STEPS,)),
         ],
         [pl.BlockSpec(memory_space=pltpu.HBM)] * len(args),
     )
 
 
 def share_kernel(plan, *refs):
-    packs, refs = refs[: plan.n_expert], refs[plan.n_expert :]
-    own, got, (payload, g_exp, states) = refs[0], refs[1:-3], refs[-3:]
-    place = lax.axis_index("expert")
-    for q, pack in enumerate(packs):
-        states[place ^ q] = pack[...]
+    own, got, (payload, g_exp) = refs[0], refs[1:-2], refs[-2:]
     total = own[...]
     for ref in got:
         total = total + ref[...].astype(f32)
@@ -208,8 +196,8 @@
 
     wa_new[...], ma_new[...], va_new[...] = adamw(g_attn[rows(place), :], wa[...], ma[...], va[...], factor)
     for e in range(plan.n_expert):
-        high, low, moment, second = [states[e, pl.ds(i * size, size), :].astype(f32) for i in range(4)]
-        weight, _, _ = adamw(g_attn[pl.ds(e * size, size), :], high + low, moment, second, factor)
+        old = [states[e, pl.ds(i * size, size), :] for i in range(3)]
+        weight, _, _ = adamw(g_attn[pl.ds(e * size, size), :], *old, factor)
         mine[pl.ds(e * size, size), :] = weight.astype(bf16)
     weight, moment, second = adamw(g_exp[...], we[...], me[...], ve[...], factor)
     we_new[...], me_new[...], ve_new[...] = weight, moment, second
@@ -288,18 +276,16 @@
     state_e = [to_blocks(value[0]) for value in (w_exp, m_exp, v_exp)]
 
     held = [pltpu.with_memory_space_constraint(x, pltpu.HBM) for x in (act_attn.T, dy_attn, act_exp[0].T, dy_exp[0])]
-    full, send, pack = make_terms(plan, *held, *[pltpu.with_memory_space_constraint(x, pltpu.HBM) for x in state_a])
+    states = lax.all_gather(jnp.concatenate(state_a), "expert")
+    full, send = make_terms(plan, *held)
     got = swap(send, "dp", 1)
-    packs = [pack] + [swap(pack, "expert", q) for q in range(1, n_expert)]
     sums = [
         full[c * chunk : (c + 1) * chunk] + got[c * chunk : (c + 1) * chunk].astype(f32) for c in range(chips)
     ]
     got = [swap(sums[c].astype(bf16), "dp", 2 * c) for c in range(1, chips)]
     shared = ((plan.all_a + 16, LANES), bf16)
-    payload, g_exp, states = call(
-        lambda *refs: share_kernel(plan, *refs),
-        packs + [sums[0]] + got,
-        [shared, ((plan.size_e, LANES), f32), ((n_expert, 4 * plan.size_a, LANES), bf16)],
+    payload, g_exp = call(
+        lambda *refs: share_kernel(plan, *refs), [sums[0]] + got, [shared, ((plan.size_e, LANES), f32)]
     )
     distance = 1
     while 2 * distance < n_expert:

time: 49.8 us -> 56.1 us (1.13)
  blocking collectives: 0 us -> 14.6 us
  starting transfers between devices: 18.6 us -> 14.4 us
  waiting for transfers between devices: 23.9 us -> 20 us
    all_gather x0 -> x1, blocking collectives: none -> 14.6 us  [body(): states = lax.all_gather(jnp.concatenate(state_a), 'expert')]
    ppermute x19 -> x16, starting transfers between devices: 18.6 us -> 14.4 us  [swap(): return lax.ppermute(value, axis, [(i, i ^ distance) for i in range(size)])]
    ppermute x19 -> x16, waiting for transfers between devices: 23.9 us -> 20 us  [swap(): return lax.ppermute(value, axis, [(i, i ^ distance) for i in range(size)])]
  transfers between devices with their start and end apart: 19 -> 16, of which waited for: 11 -> 12; matrix products, arithmetic and copies ran while one was open for 0% -> 0% of each run, Pallas kernels for 0% -> 0%
where the time goes in v6:
time: 56.1 us; the launch traced here: 55.9 us
  waiting for transfers between devices  20 us (36%)
  blocking collectives  14.6 us (26%)
  starting transfers between devices  14.4 us (26%)
  Pallas kernels  6.11 us (11%)
  between operations  0.76 us (1%)
    ppermute x16, waiting for transfers between devices, swap(): return lax.ppermute(value, axis, [(i, i ^ distance) for i in range(size)])  20 us
    all_gather x1, blocking collectives, body(): states = lax.all_gather(jnp.concatenate(state_a), 'expert')  14.6 us
    ppermute x16, starting transfers between devices, swap(): return lax.ppermute(value, axis, [(i, i ^ distance) for i in range(size)])  14.4 us
    pallas_call x6, Pallas kernels, call(): pl.pallas_call(kernel, in_specs=specs or [whole] * len(args), out_specs=[...  6.11 us
  transfers between devices with their start and end apart: 16, of which 12 were waited for; matrix products, arithmetic and copies ran while one was open for 0% of the time, Pallas kernels for 0%

profile of v6, /device:TPU:0, one launch (start us, length us, event | category | flops | bytes accessed | tf_op | source)
XLA Modules:
  0.0 55.9 jit_solution(11544586113963415723)
XLA Ops:
  0.6 3.6 %shard_map.161 = (f32[2304,128]{1,0:T(8,128)S(1)}, bf16[1152,128]{1,0:T(8,128)(2,1)S(1)}) custom-call(bf16[32,256]{1,0:T(8,128)(2,1)} %bitcast.53, bf16[256,6144]{1,0:T(8,128)(2,1)} %refs_1_.1, bf16[16,128]{1,0:T(8,128)(2,1)} %bitcast.54, bf16[128,6144]{1,0:T(8,128)(2,1)} %bitcast.52), custom_call_target="tpu_custom_call" | custom-call | tf_op jit(solution)/shard_map/pallas_call | solution.py:58
  4.2 0.0 copy-start
  4.2 0.0 copy-start.3
  4.3 0.5 collective-permute-start
  4.8 1.2 %collective-permute-done = bf16[1152,128]{1,0:T(8,128)(2,1)S(1)} collective-permute-done((bf16[1152,128]{1,0:T(8,128)(2,1)S(1)}, bf16[1152,128]{1,0:T(8,128)(2,1)S(1)}, u32[]{:S(2)}, u32[]{:S(2)}) %collective-permute-start) | collective-permute-done | bytes 294944 | tf_op jit(solution)/shard_map/ppermute | solution.py:254
  6.0 0.1 add_convert_fusion
  6.1 2.9 %collective-permute-start.1 = (bf16[288,128]{1,0:T(8,128)(2,1)S(1)}, bf16[288,128]{1,0:T(8,128)(2,1)S(1)}, u32[]{:S(2)}, u32[]{:S(2)}) collective-permute-start(bf16[288,128]{1,0:T(8,128)(2,1)S(1)} %get-tuple-element.40), channel_id=1, source_target_pairs={{0,2},{1,3},{2,0},{3,1},{4,6},{5,7},{6,4},{7,5},{8,10},{9,11},{10,... | collective-permute-start | bytes 221192 | tf_op jit(solution)/shard_map/ppermute | solution.py:254
  9.0 1.5 %collective-permute-start.2 = (bf16[288,128]{1,0:T(8,128)(2,1)S(1)}, bf16[288,128]{1,0:T(8,128)(2,1)S(1)}, u32[]{:S(2)}, u32[]{:S(2)}) collective-permute-start(bf16[288,128]{1,0:T(8,128)(2,1)S(1)} %get-tuple-element.39), channel_id=1, source_target_pairs={{0,4},{1,5},{2,6},{3,7},{4,0},{5,1},{6,2},{7,3},{8,12},{9,13},{10,... | collective-permute-start | bytes 221192 | tf_op jit(solution)/shard_map/ppermute | solution.py:254
  10.5 0.0 collective-permute-start.3
  10.5 1.0 %collective-permute-done.1.refs_1_ = bf16[288,128]{1,0:T(8,128)(2,1)S(1)} collective-permute-done((bf16[288,128]{1,0:T(8,128)(2,1)S(1)}, bf16[288,128]{1,0:T(8,128)(2,1)S(1)}, u32[]{:S(2)}, u32[]{:S(2)}) %collective-permute-start.1) | collective-permute-done | bytes 73760 | tf_op jit(solution)/shard_map/ppermute | solution.py:254
  11.6 1.8 %collective-permute-done.2.refs_2_ = bf16[288,128]{1,0:T(8,128)(2,1)S(1)} collective-permute-done((bf16[288,128]{1,0:T(8,128)(2,1)S(1)}, bf16[288,128]{1,0:T(8,128)(2,1)S(1)}, u32[]{:S(2)}, u32[]{:S(2)}) %collective-permute-start.2) | collective-permute-done | bytes 73760 | tf_op jit(solution)/shard_map/ppermute | solution.py:254
  13.3 2.4 %collective-permute-done.3.refs_3_ = bf16[288,128]{1,0:T(8,128)(2,1)S(1)} collective-permute-done((bf16[288,128]{1,0:T(8,128)(2,1)S(1)}, bf16[288,128]{1,0:T(8,128)(2,1)S(1)}, u32[]{:S(2)}, u32[]{:S(2)}) %collective-permute-start.3) | collective-permute-done | bytes 73760 | tf_op jit(solution)/shard_map/ppermute | solution.py:254
  15.8 1.6 %collective-permute-start.4 = (bf16[208,128]{1,0:T(8,128)(2,1)S(1)}, bf16[208,128]{1,0:T(8,128)(2,1)S(1)}, u32[]{:S(2)}, u32[]{:S(2)}) collective-permute-start(bf16[208,128]{1,0:T(8,128)(2,1)S(1)} %get-tuple-element.25.refs_0_), channel_id=1, source_target_pairs={{0,8},{8,0},{16,24},{24,16},{1,9},{9,1},{17,25},{25,17},{2,10},{10... | collective-permute-start | bytes 159752 | tf_op jit(solution)/shard_map/ppermute | solution.py:254
  17.5 2.6 %collective-permute-done.4.refs_1_ = bf16[208,128]{1,0:T(8,128)(2,1)S(1)} collective-permute-done((bf16[208,128]{1,0:T(8,128)(2,1)S(1)}, bf16[208,128]{1,0:T(8,128)(2,1)S(1)}, u32[]{:S(2)}, u32[]{:S(2)}) %collective-permute-start.4) | collective-permute-done | bytes 53280 | tf_op jit(solution)/shard_map/ppermute | solution.py:254
  20.0 2.9 %collective-permute-start.5 = (bf16[208,128]{1,0:T(8,128)(2,1)S(1)}, bf16[208,128]{1,0:T(8,128)(2,1)S(1)}, u32[]{:S(2)}, u32[]{:S(2)}) collective-permute-start(bf16[208,128]{1,0:T(8,128)(2,1)S(1)} %shard_map.163.refs_0_), channel_id=1, source_target_pairs={{0,16},{8,24},{16,0},{24,8},{1,17},{9,25},{17,1},{25,9},{2,18},{10... | collective-permute-start | bytes 159752 | tf_op jit(solution)/shard_map/ppermute | solution.py:254
  22.9 2.2 %collective-permute-done.5.refs_1_ = bf16[208,128]{1,0:T(8,128)(2,1)S(1)} collective-permute-done((bf16[208,128]{1,0:T(8,128)(2,1)S(1)}, bf16[208,128]{1,0:T(8,128)(2,1)S(1)}, u32[]{:S(2)}, u32[]{:S(2)}) %collective-permute-start.5) | collective-permute-done | bytes 53280 | tf_op jit(solution)/shard_map/ppermute | solution.py:254
  25.2 0.1 collective-permute-start.6
  25.2 1.2 %collective-permute-done.6 = f32[8,128]{1,0:T(8,128)S(1)} collective-permute-done((f32[8,128]{1,0:T(8,128)S(1)}, f32[8,128]{1,0:T(8,128)S(1)}, u32[]{:S(2)}, u32[]{:S(2)}) %collective-permute-start.6) | collective-permute-done | bytes 4128 | tf_op jit(solution)/shard_map/ppermute | solution.py:254
  26.4 0.5 collective-permute-start.7
  26.9 3.1 %collective-permute-done.7 = f32[8,128]{1,0:T(8,128)S(1)} collective-permute-done((f32[8,128]{1,0:T(8,128)S(1)}, f32[8,128]{1,0:T(8,128)S(1)}, u32[]{:S(2)}, u32[]{:S(2)}) %collective-permute-start.7) | collective-permute-done | bytes 4128 | tf_op jit(solution)/shard_map/ppermute | solution.py:254
  30.0 0.7 %collective-permute-start.8 = (f32[8,128]{1,0:T(8,128)S(1)}, f32[8,128]{1,0:T(8,128)S(1)}, u32[]{:S(2)}, u32[]{:S(2)}) collective-permute-start(f32[8,128]{1,0:T(8,128)S(1)} %add.26), channel_id=1, source_target_pairs={{0,4},{1,5},{2,6},{3,7},{4,0},{5,1},{6,2},{7,3},{8,12},{9,13},{10,... | collective-permute-start | bytes 12296 | tf_op jit(solution)/shard_map/ppermute | solution.py:254
  30.7 14.6 %all-gather = f32[576,128]{1,0:T(8,128)S(1)} all-gather(f32[144,128]{1,0:T(8,128)S(1)} %pad_maximum_fusion), channel_id=2, replica_groups=mesh['expert'=4,'dp'=8] {'expert'}, dimensions={0}, use_global_device_ids=true | all-gather | bytes 368640 | tf_op jit(solution)/shard_map/all_gather | solution.py:279
  45.3 0.9 %shard_map.165 = (f32[48,128]{1,0:T(8,128)}, f32[48,128]{1,0:T(8,128)}, f32[48,128]{1,0:T(8,128)}, f32[96,128]{1,0:T(8,128)}, f32[96,128]{1,0:T(8,128)}, /*index...) custom-call(f32[8,128]{1,0:T(8,128)S(1)} %add.27.refs_0_, f32[192,128]{1,0:T(8,128)S(1)} %get-tuple-element.27.refs_1_, ...), custom_call_target="tpu_custom_call" | custom-call | tf_op jit(solution)/shard_map/pallas_call | solution.py:58
  46.2 0.5 collective-permute-start.9
  46.6 1.1 %collective-permute-start.10 = (bf16[288,128]{1,0:T(8,128)(2,1)S(1)}, bf16[288,128]{1,0:T(8,128)(2,1)S(1)}, u32[]{:S(2)}, u32[]{:S(2)}) collective-permute-start(bf16[288,128]{1,0:T(8,128)(2,1)S(1)} %get-tuple-element.35.refs_0_), channel_id=1, source_target_pairs={{0,4},{1,5},{2,6},{3,7},{4,0},{5,1},{6,2},{7,3},{8,12},{9,13},{10,... | collective-permute-start | bytes 221192 | tf_op jit(solution)/shard_map/ppermute | solution.py:254
  47.8 1.9 %collective-permute-start.11 = (bf16[288,128]{1,0:T(8,128)(2,1)S(1)}, bf16[288,128]{1,0:T(8,128)(2,1)S(1)}, u32[]{:S(2)}, u32[]{:S(2)}) collective-permute-start(bf16[288,128]{1,0:T(8,128)(2,1)S(1)} %get-tuple-element.35.refs_0_), channel_id=1, source_target_pairs={{0,6},{1,7},{2,4},{3,5},{4,2},{5,3},{6,0},{7,1},{8,14},{9,15},{10,... | collective-permute-start | bytes 221192 | tf_op jit(solution)/shard_map/ppermute | solution.py:254
  49.6 0.9 %collective-permute-done.9.refs_1_ = bf16[288,128]{1,0:T(8,128)(2,1)S(1)} collective-permute-done((bf16[288,128]{1,0:T(8,128)(2,1)S(1)}, bf16[288,128]{1,0:T(8,128)(2,1)S(1)}, u32[]{:S(2)}, u32[]{:S(2)}) %collective-permute-start.9) | collective-permute-done | bytes 73760 | tf_op jit(solution)/shard_map/ppermute | solution.py:254
  50.5 0.5 collective-permute-done.10.refs_2_
  51.0 0.1 collective-permute-start.14
  51.0 2.0 %collective-permute-done.11.refs_3_ = bf16[288,128]{1,0:T(8,128)(2,1)S(1)} collective-permute-done((bf16[288,128]{1,0:T(8,128)(2,1)S(1)}, bf16[288,128]{1,0:T(8,128)(2,1)S(1)}, u32[]{:S(2)}, u32[]{:S(2)}) %collective-permute-start.11) | collective-permute-done | bytes 73760 | tf_op jit(solution)/shard_map/ppermute | solution.py:254
  53.0 1.2 %collective-permute-done.15.refs_7_ = bf16[288,128]{1,0:T(8,128)(2,1)S(1)} collective-permute-done((bf16[288,128]{1,0:T(8,128)(2,1)S(1)}, bf16[288,128]{1,0:T(8,128)(2,1)S(1)}, u32[]{:S(2)}, u32[]{:S(2)}) %collective-permute-start.15) | collective-permute-done | bytes 73760 | tf_op jit(solution)/shard_map/ppermute | solution.py:254
  54.3 1.6 %shard_map.166 = (bf16[32,6144]{1,0:T(8,128)(2,1)}, bf16[1,16,6144]{2,1,0:T(8,128)(2,1)}) custom-call(bf16[288,128]{1,0:T(8,128)(2,1)S(1)} %get-tuple-element.35.refs_0_, bf16[288,128]{1,0:T(8,128)(2,1)S(1)} %collective-permute-done.9.refs_1_, bf16[288,128]{1,0:T(8,128)(2,1)S(1)} %collective-permute-done.10.refs_2_, ...), custom_call_target="tpu_custom_call" | custom-call | tf_op jit(solution)/shard_map/pallas_call | solution.py:58
  (24 shorter events, 0.2 us)
Async XLA Ops:
  4.2 22.7 %copy-start = (f32[1,6144]{1,0:T(1,128)S(1)}, f32[1,6144]{1,0:T(1,128)}, u32[]{:S(2)}) copy-start(f32[1,6144]{1,0:T(1,128)} %param.14) | copy-start | bytes 73732
  4.2 22.7 %copy-start.1 = (f32[1,6144]{1,0:T(1,128)S(1)}, f32[1,6144]{1,0:T(1,128)}, u32[]{:S(2)}) copy-start(f32[1,6144]{1,0:T(1,128)} %param.15) | copy-start | bytes 73732
  4.2 22.7 %copy-start.2 = (f32[1,6144]{1,0:T(1,128)S(1)}, f32[1,6144]{1,0:T(1,128)}, u32[]{:S(2)}) copy-start(f32[1,6144]{1,0:T(1,128)} %param.16) | copy-start | bytes 73732
  4.2 41.0 %copy-start.3 = (f32[1,2,6144]{2,1,0:T(2,128)S(1)}, f32[1,2,6144]{2,1,0:T(2,128)}, u32[]{:S(2)}) copy-start(f32[1,2,6144]{2,1,0:T(2,128)} %param.17) | copy-start | bytes 147460
  4.3 41.0 %copy-start.4 = (f32[1,2,6144]{2,1,0:T(2,128)S(1)}, f32[1,2,6144]{2,1,0:T(2,128)}, u32[]{:S(2)}) copy-start(f32[1,2,6144]{2,1,0:T(2,128)} %param.18) | copy-start | bytes 147460
  4.3 41.0 %copy-start.5 = (f32[1,2,6144]{2,1,0:T(2,128)S(1)}, f32[1,2,6144]{2,1,0:T(2,128)}, u32[]{:S(2)}) copy-start(f32[1,2,6144]{2,1,0:T(2,128)} %param.19) | copy-start | bytes 147460
  4.3 1.7 %collective-permute-start = (bf16[1152,128]{1,0:T(8,128)(2,1)S(1)}, bf16[1152,128]{1,0:T(8,128)(2,1)S(1)}, u32[]{:S(2)}, u32[]{:S(2)}) collective-permute-start(bf16[1152,128]{1,0:T(8,128)(2,1)S(1)} %get-tuple-element.24), channel_id=1, source_target_pairs={{0,1},{1,0},{2,3},{3,2},{4,5},{5,4},{6,7},{7,6},{8,9},{9,8},{10,11... | collective-permute-start | bytes 884744 | tf_op jit(solution)/shard_map/ppermute | solution.py:254
  6.1 5.5 %collective-permute-start.1 = (bf16[288,128]{1,0:T(8,128)(2,1)S(1)}, bf16[288,128]{1,0:T(8,128)(2,1)S(1)}, u32[]{:S(2)}, u32[]{:S(2)}) collective-permute-start(bf16[288,128]{1,0:T(8,128)(2,1)S(1)} %get-tuple-element.40), channel_id=1, source_target_pairs={{0,2},{1,3},{2,0},{3,1},{4,6},{5,7},{6,4},{7,5},{8,10},{9,11},{10,... | collective-permute-start | bytes 221192 | tf_op jit(solution)/shard_map/ppermute | solution.py:254
  9.0 4.4 %collective-permute-start.2 = (bf16[288,128]{1,0:T(8,128)(2,1)S(1)}, bf16[288,128]{1,0:T(8,128)(2,1)S(1)}, u32[]{:S(2)}, u32[]{:S(2)}) collective-permute-start(bf16[288,128]{1,0:T(8,128)(2,1)S(1)} %get-tuple-element.39), channel_id=1, source_target_pairs={{0,4},{1,5},{2,6},{3,7},{4,0},{5,1},{6,2},{7,3},{8,12},{9,13},{10,... | collective-permute-start | bytes 221192 | tf_op jit(solution)/shard_map/ppermute | solution.py:254
  10.5 5.3 %collective-permute-start.3 = (bf16[288,128]{1,0:T(8,128)(2,1)S(1)}, bf16[288,128]{1,0:T(8,128)(2,1)S(1)}, u32[]{:S(2)}, u32[]{:S(2)}) collective-permute-start(bf16[288,128]{1,0:T(8,128)(2,1)S(1)} %get-tuple-element.38), channel_id=1, source_target_pairs={{0,6},{1,7},{2,4},{3,5},{4,2},{5,3},{6,0},{7,1},{8,14},{9,15},{10,... | collective-permute-start | bytes 221192 | tf_op jit(solution)/shard_map/ppermute | solution.py:254
  15.8 4.2 %collective-permute-start.4 = (bf16[208,128]{1,0:T(8,128)(2,1)S(1)}, bf16[208,128]{1,0:T(8,128)(2,1)S(1)}, u32[]{:S(2)}, u32[]{:S(2)}) collective-permute-start(bf16[208,128]{1,0:T(8,128)(2,1)S(1)} %get-tuple-element.25.refs_0_), channel_id=1, source_target_pairs={{0,8},{8,0},{16,24},{24,16},{1,9},{9,1},{17,25},{25,17},{2,10},{10... | collective-permute-start | bytes 159752 | tf_op jit(solution)/shard_map/ppermute | solution.py:254
  20.0 5.1 %collective-permute-start.5 = (bf16[208,128]{1,0:T(8,128)(2,1)S(1)}, bf16[208,128]{1,0:T(8,128)(2,1)S(1)}, u32[]{:S(2)}, u32[]{:S(2)}) collective-permute-start(bf16[208,128]{1,0:T(8,128)(2,1)S(1)} %shard_map.163.refs_0_), channel_id=1, source_target_pairs={{0,16},{8,24},{16,0},{24,8},{1,17},{9,25},{17,1},{25,9},{2,18},{10... | collective-permute-start | bytes 159752 | tf_op jit(solution)/shard_map/ppermute | solution.py:254
  25.2 1.2 %collective-permute-start.6 = (f32[8,128]{1,0:T(8,128)S(1)}, f32[8,128]{1,0:T(8,128)S(1)}, u32[]{:S(2)}, u32[]{:S(2)}) collective-permute-start(f32[8,128]{1,0:T(8,128)S(1)} %get-tuple-element.26), channel_id=1, source_target_pairs={{0,1},{1,0},{2,3},{3,2},{4,5},{5,4},{6,7},{7,6},{8,9},{9,8},{10,11... | collective-permute-start | bytes 12296 | tf_op jit(solution)/shard_map/ppermute | solution.py:254
  26.4 3.6 %collective-permute-start.7 = (f32[8,128]{1,0:T(8,128)S(1)}, f32[8,128]{1,0:T(8,128)S(1)}, u32[]{:S(2)}, u32[]{:S(2)}) collective-permute-start(f32[8,128]{1,0:T(8,128)S(1)} %add.25), channel_id=1, source_target_pairs={{0,2},{1,3},{2,0},{3,1},{4,6},{5,7},{6,4},{7,5},{8,10},{9,11},{10,... | collective-permute-start | bytes 12296 | tf_op jit(solution)/shard_map/ppermute | solution.py:254
  30.0 15.2 %collective-permute-start.8 = (f32[8,128]{1,0:T(8,128)S(1)}, f32[8,128]{1,0:T(8,128)S(1)}, u32[]{:S(2)}, u32[]{:S(2)}) collective-permute-start(f32[8,128]{1,0:T(8,128)S(1)} %add.26), channel_id=1, source_target_pairs={{0,4},{1,5},{2,6},{3,7},{4,0},{5,1},{6,2},{7,3},{8,12},{9,13},{10,... | collective-permute-start | bytes 12296 | tf_op jit(solution)/shard_map/ppermute | solution.py:254
  46.2 4.4 %collective-permute-start.9 = (bf16[288,128]{1,0:T(8,128)(2,1)S(1)}, bf16[288,128]{1,0:T(8,128)(2,1)S(1)}, u32[]{:S(2)}, u32[]{:S(2)}) collective-permute-start(bf16[288,128]{1,0:T(8,128)(2,1)S(1)} %get-tuple-element.35.refs_0_), channel_id=1, source_target_pairs={{0,2},{1,3},{2,0},{3,1},{4,6},{5,7},{6,4},{7,5},{8,10},{9,11},{10,... | collective-permute-start | bytes 221192 | tf_op jit(solution)/shard_map/ppermute | solution.py:254
  46.6 4.4 %collective-permute-start.10 = (bf16[288,128]{1,0:T(8,128)(2,1)S(1)}, bf16[288,128]{1,0:T(8,128)(2,1)S(1)}, u32[]{:S(2)}, u32[]{:S(2)}) collective-permute-start(bf16[288,128]{1,0:T(8,128)(2,1)S(1)} %get-tuple-element.35.refs_0_), channel_id=1, source_target_pairs={{0,4},{1,5},{2,6},{3,7},{4,0},{5,1},{6,2},{7,3},{8,12},{9,13},{10,... | collective-permute-start | bytes 221192 | tf_op jit(solution)/shard_map/ppermute | solution.py:254
  47.8 5.3 %collective-permute-start.11 = (bf16[288,128]{1,0:T(8,128)(2,1)S(1)}, bf16[288,128]{1,0:T(8,128)(2,1)S(1)}, u32[]{:S(2)}, u32[]{:S(2)}) collective-permute-start(bf16[288,128]{1,0:T(8,128)(2,1)S(1)} %get-tuple-element.35.refs_0_), channel_id=1, source_target_pairs={{0,6},{1,7},{2,4},{3,5},{4,2},{5,3},{6,0},{7,1},{8,14},{9,15},{10,... | collective-permute-start | bytes 221192 | tf_op jit(solution)/shard_map/ppermute | solution.py:254
  49.6 3.4 %collective-permute-start.12 = (bf16[288,128]{1,0:T(8,128)(2,1)S(1)}, bf16[288,128]{1,0:T(8,128)(2,1)S(1)}, u32[]{:S(2)}, u32[]{:S(2)}) collective-permute-start(bf16[288,128]{1,0:T(8,128)(2,1)S(1)} %get-tuple-element.35.refs_0_), channel_id=1, source_target_pairs={{0,1},{1,0},{2,3},{3,2},{4,5},{5,4},{6,7},{7,6},{8,9},{9,8},{10,11... | collective-permute-start | bytes 221192 | tf_op jit(solution)/shard_map/ppermute | solution.py:254
  50.5 2.5 %collective-permute-start.13 = (bf16[288,128]{1,0:T(8,128)(2,1)S(1)}, bf16[288,128]{1,0:T(8,128)(2,1)S(1)}, u32[]{:S(2)}, u32[]{:S(2)}) collective-permute-start(bf16[288,128]{1,0:T(8,128)(2,1)S(1)} %collective-permute-done.9.refs_1_), channel_id=1, source_target_pairs={{0,1},{1,0},{2,3},{3,2},{4,5},{5,4},{6,7},{7,6},{8,9},{9,8},{10,11... | collective-permute-start | bytes 221192 | tf_op jit(solution)/shard_map/ppermute | solution.py:254
  51.0 2.1 %collective-permute-start.14 = (bf16[288,128]{1,0:T(8,128)(2,1)S(1)}, bf16[288,128]{1,0:T(8,128)(2,1)S(1)}, u32[]{:S(2)}, u32[]{:S(2)}) collective-permute-start(bf16[288,128]{1,0:T(8,128)(2,1)S(1)} %collective-permute-done.10.refs_2_), channel_id=1, source_target_pairs={{0,1},{1,0},{2,3},{3,2},{4,5},{5,4},{6,7},{7,6},{8,9},{9,8},{10,11... | collective-permute-start | bytes 221192 | tf_op jit(solution)/shard_map/ppermute | solution.py:254
  53.0 1.3 %collective-permute-start.15 = (bf16[288,128]{1,0:T(8,128)(2,1)S(1)}, bf16[288,128]{1,0:T(8,128)(2,1)S(1)}, u32[]{:S(2)}, u32[]{:S(2)}) collective-permute-start(bf16[288,128]{1,0:T(8,128)(2,1)S(1)} %collective-permute-done.11.refs_3_), channel_id=1, source_target_pairs={{0,1},{1,0},{2,3},{3,2},{4,5},{5,4},{6,7},{7,6},{8,9},{9,8},{10,11... | collective-permute-start | bytes 221192 | tf_op jit(solution)/shard_map/ppermute | solution.py:254

commit v7 on v6

v7 whole, which is shorter than its diff:
```python
import math

import jax
import jax.numpy as jnp
from jax import lax
from jax.experimental import pallas as pl
from jax.experimental.pallas import tpu as pltpu
from jax.sharding import PartitionSpec as P

beta_first = 0.9
beta_second = 0.95
bias_first = 1.0 - 0.9**10
bias_second = 1.0 - 0.95**10
learn_rate = 0.01
decay_rate = 0.1
adam_eps = 1e-08

LANES = 128
STEPS = 4
f32, bf16 = jnp.float32, jnp.bfloat16


def adamw(grad, weight, moment, second, factor):
    scaled = factor * grad
    moment_new = beta_first * moment + (1.0 - beta_first) * scaled
    second_new = beta_second * second + (1.0 - beta_second) * scaled * scaled
    update = moment_new / bias_first / (jnp.sqrt(second_new / bias_second) + adam_eps)
    weight_new = weight - learn_rate * (update + decay_rate * weight)
    return (weight_new, moment_new, second_new)


class Plan:
    def __init__(self, n_expert, n_dp, rows_a, rows_e, width):
        self.n_expert, self.n_dp, self.rows_a, self.rows_e = n_expert, n_dp, rows_a, rows_e
        self.width = width
        self.chips = n_dp // 2
        self.blocks = width // LANES
        self.size_a = self.blocks * rows_a
        self.size_e = self.blocks * rows_e
        self.all_a = n_expert * self.size_a
        self.chunk = self.all_a + self.size_e
        self.pair = 2 * self.chunk
        self.pack = 3 * (self.size_a + self.size_e)

    def places(self, block):
        attn = [
            (e * self.rows_a + r, e * self.size_a + block * self.rows_a + r)
            for e in range(self.n_expert)
            for r in range(self.rows_a)
        ]
        exp = [(r, self.all_a + block * self.rows_e + r) for r in range(self.rows_e)]
        return attn, exp


def dot(left, right):
    return lax.dot_general(left, right, (((1,), (0,)), ((), ())), preferred_element_type=f32)


def call(kernel, args, outs, scratch=(), in_specs=None, out_specs=None):
    whole = pl.BlockSpec(memory_space=pltpu.VMEM)
    return pl.pallas_call(
        kernel,
        in_specs=in_specs or [whole] * len(args),
        out_specs=out_specs or [whole] * len(outs),
        out_shape=[jax.ShapeDtypeStruct(shape, dtype) for shape, dtype in outs],
        scratch_shapes=list(scratch),
        compiler_params=pltpu.CompilerParams(vmem_limit_bytes=56 * 1024 * 1024),
    )(*args)


def two_pieces(value):
    high = value.astype(bf16).astype(f32)
    return jnp.concatenate([high, value - high], axis=0).astype(bf16)


def one_value(pieces):
    pieces = pieces.astype(f32)
    half = pieces.shape[0] // 2
    return pieces[:half] + pieces[half:]


def by_eights(value):
    return jnp.sum(value.reshape(-1, 8, LANES), axis=0)


def each(count, step, unrolled):
    if unrolled:
        for i in range(count):
            step(i)
    else:
        pl.loop(0, count)(step)


def aligned(index, unit):
    return index * unit if isinstance(index, int) else pl.multiple_of(index * unit, unit)


def terms_kernel(plan, act_a, dy_a, act_e, dy_e, wa, ma, va, we, me, ve, full, send, *scratch):
    act_a_v, dy_a_v, act_e_v, dy_e_v, state_a, state_e, sems = scratch
    tile = plan.width // STEPS
    small = [
        pltpu.make_async_copy(act_a, act_a_v, sems.at[0]),
        pltpu.make_async_copy(act_e, act_e_v, sems.at[1]),
    ]
    big = []
    for t in range(STEPS):
        cols = pl.ds(t * tile, tile)
        big.append(pltpu.make_async_copy(dy_a.at[:, cols], dy_a_v.at[:, cols], sems.at[2 + 2 * t]))
        big.append(pltpu.make_async_copy(dy_e.at[:, cols], dy_e_v.at[:, cols], sems.at[3 + 2 * t]))
    base = 2 + 2 * STEPS
    extra = [pltpu.make_async_copy(ref, state_a.at[i], sems.at[base + i]) for i, ref in enumerate((wa, ma, va))]
    extra += [pltpu.make_async_copy(ref, state_e.at[i], sems.at[base + 3 + i]) for i, ref in enumerate((we, me, ve))]
    for copy in small + big + extra:
        copy.start()

    chip = lax.axis_index("dp") // 2
    n_dp = plan.n_dp

    def pick(groups, per_owner, count):
        shape = (groups * n_dp, count)
        row = lax.broadcasted_iota(jnp.int32, shape, 0)
        col = lax.broadcasted_iota(jnp.int32, shape, 1)
        group, place = row // n_dp, row % n_dp
        owner = 2 * ((place // 2) ^ chip) + place % 2
        want = ((group // per_owner) * n_dp + owner) * per_owner + group % per_owner
        return (want == col).astype(bf16)

    pick_a = pick(plan.n_expert * plan.rows_a, plan.rows_a, act_a.shape[0])
    pick_e = pick(plan.rows_e, plan.rows_e, act_e.shape[0])
    for copy in small:
        copy.wait()
    left_a = dot(pick_a, act_a_v[...]).astype(bf16)
    left_e = dot(pick_e, act_e_v[...]).astype(bf16)
    for t in range(STEPS):
        cols = pl.ds(t * tile, tile)
        big[2 * t].wait()
        terms_a = dot(left_a, dy_a_v[:, cols])
        big[2 * t + 1].wait()
        terms_e = dot(left_e, dy_e_v[:, cols])
        for b in range(tile // LANES):
            attn, exp = plan.places(t * (tile // LANES) + b)
            span = slice(b * LANES, (b + 1) * LANES)
            for terms, places in ((terms_a, attn), (terms_e, exp)):
                for group, start in places:
                    full[pl.ds(start, n_dp, stride=plan.chunk), :] = terms[group * n_dp : (group + 1) * n_dp, span]
    for copy in extra:
        copy.wait()
    for i in range(3):
        send[pl.ds(i * plan.size_a, plan.size_a), :] = state_a[i].astype(bf16)
        send[pl.ds(3 * plan.size_a + i * plan.size_e, plan.size_e), :] = state_e[i].astype(bf16)

    def cast(p):
        send[pl.ds(plan.pack + aligned(p, plan.chunk), plan.chunk), :] = full[
            pl.ds(aligned(p, plan.chunk), plan.chunk), :
        ].astype(bf16)

    each(n_dp, cast, n_dp <= 8)


def make_terms(plan, args):
    act_a, dy_a, act_e, dy_e = args[:4]
    rows = n_rows = plan.n_dp * plan.chunk
    return call(
        lambda *refs: terms_kernel(plan, *refs),
        [pltpu.with_memory_space_constraint(arg, pltpu.HBM) for arg in args],
        [((rows, LANES), f32), ((plan.pack + n_rows, LANES), bf16)],
        [
            pltpu.VMEM(act_a.shape, bf16),
            pltpu.VMEM(dy_a.shape, bf16),
            pltpu.VMEM(act_e.shape, bf16),
            pltpu.VMEM(dy_e.shape, bf16),
            pltpu.VMEM((3, plan.size_a, LANES), f32),
            pltpu.VMEM((3, plan.size_e, LANES), f32),
            pltpu.SemaphoreType.DMA((8 + 2 * STEPS,)),
        ],
        in_specs=[pl.BlockSpec(memory_space=pltpu.HBM)] * len(args),
    )


def share_kernel(plan, *refs):
    own, got, (payload, g_exp) = refs[0], refs[1:-2], refs[-2:]
    square = jnp.zeros((8, LANES), f32)
    for k in range(2):
        a, e = plan.all_a, plan.size_e

        def total(start, size):
            value = own[pl.ds(start, size), :]
            for ref in got:
                value = value + ref[pl.ds(start, size), :].astype(f32)
            return value

        payload[pl.ds(k * a, a), :] = total(k * plan.chunk, a).astype(bf16)
        exp = total(k * plan.chunk + a, e)
        g_exp[pl.ds(k * e, e), :] = exp.astype(bf16)
        square = square + by_eights(exp * exp)
    payload[pl.ds(2 * plan.all_a, 16), :] = two_pieces(square)


def pair_sum(plan, mine, other):
    a = 2 * plan.all_a
    attn = mine[:a, :].astype(f32) + other[:a, :].astype(f32)
    return attn, one_value(mine[a:, :]) + one_value(other[a:, :])


def again_kernel(plan, mine, other, payload):
    attn, square = pair_sum(plan, mine, other)
    a = 2 * plan.all_a
    payload[:a, :] = attn.astype(bf16)
    payload[a:, :] = two_pieces(square)


def last_kernel(plan, mine, other, g_exp, rows):
    attn, square = pair_sum(plan, mine, other)
    square = square + by_eights(attn * attn)
    a, e = plan.all_a, plan.size_e
    for k in range(2):
        rows[pl.ds(k * plan.chunk, a), :] = attn[k * a : (k + 1) * a].astype(bf16)
        rows[pl.ds(k * plan.chunk + a, e), :] = g_exp[pl.ds(k * e, e), :]
    rows[pl.ds(plan.pair, 16), :] = two_pieces(square)


def state_kernel(plan, mine, other, *refs):
    packs, states = refs[:-1], refs[-1]
    place = lax.axis_index("expert")
    a, e = plan.size_a, plan.size_e
    for k, own in enumerate((mine, other)):
        for i in range(3):
            start = (k * 3 + i) * plan.chunk
            for q, pack in enumerate((None,) + packs):
                part = own[pl.ds(i * a, a), :] if pack is None else pack[pl.ds((k * 3 + i) * a, a), :]
                states[pl.ds(pl.multiple_of(start + (place ^ q) * a, 16), a), :] = part
            states[pl.ds(start + plan.all_a, e), :] = own[pl.ds(3 * a + i * e, e), :]


def tree_sum(values):
    while len(values) > 1:
        values = [values[i] + values[i + 1] for i in range(0, len(values), 2)]
    return values[0]


def update_kernel(plan, limit, *refs):
    chips, chunk = plan.chips, plan.chunk
    near_g, far_g, near_s, far_s = [refs[i * chips : (i + 1) * chips] for i in range(4)]
    refs = refs[4 * chips :]
    state, new, (attn, exp) = refs[:6], refs[6:12], refs[12:14]
    held, (rows, rows_a, rows_e, sems) = refs[14:20], refs[20:]
    me, place = lax.axis_index("dp"), lax.axis_index("expert")
    lead = (me % 2) == 1

    def grad(c, start, size):
        return jnp.where(lead, near_g[c][pl.ds(start, size), :], far_g[c][pl.ds(start, size), :])

    def old(c, start, size):
        return jnp.where(lead, far_s[c][pl.ds(start, size), :], near_s[c][pl.ds(start, size), :]).astype(f32)

    square = tree_sum([one_value(grad(c, plan.pair, 16)) for c in range(chips)])
    norm = jnp.sqrt(jnp.sum(square, keepdims=True))
    factor = jnp.minimum(1.0, limit / (norm + 1e-06))

    start = pl.multiple_of((me % 2) * chunk + place * plan.size_a, 16)
    own_a = grad(0, start, plan.size_a).astype(f32)
    start = pl.multiple_of((me % 2) * chunk + plan.all_a, 16)
    own_e = grad(0, start, plan.size_e).astype(f32)
    copies = []
    for b, own in enumerate((own_a, own_e)):
        values = adamw(own, *[ref[...] for ref in state[3 * b : 3 * b + 3]], factor)
        for i, value in enumerate(values):
            held[3 * b + i][...] = value
            copies.append(pltpu.make_async_copy(held[3 * b + i], new[3 * b + i], sems.at[3 * b + i]))
    for copy in copies:
        copy.start()

    piece = plan.size_a
    for c in range(chips):
        for k in range(2):
            owner = 2 * (c ^ (me // 2)) + k

            def one(p):
                weight, moment, second = [old(c, (k * 3 + i) * chunk + aligned(p, piece), piece) for i in range(3)]
                value = grad(c, k * chunk + aligned(p, piece), piece).astype(f32)
                weight, _, _ = adamw(value, weight, moment, second, factor)
                rows[pl.ds(pl.multiple_of(owner * chunk + aligned(p, piece), 16), piece), :] = weight

            each(chunk // piece, one, chips <= 4)

    count_e, n_dp = exp.shape[1], plan.n_dp

    def order(b):
        places_a, places_e = plan.places(b)
        span = pl.ds(aligned(b, LANES), LANES)
        values = [rows[pl.ds(start, n_dp, stride=chunk), :] for _, start in places_a]
        if plan.rows_a == 1:
            attn[:, span] = jnp.concatenate(values, axis=0).astype(bf16)
        else:
            for (group, _), value in zip(places_a, values):
                start = (group // plan.rows_a) * n_dp * plan.rows_a + group % plan.rows_a
                rows_a[pl.ds(start, n_dp, stride=plan.rows_a), :] = value
            attn[:, span] = rows_a[...].astype(bf16)
        for r, start in places_e:
            rows_e[pl.ds(b * count_e + r, n_dp, stride=plan.rows_e), :] = rows[pl.ds(start, n_dp, stride=chunk), :]

    each(plan.blocks, order, n_dp <= 8)
    for b in range(plan.blocks):
        exp[0, :, pl.ds(b * LANES, LANES)] = rows_e[pl.ds(b * count_e, count_e), :].astype(bf16)
    for copy in copies:
        copy.wait()


def update(plan, limit, gathered, state):
    count_a = plan.n_expert * plan.n_dp * plan.rows_a
    count_e = plan.n_dp * plan.rows_e
    vmem, hbm = pl.BlockSpec(memory_space=pltpu.VMEM), pl.BlockSpec(memory_space=pltpu.HBM)
    own = [((plan.size_a, LANES), f32)] * 3 + [((plan.size_e, LANES), f32)] * 3
    return call(
        lambda *refs: update_kernel(plan, limit, *refs),
        gathered + state,
        own + [((count_a, plan.width), bf16), ((1, count_e, plan.width), bf16)],
        [pltpu.VMEM(shape, dtype) for shape, dtype in own]
        + [
            pltpu.VMEM((plan.n_dp * plan.chunk, LANES), f32),
            pltpu.VMEM((count_a, LANES), f32),
            pltpu.VMEM((plan.blocks * count_e, LANES), f32),
            pltpu.SemaphoreType.DMA((6,)),
        ],
        out_specs=[hbm] * 6 + [vmem] * 2,
    )


def swap(value, axis, distance, cores=(0, 1)):
    size = lax.axis_size(axis)
    if axis == "dp":
        return lax.ppermute(value, axis, [(i, i ^ distance) for i in range(size) if i % 2 in cores])
    n_dp = lax.axis_size("dp")
    pairs = [(i * n_dp + j, (i ^ distance) * n_dp + j) for i in range(size) for j in range(n_dp) if j % 2 in cores]
    return lax.ppermute(value, ("expert", "dp"), pairs)


def to_blocks(value):
    rows, width = value.shape
    return value.reshape(rows, width // LANES, LANES).transpose(1, 0, 2).reshape(-1, LANES)


def from_blocks(value, rows):
    return value.reshape(-1, rows, LANES).transpose(1, 0, 2).reshape(rows, -1)


EVEN, ODD = (0,), (1,)


def body(act_attn, dy_attn, act_exp, dy_exp, w_attn, m_attn, v_attn, w_exp, m_exp, v_exp):
    width = w_attn.shape[1]
    n_expert = lax.axis_size("expert")
    n_dp = lax.axis_size("dp")
    rows_a, rows_e = w_attn.shape[0], w_exp.shape[1]
    plan = Plan(n_expert, n_dp, rows_a, rows_e, width)
    total_params = width * (act_attn.shape[1] + n_expert * act_exp.shape[2])
    limit = 0.5 * math.sqrt(total_params)
    chips, pair, size_a = plan.chips, plan.pair, plan.size_a
    state = [to_blocks(value) for value in (w_attn, m_attn, v_attn)]
    state += [to_blocks(value[0]) for value in (w_exp, m_exp, v_exp)]

    full, send = make_terms(plan, [act_attn.T, dy_attn, act_exp[0].T, dy_exp[0], *state])
    got = swap(send, "dp", 1)

    sums = [
        full[c * pair : (c + 1) * pair] + got[plan.pack + c * pair : plan.pack + (c + 1) * pair].astype(f32)
        for c in range(chips)
    ]
    parts = [swap(sums[c].astype(bf16), "dp", 2 * c, ODD) for c in range(1, chips)]
    shared = ((2 * plan.all_a + 16, LANES), bf16)
    payload, g_exp = call(
        lambda *refs: share_kernel(plan, *refs), [sums[0]] + parts, [shared, ((2 * plan.size_e, LANES), bf16)]
    )
    distance = 1
    while 2 * distance < n_expert:
        other = swap(payload, "expert", distance, ODD)
        (payload,) = call(lambda *refs: again_kernel(plan, *refs), [payload, other], [shared])
        distance *= 2
    other = swap(payload, "expert", distance, ODD)
    (grads,) = call(
        lambda *refs: last_kernel(plan, *refs), [payload, other, g_exp], [((pair + 16, LANES), bf16)]
    )
    near_g = [grads] + [swap(grads, "dp", 2 * c, ODD) for c in range(1, chips)]
    far_g = [swap(value, "dp", 1, ODD) for value in near_g]

    mine, other = send[: plan.pack], got[: plan.pack]
    packs = jnp.concatenate([mine[: 3 * size_a], other[: 3 * size_a]])
    packs = [swap(packs, "expert", q, EVEN) for q in range(1, n_expert)]
    (states,) = call(
        lambda *refs: state_kernel(plan, *refs), [mine, other, *packs], [((3 * pair, LANES), bf16)]
    )
    near_s = [states] + [swap(states, "dp", 2 * c, EVEN) for c in range(1, chips)]
    far_s = [swap(value, "dp", 1, EVEN) for value in near_s]

    *new, attn_full, expert_full = update(plan, limit, near_g + far_g + near_s + far_s, state)
    new_a = [from_blocks(value, rows_a) for value in new[:3]]
    new_e = [from_blocks(value, rows_e)[None] for value in new[3:]]
    return (*new_a, *new_e, attn_full, expert_full)


def solution(mesh):
    return jax.shard_map(
        body,
        mesh=mesh,
        in_specs=(
            P(("expert", "dp"), None),
            P(("expert", "dp"), None),
            P("expert", "dp", None),
            P("expert", "dp", None),
            P(("expert", "dp"), None),
            P(("expert", "dp"), None),
            P(("expert", "dp"), None),
            P("expert", "dp", None),
            P("expert", "dp", None),
            P("expert", "dp", None),
        ),
        out_specs=(
            P(("expert", "dp"), None),
            P(("expert", "dp"), None),
            P(("expert", "dp"), None),
            P("expert", "dp", None),
            P("expert", "dp", None),
            P("expert", "dp", None),
            P(),
            P("expert", None, None),
        ),
        check_vma=False,
    )
```

time: 56.1 us -> 84.1 us (1.50)
  starting transfers between devices: 14.4 us -> 46 us
  blocking collectives: 14.6 us -> 0 us
  Pallas kernels: 6.11 us -> 17.4 us
  waiting for transfers between devices: 20 us -> 9.46 us
  local copies, waits for them, and re-layouts: 0.04 us -> 7.28 us
  other arithmetic: 0.07 us -> 2.06 us
    ppermute x16 -> x23, starting transfers between devices: 14.4 us -> 46 us  [the longest x18 33.4 us: swap(): lax.ppermute(value, axis, [(i, i ^ distance) for i in range(size) if i %...]
    all_gather x1 -> x0, blocking collectives: 14.6 us -> none  [body(): states = lax.all_gather(jnp.concatenate(state_a), 'expert')]
    pallas_call x6, Pallas kernels: 6.11 us -> 17.4 us  [call(): pl.pallas_call(kernel, in_specs=in_specs or [whole] * len(args), out_spec...]
    ppermute x16 -> x23, waiting for transfers between devices: 20 us -> 9.46 us  [the longest x18 7.63 us: swap(): lax.ppermute(value, axis, [(i, i ^ distance) for i in range(size) if i %...]
    unnamed x12 -> x44, local copies, waits for them, and re-layouts: 0.04 us -> 4.31 us
    slice x0 -> x4, local copies, waits for them, and re-layouts: none -> 2.98 us  [the longest x2 2.2 us: body(): mine, other = (send[:plan.pack], got[:plan.pack])]
    convert_element_type x1, other arithmetic: 0.06 us -> 2.05 us  [body(): sums[c].astype(bf16)]
  transfers between devices with their start and end apart: 16 -> 23, of which waited for: 12 -> 6; matrix products, arithmetic and copies ran while one was open for 0% -> 4% of each run, Pallas kernels for 0% -> 6%
where the time goes in v7:
time: 84.1 us; the launch traced here: 83.4 us
  starting transfers between devices  46 us (55%)
  Pallas kernels  17.4 us (21%)
  waiting for transfers between devices  9.46 us (11%)
  local copies, waits for them, and re-layouts  7.28 us (9%)
  other arithmetic  2.06 us (2%)
  between operations  1.13 us (1%)
    ppermute x18, starting transfers between devices, swap(): lax.ppermute(value, axis, [(i, i ^ distance) for i in range(size) if i %...  33.4 us
    pallas_call x6, Pallas kernels, call(): pl.pallas_call(kernel, in_specs=in_specs or [whole] * len(args), out_spec...  17.4 us
    ppermute x5, starting transfers between devices, swap(): return lax.ppermute(value, ('expert', 'dp'), pairs)  12.6 us
    ppermute x18, waiting for transfers between devices, swap(): lax.ppermute(value, axis, [(i, i ^ distance) for i in range(size) if i %...  7.63 us
    unnamed x44, local copies, waits for them, and re-layouts  4.31 us
    slice x2, local copies, waits for them, and re-layouts, body(): mine, other = (send[:plan.pack], got[:plan.pack])  2.2 us
    convert_element_type x1, other arithmetic, body(): sums[c].astype(bf16)  2.05 us
    ppermute x5, waiting for transfers between devices, swap(): return lax.ppermute(value, ('expert', 'dp'), pairs)  1.83 us
  transfers between devices with their start and end apart: 23, of which 6 were waited for; matrix products, arithmetic and copies ran while one was open for 4% of the time, Pallas kernels for 6%

profile of v7, /device:TPU:0, one launch (start us, length us, event | category | flops | bytes accessed | tf_op | source)
XLA Modules:
  0.0 83.4 jit_solution(12469791933809446945)
XLA Ops:
  0.6 4.9 %shard_map.161 = (f32[2304,128]{1,0:T(8,128)}, bf16[2736,128]{1,0:T(8,128)(2,1)}) custom-call(bf16[32,256]{1,0:T(8,128)(2,1)} %bitcast.54, bf16[256,6144]{1,0:T(8,128)(2,1)} %refs_1_.1, bf16[16,128]{1,0:T(8,128)(2,1)} %bitcast.55, bf16[128,6144]{1,0:T(8,128)(2,1)} %bitcast.41, f32[48,128]{1,0:T(8,128)} %bitcast.48, f32[48,128]{1,0:T(8,128)} %bitcast.50, ...), custom_call_target="tpu_custom_call" | custom-call | tf_op jit(solution)/shard_map/pallas_call | solution.py:61
  6.0 2.0 %collective-permute-done = bf16[2736,128]{1,0:T(8,128)(2,1)S(1)} collective-permute-done((bf16[2736,128]{1,0:T(8,128)(2,1)}, bf16[2736,128]{1,0:T(8,128)(2,1)S(1)}, u32[]{:S(2)}, u32[]{:S(2)}) %collective-permute-start) | collective-permute-done | bytes 700448 | tf_op jit(solution)/shard_map/ppermute | solution.py:332
  8.0 2.0 %add_convert_fusion = (bf16[576,128]{1,0:T(8,128)(2,1)S(1)}, bf16[576,128]{1,0:T(8,128)(2,1)S(1)}, bf16[576,128]{1,0:T(8,128)(2,1)S(1)}, f32[576,128]{1,0:T(8,128)}) fusion(f32[2304,128]{1,0:T(8,128)} %get-tuple-element.20, bf16[2736,128]{1,0:T(8,128)(2,1)S(1)} %collective-permute-done), kind=kLoop, calls=%fused_computation | loop fusion | flops 811008 | bytes 2506752 | tf_op jit(solution)/shard_map/convert_element_type | solution.py:369
  10.7 0.7 collective-permute-start.2
  11.4 0.7 collective-permute-start.1
  12.1 0.8 slice.48
  13.6 1.9 %shard_map.162 = (bf16[400,128]{1,0:T(8,128)(2,1)}, bf16[192,128]{1,0:T(8,128)(2,1)}) custom-call(f32[576,128]{1,0:T(8,128)} %get-tuple-element.35.refs_0_, bf16[576,128]{1,0:T(8,128)(2,1)} %copy-done.16, bf16[576,128]{1,0:T(8,128)(2,1)} %copy-done.15, bf16[576,128]{1,0:T(8,128)(2,1)} %copy-done.14), custom_call_target="tpu_custom_call" | custom-call | tf_op jit(solution)/shard_map/pallas_call | solution.py:61
  16.2 6.9 %collective-permute-start.15 = (bf16[288,128]{1,0:T(8,128)(2,1)S(1)}, bf16[288,128]{1,0:T(8,128)(2,1)S(1)}, u32[]{:S(2)}, u32[]{:S(2)}) collective-permute-start(bf16[288,128]{1,0:T(8,128)(2,1)S(1)} %pad_maximum_fusion), channel_id=1, source_target_pairs={{0,24},{2,26},{4,28},{6,30},{8,16},{10,18},{12,20},{14,22},{16,8},... | collective-permute-start | bytes 221192 | tf_op jit(solution)/shard_map/ppermute | solution.py:335
  23.1 1.9 %collective-permute-start.14 = (bf16[288,128]{1,0:T(8,128)(2,1)S(1)}, bf16[288,128]{1,0:T(8,128)(2,1)S(1)}, u32[]{:S(2)}, u32[]{:S(2)}) collective-permute-start(bf16[288,128]{1,0:T(8,128)(2,1)S(1)} %pad_maximum_fusion), channel_id=1, source_target_pairs={{0,16},{2,18},{4,20},{6,22},{8,24},{10,26},{12,28},{14,30},{16,0},... | collective-permute-start | bytes 221192 | tf_op jit(solution)/shard_map/ppermute | solution.py:335
  25.0 2.5 %collective-permute-start.13 = (bf16[288,128]{1,0:T(8,128)(2,1)S(1)}, bf16[288,128]{1,0:T(8,128)(2,1)S(1)}, u32[]{:S(2)}, u32[]{:S(2)}) collective-permute-start(bf16[288,128]{1,0:T(8,128)(2,1)S(1)} %pad_maximum_fusion), channel_id=1, source_target_pairs={{0,8},{2,10},{4,12},{6,14},{8,0},{10,2},{12,4},{14,6},{16,24},{18,... | collective-permute-start | bytes 221192 | tf_op jit(solution)/shard_map/ppermute | solution.py:335
  27.5 1.5 %slice.46.refs_0_ = bf16[432,128]{1,0:T(8,128)(2,1)} slice(bf16[2736,128]{1,0:T(8,128)(2,1)} %get-tuple-element.21), slice={[0:432], [0:128]} | slice | bytes 221184 | tf_op jit(solution)/shard_map/slice | solution.py:386
  30.2 1.3 %collective-permute-done.13.refs_2_ = bf16[288,128]{1,0:T(8,128)(2,1)S(1)} collective-permute-done((bf16[288,128]{1,0:T(8,128)(2,1)S(1)}, bf16[288,128]{1,0:T(8,128)(2,1)S(1)}, u32[]{:S(2)}, u32[]{:S(2)}) %collective-permute-start.13) | collective-permute-done | bytes 73760 | tf_op jit(solution)/shard_map/ppermute | solution.py:335
  32.2 1.9 %shard_map.165.refs_8_ = bf16[1728,128]{1,0:T(8,128)(2,1)} custom-call(bf16[432,128]{1,0:T(8,128)(2,1)} %slice.46.refs_0_, bf16[432,128]{1,0:T(8,128)(2,1)} %slice.54.refs_1_, bf16[288,128]{1,0:T(8,128)(2,1)} %copy-done.21, bf16[288,128]{1,0:T(8,128)(2,1)} %copy-done.20, bf16[288,128]{1,0:T(8,128)(2,1)} %copy-done.19), custom_call_target="tpu_custom_call" | custom-call | tf_op jit(solution)/shard_map/pallas_call | solution.py:61
  34.0 4.9 %collective-permute-start.18 = (bf16[1728,128]{1,0:T(8,128)(2,1)}, bf16[1728,128]{1,0:T(8,128)(2,1)S(1)}, u32[]{:S(2)}, u32[]{:S(2)}) collective-permute-start(bf16[1728,128]{1,0:T(8,128)(2,1)} %shard_map.165.refs_8_), channel_id=1, source_target_pairs={{0,6},{2,4},{4,2},{6,0},{8,14},{10,12},{12,10},{14,8},{16,22},{18,... | collective-permute-start | bytes 1327112 | tf_op jit(solution)/shard_map/ppermute | solution.py:332
  38.9 2.4 %collective-permute-start.17 = (bf16[1728,128]{1,0:T(8,128)(2,1)}, bf16[1728,128]{1,0:T(8,128)(2,1)S(1)}, u32[]{:S(2)}, u32[]{:S(2)}) collective-permute-start(bf16[1728,128]{1,0:T(8,128)(2,1)} %shard_map.165.refs_8_), channel_id=1, source_target_pairs={{0,4},{2,6},{4,0},{6,2},{8,12},{10,14},{12,8},{14,10},{16,20},{18,... | collective-permute-start | bytes 1327112 | tf_op jit(solution)/shard_map/ppermute | solution.py:332
  41.3 2.0 %collective-permute-start.16 = (bf16[1728,128]{1,0:T(8,128)(2,1)}, bf16[1728,128]{1,0:T(8,128)(2,1)S(1)}, u32[]{:S(2)}, u32[]{:S(2)}) collective-permute-start(bf16[1728,128]{1,0:T(8,128)(2,1)} %shard_map.165.refs_8_), channel_id=1, source_target_pairs={{0,2},{2,0},{4,6},{6,4},{8,10},{10,8},{12,14},{14,12},{16,18},{18,... | collective-permute-start | bytes 1327112 | tf_op jit(solution)/shard_map/ppermute | solution.py:332
  44.0 1.6 %shard_map.163.refs_0_ = bf16[400,128]{1,0:T(8,128)(2,1)} custom-call(bf16[400,128]{1,0:T(8,128)(2,1)} %get-tuple-element.22.refs_0_, bf16[400,128]{1,0:T(8,128)(2,1)} %copy-done.17), custom_call_target="tpu_custom_call" | custom-call | tf_op jit(solution)/shard_map/pallas_call | solution.py:61
  46.9 1.7 %shard_map.164.refs_0_ = bf16[592,128]{1,0:T(8,128)(2,1)} custom-call(bf16[400,128]{1,0:T(8,128)(2,1)} %shard_map.163.refs_0_, bf16[400,128]{1,0:T(8,128)(2,1)} %copy-done.18, bf16[192,128]{1,0:T(8,128)(2,1)} %get-tuple-element.23.refs_2_), custom_call_target="tpu_custom_call" | custom-call | tf_op jit(solution)/shard_map/pallas_call | solution.py:61
  48.6 1.3 %collective-permute-start.9 = (bf16[592,128]{1,0:T(8,128)(2,1)}, bf16[592,128]{1,0:T(8,128)(2,1)S(1)}, u32[]{:S(2)}, u32[]{:S(2)}) collective-permute-start(bf16[592,128]{1,0:T(8,128)(2,1)} %shard_map.164.refs_0_), channel_id=1, source_target_pairs={{1,0},{3,2},{5,4},{7,6},{9,8},{11,10},{13,12},{15,14},{17,16},{19,... | collective-permute-start | bytes 454664 | tf_op jit(solution)/shard_map/ppermute | solution.py:332
  49.8 0.7 collective-permute-start.8
  50.5 3.0 %collective-permute-done.9.refs_4_ = bf16[592,128]{1,0:T(8,128)(2,1)S(1)} collective-permute-done((bf16[592,128]{1,0:T(8,128)(2,1)}, bf16[592,128]{1,0:T(8,128)(2,1)S(1)}, u32[]{:S(2)}, u32[]{:S(2)}) %collective-permute-start.9) | collective-permute-done | bytes 151584 | tf_op jit(solution)/shard_map/ppermute | solution.py:332
  54.2 7.2 %collective-permute-start.19 = (bf16[1728,128]{1,0:T(8,128)(2,1)}, bf16[1728,128]{1,0:T(8,128)(2,1)S(1)}, u32[]{:S(2)}, u32[]{:S(2)}) collective-permute-start(bf16[1728,128]{1,0:T(8,128)(2,1)} %shard_map.165.refs_8_), channel_id=1, source_target_pairs={{0,1},{2,3},{4,5},{6,7},{8,9},{10,11},{12,13},{14,15},{16,17},{18,... | collective-permute-start | bytes 1327112 | tf_op jit(solution)/shard_map/ppermute | solution.py:332
  61.4 0.7 collective-permute-start.6
  62.1 4.7 %collective-permute-start.22 = (bf16[1728,128]{1,0:T(8,128)(2,1)S(1)}, bf16[1728,128]{1,0:T(8,128)(2,1)S(1)}, u32[]{:S(2)}, u32[]{:S(2)}) collective-permute-start(bf16[1728,128]{1,0:T(8,128)(2,1)S(1)} %collective-permute-done.18.refs_11_), channel_id=1, source_target_pairs={{0,1},{2,3},{4,5},{6,7},{8,9},{10,11},{12,13},{14,15},{16,17},{18,... | collective-permute-start | bytes 1327112 | tf_op jit(solution)/shard_map/ppermute | solution.py:332
  66.8 1.3 %collective-permute-start.21 = (bf16[1728,128]{1,0:T(8,128)(2,1)S(1)}, bf16[1728,128]{1,0:T(8,128)(2,1)S(1)}, u32[]{:S(2)}, u32[]{:S(2)}) collective-permute-start(bf16[1728,128]{1,0:T(8,128)(2,1)S(1)} %collective-permute-done.17.refs_10_), channel_id=1, source_target_pairs={{0,1},{2,3},{4,5},{6,7},{8,9},{10,11},{12,13},{14,15},{16,17},{18,... | collective-permute-start | bytes 1327112 | tf_op jit(solution)/shard_map/ppermute | solution.py:332
  68.2 1.3 %collective-permute-start.20 = (bf16[1728,128]{1,0:T(8,128)(2,1)S(1)}, bf16[1728,128]{1,0:T(8,128)(2,1)S(1)}, u32[]{:S(2)}, u32[]{:S(2)}) collective-permute-start(bf16[1728,128]{1,0:T(8,128)(2,1)S(1)} %collective-permute-done.16.refs_9_), channel_id=1, source_target_pairs={{0,1},{2,3},{4,5},{6,7},{8,9},{10,11},{12,13},{14,15},{16,17},{18,... | collective-permute-start | bytes 1327112 | tf_op jit(solution)/shard_map/ppermute | solution.py:332
  69.5 1.3 %collective-permute-start.12 = (bf16[592,128]{1,0:T(8,128)(2,1)S(1)}, bf16[592,128]{1,0:T(8,128)(2,1)S(1)}, u32[]{:S(2)}, u32[]{:S(2)}) collective-permute-start(bf16[592,128]{1,0:T(8,128)(2,1)S(1)} %collective-permute-done.8.refs_3_), channel_id=1, source_target_pairs={{1,0},{3,2},{5,4},{7,6},{9,8},{11,10},{13,12},{15,14},{17,16},{19,... | collective-permute-start | bytes 454664 | tf_op jit(solution)/shard_map/ppermute | solution.py:332
  70.8 1.3 %collective-permute-start.11 = (bf16[592,128]{1,0:T(8,128)(2,1)S(1)}, bf16[592,128]{1,0:T(8,128)(2,1)S(1)}, u32[]{:S(2)}, u32[]{:S(2)}) collective-permute-start(bf16[592,128]{1,0:T(8,128)(2,1)S(1)} %collective-permute-done.7.refs_2_), channel_id=1, source_target_pairs={{1,0},{3,2},{5,4},{7,6},{9,8},{11,10},{13,12},{15,14},{17,16},{19,... | collective-permute-start | bytes 454664 | tf_op jit(solution)/shard_map/ppermute | solution.py:332
  72.8 1.3 %collective-permute-start.10 = (bf16[592,128]{1,0:T(8,128)(2,1)S(1)}, bf16[592,128]{1,0:T(8,128)(2,1)S(1)}, u32[]{:S(2)}, u32[]{:S(2)}) collective-permute-start(bf16[592,128]{1,0:T(8,128)(2,1)S(1)} %collective-permute-done.6.refs_1_), channel_id=1, source_target_pairs={{1,0},{3,2},{5,4},{7,6},{9,8},{11,10},{13,12},{15,14},{17,16},{19,... | collective-permute-start | bytes 454664 | tf_op jit(solution)/shard_map/ppermute | solution.py:332
  74.1 1.9 %collective-permute-done.10.refs_5_ = bf16[592,128]{1,0:T(8,128)(2,1)S(1)} collective-permute-done((bf16[592,128]{1,0:T(8,128)(2,1)S(1)}, bf16[592,128]{1,0:T(8,128)(2,1)S(1)}, u32[]{:S(2)}, u32[]{:S(2)}) %collective-permute-start.10) | collective-permute-done | bytes 151584 | tf_op jit(solution)/shard_map/ppermute | solution.py:332
  77.1 0.8 copy-done.6
  77.8 5.5 %shard_map.166 = (f32[48,128]{1,0:T(8,128)}, f32[48,128]{1,0:T(8,128)}, f32[48,128]{1,0:T(8,128)}, f32[96,128]{1,0:T(8,128)}, f32[96,128]{1,0:T(8,128)}, /*index...) custom-call(bf16[592,128]{1,0:T(8,128)(2,1)} %shard_map.164.refs_0_, ...), custom_call_target="tpu_custom_call" | custom-call | tf_op jit(solution)/shard_map/pallas_call | solution.py:61
  (70 shorter events, 8.6 us)
Async XLA Ops:
  5.5 2.5 %collective-permute-start = (bf16[2736,128]{1,0:T(8,128)(2,1)}, bf16[2736,128]{1,0:T(8,128)(2,1)S(1)}, u32[]{:S(2)}, u32[]{:S(2)}) collective-permute-start(bf16[2736,128]{1,0:T(8,128)(2,1)} %get-tuple-element.21), channel_id=1, source_target_pairs={{0,1},{1,0},{2,3},{3,2},{4,5},{5,4},{6,7},{7,6},{8,9},{9,8},{10,11... | collective-permute-start | bytes 2101256 | tf_op jit(solution)/shard_map/ppermute | solution.py:332
  10.1 2.8 %collective-permute-start.3 = (bf16[576,128]{1,0:T(8,128)(2,1)S(1)}, bf16[576,128]{1,0:T(8,128)(2,1)S(1)}, u32[]{:S(2)}, u32[]{:S(2)}) collective-permute-start(bf16[576,128]{1,0:T(8,128)(2,1)S(1)} %get-tuple-element.32), channel_id=1, source_target_pairs={{1,7},{3,5},{5,3},{7,1},{9,15},{11,13},{13,11},{15,9},{17,23},{19,... | collective-permute-start | bytes 442376 | tf_op jit(solution)/shard_map/ppermute | solution.py:332
  10.7 2.2 %collective-permute-start.2 = (bf16[576,128]{1,0:T(8,128)(2,1)S(1)}, bf16[576,128]{1,0:T(8,128)(2,1)S(1)}, u32[]{:S(2)}, u32[]{:S(2)}) collective-permute-start(bf16[576,128]{1,0:T(8,128)(2,1)S(1)} %get-tuple-element.33), channel_id=1, source_target_pairs={{1,5},{3,7},{5,1},{7,3},{9,13},{11,15},{13,9},{15,11},{17,21},{19,... | collective-permute-start | bytes 442376 | tf_op jit(solution)/shard_map/ppermute | solution.py:332
  11.4 1.5 %collective-permute-start.1 = (bf16[576,128]{1,0:T(8,128)(2,1)S(1)}, bf16[576,128]{1,0:T(8,128)(2,1)S(1)}, u32[]{:S(2)}, u32[]{:S(2)}) collective-permute-start(bf16[576,128]{1,0:T(8,128)(2,1)S(1)} %get-tuple-element.34), channel_id=1, source_target_pairs={{1,3},{3,1},{5,7},{7,5},{9,11},{11,9},{13,15},{15,13},{17,19},{19,... | collective-permute-start | bytes 442376 | tf_op jit(solution)/shard_map/ppermute | solution.py:332
  15.5 27.8 %collective-permute-start.4 = (bf16[400,128]{1,0:T(8,128)(2,1)}, bf16[400,128]{1,0:T(8,128)(2,1)S(1)}, u32[]{:S(2)}, u32[]{:S(2)}) collective-permute-start(bf16[400,128]{1,0:T(8,128)(2,1)} %get-tuple-element.22.refs_0_), channel_id=1, source_target_pairs={{1,9},{3,11},{5,13},{7,15},{9,1},{11,3},{13,5},{15,7},{17,25},{19,... | collective-permute-start | bytes 307208 | tf_op jit(solution)/shard_map/ppermute | solution.py:335
  16.2 13.5 %collective-permute-start.15 = (bf16[288,128]{1,0:T(8,128)(2,1)S(1)}, bf16[288,128]{1,0:T(8,128)(2,1)S(1)}, u32[]{:S(2)}, u32[]{:S(2)}) collective-permute-start(bf16[288,128]{1,0:T(8,128)(2,1)S(1)} %pad_maximum_fusion), channel_id=1, source_target_pairs={{0,24},{2,26},{4,28},{6,30},{8,16},{10,18},{12,20},{14,22},{16,8},... | collective-permute-start | bytes 221192 | tf_op jit(solution)/shard_map/ppermute | solution.py:335
  23.1 7.1 %collective-permute-start.14 = (bf16[288,128]{1,0:T(8,128)(2,1)S(1)}, bf16[288,128]{1,0:T(8,128)(2,1)S(1)}, u32[]{:S(2)}, u32[]{:S(2)}) collective-permute-start(bf16[288,128]{1,0:T(8,128)(2,1)S(1)} %pad_maximum_fusion), channel_id=1, source_target_pairs={{0,16},{2,18},{4,20},{6,22},{8,24},{10,26},{12,28},{14,30},{16,0},... | collective-permute-start | bytes 221192 | tf_op jit(solution)/shard_map/ppermute | solution.py:335
  25.0 6.5 %collective-permute-start.13 = (bf16[288,128]{1,0:T(8,128)(2,1)S(1)}, bf16[288,128]{1,0:T(8,128)(2,1)S(1)}, u32[]{:S(2)}, u32[]{:S(2)}) collective-permute-start(bf16[288,128]{1,0:T(8,128)(2,1)S(1)} %pad_maximum_fusion), channel_id=1, source_target_pairs={{0,8},{2,10},{4,12},{6,14},{8,0},{10,2},{12,4},{14,6},{16,24},{18,... | collective-permute-start | bytes 221192 | tf_op jit(solution)/shard_map/ppermute | solution.py:335
  34.0 28.1 %collective-permute-start.18 = (bf16[1728,128]{1,0:T(8,128)(2,1)}, bf16[1728,128]{1,0:T(8,128)(2,1)S(1)}, u32[]{:S(2)}, u32[]{:S(2)}) collective-permute-start(bf16[1728,128]{1,0:T(8,128)(2,1)} %shard_map.165.refs_8_), channel_id=1, source_target_pairs={{0,6},{2,4},{4,2},{6,0},{8,14},{10,12},{12,10},{14,8},{16,22},{18,... | collective-permute-start | bytes 1327112 | tf_op jit(solution)/shard_map/ppermute | solution.py:332
  38.9 27.9 %collective-permute-start.17 = (bf16[1728,128]{1,0:T(8,128)(2,1)}, bf16[1728,128]{1,0:T(8,128)(2,1)S(1)}, u32[]{:S(2)}, u32[]{:S(2)}) collective-permute-start(bf16[1728,128]{1,0:T(8,128)(2,1)} %shard_map.165.refs_8_), channel_id=1, source_target_pairs={{0,4},{2,6},{4,0},{6,2},{8,12},{10,14},{12,8},{14,10},{16,20},{18,... | collective-permute-start | bytes 1327112 | tf_op jit(solution)/shard_map/ppermute | solution.py:332
  41.3 26.8 %collective-permute-start.16 = (bf16[1728,128]{1,0:T(8,128)(2,1)}, bf16[1728,128]{1,0:T(8,128)(2,1)S(1)}, u32[]{:S(2)}, u32[]{:S(2)}) collective-permute-start(bf16[1728,128]{1,0:T(8,128)(2,1)} %shard_map.165.refs_8_), channel_id=1, source_target_pairs={{0,2},{2,0},{4,6},{6,4},{8,10},{10,8},{12,14},{14,12},{16,18},{18,... | collective-permute-start | bytes 1327112 | tf_op jit(solution)/shard_map/ppermute | solution.py:332
  45.6 0.7 collective-permute-start.5
  48.6 4.9 %collective-permute-start.9 = (bf16[592,128]{1,0:T(8,128)(2,1)}, bf16[592,128]{1,0:T(8,128)(2,1)S(1)}, u32[]{:S(2)}, u32[]{:S(2)}) collective-permute-start(bf16[592,128]{1,0:T(8,128)(2,1)} %shard_map.164.refs_0_), channel_id=1, source_target_pairs={{1,0},{3,2},{5,4},{7,6},{9,8},{11,10},{13,12},{15,14},{17,16},{19,... | collective-permute-start | bytes 454664 | tf_op jit(solution)/shard_map/ppermute | solution.py:332
  49.8 4.3 %collective-permute-start.8 = (bf16[592,128]{1,0:T(8,128)(2,1)}, bf16[592,128]{1,0:T(8,128)(2,1)S(1)}, u32[]{:S(2)}, u32[]{:S(2)}) collective-permute-start(bf16[592,128]{1,0:T(8,128)(2,1)} %shard_map.164.refs_0_), channel_id=1, source_target_pairs={{1,7},{3,5},{5,3},{7,1},{9,15},{11,13},{13,11},{15,9},{17,23},{19,... | collective-permute-start | bytes 454664 | tf_op jit(solution)/shard_map/ppermute | solution.py:332
  53.5 22.6 %copy-start.7 = (bf16[592,128]{1,0:T(8,128)(2,1)}, bf16[592,128]{1,0:T(8,128)(2,1)S(1)}, u32[]{:S(2)}) copy-start(bf16[592,128]{1,0:T(8,128)(2,1)S(1)} %collective-permute-done.9.refs_4_) | copy-start | bytes 454660
  53.5 7.9 %collective-permute-start.7 = (bf16[592,128]{1,0:T(8,128)(2,1)}, bf16[592,128]{1,0:T(8,128)(2,1)S(1)}, u32[]{:S(2)}, u32[]{:S(2)}) collective-permute-start(bf16[592,128]{1,0:T(8,128)(2,1)} %shard_map.164.refs_0_), channel_id=1, source_target_pairs={{1,5},{3,7},{5,1},{7,3},{9,13},{11,15},{13,9},{15,11},{17,21},{19,... | collective-permute-start | bytes 454664 | tf_op jit(solution)/shard_map/ppermute | solution.py:332
  54.2 21.9 %copy-start.8 = (bf16[592,128]{1,0:T(8,128)(2,1)}, bf16[592,128]{1,0:T(8,128)(2,1)S(1)}, u32[]{:S(2)}) copy-start(bf16[592,128]{1,0:T(8,128)(2,1)S(1)} %collective-permute-done.8.refs_3_) | copy-start | bytes 454660
  54.2 16.6 %collective-permute-start.19 = (bf16[1728,128]{1,0:T(8,128)(2,1)}, bf16[1728,128]{1,0:T(8,128)(2,1)S(1)}, u32[]{:S(2)}, u32[]{:S(2)}) collective-permute-start(bf16[1728,128]{1,0:T(8,128)(2,1)} %shard_map.165.refs_8_), channel_id=1, source_target_pairs={{0,1},{2,3},{4,5},{6,7},{8,9},{10,11},{12,13},{14,15},{16,17},{18,... | collective-permute-start | bytes 1327112 | tf_op jit(solution)/shard_map/ppermute | solution.py:332
  61.4 14.7 %copy-start.9 = (bf16[592,128]{1,0:T(8,128)(2,1)}, bf16[592,128]{1,0:T(8,128)(2,1)S(1)}, u32[]{:S(2)}) copy-start(bf16[592,128]{1,0:T(8,128)(2,1)S(1)} %collective-permute-done.7.refs_2_) | copy-start | bytes 454660
  61.4 8.1 %collective-permute-start.6 = (bf16[592,128]{1,0:T(8,128)(2,1)}, bf16[592,128]{1,0:T(8,128)(2,1)S(1)}, u32[]{:S(2)}, u32[]{:S(2)}) collective-permute-start(bf16[592,128]{1,0:T(8,128)(2,1)} %shard_map.164.refs_0_), channel_id=1, source_target_pairs={{1,3},{3,1},{5,7},{7,5},{9,11},{11,9},{13,15},{15,13},{17,19},{19,... | collective-permute-start | bytes 454664 | tf_op jit(solution)/shard_map/ppermute | solution.py:332
  62.1 14.0 %copy-start = (bf16[1728,128]{1,0:T(8,128)(2,1)}, bf16[1728,128]{1,0:T(8,128)(2,1)S(1)}, u32[]{:S(2)}) copy-start(bf16[1728,128]{1,0:T(8,128)(2,1)S(1)} %collective-permute-done.18.refs_11_) | copy-start | bytes 1327108
  62.1 13.9 %collective-permute-start.22 = (bf16[1728,128]{1,0:T(8,128)(2,1)S(1)}, bf16[1728,128]{1,0:T(8,128)(2,1)S(1)}, u32[]{:S(2)}, u32[]{:S(2)}) collective-permute-start(bf16[1728,128]{1,0:T(8,128)(2,1)S(1)} %collective-permute-done.18.refs_11_), channel_id=1, source_target_pairs={{0,1},{2,3},{4,5},{6,7},{8,9},{10,11},{12,13},{14,15},{16,17},{18,... | collective-permute-start | bytes 1327112 | tf_op jit(solution)/shard_map/ppermute | solution.py:332
  66.8 9.3 %copy-start.1 = (bf16[1728,128]{1,0:T(8,128)(2,1)}, bf16[1728,128]{1,0:T(8,128)(2,1)S(1)}, u32[]{:S(2)}) copy-start(bf16[1728,128]{1,0:T(8,128)(2,1)S(1)} %collective-permute-done.17.refs_10_) | copy-start | bytes 1327108
  66.8 9.2 %collective-permute-start.21 = (bf16[1728,128]{1,0:T(8,128)(2,1)S(1)}, bf16[1728,128]{1,0:T(8,128)(2,1)S(1)}, u32[]{:S(2)}, u32[]{:S(2)}) collective-permute-start(bf16[1728,128]{1,0:T(8,128)(2,1)S(1)} %collective-permute-done.17.refs_10_), channel_id=1, source_target_pairs={{0,1},{2,3},{4,5},{6,7},{8,9},{10,11},{12,13},{14,15},{16,17},{18,... | collective-permute-start | bytes 1327112 | tf_op jit(solution)/shard_map/ppermute | solution.py:332
  68.2 8.0 %copy-start.2 = (bf16[1728,128]{1,0:T(8,128)(2,1)}, bf16[1728,128]{1,0:T(8,128)(2,1)S(1)}, u32[]{:S(2)}) copy-start(bf16[1728,128]{1,0:T(8,128)(2,1)S(1)} %collective-permute-done.16.refs_9_) | copy-start | bytes 1327108
  68.2 7.9 %collective-permute-start.20 = (bf16[1728,128]{1,0:T(8,128)(2,1)S(1)}, bf16[1728,128]{1,0:T(8,128)(2,1)S(1)}, u32[]{:S(2)}, u32[]{:S(2)}) collective-permute-start(bf16[1728,128]{1,0:T(8,128)(2,1)S(1)} %collective-permute-done.16.refs_9_), channel_id=1, source_target_pairs={{0,1},{2,3},{4,5},{6,7},{8,9},{10,11},{12,13},{14,15},{16,17},{18,... | collective-permute-start | bytes 1327112 | tf_op jit(solution)/shard_map/ppermute | solution.py:332
  69.5 6.6 %copy-start.10 = (bf16[592,128]{1,0:T(8,128)(2,1)}, bf16[592,128]{1,0:T(8,128)(2,1)S(1)}, u32[]{:S(2)}) copy-start(bf16[592,128]{1,0:T(8,128)(2,1)S(1)} %collective-permute-done.6.refs_1_) | copy-start | bytes 454660
  69.5 3.3 %collective-permute-start.12 = (bf16[592,128]{1,0:T(8,128)(2,1)S(1)}, bf16[592,128]{1,0:T(8,128)(2,1)S(1)}, u32[]{:S(2)}, u32[]{:S(2)}) collective-permute-start(bf16[592,128]{1,0:T(8,128)(2,1)S(1)} %collective-permute-done.8.refs_3_), channel_id=1, source_target_pairs={{1,0},{3,2},{5,4},{7,6},{9,8},{11,10},{13,12},{15,14},{17,16},{19,... | collective-permute-start | bytes 454664 | tf_op jit(solution)/shard_map/ppermute | solution.py:332
  70.8 5.3 %copy-start.3 = (bf16[1728,128]{1,0:T(8,128)(2,1)}, bf16[1728,128]{1,0:T(8,128)(2,1)S(1)}, u32[]{:S(2)}) copy-start(bf16[1728,128]{1,0:T(8,128)(2,1)S(1)} %collective-permute-done.19.refs_12_) | copy-start | bytes 1327108
  70.8 3.3 %collective-permute-start.11 = (bf16[592,128]{1,0:T(8,128)(2,1)S(1)}, bf16[592,128]{1,0:T(8,128)(2,1)S(1)}, u32[]{:S(2)}, u32[]{:S(2)}) collective-permute-start(bf16[592,128]{1,0:T(8,128)(2,1)S(1)} %collective-permute-done.7.refs_2_), channel_id=1, source_target_pairs={{1,0},{3,2},{5,4},{7,6},{9,8},{11,10},{13,12},{15,14},{17,16},{19,... | collective-permute-start | bytes 454664 | tf_op jit(solution)/shard_map/ppermute | solution.py:332
  72.8 3.4 %copy-start.11 = (bf16[592,128]{1,0:T(8,128)(2,1)}, bf16[592,128]{1,0:T(8,128)(2,1)S(1)}, u32[]{:S(2)}) copy-start(bf16[592,128]{1,0:T(8,128)(2,1)S(1)} %collective-permute-done.12.refs_7_) | copy-start | bytes 454660
  72.8 3.3 %collective-permute-start.10 = (bf16[592,128]{1,0:T(8,128)(2,1)S(1)}, bf16[592,128]{1,0:T(8,128)(2,1)S(1)}, u32[]{:S(2)}, u32[]{:S(2)}) collective-permute-start(bf16[592,128]{1,0:T(8,128)(2,1)S(1)} %collective-permute-done.6.refs_1_), channel_id=1, source_target_pairs={{1,0},{3,2},{5,4},{7,6},{9,8},{11,10},{13,12},{15,14},{17,16},{19,... | collective-permute-start | bytes 454664 | tf_op jit(solution)/shard_map/ppermute | solution.py:332
  (13 other events, 12.5 us)

commit v8 on v7

--- a/solution.py
+++ b/solution.py
@@ -56,15 +56,22 @@
     return lax.dot_general(left, right, (((1,), (0,)), ((), ())), preferred_element_type=f32)
 
 
+def size_of(shape, dtype):
+    return math.prod(shape) * jnp.dtype(dtype).itemsize
+
+
 def call(kernel, args, outs, scratch=(), in_specs=None, out_specs=None):
     whole = pl.BlockSpec(memory_space=pltpu.VMEM)
+    held = sum(size_of(arg.shape, arg.dtype) for arg in args if not in_specs)
+    held += sum(size_of(*out) for out in outs) + sum(size_of(*buffer) for buffer in scratch)
+    semaphores = [] if not scratch else [pltpu.SemaphoreType.DMA((64,))]
     return pl.pallas_call(
         kernel,
         in_specs=in_specs or [whole] * len(args),
         out_specs=out_specs or [whole] * len(outs),
         out_shape=[jax.ShapeDtypeStruct(shape, dtype) for shape, dtype in outs],
-        scratch_shapes=list(scratch),
-        compiler_params=pltpu.CompilerParams(vmem_limit_bytes=56 * 1024 * 1024),
+        scratch_shapes=[pltpu.VMEM(*buffer) for buffer in scratch] + semaphores,
+        compiler_params=pltpu.CompilerParams(vmem_limit_bytes=held + 4 * 1024 * 1024),
     )(*args)
 
 
@@ -165,13 +172,12 @@
         [pltpu.with_memory_space_constraint(arg, pltpu.HBM) for arg in args],
         [((rows, LANES), f32), ((plan.pack + n_rows, LANES), bf16)],
         [
-            pltpu.VMEM(act_a.shape, bf16),
-            pltpu.VMEM(dy_a.shape, bf16),
-            pltpu.VMEM(act_e.shape, bf16),
-            pltpu.VMEM(dy_e.shape, bf16),
-            pltpu.VMEM((3, plan.size_a, LANES), f32),
-            pltpu.VMEM((3, plan.size_e, LANES), f32),
-            pltpu.SemaphoreType.DMA((8 + 2 * STEPS,)),
+            (act_a.shape, bf16),
+            (dy_a.shape, bf16),
+            (act_e.shape, bf16),
+            (dy_e.shape, bf16),
+            ((3, plan.size_a, LANES), f32),
+            ((3, plan.size_e, LANES), f32),
         ],
         in_specs=[pl.BlockSpec(memory_space=pltpu.HBM)] * len(args),
     )
@@ -219,16 +225,22 @@
     rows[pl.ds(plan.pair, 16), :] = two_pieces(square)
 
 
-def state_kernel(plan, mine, other, *refs):
-    packs, states = refs[:-1], refs[-1]
+def packs_kernel(plan, mine, other, both):
+    size = 3 * plan.size_a
+    both[:size, :] = mine[:size, :]
+    both[size:, :] = other[:size, :]
+
+
+def state_kernel(plan, mine, other, both, *refs):
+    packs, states = (both,) + refs[:-1], refs[-1]
     place = lax.axis_index("expert")
     a, e = plan.size_a, plan.size_e
     for k, own in enumerate((mine, other)):
         for i in range(3):
             start = (k * 3 + i) * plan.chunk
-            for q, pack in enumerate((None,) + packs):
-                part = own[pl.ds(i * a, a), :] if pack is None else pack[pl.ds((k * 3 + i) * a, a), :]
-                states[pl.ds(pl.multiple_of(start + (place ^ q) * a, 16), a), :] = part
+            for q, pack in enumerate(packs):
+                rows = pl.ds(pl.multiple_of(start + (place ^ q) * a, 16), a)
+                states[rows, :] = pack[pl.ds((k * 3 + i) * a, a), :]
             states[pl.ds(start + plan.all_a, e), :] = own[pl.ds(3 * a + i * e, e), :]
 
 
@@ -315,23 +327,23 @@
         lambda *refs: update_kernel(plan, limit, *refs),
         gathered + state,
         own + [((count_a, plan.width), bf16), ((1, count_e, plan.width), bf16)],
-        [pltpu.VMEM(shape, dtype) for shape, dtype in own]
+        own
         + [
-            pltpu.VMEM((plan.n_dp * plan.chunk, LANES), f32),
-            pltpu.VMEM((count_a, LANES), f32),
-            pltpu.VMEM((plan.blocks * count_e, LANES), f32),
-            pltpu.SemaphoreType.DMA((6,)),
+            ((plan.n_dp * plan.chunk, LANES), f32),
+            ((count_a, LANES), f32),
+            ((plan.blocks * count_e, LANES), f32),
         ],
         out_specs=[hbm] * 6 + [vmem] * 2,
     )
 
 
 def swap(value, axis, distance, cores=(0, 1)):
-    size = lax.axis_size(axis)
+    size, n_dp = lax.axis_size(axis), lax.axis_size("dp")
     if axis == "dp":
-        return lax.ppermute(value, axis, [(i, i ^ distance) for i in range(size) if i % 2 in cores])
-    n_dp = lax.axis_size("dp")
-    pairs = [(i * n_dp + j, (i ^ distance) * n_dp + j) for i in range(size) for j in range(n_dp) if j % 2 in cores]
+        return lax.ppermute(value, axis, [(i, i ^ distance if i % 2 in cores else i) for i in range(size)])
+    pairs = [
+        (i * n_dp + j, (i ^ distance if j % 2 in cores else i) * n_dp + j) for i in range(size) for j in range(n_dp)
+    ]
     return lax.ppermute(value, ("expert", "dp"), pairs)
 
 
@@ -381,16 +393,15 @@
         lambda *refs: last_kernel(plan, *refs), [payload, other, g_exp], [((pair + 16, LANES), bf16)]
     )
     near_g = [grads] + [swap(grads, "dp", 2 * c, ODD) for c in range(1, chips)]
-    far_g = [swap(value, "dp", 1, ODD) for value in near_g]
-
-    mine, other = send[: plan.pack], got[: plan.pack]
-    packs = jnp.concatenate([mine[: 3 * size_a], other[: 3 * size_a]])
-    packs = [swap(packs, "expert", q, EVEN) for q in range(1, n_expert)]
+    far_g = [swap(value, "dp", 1) for value in near_g]
+
+    (both,) = call(lambda *refs: packs_kernel(plan, *refs), [send, got], [((6 * size_a, LANES), bf16)])
+    packs = [swap(both, "expert", q, EVEN) for q in range(1, n_expert)]
     (states,) = call(
-        lambda *refs: state_kernel(plan, *refs), [mine, other, *packs], [((3 * pair, LANES), bf16)]
+        lambda *refs: state_kernel(plan, *refs), [send, got, both, *packs], [((3 * pair, LANES), bf16)]
     )
     near_s = [states] + [swap(states, "dp", 2 * c, EVEN) for c in range(1, chips)]
-    far_s = [swap(value, "dp", 1, EVEN) for value in near_s]
+    far_s = [swap(value, "dp", 1) for value in near_s]
 
     *new, attn_full, expert_full = update(plan, limit, near_g + far_g + near_s + far_s, state)
     new_a = [from_blocks(value, rows_a) for value in new[:3]]

time: 84.1 us -> 59.3 us (0.71)
  Pallas kernels: 17.4 us -> 7.98 us
  local copies, waits for them, and re-layouts: 7.28 us -> 0.04 us
  starting transfers between devices: 46 us -> 41.7 us
  other arithmetic: 2.06 us -> 0.14 us
  waiting for transfers between devices: 9.46 us -> 7.95 us
    pallas_call x6 -> x7, Pallas kernels: 17.4 us -> 7.98 us  [call(): pl.pallas_call(kernel, in_specs=in_specs or [whole] * len(args), out_spec...]
    ppermute x18, starting transfers between devices: 33.4 us -> 29 us  [swap(): lax.ppermute(value, axis, [(i, i ^ distance if i % 2 in cores else i) for...]
    unnamed x44 -> x12, local copies, waits for them, and re-layouts: 4.31 us -> 0.04 us
    ppermute x18, waiting for transfers between devices: 7.63 us -> 4.19 us  [swap(): lax.ppermute(value, axis, [(i, i ^ distance if i % 2 in cores else i) for...]
    slice x4 -> x0, local copies, waits for them, and re-layouts: 2.98 us -> none  [the longest x2 2.2 us: body(): mine, other = (send[:plan.pack], got[:plan.pack])]
    ppermute x5, waiting for transfers between devices: 1.83 us -> 3.76 us  [swap(): return lax.ppermute(value, ('expert', 'dp'), pairs)]
    convert_element_type x1, other arithmetic: 2.05 us -> 0.14 us  [body(): sums[c].astype(bf16)]
  transfers between devices with their start and end apart: 23 -> 23, of which waited for: 6 -> 6; matrix products, arithmetic and copies ran while one was open for 4% -> 0% of each run, Pallas kernels for 6% -> 0%
where the time goes in v8:
time: 59.3 us; the launch traced here: 58.8 us
  starting transfers between devices  41.7 us (70%)
  Pallas kernels  7.98 us (13%)
  waiting for transfers between devices  7.95 us (13%)
  between operations  0.95 us (2%)
    ppermute x18, starting transfers between devices, swap(): lax.ppermute(value, axis, [(i, i ^ distance if i % 2 in cores else i) for...  29 us
    ppermute x5, starting transfers between devices, swap(): return lax.ppermute(value, ('expert', 'dp'), pairs)  12.7 us
    pallas_call x7, Pallas kernels, call(): pl.pallas_call(kernel, in_specs=in_specs or [whole] * len(args), out_spec...  7.98 us
    ppermute x18, waiting for transfers between devices, swap(): lax.ppermute(value, axis, [(i, i ^ distance if i % 2 in cores else i) for...  4.19 us
    ppermute x5, waiting for transfers between devices, swap(): return lax.ppermute(value, ('expert', 'dp'), pairs)  3.76 us
  transfers between devices with their start and end apart: 23, of which 6 were waited for; matrix products, arithmetic and copies ran while one was open for 0% of the time, Pallas kernels for 0%

profile of v8, /device:TPU:0, one launch (start us, length us, event | category | flops | bytes accessed | tf_op | source)
XLA Modules:
  0.0 58.8 jit_solution(4461493409003808986)
XLA Ops:
  0.6 4.1 %shard_map.161 = (f32[2304,128]{1,0:T(8,128)S(1)}, bf16[2736,128]{1,0:T(8,128)(2,1)S(1)}) custom-call(bf16[32,256]{1,0:T(8,128)(2,1)} %bitcast.54, bf16[256,6144]{1,0:T(8,128)(2,1)} %refs_1_.1, bf16[16,128]{1,0:T(8,128)(2,1)} %bitcast.55, bf16[128,6144]{1,0:T(8,128)(2,1)} %bitcast.53, f32[48,128]{1,0:T(8,128)} %bitcast.47, f32[48,128]{1,0:T(8,128)} %bitcast.49, ...), custom_call_target="tpu_custom_call" | custom-call | tf_op jit(solution)/shard_map/pallas_call | solution.py:68
  4.7 0.5 collective-permute-start
  5.2 1.8 %collective-permute-done.refs_1_ = bf16[2736,128]{1,0:T(8,128)(2,1)S(1)} collective-permute-done((bf16[2736,128]{1,0:T(8,128)(2,1)S(1)}, bf16[2736,128]{1,0:T(8,128)(2,1)S(1)}, u32[]{:S(2)}, u32[]{:S(2)}) %collective-permute-start) | collective-permute-done | bytes 700448 | tf_op jit(solution)/shard_map/ppermute | solution.py:343
  7.0 0.1 add_convert_fusion
  7.2 0.7 %collective-permute-start.3 = (bf16[576,128]{1,0:T(8,128)(2,1)S(1)}, bf16[576,128]{1,0:T(8,128)(2,1)S(1)}, u32[]{:S(2)}, u32[]{:S(2)}) collective-permute-start(bf16[576,128]{1,0:T(8,128)(2,1)S(1)} %get-tuple-element.32), channel_id=1, source_target_pairs={{0,0},{1,7},{2,2},{3,5},{4,4},{5,3},{6,6},{7,1},{8,8},{9,15},{10,1... | collective-permute-start | bytes 442376 | tf_op jit(solution)/shard_map/ppermute | solution.py:343
  7.9 0.7 %collective-permute-start.2 = (bf16[576,128]{1,0:T(8,128)(2,1)S(1)}, bf16[576,128]{1,0:T(8,128)(2,1)S(1)}, u32[]{:S(2)}, u32[]{:S(2)}) collective-permute-start(bf16[576,128]{1,0:T(8,128)(2,1)S(1)} %get-tuple-element.33), channel_id=1, source_target_pairs={{0,0},{1,5},{2,2},{3,7},{4,4},{5,1},{6,6},{7,3},{8,8},{9,13},{10,1... | collective-permute-start | bytes 442376 | tf_op jit(solution)/shard_map/ppermute | solution.py:343
  8.5 0.7 %collective-permute-start.1 = (bf16[576,128]{1,0:T(8,128)(2,1)S(1)}, bf16[576,128]{1,0:T(8,128)(2,1)S(1)}, u32[]{:S(2)}, u32[]{:S(2)}) collective-permute-start(bf16[576,128]{1,0:T(8,128)(2,1)S(1)} %get-tuple-element.34), channel_id=1, source_target_pairs={{0,0},{1,3},{2,2},{3,1},{4,4},{5,7},{6,6},{7,5},{8,8},{9,11},{10,1... | collective-permute-start | bytes 442376 | tf_op jit(solution)/shard_map/ppermute | solution.py:343
  9.2 0.1 shard_map.162
  9.3 0.7 %collective-permute-start.4 = (bf16[400,128]{1,0:T(8,128)(2,1)S(1)}, bf16[400,128]{1,0:T(8,128)(2,1)S(1)}, u32[]{:S(2)}, u32[]{:S(2)}) collective-permute-start(bf16[400,128]{1,0:T(8,128)(2,1)S(1)} %get-tuple-element.22.refs_0_), channel_id=1, source_target_pairs={{0,0},{1,9},{2,2},{3,11},{4,4},{5,13},{6,6},{7,15},{8,8},{9,1},{10... | collective-permute-start | bytes 307208 | tf_op jit(solution)/shard_map/ppermute | solution.py:347
  10.1 7.0 %collective-permute-start.15 = (bf16[288,128]{1,0:T(8,128)(2,1)S(1)}, bf16[288,128]{1,0:T(8,128)(2,1)S(1)}, u32[]{:S(2)}, u32[]{:S(2)}) collective-permute-start(bf16[288,128]{1,0:T(8,128)(2,1)S(1)} %shard_map.165.refs_2_), channel_id=1, source_target_pairs={{0,24},{1,1},{2,26},{3,3},{4,28},{5,5},{6,30},{7,7},{8,16},{9,9},{... | collective-permute-start | bytes 221192 | tf_op jit(solution)/shard_map/ppermute | solution.py:347
  17.1 1.9 %collective-permute-start.14 = (bf16[288,128]{1,0:T(8,128)(2,1)S(1)}, bf16[288,128]{1,0:T(8,128)(2,1)S(1)}, u32[]{:S(2)}, u32[]{:S(2)}) collective-permute-start(bf16[288,128]{1,0:T(8,128)(2,1)S(1)} %shard_map.165.refs_2_), channel_id=1, source_target_pairs={{0,16},{1,1},{2,18},{3,3},{4,20},{5,5},{6,22},{7,7},{8,24},{9,9},{... | collective-permute-start | bytes 221192 | tf_op jit(solution)/shard_map/ppermute | solution.py:347
  19.0 2.5 %collective-permute-start.13 = (bf16[288,128]{1,0:T(8,128)(2,1)S(1)}, bf16[288,128]{1,0:T(8,128)(2,1)S(1)}, u32[]{:S(2)}, u32[]{:S(2)}) collective-permute-start(bf16[288,128]{1,0:T(8,128)(2,1)S(1)} %shard_map.165.refs_2_), channel_id=1, source_target_pairs={{0,8},{1,1},{2,10},{3,3},{4,12},{5,5},{6,14},{7,7},{8,0},{9,9},{10... | collective-permute-start | bytes 221192 | tf_op jit(solution)/shard_map/ppermute | solution.py:347
  21.5 2.7 %collective-permute-done.14.refs_4_ = bf16[288,128]{1,0:T(8,128)(2,1)S(1)} collective-permute-done((bf16[288,128]{1,0:T(8,128)(2,1)S(1)}, bf16[288,128]{1,0:T(8,128)(2,1)S(1)}, u32[]{:S(2)}, u32[]{:S(2)}) %collective-permute-start.14) | collective-permute-done | bytes 73760 | tf_op jit(solution)/shard_map/ppermute | solution.py:347
  24.3 1.0 %collective-permute-done.13.refs_3_ = bf16[288,128]{1,0:T(8,128)(2,1)S(1)} collective-permute-done((bf16[288,128]{1,0:T(8,128)(2,1)S(1)}, bf16[288,128]{1,0:T(8,128)(2,1)S(1)}, u32[]{:S(2)}, u32[]{:S(2)}) %collective-permute-start.13) | collective-permute-done | bytes 73760 | tf_op jit(solution)/shard_map/ppermute | solution.py:347
  25.4 5.1 %collective-permute-start.18 = (bf16[1728,128]{1,0:T(8,128)(2,1)S(1)}, bf16[1728,128]{1,0:T(8,128)(2,1)S(1)}, u32[]{:S(2)}, u32[]{:S(2)}) collective-permute-start(bf16[1728,128]{1,0:T(8,128)(2,1)S(1)} %shard_map.166.refs_8_), channel_id=1, source_target_pairs={{0,6},{1,1},{2,4},{3,3},{4,2},{5,5},{6,0},{7,7},{8,14},{9,9},{10,1... | collective-permute-start | bytes 1327112 | tf_op jit(solution)/shard_map/ppermute | solution.py:343
  30.5 2.4 %collective-permute-start.17 = (bf16[1728,128]{1,0:T(8,128)(2,1)S(1)}, bf16[1728,128]{1,0:T(8,128)(2,1)S(1)}, u32[]{:S(2)}, u32[]{:S(2)}) collective-permute-start(bf16[1728,128]{1,0:T(8,128)(2,1)S(1)} %shard_map.166.refs_8_), channel_id=1, source_target_pairs={{0,4},{1,1},{2,6},{3,3},{4,0},{5,5},{6,2},{7,7},{8,12},{9,9},{10,1... | collective-permute-start | bytes 1327112 | tf_op jit(solution)/shard_map/ppermute | solution.py:343
  32.9 2.0 %collective-permute-start.16 = (bf16[1728,128]{1,0:T(8,128)(2,1)S(1)}, bf16[1728,128]{1,0:T(8,128)(2,1)S(1)}, u32[]{:S(2)}, u32[]{:S(2)}) collective-permute-start(bf16[1728,128]{1,0:T(8,128)(2,1)S(1)} %shard_map.166.refs_8_), channel_id=1, source_target_pairs={{0,2},{1,1},{2,0},{3,3},{4,6},{5,5},{6,4},{7,7},{8,10},{9,9},{10,8... | collective-permute-start | bytes 1327112 | tf_op jit(solution)/shard_map/ppermute | solution.py:343
  35.0 0.7 %collective-permute-start.5 = (bf16[400,128]{1,0:T(8,128)(2,1)S(1)}, bf16[400,128]{1,0:T(8,128)(2,1)S(1)}, u32[]{:S(2)}, u32[]{:S(2)}) collective-permute-start(bf16[400,128]{1,0:T(8,128)(2,1)S(1)} %shard_map.163.refs_0_), channel_id=1, source_target_pairs={{0,0},{1,17},{2,2},{3,19},{4,4},{5,21},{6,6},{7,23},{8,8},{9,25},{... | collective-permute-start | bytes 307208 | tf_op jit(solution)/shard_map/ppermute | solution.py:347
  35.7 0.7 %collective-permute-start.9 = (bf16[592,128]{1,0:T(8,128)(2,1)S(1)}, bf16[592,128]{1,0:T(8,128)(2,1)S(1)}, u32[]{:S(2)}, u32[]{:S(2)}) collective-permute-start(bf16[592,128]{1,0:T(8,128)(2,1)S(1)} %shard_map.164.refs_0_), channel_id=1, source_target_pairs={{0,1},{1,0},{2,3},{3,2},{4,5},{5,4},{6,7},{7,6},{8,9},{9,8},{10,11... | collective-permute-start | bytes 454664 | tf_op jit(solution)/shard_map/ppermute | solution.py:343
  36.4 0.7 %collective-permute-start.8 = (bf16[592,128]{1,0:T(8,128)(2,1)S(1)}, bf16[592,128]{1,0:T(8,128)(2,1)S(1)}, u32[]{:S(2)}, u32[]{:S(2)}) collective-permute-start(bf16[592,128]{1,0:T(8,128)(2,1)S(1)} %shard_map.164.refs_0_), channel_id=1, source_target_pairs={{0,0},{1,7},{2,2},{3,5},{4,4},{5,3},{6,6},{7,1},{8,8},{9,15},{10,1... | collective-permute-start | bytes 454664 | tf_op jit(solution)/shard_map/ppermute | solution.py:343
  37.1 0.3 collective-permute-done.9.refs_4_
  37.4 0.7 %collective-permute-start.7 = (bf16[592,128]{1,0:T(8,128)(2,1)S(1)}, bf16[592,128]{1,0:T(8,128)(2,1)S(1)}, u32[]{:S(2)}, u32[]{:S(2)}) collective-permute-start(bf16[592,128]{1,0:T(8,128)(2,1)S(1)} %shard_map.164.refs_0_), channel_id=1, source_target_pairs={{0,0},{1,5},{2,2},{3,7},{4,4},{5,1},{6,6},{7,3},{8,8},{9,13},{10,1... | collective-permute-start | bytes 454664 | tf_op jit(solution)/shard_map/ppermute | solution.py:343
  38.1 7.0 %collective-permute-start.19 = (bf16[1728,128]{1,0:T(8,128)(2,1)S(1)}, bf16[1728,128]{1,0:T(8,128)(2,1)S(1)}, u32[]{:S(2)}, u32[]{:S(2)}) collective-permute-start(bf16[1728,128]{1,0:T(8,128)(2,1)S(1)} %shard_map.166.refs_8_), channel_id=1, source_target_pairs={{0,1},{1,0},{2,3},{3,2},{4,5},{5,4},{6,7},{7,6},{8,9},{9,8},{10,11... | collective-permute-start | bytes 1327112 | tf_op jit(solution)/shard_map/ppermute | solution.py:343
  45.1 0.7 %collective-permute-start.6 = (bf16[592,128]{1,0:T(8,128)(2,1)S(1)}, bf16[592,128]{1,0:T(8,128)(2,1)S(1)}, u32[]{:S(2)}, u32[]{:S(2)}) collective-permute-start(bf16[592,128]{1,0:T(8,128)(2,1)S(1)} %shard_map.164.refs_0_), channel_id=1, source_target_pairs={{0,0},{1,3},{2,2},{3,1},{4,4},{5,7},{6,6},{7,5},{8,8},{9,11},{10,1... | collective-permute-start | bytes 454664 | tf_op jit(solution)/shard_map/ppermute | solution.py:343
  45.7 3.1 %collective-permute-start.22 = (bf16[1728,128]{1,0:T(8,128)(2,1)S(1)}, bf16[1728,128]{1,0:T(8,128)(2,1)S(1)}, u32[]{:S(2)}, u32[]{:S(2)}) collective-permute-start(bf16[1728,128]{1,0:T(8,128)(2,1)S(1)} %collective-permute-done.18.refs_11_), channel_id=1, source_target_pairs={{0,1},{1,0},{2,3},{3,2},{4,5},{5,4},{6,7},{7,6},{8,9},{9,8},{10,11... | collective-permute-start | bytes 1327112 | tf_op jit(solution)/shard_map/ppermute | solution.py:343
  48.9 0.1 collective-permute-start.21
  49.0 0.4 collective-permute-start.20
  49.4 3.3 %collective-permute-start.12 = (bf16[592,128]{1,0:T(8,128)(2,1)S(1)}, bf16[592,128]{1,0:T(8,128)(2,1)S(1)}, u32[]{:S(2)}, u32[]{:S(2)}) collective-permute-start(bf16[592,128]{1,0:T(8,128)(2,1)S(1)} %collective-permute-done.8.refs_3_), channel_id=1, source_target_pairs={{0,1},{1,0},{2,3},{3,2},{4,5},{5,4},{6,7},{7,6},{8,9},{9,8},{10,11... | collective-permute-start | bytes 454664 | tf_op jit(solution)/shard_map/ppermute | solution.py:343
  52.7 1.0 %collective-permute-done.12.refs_7_ = bf16[592,128]{1,0:T(8,128)(2,1)S(1)} collective-permute-done((bf16[592,128]{1,0:T(8,128)(2,1)S(1)}, bf16[592,128]{1,0:T(8,128)(2,1)S(1)}, u32[]{:S(2)}, u32[]{:S(2)}) %collective-permute-start.12) | collective-permute-done | bytes 151584 | tf_op jit(solution)/shard_map/ppermute | solution.py:343
  53.7 0.4 collective-permute-start.10
  54.1 1.0 %collective-permute-done.10.refs_5_ = bf16[592,128]{1,0:T(8,128)(2,1)S(1)} collective-permute-done((bf16[592,128]{1,0:T(8,128)(2,1)S(1)}, bf16[592,128]{1,0:T(8,128)(2,1)S(1)}, u32[]{:S(2)}, u32[]{:S(2)}) %collective-permute-start.10) | collective-permute-done | bytes 151584 | tf_op jit(solution)/shard_map/ppermute | solution.py:343
  55.1 3.6 %shard_map.167 = (f32[48,128]{1,0:T(8,128)}, f32[48,128]{1,0:T(8,128)}, f32[48,128]{1,0:T(8,128)}, f32[96,128]{1,0:T(8,128)}, f32[96,128]{1,0:T(8,128)}, /*index...) custom-call(bf16[592,128]{1,0:T(8,128)(2,1)S(1)} %shard_map.164.refs_0_, ...), custom_call_target="tpu_custom_call" | custom-call | tf_op jit(solution)/shard_map/pallas_call | solution.py:68
  (34 shorter events, 0.2 us)
Async XLA Ops:
  4.7 2.3 %collective-permute-start = (bf16[2736,128]{1,0:T(8,128)(2,1)S(1)}, bf16[2736,128]{1,0:T(8,128)(2,1)S(1)}, u32[]{:S(2)}, u32[]{:S(2)}) collective-permute-start(bf16[2736,128]{1,0:T(8,128)(2,1)S(1)} %get-tuple-element.21.refs_0_), channel_id=1, source_target_pairs={{0,1},{1,0},{2,3},{3,2},{4,5},{5,4},{6,7},{7,6},{8,9},{9,8},{10,11... | collective-permute-start | bytes 2101256 | tf_op jit(solution)/shard_map/ppermute | solution.py:343
  7.2 2.0 %collective-permute-start.3 = (bf16[576,128]{1,0:T(8,128)(2,1)S(1)}, bf16[576,128]{1,0:T(8,128)(2,1)S(1)}, u32[]{:S(2)}, u32[]{:S(2)}) collective-permute-start(bf16[576,128]{1,0:T(8,128)(2,1)S(1)} %get-tuple-element.32), channel_id=1, source_target_pairs={{0,0},{1,7},{2,2},{3,5},{4,4},{5,3},{6,6},{7,1},{8,8},{9,15},{10,1... | collective-permute-start | bytes 442376 | tf_op jit(solution)/shard_map/ppermute | solution.py:343
  7.9 1.4 %collective-permute-start.2 = (bf16[576,128]{1,0:T(8,128)(2,1)S(1)}, bf16[576,128]{1,0:T(8,128)(2,1)S(1)}, u32[]{:S(2)}, u32[]{:S(2)}) collective-permute-start(bf16[576,128]{1,0:T(8,128)(2,1)S(1)} %get-tuple-element.33), channel_id=1, source_target_pairs={{0,0},{1,5},{2,2},{3,7},{4,4},{5,1},{6,6},{7,3},{8,8},{9,13},{10,1... | collective-permute-start | bytes 442376 | tf_op jit(solution)/shard_map/ppermute | solution.py:343
  8.5 0.7 %collective-permute-start.1 = (bf16[576,128]{1,0:T(8,128)(2,1)S(1)}, bf16[576,128]{1,0:T(8,128)(2,1)S(1)}, u32[]{:S(2)}, u32[]{:S(2)}) collective-permute-start(bf16[576,128]{1,0:T(8,128)(2,1)S(1)} %get-tuple-element.34), channel_id=1, source_target_pairs={{0,0},{1,3},{2,2},{3,1},{4,4},{5,7},{6,6},{7,5},{8,8},{9,11},{10,1... | collective-permute-start | bytes 442376 | tf_op jit(solution)/shard_map/ppermute | solution.py:343
  9.3 25.6 %collective-permute-start.4 = (bf16[400,128]{1,0:T(8,128)(2,1)S(1)}, bf16[400,128]{1,0:T(8,128)(2,1)S(1)}, u32[]{:S(2)}, u32[]{:S(2)}) collective-permute-start(bf16[400,128]{1,0:T(8,128)(2,1)S(1)} %get-tuple-element.22.refs_0_), channel_id=1, source_target_pairs={{0,0},{1,9},{2,2},{3,11},{4,4},{5,13},{6,6},{7,15},{8,8},{9,1},{10... | collective-permute-start | bytes 307208 | tf_op jit(solution)/shard_map/ppermute | solution.py:347
  10.0 45.1 %copy-start = (f32[1,2,6144]{2,1,0:T(2,128)S(1)}, f32[1,2,6144]{2,1,0:T(2,128)}, u32[]{:S(2)}) copy-start(f32[1,2,6144]{2,1,0:T(2,128)} %param.17) | copy-start | bytes 147460
  10.0 45.1 %copy-start.1 = (f32[1,2,6144]{2,1,0:T(2,128)S(1)}, f32[1,2,6144]{2,1,0:T(2,128)}, u32[]{:S(2)}) copy-start(f32[1,2,6144]{2,1,0:T(2,128)} %param.18) | copy-start | bytes 147460
  10.1 45.1 %copy-start.2 = (f32[1,2,6144]{2,1,0:T(2,128)S(1)}, f32[1,2,6144]{2,1,0:T(2,128)}, u32[]{:S(2)}) copy-start(f32[1,2,6144]{2,1,0:T(2,128)} %param.19) | copy-start | bytes 147460
  10.1 45.1 %copy-start.3 = (f32[1,6144]{1,0:T(1,128)S(1)}, f32[1,6144]{1,0:T(1,128)}, u32[]{:S(2)}) copy-start(f32[1,6144]{1,0:T(1,128)} %param.14) | copy-start | bytes 73732
  10.1 45.1 %copy-start.4 = (f32[1,6144]{1,0:T(1,128)S(1)}, f32[1,6144]{1,0:T(1,128)}, u32[]{:S(2)}) copy-start(f32[1,6144]{1,0:T(1,128)} %param.15) | copy-start | bytes 73732
  10.1 45.0 %copy-start.5 = (f32[1,6144]{1,0:T(1,128)S(1)}, f32[1,6144]{1,0:T(1,128)}, u32[]{:S(2)}) copy-start(f32[1,6144]{1,0:T(1,128)} %param.16) | copy-start | bytes 73732
  10.1 11.4 %collective-permute-start.15 = (bf16[288,128]{1,0:T(8,128)(2,1)S(1)}, bf16[288,128]{1,0:T(8,128)(2,1)S(1)}, u32[]{:S(2)}, u32[]{:S(2)}) collective-permute-start(bf16[288,128]{1,0:T(8,128)(2,1)S(1)} %shard_map.165.refs_2_), channel_id=1, source_target_pairs={{0,24},{1,1},{2,26},{3,3},{4,28},{5,5},{6,30},{7,7},{8,16},{9,9},{... | collective-permute-start | bytes 221192 | tf_op jit(solution)/shard_map/ppermute | solution.py:347
  17.1 7.1 %collective-permute-start.14 = (bf16[288,128]{1,0:T(8,128)(2,1)S(1)}, bf16[288,128]{1,0:T(8,128)(2,1)S(1)}, u32[]{:S(2)}, u32[]{:S(2)}) collective-permute-start(bf16[288,128]{1,0:T(8,128)(2,1)S(1)} %shard_map.165.refs_2_), channel_id=1, source_target_pairs={{0,16},{1,1},{2,18},{3,3},{4,20},{5,5},{6,22},{7,7},{8,24},{9,9},{... | collective-permute-start | bytes 221192 | tf_op jit(solution)/shard_map/ppermute | solution.py:347
  19.0 6.2 %collective-permute-start.13 = (bf16[288,128]{1,0:T(8,128)(2,1)S(1)}, bf16[288,128]{1,0:T(8,128)(2,1)S(1)}, u32[]{:S(2)}, u32[]{:S(2)}) collective-permute-start(bf16[288,128]{1,0:T(8,128)(2,1)S(1)} %shard_map.165.refs_2_), channel_id=1, source_target_pairs={{0,8},{1,1},{2,10},{3,3},{4,12},{5,5},{6,14},{7,7},{8,0},{9,9},{10... | collective-permute-start | bytes 221192 | tf_op jit(solution)/shard_map/ppermute | solution.py:347
  25.4 20.4 %collective-permute-start.18 = (bf16[1728,128]{1,0:T(8,128)(2,1)S(1)}, bf16[1728,128]{1,0:T(8,128)(2,1)S(1)}, u32[]{:S(2)}, u32[]{:S(2)}) collective-permute-start(bf16[1728,128]{1,0:T(8,128)(2,1)S(1)} %shard_map.166.refs_8_), channel_id=1, source_target_pairs={{0,6},{1,1},{2,4},{3,3},{4,2},{5,5},{6,0},{7,7},{8,14},{9,9},{10,1... | collective-permute-start | bytes 1327112 | tf_op jit(solution)/shard_map/ppermute | solution.py:343
  30.5 18.4 %collective-permute-start.17 = (bf16[1728,128]{1,0:T(8,128)(2,1)S(1)}, bf16[1728,128]{1,0:T(8,128)(2,1)S(1)}, u32[]{:S(2)}, u32[]{:S(2)}) collective-permute-start(bf16[1728,128]{1,0:T(8,128)(2,1)S(1)} %shard_map.166.refs_8_), channel_id=1, source_target_pairs={{0,4},{1,1},{2,6},{3,3},{4,0},{5,5},{6,2},{7,7},{8,12},{9,9},{10,1... | collective-permute-start | bytes 1327112 | tf_op jit(solution)/shard_map/ppermute | solution.py:343
  32.9 16.0 %collective-permute-start.16 = (bf16[1728,128]{1,0:T(8,128)(2,1)S(1)}, bf16[1728,128]{1,0:T(8,128)(2,1)S(1)}, u32[]{:S(2)}, u32[]{:S(2)}) collective-permute-start(bf16[1728,128]{1,0:T(8,128)(2,1)S(1)} %shard_map.166.refs_8_), channel_id=1, source_target_pairs={{0,2},{1,1},{2,0},{3,3},{4,6},{5,5},{6,4},{7,7},{8,10},{9,9},{10,8... | collective-permute-start | bytes 1327112 | tf_op jit(solution)/shard_map/ppermute | solution.py:343
  35.0 0.7 %collective-permute-start.5 = (bf16[400,128]{1,0:T(8,128)(2,1)S(1)}, bf16[400,128]{1,0:T(8,128)(2,1)S(1)}, u32[]{:S(2)}, u32[]{:S(2)}) collective-permute-start(bf16[400,128]{1,0:T(8,128)(2,1)S(1)} %shard_map.163.refs_0_), channel_id=1, source_target_pairs={{0,0},{1,17},{2,2},{3,19},{4,4},{5,21},{6,6},{7,23},{8,8},{9,25},{... | collective-permute-start | bytes 307208 | tf_op jit(solution)/shard_map/ppermute | solution.py:347
  35.7 1.7 %collective-permute-start.9 = (bf16[592,128]{1,0:T(8,128)(2,1)S(1)}, bf16[592,128]{1,0:T(8,128)(2,1)S(1)}, u32[]{:S(2)}, u32[]{:S(2)}) collective-permute-start(bf16[592,128]{1,0:T(8,128)(2,1)S(1)} %shard_map.164.refs_0_), channel_id=1, source_target_pairs={{0,1},{1,0},{2,3},{3,2},{4,5},{5,4},{6,7},{7,6},{8,9},{9,8},{10,11... | collective-permute-start | bytes 454664 | tf_op jit(solution)/shard_map/ppermute | solution.py:343
  36.4 1.7 %collective-permute-start.8 = (bf16[592,128]{1,0:T(8,128)(2,1)S(1)}, bf16[592,128]{1,0:T(8,128)(2,1)S(1)}, u32[]{:S(2)}, u32[]{:S(2)}) collective-permute-start(bf16[592,128]{1,0:T(8,128)(2,1)S(1)} %shard_map.164.refs_0_), channel_id=1, source_target_pairs={{0,0},{1,7},{2,2},{3,5},{4,4},{5,3},{6,6},{7,1},{8,8},{9,15},{10,1... | collective-permute-start | bytes 454664 | tf_op jit(solution)/shard_map/ppermute | solution.py:343
  37.4 7.7 %collective-permute-start.7 = (bf16[592,128]{1,0:T(8,128)(2,1)S(1)}, bf16[592,128]{1,0:T(8,128)(2,1)S(1)}, u32[]{:S(2)}, u32[]{:S(2)}) collective-permute-start(bf16[592,128]{1,0:T(8,128)(2,1)S(1)} %shard_map.164.refs_0_), channel_id=1, source_target_pairs={{0,0},{1,5},{2,2},{3,7},{4,4},{5,1},{6,6},{7,3},{8,8},{9,13},{10,1... | collective-permute-start | bytes 454664 | tf_op jit(solution)/shard_map/ppermute | solution.py:343
  38.1 14.6 %collective-permute-start.19 = (bf16[1728,128]{1,0:T(8,128)(2,1)S(1)}, bf16[1728,128]{1,0:T(8,128)(2,1)S(1)}, u32[]{:S(2)}, u32[]{:S(2)}) collective-permute-start(bf16[1728,128]{1,0:T(8,128)(2,1)S(1)} %shard_map.166.refs_8_), channel_id=1, source_target_pairs={{0,1},{1,0},{2,3},{3,2},{4,5},{5,4},{6,7},{7,6},{8,9},{9,8},{10,11... | collective-permute-start | bytes 1327112 | tf_op jit(solution)/shard_map/ppermute | solution.py:343
  45.1 4.3 %collective-permute-start.6 = (bf16[592,128]{1,0:T(8,128)(2,1)S(1)}, bf16[592,128]{1,0:T(8,128)(2,1)S(1)}, u32[]{:S(2)}, u32[]{:S(2)}) collective-permute-start(bf16[592,128]{1,0:T(8,128)(2,1)S(1)} %shard_map.164.refs_0_), channel_id=1, source_target_pairs={{0,0},{1,3},{2,2},{3,1},{4,4},{5,7},{6,6},{7,5},{8,8},{9,11},{10,1... | collective-permute-start | bytes 454664 | tf_op jit(solution)/shard_map/ppermute | solution.py:343
  45.7 9.3 %collective-permute-start.22 = (bf16[1728,128]{1,0:T(8,128)(2,1)S(1)}, bf16[1728,128]{1,0:T(8,128)(2,1)S(1)}, u32[]{:S(2)}, u32[]{:S(2)}) collective-permute-start(bf16[1728,128]{1,0:T(8,128)(2,1)S(1)} %collective-permute-done.18.refs_11_), channel_id=1, source_target_pairs={{0,1},{1,0},{2,3},{3,2},{4,5},{5,4},{6,7},{7,6},{8,9},{9,8},{10,11... | collective-permute-start | bytes 1327112 | tf_op jit(solution)/shard_map/ppermute | solution.py:343
  48.9 6.2 %collective-permute-start.21 = (bf16[1728,128]{1,0:T(8,128)(2,1)S(1)}, bf16[1728,128]{1,0:T(8,128)(2,1)S(1)}, u32[]{:S(2)}, u32[]{:S(2)}) collective-permute-start(bf16[1728,128]{1,0:T(8,128)(2,1)S(1)} %collective-permute-done.17.refs_10_), channel_id=1, source_target_pairs={{0,1},{1,0},{2,3},{3,2},{4,5},{5,4},{6,7},{7,6},{8,9},{9,8},{10,11... | collective-permute-start | bytes 1327112 | tf_op jit(solution)/shard_map/ppermute | solution.py:343
  49.0 6.1 %collective-permute-start.20 = (bf16[1728,128]{1,0:T(8,128)(2,1)S(1)}, bf16[1728,128]{1,0:T(8,128)(2,1)S(1)}, u32[]{:S(2)}, u32[]{:S(2)}) collective-permute-start(bf16[1728,128]{1,0:T(8,128)(2,1)S(1)} %collective-permute-done.16.refs_9_), channel_id=1, source_target_pairs={{0,1},{1,0},{2,3},{3,2},{4,5},{5,4},{6,7},{7,6},{8,9},{9,8},{10,11... | collective-permute-start | bytes 1327112 | tf_op jit(solution)/shard_map/ppermute | solution.py:343
  49.4 4.3 %collective-permute-start.12 = (bf16[592,128]{1,0:T(8,128)(2,1)S(1)}, bf16[592,128]{1,0:T(8,128)(2,1)S(1)}, u32[]{:S(2)}, u32[]{:S(2)}) collective-permute-start(bf16[592,128]{1,0:T(8,128)(2,1)S(1)} %collective-permute-done.8.refs_3_), channel_id=1, source_target_pairs={{0,1},{1,0},{2,3},{3,2},{4,5},{5,4},{6,7},{7,6},{8,9},{9,8},{10,11... | collective-permute-start | bytes 454664 | tf_op jit(solution)/shard_map/ppermute | solution.py:343
  52.7 1.4 %collective-permute-start.11 = (bf16[592,128]{1,0:T(8,128)(2,1)S(1)}, bf16[592,128]{1,0:T(8,128)(2,1)S(1)}, u32[]{:S(2)}, u32[]{:S(2)}) collective-permute-start(bf16[592,128]{1,0:T(8,128)(2,1)S(1)} %collective-permute-done.7.refs_2_), channel_id=1, source_target_pairs={{0,1},{1,0},{2,3},{3,2},{4,5},{5,4},{6,7},{7,6},{8,9},{9,8},{10,11... | collective-permute-start | bytes 454664 | tf_op jit(solution)/shard_map/ppermute | solution.py:343
  53.7 1.4 %collective-permute-start.10 = (bf16[592,128]{1,0:T(8,128)(2,1)S(1)}, bf16[592,128]{1,0:T(8,128)(2,1)S(1)}, u32[]{:S(2)}, u32[]{:S(2)}) collective-permute-start(bf16[592,128]{1,0:T(8,128)(2,1)S(1)} %collective-permute-done.6.refs_1_), channel_id=1, source_target_pairs={{0,1},{1,0},{2,3},{3,2},{4,5},{5,4},{6,7},{7,6},{8,9},{9,8},{10,11... | collective-permute-start | bytes 454664 | tf_op jit(solution)/shard_map/ppermute | solution.py:343

commit v9 on v4

--- a/solution.py
+++ b/solution.py
@@ -53,15 +53,22 @@
     return lax.dot_general(left, right, (((1,), (0,)), ((), ())), preferred_element_type=f32)
 
 
-def call(kernel, args, outs, scratch=(), specs=None):
+def size_of(shape, dtype):
+    return math.prod(shape) * jnp.dtype(dtype).itemsize
+
+
+def call(kernel, args, outs, scratch=(), in_specs=None):
     whole = pl.BlockSpec(memory_space=pltpu.VMEM)
+    held = sum(size_of(arg.shape, arg.dtype) for arg in args if not in_specs)
+    held += sum(size_of(*out) for out in outs) + sum(size_of(*buffer) for buffer in scratch)
+    semaphores = [pltpu.SemaphoreType.DMA((16,))] if in_specs else []
     return pl.pallas_call(
         kernel,
-        in_specs=specs or [whole] * len(args),
+        in_specs=in_specs or [whole] * len(args),
         out_specs=[whole] * len(outs),
         out_shape=[jax.ShapeDtypeStruct(shape, dtype) for shape, dtype in outs],
-        scratch_shapes=list(scratch),
-        compiler_params=pltpu.CompilerParams(vmem_limit_bytes=48 * 1024 * 1024),
+        scratch_shapes=[pltpu.VMEM(*buffer) for buffer in scratch] + semaphores,
+        compiler_params=pltpu.CompilerParams(vmem_limit_bytes=held + 4 * 1024 * 1024),
     )(*args)
 
 
@@ -97,7 +104,7 @@
         big.append(pltpu.make_async_copy(dy_a.at[:, cols], dy_a_v.at[:, cols], sems.at[2 + 2 * t]))
         big.append(pltpu.make_async_copy(dy_e.at[:, cols], dy_e_v.at[:, cols], sems.at[3 + 2 * t]))
     extra = [pltpu.make_async_copy(ref, state.at[i], sems.at[2 + 2 * STEPS + i]) for i, ref in enumerate((w, m, v))]
-    for copy in small + big + extra:
+    for copy in small + big[:4]:
         copy.start()
 
     me = lax.axis_index("dp")
@@ -121,6 +128,8 @@
         big[2 * t].wait()
         terms_a = dot(left_a, dy_a_v[:, cols])
         big[2 * t + 1].wait()
+        for copy in big[2 * t + 4 : 2 * t + 6] if t + 2 < STEPS else extra if t + 2 == STEPS else []:
+            copy.start()
         terms_e = dot(left_e, dy_e_v[:, cols])
         for b in range(tile // LANES):
             attn, exp = plan.places(t * (tile // LANES) + b)
@@ -148,23 +157,18 @@
         args,
         [((2 * half, LANES), f32), ((half, LANES), bf16), ((4 * plan.size_a, LANES), bf16)],
         [
-            pltpu.VMEM(act_a.shape, bf16),
-            pltpu.VMEM(dy_a.shape, bf16),
-            pltpu.VMEM(act_e.shape, bf16),
-            pltpu.VMEM(dy_e.shape, bf16),
-            pltpu.VMEM((3,) + w.shape, f32),
-            pltpu.SemaphoreType.DMA((5 + 2 * STEPS,)),
+            (act_a.shape, bf16),
+            (dy_a.shape, bf16),
+            (act_e.shape, bf16),
+            (dy_e.shape, bf16),
+            ((3,) + w.shape, f32),
         ],
         [pl.BlockSpec(memory_space=pltpu.HBM)] * len(args),
     )
 
 
 def share_kernel(plan, *refs):
-    packs, refs = refs[: plan.n_expert], refs[plan.n_expert :]
-    own, got, (payload, g_exp, states) = refs[0], refs[1:-3], refs[-3:]
-    place = lax.axis_index("expert")
-    for q, pack in enumerate(packs):
-        states[place ^ q] = pack[...]
+    own, got, (payload, g_exp) = refs[0], refs[1:-2], refs[-2:]
     total = own[...]
     for ref in got:
         total = total + ref[...].astype(f32)
@@ -182,38 +186,53 @@
     return attn, (one[:8] + one[8:]) + (two[:8] + two[8:])
 
 
-def again_kernel(plan, mine, other, payload):
+def again_kernel(plan, distance, mine, other, held, far, payload, both):
     attn, square = pair_sum(plan, mine, other)
     a = plan.all_a
     payload[:a, :] = attn.astype(bf16)
     payload[a:, :] = jnp.concatenate(two_pieces(square), axis=0).astype(bf16)
+    bit = (lax.axis_index("expert") // distance) % 2
+    size = held.shape[0]
+    both[pl.ds(pl.multiple_of(bit * size, 16), size), :] = held[...]
+    both[pl.ds(pl.multiple_of((1 - bit) * size, 16), size), :] = far[...]
 
 
 def last_kernel(plan, mine, other, g_attn, square):
     attn, partial = pair_sum(plan, mine, other)
     g_attn[...] = attn
-    square[...] = partial + by_eights(attn * attn)
-
-
-def update_kernel(plan, limit, *refs):
-    square, g_attn, g_exp, wa, ma, va, we, me, ve = refs[:9]
-    states, wa_new, ma_new, va_new, we_new, me_new, ve_new, mine = refs[9:]
-    norm = jnp.sqrt(jnp.sum(square[...], keepdims=True))
-    factor = jnp.minimum(1.0, limit / (norm + 1e-06))
-    place = lax.axis_index("expert")
-    size = plan.size_a
-
-    def rows(expert):
-        return pl.ds(pl.multiple_of(expert * size, 16), size)
-
-    wa_new[...], ma_new[...], va_new[...] = adamw(g_attn[rows(place), :], wa[...], ma[...], va[...], factor)
-    for e in range(plan.n_expert):
-        high, low, moment, second = [states[e, pl.ds(i * size, size), :].astype(f32) for i in range(4)]
-        weight, _, _ = adamw(g_attn[pl.ds(e * size, size), :], high + low, moment, second, factor)
-        mine[pl.ds(e * size, size), :] = weight.astype(bf16)
-    weight, moment, second = adamw(g_exp[...], we[...], me[...], ve[...], factor)
-    we_new[...], me_new[...], ve_new[...] = weight, moment, second
+    square[...] = jnp.broadcast_to((partial + by_eights(attn * attn))[None], square.shape)
+
+
+def clip_factor(limit, square):
+    norm = jnp.sqrt(jnp.sum(jnp.sum(square[...], axis=0), keepdims=True))
+    return jnp.minimum(1.0, limit / (norm + 1e-06))
+
+
+def rows_kernel(plan, limit, square, g_attn, g_exp, we, me, ve, held, far, mine):
+    factor = clip_factor(limit, square)
+    size, half = plan.size_a, plan.n_expert // 2
+    bit = (lax.axis_index("expert") // half) % 2
+    for side, states in enumerate((held, far)):
+        for i in range(half):
+            rows = pl.ds(pl.multiple_of((((bit + side) % 2) * half + i) * size, 16), size)
+            high, low, moment, second = [
+                states[pl.ds((i * 4 + j) * size, size), :].astype(f32) for j in range(4)
+            ]
+            weight, _, _ = adamw(g_attn[rows, :], high + low, moment, second, factor)
+            mine[rows, :] = weight.astype(bf16)
+    weight, _, _ = adamw(g_exp[...], we[...], me[...], ve[...], factor)
     mine[plan.all_a :, :] = weight.astype(bf16)
+
+
+def own_kernel(plan, limit, *refs):
+    square, g_attn, g_exp = refs[:3]
+    state, new = refs[3:9], refs[9:]
+    factor = clip_factor(limit, square)
+    rows = pl.ds(pl.multiple_of(lax.axis_index("expert") * plan.size_a, 16), plan.size_a)
+    for b, grad in enumerate((g_attn[rows, :], g_exp[...])):
+        values = adamw(grad, *[ref[...] for ref in state[3 * b : 3 * b + 3]], factor)
+        for ref, value in zip(new[3 * b : 3 * b + 3], values):
+            ref[...] = value
 
 
 def order_kernel(plan, *refs):
@@ -254,9 +273,9 @@
         parts,
         [((count_a, plan.width), bf16), ((1, count_e, plan.width), bf16)],
         [
-            pltpu.VMEM((plan.n_dp * plan.chunk, LANES), f32),
-            pltpu.VMEM((count_a, LANES), f32),
-            pltpu.VMEM((plan.blocks * count_e, LANES), f32),
+            ((plan.n_dp * plan.chunk, LANES), f32),
+            ((count_a, LANES), f32),
+            ((plan.blocks * count_e, LANES), f32),
         ],
     )
 
@@ -290,35 +309,38 @@
     held = [pltpu.with_memory_space_constraint(x, pltpu.HBM) for x in (act_attn.T, dy_attn, act_exp[0].T, dy_exp[0])]
     full, send, pack = make_terms(plan, *held, *[pltpu.with_memory_space_constraint(x, pltpu.HBM) for x in state_a])
     got = swap(send, "dp", 1)
-    packs = [pack] + [swap(pack, "expert", q) for q in range(1, n_expert)]
     sums = [
         full[c * chunk : (c + 1) * chunk] + got[c * chunk : (c + 1) * chunk].astype(f32) for c in range(chips)
     ]
     got = [swap(sums[c].astype(bf16), "dp", 2 * c) for c in range(1, chips)]
     shared = ((plan.all_a + 16, LANES), bf16)
-    payload, g_exp, states = call(
-        lambda *refs: share_kernel(plan, *refs),
-        packs + [sums[0]] + got,
-        [shared, ((plan.size_e, LANES), f32), ((n_expert, 4 * plan.size_a, LANES), bf16)],
+    payload, g_exp = call(
+        lambda *refs: share_kernel(plan, *refs), [sums[0]] + got, [shared, ((plan.size_e, LANES), f32)]
     )
     distance = 1
     while 2 * distance < n_expert:
-        other = swap(payload, "expert", distance)
-        (payload,) = call(lambda *refs: again_kernel(plan, *refs), [payload, other], [shared])
+        other, far = swap(payload, "expert", distance), swap(pack, "expert", distance)
+        payload, pack = call(
+            lambda *refs: again_kernel(plan, distance, *refs),
+            [payload, other, pack, far],
+            [shared, ((8 * distance * plan.size_a, LANES), bf16)],
+        )
         distance *= 2
-    other = swap(payload, "expert", distance)
+    other, far = swap(payload, "expert", distance), swap(pack, "expert", distance)
     g_attn, square = call(
-        lambda *refs: last_kernel(plan, *refs), [payload, other], [((plan.all_a, LANES), f32), ((8, LANES), f32)]
-    )
-    distance = 1
-    while distance < n_dp:
-        square = square + swap(square, "dp", distance)
-        distance *= 2
+        lambda *refs: last_kernel(plan, *refs), [payload, other], [((plan.all_a, LANES), f32), ((n_dp, 8, LANES), f32)]
+    )
+    square = lax.all_to_all(square, "dp", 0, 0, tiled=True)
     block_a, block_e = ((plan.size_a, LANES), f32), ((plan.size_e, LANES), f32)
-    wa, ma, va, we, me, ve, mine = call(
-        lambda *refs: update_kernel(plan, limit, *refs),
-        [square, g_attn, g_exp, *state_a, *state_e, states],
-        [block_a] * 3 + [block_e] * 3 + [((chunk, LANES), bf16)],
+    (mine,) = call(
+        lambda *refs: rows_kernel(plan, limit, *refs),
+        [square, g_attn, g_exp, *state_e, pack, far],
+        [((chunk, LANES), bf16)],
+    )
+    wa, ma, va, we, me, ve = call(
+        lambda *refs: own_kernel(plan, limit, *refs),
+        [square, g_attn, g_exp, *state_a, *state_e],
+        [block_a] * 3 + [block_e] * 3,
     )
     near = [mine] + [swap(mine, "dp", 2 * c) for c in range(1, chips)]
     far = [swap(piece, "dp", 1) for piece in near]

time: 49.8 us -> 47.7 us (0.958)
  blocking collectives: 0 us -> 7.21 us
  waiting for transfers between devices: 23.9 us -> 18.2 us
  starting transfers between devices: 18.6 us -> 14.3 us
  Pallas kernels: 6.16 us -> 6.9 us
    all_to_all x0 -> x1, blocking collectives: none -> 7.21 us  [body(): square = lax.all_to_all(square, 'dp', 0, 0, tiled=True)]
    ppermute x19 -> x15, waiting for transfers between devices: 23.9 us -> 18.2 us  [swap(): return lax.ppermute(value, axis, [(i, i ^ distance) for i in range(size)])]
    ppermute x19 -> x15, starting transfers between devices: 18.6 us -> 14.3 us  [swap(): return lax.ppermute(value, axis, [(i, i ^ distance) for i in range(size)])]
    pallas_call x6 -> x7, Pallas kernels: 6.16 us -> 6.9 us  [call(): pl.pallas_call(kernel, in_specs=in_specs or [whole] * len(args), out_spec...]
  transfers between devices with their start and end apart: 19 -> 15, of which waited for: 11 -> 8; matrix products, arithmetic and copies ran while one was open for 0% -> 0% of each run, Pallas kernels for 0% -> 2%
where the time goes in v9:
time: 47.7 us; the launch traced here: 47.5 us
  waiting for transfers between devices  18.2 us (38%)
  starting transfers between devices  14.3 us (30%)
  blocking collectives  7.21 us (15%)
  Pallas kernels  6.9 us (14%)
  between operations  0.75 us (2%)
    ppermute x15, waiting for transfers between devices, swap(): return lax.ppermute(value, axis, [(i, i ^ distance) for i in range(size)])  18.2 us
    ppermute x15, starting transfers between devices, swap(): return lax.ppermute(value, axis, [(i, i ^ distance) for i in range(size)])  14.3 us
    all_to_all x1, blocking collectives, body(): square = lax.all_to_all(square, 'dp', 0, 0, tiled=True)  7.21 us
    pallas_call x7, Pallas kernels, call(): pl.pallas_call(kernel, in_specs=in_specs or [whole] * len(args), out_spec...  6.9 us
  transfers between devices with their start and end apart: 15, of which 8 were waited for; matrix products, arithmetic and copies ran while one was open for 0% of the time, Pallas kernels for 2%

profile of v9, /device:TPU:0, one launch (start us, length us, event | category | flops | bytes accessed | tf_op | source)
XLA Modules:
  0.0 47.5 jit_solution(9822560979083743564)
XLA Ops:
  0.6 4.1 %shard_map.161 = (f32[2304,128]{1,0:T(8,128)S(1)}, bf16[1152,128]{1,0:T(8,128)(2,1)S(1)}, bf16[192,128]{1,0:T(8,128)(2,1)S(1)}) custom-call(bf16[32,256]{1,0:T(8,128)(2,1)} %bitcast.54, bf16[256,6144]{1,0:T(8,128)(2,1)} %refs_1_.1, bf16[16,128]{1,0:T(8,128)(2,1)} %bitcast.55, bf16[128,6144]{1,0:T(8,128)(2,1)} %bitcast.53, f32[48,128]{1,0:T(8,128)} %bitcast.47, ...), custom_call_target="tpu_custom_call" | custom-call | tf_op jit(solution)/shard_map/pallas_call | solution.py:65
  4.7 0.0 copy-start
  4.8 0.0 copy-start.1
  4.8 0.0 copy-start.2
  4.8 0.0 copy-start.3
  4.8 0.0 copy-start.5
  4.8 0.5 %collective-permute-start = (bf16[1152,128]{1,0:T(8,128)(2,1)S(1)}, bf16[1152,128]{1,0:T(8,128)(2,1)S(1)}, u32[]{:S(2)}, u32[]{:S(2)}) collective-permute-start(bf16[1152,128]{1,0:T(8,128)(2,1)S(1)} %get-tuple-element.26), channel_id=1, source_target_pairs={{0,1},{1,0},{2,3},{3,2},{4,5},{5,4},{6,7},{7,6},{8,9},{9,8},{10,11... | collective-permute-start | bytes 884744 | tf_op jit(solution)/shard_map/ppermute | solution.py:285
  5.3 1.2 %collective-permute-done = bf16[1152,128]{1,0:T(8,128)(2,1)S(1)} collective-permute-done((bf16[1152,128]{1,0:T(8,128)(2,1)S(1)}, bf16[1152,128]{1,0:T(8,128)(2,1)S(1)}, u32[]{:S(2)}, u32[]{:S(2)}) %collective-permute-start) | collective-permute-done | bytes 294944 | tf_op jit(solution)/shard_map/ppermute | solution.py:285
  6.5 0.1 add_convert_fusion
  6.6 2.9 %collective-permute-start.1 = (bf16[288,128]{1,0:T(8,128)(2,1)S(1)}, bf16[288,128]{1,0:T(8,128)(2,1)S(1)}, u32[]{:S(2)}, u32[]{:S(2)}) collective-permute-start(bf16[288,128]{1,0:T(8,128)(2,1)S(1)} %get-tuple-element.44), channel_id=1, source_target_pairs={{0,2},{1,3},{2,0},{3,1},{4,6},{5,7},{6,4},{7,5},{8,10},{9,11},{10,... | collective-permute-start | bytes 221192 | tf_op jit(solution)/shard_map/ppermute | solution.py:285
  9.5 1.5 %collective-permute-start.2 = (bf16[288,128]{1,0:T(8,128)(2,1)S(1)}, bf16[288,128]{1,0:T(8,128)(2,1)S(1)}, u32[]{:S(2)}, u32[]{:S(2)}) collective-permute-start(bf16[288,128]{1,0:T(8,128)(2,1)S(1)} %get-tuple-element.43), channel_id=1, source_target_pairs={{0,4},{1,5},{2,6},{3,7},{4,0},{5,1},{6,2},{7,3},{8,12},{9,13},{10,... | collective-permute-start | bytes 221192 | tf_op jit(solution)/shard_map/ppermute | solution.py:285
  11.1 0.0 collective-permute-start.3
  11.1 1.0 %collective-permute-done.1.refs_1_ = bf16[288,128]{1,0:T(8,128)(2,1)S(1)} collective-permute-done((bf16[288,128]{1,0:T(8,128)(2,1)S(1)}, bf16[288,128]{1,0:T(8,128)(2,1)S(1)}, u32[]{:S(2)}, u32[]{:S(2)}) %collective-permute-start.1) | collective-permute-done | bytes 73760 | tf_op jit(solution)/shard_map/ppermute | solution.py:285
  12.1 1.8 %collective-permute-done.2.refs_2_ = bf16[288,128]{1,0:T(8,128)(2,1)S(1)} collective-permute-done((bf16[288,128]{1,0:T(8,128)(2,1)S(1)}, bf16[288,128]{1,0:T(8,128)(2,1)S(1)}, u32[]{:S(2)}, u32[]{:S(2)}) %collective-permute-start.2) | collective-permute-done | bytes 73760 | tf_op jit(solution)/shard_map/ppermute | solution.py:285
  13.9 2.4 %collective-permute-done.3.refs_3_ = bf16[288,128]{1,0:T(8,128)(2,1)S(1)} collective-permute-done((bf16[288,128]{1,0:T(8,128)(2,1)S(1)}, bf16[288,128]{1,0:T(8,128)(2,1)S(1)}, u32[]{:S(2)}, u32[]{:S(2)}) %collective-permute-start.3) | collective-permute-done | bytes 73760 | tf_op jit(solution)/shard_map/ppermute | solution.py:285
  16.4 1.6 %collective-permute-start.4 = (bf16[208,128]{1,0:T(8,128)(2,1)S(1)}, bf16[208,128]{1,0:T(8,128)(2,1)S(1)}, u32[]{:S(2)}, u32[]{:S(2)}) collective-permute-start(bf16[208,128]{1,0:T(8,128)(2,1)S(1)} %get-tuple-element.27.refs_0_), channel_id=1, source_target_pairs={{0,8},{8,0},{16,24},{24,16},{1,9},{9,1},{17,25},{25,17},{2,10},{10... | collective-permute-start | bytes 159752 | tf_op jit(solution)/shard_map/ppermute | solution.py:285
  18.0 0.4 collective-permute-start.5
  18.5 3.6 %collective-permute-done.5.refs_3_ = bf16[192,128]{1,0:T(8,128)(2,1)S(1)} collective-permute-done((bf16[192,128]{1,0:T(8,128)(2,1)S(1)}, bf16[192,128]{1,0:T(8,128)(2,1)S(1)}, u32[]{:S(2)}, u32[]{:S(2)}) %collective-permute-start.5) | collective-permute-done | bytes 49184 | tf_op jit(solution)/shard_map/ppermute | solution.py:285
  22.1 3.1 %collective-permute-start.7 = (bf16[384,128]{1,0:T(8,128)(2,1)S(1)}, bf16[384,128]{1,0:T(8,128)(2,1)S(1)}, u32[]{:S(2)}, u32[]{:S(2)}) collective-permute-start(bf16[384,128]{1,0:T(8,128)(2,1)S(1)} %get-tuple-element.39.refs_6_), channel_id=1, source_target_pairs={{0,16},{8,24},{16,0},{24,8},{1,17},{9,25},{17,1},{25,9},{2,18},{10... | collective-permute-start | bytes 294920 | tf_op jit(solution)/shard_map/ppermute | solution.py:285
  25.2 0.1 collective-permute-start.6
  25.3 5.1 %collective-permute-done.6.refs_1_ = bf16[208,128]{1,0:T(8,128)(2,1)S(1)} collective-permute-done((bf16[208,128]{1,0:T(8,128)(2,1)S(1)}, bf16[208,128]{1,0:T(8,128)(2,1)S(1)}, u32[]{:S(2)}, u32[]{:S(2)}) %collective-permute-start.6) | collective-permute-done | bytes 53280 | tf_op jit(solution)/shard_map/ppermute | solution.py:285
  30.4 7.2 %all_to_all.5.refs_0_ = f32[8,8,128]{2,1,0:T(8,128)S(1)} all-to-all(f32[8,8,128]{2,1,0:T(8,128)S(1)} %get-tuple-element.30), channel_id=1, replica_groups=mesh['expert'=4,'dp'=8] {'dp'}, dimensions={0} | all-to-all | bytes 65536 | tf_op jit(solution)/shard_map/all_to_all | solution.py:333
  37.7 0.3 shard_map.166.refs_0_
  37.9 0.6 %collective-permute-start.8 = (bf16[288,128]{1,0:T(8,128)(2,1)S(1)}, bf16[288,128]{1,0:T(8,128)(2,1)S(1)}, u32[]{:S(2)}, u32[]{:S(2)}) collective-permute-start(bf16[288,128]{1,0:T(8,128)(2,1)S(1)} %shard_map.166.refs_0_), channel_id=1, source_target_pairs={{0,2},{1,3},{2,0},{3,1},{4,6},{5,7},{6,4},{7,5},{8,10},{9,11},{10,... | collective-permute-start | bytes 221192 | tf_op jit(solution)/shard_map/ppermute | solution.py:285
  38.6 0.6 %collective-permute-start.9 = (bf16[288,128]{1,0:T(8,128)(2,1)S(1)}, bf16[288,128]{1,0:T(8,128)(2,1)S(1)}, u32[]{:S(2)}, u32[]{:S(2)}) collective-permute-start(bf16[288,128]{1,0:T(8,128)(2,1)S(1)} %shard_map.166.refs_0_), channel_id=1, source_target_pairs={{0,4},{1,5},{2,6},{3,7},{4,0},{5,1},{6,2},{7,3},{8,12},{9,13},{10,... | collective-permute-start | bytes 221192 | tf_op jit(solution)/shard_map/ppermute | solution.py:285
  39.1 2.4 %collective-permute-start.10 = (bf16[288,128]{1,0:T(8,128)(2,1)S(1)}, bf16[288,128]{1,0:T(8,128)(2,1)S(1)}, u32[]{:S(2)}, u32[]{:S(2)}) collective-permute-start(bf16[288,128]{1,0:T(8,128)(2,1)S(1)} %shard_map.166.refs_0_), channel_id=1, source_target_pairs={{0,6},{1,7},{2,4},{3,5},{4,2},{5,3},{6,0},{7,1},{8,14},{9,15},{10,... | collective-permute-start | bytes 221192 | tf_op jit(solution)/shard_map/ppermute | solution.py:285
  41.5 1.2 %collective-permute-done.8.refs_1_ = bf16[288,128]{1,0:T(8,128)(2,1)S(1)} collective-permute-done((bf16[288,128]{1,0:T(8,128)(2,1)S(1)}, bf16[288,128]{1,0:T(8,128)(2,1)S(1)}, u32[]{:S(2)}, u32[]{:S(2)}) %collective-permute-start.8) | collective-permute-done | bytes 73760 | tf_op jit(solution)/shard_map/ppermute | solution.py:285
  42.7 1.8 %collective-permute-done.9.refs_2_ = bf16[288,128]{1,0:T(8,128)(2,1)S(1)} collective-permute-done((bf16[288,128]{1,0:T(8,128)(2,1)S(1)}, bf16[288,128]{1,0:T(8,128)(2,1)S(1)}, u32[]{:S(2)}, u32[]{:S(2)}) %collective-permute-start.9) | collective-permute-done | bytes 73760 | tf_op jit(solution)/shard_map/ppermute | solution.py:285
  44.5 0.5 %collective-permute-start.14 = (bf16[288,128]{1,0:T(8,128)(2,1)S(1)}, bf16[288,128]{1,0:T(8,128)(2,1)S(1)}, u32[]{:S(2)}, u32[]{:S(2)}) collective-permute-start(bf16[288,128]{1,0:T(8,128)(2,1)S(1)} %collective-permute-done.10.refs_3_), channel_id=1, source_target_pairs={{0,1},{1,0},{2,3},{3,2},{4,5},{5,4},{6,7},{7,6},{8,9},{9,8},{10,11... | collective-permute-start | bytes 221192 | tf_op jit(solution)/shard_map/ppermute | solution.py:285
  45.0 0.9 %shard_map.165 = (f32[48,128]{1,0:T(8,128)}, f32[48,128]{1,0:T(8,128)}, f32[48,128]{1,0:T(8,128)}, f32[96,128]{1,0:T(8,128)}, f32[96,128]{1,0:T(8,128)}, /*index=5*/f32[96,128]{1,0:T(8,128)}) custom-call(f32[8,8,128]{2,1,0:T(8,128)S(1)} %all_to_all.5.refs_0_, f32[192,128]{1,0:T(8,128)S(1)} %get-tuple-element.31.refs_1_, ...), custom_call_target="tpu_custom_call" | custom-call | tf_op jit(solution)/shard_map/pallas_call | solution.py:65
  45.8 0.0 collective-permute-done.14.refs_7_
  45.9 1.6 %shard_map.167 = (bf16[32,6144]{1,0:T(8,128)(2,1)}, bf16[1,16,6144]{2,1,0:T(8,128)(2,1)}) custom-call(bf16[288,128]{1,0:T(8,128)(2,1)S(1)} %shard_map.166.refs_0_, bf16[288,128]{1,0:T(8,128)(2,1)S(1)} %collective-permute-done.8.refs_1_, bf16[288,128]{1,0:T(8,128)(2,1)S(1)} %collective-permute-done.9.refs_2_, ...), custom_call_target="tpu_custom_call" | custom-call | tf_op jit(solution)/shard_map/pallas_call | solution.py:65
  (19 shorter events, 0.1 us)
Async XLA Ops:
  4.7 32.9 %copy-start = (f32[1,2,6144]{2,1,0:T(2,128)S(1)}, f32[1,2,6144]{2,1,0:T(2,128)}, u32[]{:S(2)}) copy-start(f32[1,2,6144]{2,1,0:T(2,128)} %param.17) | copy-start | bytes 147460
  4.8 32.9 %copy-start.1 = (f32[1,2,6144]{2,1,0:T(2,128)S(1)}, f32[1,2,6144]{2,1,0:T(2,128)}, u32[]{:S(2)}) copy-start(f32[1,2,6144]{2,1,0:T(2,128)} %param.18) | copy-start | bytes 147460
  4.8 32.9 %copy-start.2 = (f32[1,2,6144]{2,1,0:T(2,128)S(1)}, f32[1,2,6144]{2,1,0:T(2,128)}, u32[]{:S(2)}) copy-start(f32[1,2,6144]{2,1,0:T(2,128)} %param.19) | copy-start | bytes 147460
  4.8 40.2 %copy-start.3 = (f32[1,6144]{1,0:T(1,128)S(1)}, f32[1,6144]{1,0:T(1,128)}, u32[]{:S(2)}) copy-start(f32[1,6144]{1,0:T(1,128)} %param.14) | copy-start | bytes 73732
  4.8 40.2 %copy-start.4 = (f32[1,6144]{1,0:T(1,128)S(1)}, f32[1,6144]{1,0:T(1,128)}, u32[]{:S(2)}) copy-start(f32[1,6144]{1,0:T(1,128)} %param.15) | copy-start | bytes 73732
  4.8 40.2 %copy-start.5 = (f32[1,6144]{1,0:T(1,128)S(1)}, f32[1,6144]{1,0:T(1,128)}, u32[]{:S(2)}) copy-start(f32[1,6144]{1,0:T(1,128)} %param.16) | copy-start | bytes 73732
  4.8 1.7 %collective-permute-start = (bf16[1152,128]{1,0:T(8,128)(2,1)S(1)}, bf16[1152,128]{1,0:T(8,128)(2,1)S(1)}, u32[]{:S(2)}, u32[]{:S(2)}) collective-permute-start(bf16[1152,128]{1,0:T(8,128)(2,1)S(1)} %get-tuple-element.26), channel_id=1, source_target_pairs={{0,1},{1,0},{2,3},{3,2},{4,5},{5,4},{6,7},{7,6},{8,9},{9,8},{10,11... | collective-permute-start | bytes 884744 | tf_op jit(solution)/shard_map/ppermute | solution.py:285
  6.6 5.5 %collective-permute-start.1 = (bf16[288,128]{1,0:T(8,128)(2,1)S(1)}, bf16[288,128]{1,0:T(8,128)(2,1)S(1)}, u32[]{:S(2)}, u32[]{:S(2)}) collective-permute-start(bf16[288,128]{1,0:T(8,128)(2,1)S(1)} %get-tuple-element.44), channel_id=1, source_target_pairs={{0,2},{1,3},{2,0},{3,1},{4,6},{5,7},{6,4},{7,5},{8,10},{9,11},{10,... | collective-permute-start | bytes 221192 | tf_op jit(solution)/shard_map/ppermute | solution.py:285
  9.5 4.4 %collective-permute-start.2 = (bf16[288,128]{1,0:T(8,128)(2,1)S(1)}, bf16[288,128]{1,0:T(8,128)(2,1)S(1)}, u32[]{:S(2)}, u32[]{:S(2)}) collective-permute-start(bf16[288,128]{1,0:T(8,128)(2,1)S(1)} %get-tuple-element.43), channel_id=1, source_target_pairs={{0,4},{1,5},{2,6},{3,7},{4,0},{5,1},{6,2},{7,3},{8,12},{9,13},{10,... | collective-permute-start | bytes 221192 | tf_op jit(solution)/shard_map/ppermute | solution.py:285
  11.1 5.3 %collective-permute-start.3 = (bf16[288,128]{1,0:T(8,128)(2,1)S(1)}, bf16[288,128]{1,0:T(8,128)(2,1)S(1)}, u32[]{:S(2)}, u32[]{:S(2)}) collective-permute-start(bf16[288,128]{1,0:T(8,128)(2,1)S(1)} %get-tuple-element.42), channel_id=1, source_target_pairs={{0,6},{1,7},{2,4},{3,5},{4,2},{5,3},{6,0},{7,1},{8,14},{9,15},{10,... | collective-permute-start | bytes 221192 | tf_op jit(solution)/shard_map/ppermute | solution.py:285
  16.4 5.7 %collective-permute-start.4 = (bf16[208,128]{1,0:T(8,128)(2,1)S(1)}, bf16[208,128]{1,0:T(8,128)(2,1)S(1)}, u32[]{:S(2)}, u32[]{:S(2)}) collective-permute-start(bf16[208,128]{1,0:T(8,128)(2,1)S(1)} %get-tuple-element.27.refs_0_), channel_id=1, source_target_pairs={{0,8},{8,0},{16,24},{24,16},{1,9},{9,1},{17,25},{25,17},{2,10},{10... | collective-permute-start | bytes 159752 | tf_op jit(solution)/shard_map/ppermute | solution.py:285
  18.0 4.1 %collective-permute-start.5 = (bf16[192,128]{1,0:T(8,128)(2,1)S(1)}, bf16[192,128]{1,0:T(8,128)(2,1)S(1)}, u32[]{:S(2)}, u32[]{:S(2)}) collective-permute-start(bf16[192,128]{1,0:T(8,128)(2,1)S(1)} %get-tuple-element.28.refs_2_), channel_id=1, source_target_pairs={{0,8},{8,0},{16,24},{24,16},{1,9},{9,1},{17,25},{25,17},{2,10},{10... | collective-permute-start | bytes 147464 | tf_op jit(solution)/shard_map/ppermute | solution.py:285
  22.1 15.5 %collective-permute-start.7 = (bf16[384,128]{1,0:T(8,128)(2,1)S(1)}, bf16[384,128]{1,0:T(8,128)(2,1)S(1)}, u32[]{:S(2)}, u32[]{:S(2)}) collective-permute-start(bf16[384,128]{1,0:T(8,128)(2,1)S(1)} %get-tuple-element.39.refs_6_), channel_id=1, source_target_pairs={{0,16},{8,24},{16,0},{24,8},{1,17},{9,25},{17,1},{25,9},{2,18},{10... | collective-permute-start | bytes 294920 | tf_op jit(solution)/shard_map/ppermute | solution.py:285
  25.2 5.2 %collective-permute-start.6 = (bf16[208,128]{1,0:T(8,128)(2,1)S(1)}, bf16[208,128]{1,0:T(8,128)(2,1)S(1)}, u32[]{:S(2)}, u32[]{:S(2)}) collective-permute-start(bf16[208,128]{1,0:T(8,128)(2,1)S(1)} %get-tuple-element.29.refs_0_), channel_id=1, source_target_pairs={{0,16},{8,24},{16,0},{24,8},{1,17},{9,25},{17,1},{25,9},{2,18},{10... | collective-permute-start | bytes 159752 | tf_op jit(solution)/shard_map/ppermute | solution.py:285
  37.9 4.8 %collective-permute-start.8 = (bf16[288,128]{1,0:T(8,128)(2,1)S(1)}, bf16[288,128]{1,0:T(8,128)(2,1)S(1)}, u32[]{:S(2)}, u32[]{:S(2)}) collective-permute-start(bf16[288,128]{1,0:T(8,128)(2,1)S(1)} %shard_map.166.refs_0_), channel_id=1, source_target_pairs={{0,2},{1,3},{2,0},{3,1},{4,6},{5,7},{6,4},{7,5},{8,10},{9,11},{10,... | collective-permute-start | bytes 221192 | tf_op jit(solution)/shard_map/ppermute | solution.py:285
  38.6 5.9 %collective-permute-start.9 = (bf16[288,128]{1,0:T(8,128)(2,1)S(1)}, bf16[288,128]{1,0:T(8,128)(2,1)S(1)}, u32[]{:S(2)}, u32[]{:S(2)}) collective-permute-start(bf16[288,128]{1,0:T(8,128)(2,1)S(1)} %shard_map.166.refs_0_), channel_id=1, source_target_pairs={{0,4},{1,5},{2,6},{3,7},{4,0},{5,1},{6,2},{7,3},{8,12},{9,13},{10,... | collective-permute-start | bytes 221192 | tf_op jit(solution)/shard_map/ppermute | solution.py:285
  39.1 5.3 %collective-permute-start.10 = (bf16[288,128]{1,0:T(8,128)(2,1)S(1)}, bf16[288,128]{1,0:T(8,128)(2,1)S(1)}, u32[]{:S(2)}, u32[]{:S(2)}) collective-permute-start(bf16[288,128]{1,0:T(8,128)(2,1)S(1)} %shard_map.166.refs_0_), channel_id=1, source_target_pairs={{0,6},{1,7},{2,4},{3,5},{4,2},{5,3},{6,0},{7,1},{8,14},{9,15},{10,... | collective-permute-start | bytes 221192 | tf_op jit(solution)/shard_map/ppermute | solution.py:285
  41.5 4.3 %collective-permute-start.11 = (bf16[288,128]{1,0:T(8,128)(2,1)S(1)}, bf16[288,128]{1,0:T(8,128)(2,1)S(1)}, u32[]{:S(2)}, u32[]{:S(2)}) collective-permute-start(bf16[288,128]{1,0:T(8,128)(2,1)S(1)} %shard_map.166.refs_0_), channel_id=1, source_target_pairs={{0,1},{1,0},{2,3},{3,2},{4,5},{5,4},{6,7},{7,6},{8,9},{9,8},{10,11... | collective-permute-start | bytes 221192 | tf_op jit(solution)/shard_map/ppermute | solution.py:285
  42.7 3.1 %collective-permute-start.12 = (bf16[288,128]{1,0:T(8,128)(2,1)S(1)}, bf16[288,128]{1,0:T(8,128)(2,1)S(1)}, u32[]{:S(2)}, u32[]{:S(2)}) collective-permute-start(bf16[288,128]{1,0:T(8,128)(2,1)S(1)} %collective-permute-done.8.refs_1_), channel_id=1, source_target_pairs={{0,1},{1,0},{2,3},{3,2},{4,5},{5,4},{6,7},{7,6},{8,9},{9,8},{10,11... | collective-permute-start | bytes 221192 | tf_op jit(solution)/shard_map/ppermute | solution.py:285
  44.5 1.4 %collective-permute-start.13 = (bf16[288,128]{1,0:T(8,128)(2,1)S(1)}, bf16[288,128]{1,0:T(8,128)(2,1)S(1)}, u32[]{:S(2)}, u32[]{:S(2)}) collective-permute-start(bf16[288,128]{1,0:T(8,128)(2,1)S(1)} %collective-permute-done.9.refs_2_), channel_id=1, source_target_pairs={{0,1},{1,0},{2,3},{3,2},{4,5},{5,4},{6,7},{7,6},{8,9},{9,8},{10,11... | collective-permute-start | bytes 221192 | tf_op jit(solution)/shard_map/ppermute | solution.py:285
  44.5 1.4 %collective-permute-start.14 = (bf16[288,128]{1,0:T(8,128)(2,1)S(1)}, bf16[288,128]{1,0:T(8,128)(2,1)S(1)}, u32[]{:S(2)}, u32[]{:S(2)}) collective-permute-start(bf16[288,128]{1,0:T(8,128)(2,1)S(1)} %collective-permute-done.10.refs_3_), channel_id=1, source_target_pairs={{0,1},{1,0},{2,3},{3,2},{4,5},{5,4},{6,7},{7,6},{8,9},{9,8},{10,11... | collective-permute-start | bytes 221192 | tf_op jit(solution)/shard_map/ppermute | solution.py:285

commit v10 on v9

--- a/solution.py
+++ b/solution.py
@@ -57,15 +57,14 @@
     return math.prod(shape) * jnp.dtype(dtype).itemsize
 
 
-def call(kernel, args, outs, scratch=(), in_specs=None):
-    whole = pl.BlockSpec(memory_space=pltpu.VMEM)
-    held = sum(size_of(arg.shape, arg.dtype) for arg in args if not in_specs)
+def call(kernel, args, outs, scratch=(), in_space=pltpu.VMEM, out_space=pltpu.VMEM, copies=False):
+    held = sum(size_of(arg.shape, arg.dtype) for arg in args if in_space is pltpu.VMEM)
     held += sum(size_of(*out) for out in outs) + sum(size_of(*buffer) for buffer in scratch)
-    semaphores = [pltpu.SemaphoreType.DMA((16,))] if in_specs else []
+    semaphores = [pltpu.SemaphoreType.DMA((16,))] if copies else []
     return pl.pallas_call(
         kernel,
-        in_specs=in_specs or [whole] * len(args),
-        out_specs=[whole] * len(outs),
+        in_specs=[pl.BlockSpec(memory_space=in_space)] * len(args),
+        out_specs=[pl.BlockSpec(memory_space=out_space)] * len(outs),
         out_shape=[jax.ShapeDtypeStruct(shape, dtype) for shape, dtype in outs],
         scratch_shapes=[pltpu.VMEM(*buffer) for buffer in scratch] + semaphores,
         compiler_params=pltpu.CompilerParams(vmem_limit_bytes=held + 4 * 1024 * 1024),
@@ -104,7 +103,7 @@
         big.append(pltpu.make_async_copy(dy_a.at[:, cols], dy_a_v.at[:, cols], sems.at[2 + 2 * t]))
         big.append(pltpu.make_async_copy(dy_e.at[:, cols], dy_e_v.at[:, cols], sems.at[3 + 2 * t]))
     extra = [pltpu.make_async_copy(ref, state.at[i], sems.at[2 + 2 * STEPS + i]) for i, ref in enumerate((w, m, v))]
-    for copy in small + big[:4]:
+    for copy in small + big + extra:
         copy.start()
 
     me = lax.axis_index("dp")
@@ -128,8 +127,6 @@
         big[2 * t].wait()
         terms_a = dot(left_a, dy_a_v[:, cols])
         big[2 * t + 1].wait()
-        for copy in big[2 * t + 4 : 2 * t + 6] if t + 2 < STEPS else extra if t + 2 == STEPS else []:
-            copy.start()
         terms_e = dot(left_e, dy_e_v[:, cols])
         for b in range(tile // LANES):
             attn, exp = plan.places(t * (tile // LANES) + b)
@@ -144,9 +141,8 @@
     for copy in extra:
         copy.wait()
     size = plan.size_a
-    high, low = two_pieces(state[0])
-    for i, value in enumerate((high, low, state[1], state[2])):
-        pack[pl.ds(i * size, size), :] = value.astype(bf16)
+    for i in range(3):
+        pack[pl.ds(i * size, size), :] = state[i].astype(bf16)
 
 
 def make_terms(plan, act_a, dy_a, act_e, dy_e, w, m, v):
@@ -155,7 +151,7 @@
     return call(
         lambda *refs: terms_kernel(plan, *refs),
         args,
-        [((2 * half, LANES), f32), ((half, LANES), bf16), ((4 * plan.size_a, LANES), bf16)],
+        [((2 * half, LANES), f32), ((half, LANES), bf16), ((3 * plan.size_a, LANES), bf16)],
         [
             (act_a.shape, bf16),
             (dy_a.shape, bf16),
@@ -163,12 +159,14 @@
             (dy_e.shape, bf16),
             ((3,) + w.shape, f32),
         ],
-        [pl.BlockSpec(memory_space=pltpu.HBM)] * len(args),
+        in_space=pltpu.HBM,
+        copies=True,
     )
 
 
 def share_kernel(plan, *refs):
-    own, got, (payload, g_exp) = refs[0], refs[1:-2], refs[-2:]
+    held, far, own, got, (payload, g_exp, both) = *refs[:3], refs[3:-3], refs[-3:]
+    both[0], both[1] = held[...], far[...]
     total = own[...]
     for ref in got:
         total = total + ref[...].astype(f32)
@@ -186,15 +184,11 @@
     return attn, (one[:8] + one[8:]) + (two[:8] + two[8:])
 
 
-def again_kernel(plan, distance, mine, other, held, far, payload, both):
+def again_kernel(plan, mine, other, payload):
     attn, square = pair_sum(plan, mine, other)
     a = plan.all_a
     payload[:a, :] = attn.astype(bf16)
     payload[a:, :] = jnp.concatenate(two_pieces(square), axis=0).astype(bf16)
-    bit = (lax.axis_index("expert") // distance) % 2
-    size = held.shape[0]
-    both[pl.ds(pl.multiple_of(bit * size, 16), size), :] = held[...]
-    both[pl.ds(pl.multiple_of((1 - bit) * size, 16), size), :] = far[...]
 
 
 def last_kernel(plan, mine, other, g_attn, square):
@@ -208,18 +202,15 @@
     return jnp.minimum(1.0, limit / (norm + 1e-06))
 
 
-def rows_kernel(plan, limit, square, g_attn, g_exp, we, me, ve, held, far, mine):
+def rows_kernel(plan, limit, square, g_attn, g_exp, we, me, ve, both, *refs):
+    far, mine = refs[:-1], refs[-1]
     factor = clip_factor(limit, square)
-    size, half = plan.size_a, plan.n_expert // 2
-    bit = (lax.axis_index("expert") // half) % 2
-    for side, states in enumerate((held, far)):
-        for i in range(half):
-            rows = pl.ds(pl.multiple_of((((bit + side) % 2) * half + i) * size, 16), size)
-            high, low, moment, second = [
-                states[pl.ds((i * 4 + j) * size, size), :].astype(f32) for j in range(4)
-            ]
-            weight, _, _ = adamw(g_attn[rows, :], high + low, moment, second, factor)
-            mine[rows, :] = weight.astype(bf16)
+    size, place = plan.size_a, lax.axis_index("expert")
+    for q, states in enumerate([both.at[0], both.at[1], *far]):
+        rows = pl.ds(pl.multiple_of((place ^ q) * size, 16), size)
+        old = [states[pl.ds(i * size, size), :].astype(f32) for i in range(3)]
+        weight, _, _ = adamw(g_attn[rows, :], *old, factor)
+        mine[rows, :] = weight.astype(bf16)
     weight, _, _ = adamw(g_exp[...], we[...], me[...], ve[...], factor)
     mine[plan.all_a :, :] = weight.astype(bf16)
 
@@ -235,34 +226,51 @@
             ref[...] = value
 
 
+PARTS = 2
+
+
 def order_kernel(plan, *refs):
     n_dp = plan.n_dp
-    parts, (attn, exp, rows, rows_a, rows_e) = refs[:n_dp], refs[n_dp:]
+    parts, (attn, exp, rows, rows_a, rows_e, attn_v, exp_v, sems) = refs[:n_dp], refs[n_dp:]
     me = lax.axis_index("dp")
     for i, part in enumerate(parts):
-        owner = (2 * (i % plan.chips) + i // plan.chips) ^ me
+        owner = (2 * (-i % plan.chips) + i // plan.chips) ^ me
         rows[pl.ds(pl.multiple_of(owner * plan.chunk, 16), plan.chunk), :] = part[...].astype(f32)
-    count_a, count_e = attn.shape[0], exp.shape[1]
-
-    def one(b):
+    count_e = exp.shape[1]
+
+    def lanes(b):
+        return pl.ds(b * LANES if isinstance(b, int) else pl.multiple_of(b * LANES, LANES), LANES)
+
+    def gather(b):
         places_a, places_e = plan.places(b)
-        span = pl.ds(b * LANES if isinstance(b, int) else pl.multiple_of(b * LANES, LANES), LANES)
         values = [rows[pl.ds(start, n_dp, stride=plan.chunk), :] for _, start in places_a]
         if plan.rows_a == 1:
-            attn[:, span] = jnp.concatenate(values, axis=0).astype(bf16)
+            attn_v[:, lanes(b)] = jnp.concatenate(values, axis=0).astype(bf16)
         else:
             for (group, _), value in zip(places_a, values):
                 start = (group // plan.rows_a) * n_dp * plan.rows_a + group % plan.rows_a
                 rows_a[pl.ds(start, n_dp, stride=plan.rows_a), :] = value
-            attn[:, span] = rows_a[...].astype(bf16)
+            attn_v[:, lanes(b)] = rows_a[...].astype(bf16)
         for r, start in places_e:
             rows_e[pl.ds(b * count_e + r, n_dp, stride=plan.rows_e), :] = rows[
                 pl.ds(start, n_dp, stride=plan.chunk), :
             ]
 
-    each(plan.blocks, one, n_dp <= 8)
-    for b in range(plan.blocks):
-        exp[0, :, pl.ds(b * LANES, LANES)] = rows_e[pl.ds(b * count_e, count_e), :].astype(bf16)
+    def finish(b):
+        exp_v[:, lanes(b)] = rows_e[pl.ds(b * count_e, count_e), :].astype(bf16)
+
+    copies = []
+    count = plan.blocks // PARTS
+    for part in range(PARTS):
+        each(count, lambda b: gather(part * count + b), n_dp <= 8)
+        each(count, lambda b: finish(part * count + b), True)
+        cols = pl.ds(part * count * LANES, count * LANES)
+        copies.append(pltpu.make_async_copy(attn_v.at[:, cols], attn.at[:, cols], sems.at[2 * part]))
+        copies.append(pltpu.make_async_copy(exp_v.at[:, cols], exp.at[0, :, cols], sems.at[2 * part + 1]))
+        for copy in copies[-2:]:
+            copy.start()
+    for copy in copies:
+        copy.wait()
 
 
 def put_in_order(plan, parts):
@@ -276,7 +284,11 @@
             ((plan.n_dp * plan.chunk, LANES), f32),
             ((count_a, LANES), f32),
             ((plan.blocks * count_e, LANES), f32),
+            ((count_a, plan.width), bf16),
+            ((count_e, plan.width), bf16),
         ],
+        out_space=pltpu.HBM,
+        copies=True,
     )
 
 
@@ -312,21 +324,20 @@
     sums = [
         full[c * chunk : (c + 1) * chunk] + got[c * chunk : (c + 1) * chunk].astype(f32) for c in range(chips)
     ]
-    got = [swap(sums[c].astype(bf16), "dp", 2 * c) for c in range(1, chips)]
+    got = [swap(sums[c].astype(bf16), "dp", 2 * c) for c in reversed(range(1, chips))]
     shared = ((plan.all_a + 16, LANES), bf16)
-    payload, g_exp = call(
-        lambda *refs: share_kernel(plan, *refs), [sums[0]] + got, [shared, ((plan.size_e, LANES), f32)]
+    payload, g_exp, both = call(
+        lambda *refs: share_kernel(plan, *refs),
+        [pack, swap(pack, "expert", 1), sums[0]] + got,
+        [shared, ((plan.size_e, LANES), f32), ((2,) + pack.shape, bf16)],
     )
     distance = 1
     while 2 * distance < n_expert:
-        other, far = swap(payload, "expert", distance), swap(pack, "expert", distance)
-        payload, pack = call(
-            lambda *refs: again_kernel(plan, distance, *refs),
-            [payload, other, pack, far],
-            [shared, ((8 * distance * plan.size_a, LANES), bf16)],
-        )
+        other = swap(payload, "expert", distance)
+        (payload,) = call(lambda *refs: again_kernel(plan, *refs), [payload, other], [shared])
         distance *= 2
-    other, far = swap(payload, "expert", distance), swap(pack, "expert", distance)
+    other = swap(payload, "expert", distance)
+    far = [swap(pack, "expert", q) for q in range(2, n_expert)]
     g_attn, square = call(
         lambda *refs: last_kernel(plan, *refs), [payload, other], [((plan.all_a, LANES), f32), ((n_dp, 8, LANES), f32)]
     )
@@ -334,7 +345,7 @@
     block_a, block_e = ((plan.size_a, LANES), f32), ((plan.size_e, LANES), f32)
     (mine,) = call(
         lambda *refs: rows_kernel(plan, limit, *refs),
-        [square, g_attn, g_exp, *state_e, pack, far],
+        [square, g_attn, g_exp, *state_e, both, *far],
         [((chunk, LANES), bf16)],
     )
     wa, ma, va, we, me, ve = call(
@@ -342,7 +353,7 @@
         [square, g_attn, g_exp, *state_a, *state_e],
         [block_a] * 3 + [block_e] * 3,
     )
-    near = [mine] + [swap(mine, "dp", 2 * c) for c in range(1, chips)]
+    near = [mine] + [swap(mine, "dp", 2 * c) for c in reversed(range(1, chips))]
     far = [swap(piece, "dp", 1) for piece in near]
     attn_full, expert_full = put_in_order(plan, near + far)
     new_a = [from_blocks(value, rows_a) for value in (wa, ma, va)]

time: 47.7 us -> 45 us (0.943)
  starting transfers between devices: 14.3 us -> 23.2 us
  blocking collectives: 7.21 us -> 0 us
  waiting for transfers between devices: 18.2 us -> 13.6 us
    ppermute x15 -> x16, waiting for transfers between devices: 18.2 us -> 8.78 us  [swap(): return lax.ppermute(value, axis, [(i, i ^ distance) for i in range(size)])]
    all_to_all x1 -> x0, blocking collectives: 7.21 us -> none  [body(): square = lax.all_to_all(square, 'dp', 0, 0, tiled=True)]
    ppermute x15 -> x16, starting transfers between devices: 14.3 us -> 19.5 us  [swap(): return lax.ppermute(value, axis, [(i, i ^ distance) for i in range(size)])]
    all_to_all x0 -> x1, waiting for transfers between devices: none -> 4.83 us  [body(): square = lax.all_to_all(square, 'dp', 0, 0, tiled=True)]
    all_to_all x0 -> x1, starting transfers between devices: none -> 3.72 us  [body(): square = lax.all_to_all(square, 'dp', 0, 0, tiled=True)]
  transfers between devices with their start and end apart: 15 -> 17, of which waited for: 8 -> 9; matrix products, arithmetic and copies ran while one was open for 0% -> 0% of each run, Pallas kernels for 2% -> 3%
where the time goes in v10:
time: 45 us; the launch traced here: 44.7 us
  starting transfers between devices  23.2 us (52%)
  waiting for transfers between devices  13.6 us (30%)
  Pallas kernels  7.1 us (16%)
  between operations  0.75 us (2%)
    ppermute x16, starting transfers between devices, swap(): return lax.ppermute(value, axis, [(i, i ^ distance) for i in range(size)])  19.5 us
    ppermute x16, waiting for transfers between devices, swap(): return lax.ppermute(value, axis, [(i, i ^ distance) for i in range(size)])  8.78 us
    pallas_call x7, Pallas kernels, call(): pl.pallas_call(kernel, in_specs=[pl.BlockSpec(memory_space=in_space)] * l...  7.1 us
    all_to_all x1, waiting for transfers between devices, body(): square = lax.all_to_all(square, 'dp', 0, 0, tiled=True)  4.83 us
    all_to_all x1, starting transfers between devices, body(): square = lax.all_to_all(square, 'dp', 0, 0, tiled=True)  3.72 us
  transfers between devices with their start and end apart: 17, of which 9 were waited for; matrix products, arithmetic and copies ran while one was open for 0% of the time, Pallas kernels for 3%

profile of v10, /device:TPU:0, one launch (start us, length us, event | category | flops | bytes accessed | tf_op | source)
XLA Modules:
  0.0 44.7 jit_solution(16297643221354756009)
XLA Ops:
  0.6 3.6 %shard_map.161 = (f32[2304,128]{1,0:T(8,128)S(1)}, bf16[1152,128]{1,0:T(8,128)(2,1)S(1)}, bf16[144,128]{1,0:T(8,128)(2,1)S(1)}) custom-call(bf16[32,256]{1,0:T(8,128)(2,1)} %bitcast.54, bf16[256,6144]{1,0:T(8,128)(2,1)} %refs_1_.1, bf16[16,128]{1,0:T(8,128)(2,1)} %bitcast.55, bf16[128,6144]{1,0:T(8,128)(2,1)} %bitcast.53, f32[48,128]{1,0:T(8,128)} %bitcast.47, ...), custom_call_target="tpu_custom_call" | custom-call | tf_op jit(solution)/shard_map/pallas_call | solution.py:64
  4.3 0.0 copy-start.2
  4.3 0.0 copy-start.3
  4.3 0.5 %collective-permute-start.1 = (bf16[1152,128]{1,0:T(8,128)(2,1)S(1)}, bf16[1152,128]{1,0:T(8,128)(2,1)S(1)}, u32[]{:S(2)}, u32[]{:S(2)}) collective-permute-start(bf16[1152,128]{1,0:T(8,128)(2,1)S(1)} %get-tuple-element.26), channel_id=1, source_target_pairs={{0,1},{1,0},{2,3},{3,2},{4,5},{5,4},{6,7},{7,6},{8,9},{9,8},{10,11... | collective-permute-start | bytes 884744 | tf_op jit(solution)/shard_map/ppermute | solution.py:297
  4.9 1.2 %collective-permute-done.1 = bf16[1152,128]{1,0:T(8,128)(2,1)S(1)} collective-permute-done((bf16[1152,128]{1,0:T(8,128)(2,1)S(1)}, bf16[1152,128]{1,0:T(8,128)(2,1)S(1)}, u32[]{:S(2)}, u32[]{:S(2)}) %collective-permute-start.1) | collective-permute-done | bytes 294944 | tf_op jit(solution)/shard_map/ppermute | solution.py:297
  6.1 0.1 add_convert_fusion
  6.1 3.9 %collective-permute-start.2 = (bf16[288,128]{1,0:T(8,128)(2,1)S(1)}, bf16[288,128]{1,0:T(8,128)(2,1)S(1)}, u32[]{:S(2)}, u32[]{:S(2)}) collective-permute-start(bf16[288,128]{1,0:T(8,128)(2,1)S(1)} %get-tuple-element.42), channel_id=1, source_target_pairs={{0,6},{1,7},{2,4},{3,5},{4,2},{5,3},{6,0},{7,1},{8,14},{9,15},{10,... | collective-permute-start | bytes 221192 | tf_op jit(solution)/shard_map/ppermute | solution.py:297
  10.0 0.5 %collective-permute-start.3 = (bf16[288,128]{1,0:T(8,128)(2,1)S(1)}, bf16[288,128]{1,0:T(8,128)(2,1)S(1)}, u32[]{:S(2)}, u32[]{:S(2)}) collective-permute-start(bf16[288,128]{1,0:T(8,128)(2,1)S(1)} %get-tuple-element.41), channel_id=1, source_target_pairs={{0,4},{1,5},{2,6},{3,7},{4,0},{5,1},{6,2},{7,3},{8,12},{9,13},{10,... | collective-permute-start | bytes 221192 | tf_op jit(solution)/shard_map/ppermute | solution.py:297
  10.5 0.1 collective-permute-start.4
  10.7 2.0 %collective-permute-start = (bf16[144,128]{1,0:T(8,128)(2,1)S(1)}, bf16[144,128]{1,0:T(8,128)(2,1)S(1)}, u32[]{:S(2)}, u32[]{:S(2)}) collective-permute-start(bf16[144,128]{1,0:T(8,128)(2,1)S(1)} %get-tuple-element.24.refs_0_), channel_id=1, source_target_pairs={{0,8},{8,0},{16,24},{24,16},{1,9},{9,1},{17,25},{25,17},{2,10},{10... | collective-permute-start | bytes 110600 | tf_op jit(solution)/shard_map/ppermute | solution.py:297
  12.6 2.0 %collective-permute-done.refs_1_ = bf16[144,128]{1,0:T(8,128)(2,1)S(1)} collective-permute-done((bf16[144,128]{1,0:T(8,128)(2,1)S(1)}, bf16[144,128]{1,0:T(8,128)(2,1)S(1)}, u32[]{:S(2)}, u32[]{:S(2)}) %collective-permute-start) | collective-permute-done | bytes 36896 | tf_op jit(solution)/shard_map/ppermute | solution.py:297
  14.6 0.3 collective-permute-done.4.refs_5_
  14.9 1.8 %collective-permute-start.5 = (bf16[208,128]{1,0:T(8,128)(2,1)S(1)}, bf16[208,128]{1,0:T(8,128)(2,1)S(1)}, u32[]{:S(2)}, u32[]{:S(2)}) collective-permute-start(bf16[208,128]{1,0:T(8,128)(2,1)S(1)} %get-tuple-element.27.refs_0_), channel_id=1, source_target_pairs={{0,8},{8,0},{16,24},{24,16},{1,9},{9,1},{17,25},{25,17},{2,10},{10... | collective-permute-start | bytes 159752 | tf_op jit(solution)/shard_map/ppermute | solution.py:297
  16.7 2.4 %collective-permute-done.5.refs_1_ = bf16[208,128]{1,0:T(8,128)(2,1)S(1)} collective-permute-done((bf16[208,128]{1,0:T(8,128)(2,1)S(1)}, bf16[208,128]{1,0:T(8,128)(2,1)S(1)}, u32[]{:S(2)}, u32[]{:S(2)}) %collective-permute-start.5) | collective-permute-done | bytes 53280 | tf_op jit(solution)/shard_map/ppermute | solution.py:297
  19.1 2.8 %collective-permute-start.6 = (bf16[208,128]{1,0:T(8,128)(2,1)S(1)}, bf16[208,128]{1,0:T(8,128)(2,1)S(1)}, u32[]{:S(2)}, u32[]{:S(2)}) collective-permute-start(bf16[208,128]{1,0:T(8,128)(2,1)S(1)} %shard_map.163.refs_0_), channel_id=1, source_target_pairs={{0,16},{8,24},{16,0},{24,8},{1,17},{9,25},{17,1},{25,9},{2,18},{10... | collective-permute-start | bytes 159752 | tf_op jit(solution)/shard_map/ppermute | solution.py:297
  22.0 0.2 collective-permute-start.7
  22.1 3.8 %collective-permute-start.8 = (bf16[144,128]{1,0:T(8,128)(2,1)S(1)}, bf16[144,128]{1,0:T(8,128)(2,1)S(1)}, u32[]{:S(2)}, u32[]{:S(2)}) collective-permute-start(bf16[144,128]{1,0:T(8,128)(2,1)S(1)} %get-tuple-element.24.refs_0_), channel_id=1, source_target_pairs={{0,24},{8,16},{16,8},{24,0},{1,25},{9,17},{17,9},{25,1},{2,26},{10... | collective-permute-start | bytes 110600 | tf_op jit(solution)/shard_map/ppermute | solution.py:297
  25.9 0.7 %shard_map.164 = (f32[192,128]{1,0:T(8,128)S(1)}, f32[8,8,128]{2,1,0:T(8,128)}) custom-call(bf16[208,128]{1,0:T(8,128)(2,1)S(1)} %shard_map.163.refs_0_, bf16[208,128]{1,0:T(8,128)(2,1)S(1)} %collective-permute-done.6.refs_1_), custom_call_target="tpu_custom_call" | custom-call | tf_op jit(solution)/shard_map/pallas_call | solution.py:64
  26.5 3.7 %all-to-all-start = ((f32[8,8,128]{2,1,0:T(8,128)}), f32[8,8,128]{2,1,0:T(8,128)S(1)}, u32[]{:S(2)}, u32[]{:S(2)}) async-start(f32[8,8,128]{2,1,0:T(8,128)} %get-tuple-element.28), calls=%async_computation | async-start | bytes 65536 | tf_op jit(solution)/shard_map/all_to_all | solution.py:344
  30.3 4.8 %all-to-all-done.refs_0_ = f32[8,8,128]{2,1,0:T(8,128)S(1)} async-done(((f32[8,8,128]{2,1,0:T(8,128)}), f32[8,8,128]{2,1,0:T(8,128)S(1)}, u32[]{:S(2)}, u32[]{:S(2)}) %all-to-all-start) | async-done | bytes 32800 | tf_op jit(solution)/shard_map/all_to_all | solution.py:344
  35.1 0.3 shard_map.166.refs_0_
  35.4 0.6 %collective-permute-start.9 = (bf16[288,128]{1,0:T(8,128)(2,1)S(1)}, bf16[288,128]{1,0:T(8,128)(2,1)S(1)}, u32[]{:S(2)}, u32[]{:S(2)}) collective-permute-start(bf16[288,128]{1,0:T(8,128)(2,1)S(1)} %shard_map.166.refs_0_), channel_id=1, source_target_pairs={{0,6},{1,7},{2,4},{3,5},{4,2},{5,3},{6,0},{7,1},{8,14},{9,15},{10,... | collective-permute-start | bytes 221192 | tf_op jit(solution)/shard_map/ppermute | solution.py:297
  36.0 1.5 %collective-permute-start.10 = (bf16[288,128]{1,0:T(8,128)(2,1)S(1)}, bf16[288,128]{1,0:T(8,128)(2,1)S(1)}, u32[]{:S(2)}, u32[]{:S(2)}) collective-permute-start(bf16[288,128]{1,0:T(8,128)(2,1)S(1)} %shard_map.166.refs_0_), channel_id=1, source_target_pairs={{0,4},{1,5},{2,6},{3,7},{4,0},{5,1},{6,2},{7,3},{8,12},{9,13},{10,... | collective-permute-start | bytes 221192 | tf_op jit(solution)/shard_map/ppermute | solution.py:297
  37.5 1.5 %collective-permute-start.11 = (bf16[288,128]{1,0:T(8,128)(2,1)S(1)}, bf16[288,128]{1,0:T(8,128)(2,1)S(1)}, u32[]{:S(2)}, u32[]{:S(2)}) collective-permute-start(bf16[288,128]{1,0:T(8,128)(2,1)S(1)} %shard_map.166.refs_0_), channel_id=1, source_target_pairs={{0,2},{1,3},{2,0},{3,1},{4,6},{5,7},{6,4},{7,5},{8,10},{9,11},{10,... | collective-permute-start | bytes 221192 | tf_op jit(solution)/shard_map/ppermute | solution.py:297
  39.0 2.2 %collective-permute-done.9.refs_1_ = bf16[288,128]{1,0:T(8,128)(2,1)S(1)} collective-permute-done((bf16[288,128]{1,0:T(8,128)(2,1)S(1)}, bf16[288,128]{1,0:T(8,128)(2,1)S(1)}, u32[]{:S(2)}, u32[]{:S(2)}) %collective-permute-start.9) | collective-permute-done | bytes 73760 | tf_op jit(solution)/shard_map/ppermute | solution.py:297
  41.2 0.4 collective-permute-done.10.refs_2_
  41.5 0.1 collective-permute-start.14
  41.7 0.2 collective-permute-done.11.refs_3_
  41.8 0.2 collective-permute-start.15
  42.1 0.9 %shard_map.165 = (f32[48,128]{1,0:T(8,128)}, f32[48,128]{1,0:T(8,128)}, f32[48,128]{1,0:T(8,128)}, f32[96,128]{1,0:T(8,128)}, f32[96,128]{1,0:T(8,128)}, /*index=5*/f32[96,128]{1,0:T(8,128)}) custom-call(f32[8,8,128]{2,1,0:T(8,128)S(1)} %all-to-all-done.refs_0_, f32[192,128]{1,0:T(8,128)S(1)} %get-tuple-element.29.refs_1_, ...), custom_call_target="tpu_custom_call" | custom-call | tf_op jit(solution)/shard_map/pallas_call | solution.py:64
  42.9 0.2 collective-permute-done.15.refs_7_
  43.1 1.6 %shard_map.167 = (bf16[32,6144]{1,0:T(8,128)(2,1)}, bf16[1,16,6144]{2,1,0:T(8,128)(2,1)}) custom-call(bf16[288,128]{1,0:T(8,128)(2,1)S(1)} %shard_map.166.refs_0_, bf16[288,128]{1,0:T(8,128)(2,1)S(1)} %collective-permute-done.9.refs_1_, bf16[288,128]{1,0:T(8,128)(2,1)S(1)} %collective-permute-done.10.refs_2_, ...), custom_call_target="tpu_custom_call" | custom-call | tf_op jit(solution)/shard_map/pallas_call | solution.py:64
  (22 shorter events, 0.1 us)
Async XLA Ops:
  4.3 30.8 %copy-start = (f32[1,2,6144]{2,1,0:T(2,128)S(1)}, f32[1,2,6144]{2,1,0:T(2,128)}, u32[]{:S(2)}) copy-start(f32[1,2,6144]{2,1,0:T(2,128)} %param.17) | copy-start | bytes 147460
  4.3 30.8 %copy-start.1 = (f32[1,2,6144]{2,1,0:T(2,128)S(1)}, f32[1,2,6144]{2,1,0:T(2,128)}, u32[]{:S(2)}) copy-start(f32[1,2,6144]{2,1,0:T(2,128)} %param.18) | copy-start | bytes 147460
  4.3 30.8 %copy-start.2 = (f32[1,2,6144]{2,1,0:T(2,128)S(1)}, f32[1,2,6144]{2,1,0:T(2,128)}, u32[]{:S(2)}) copy-start(f32[1,2,6144]{2,1,0:T(2,128)} %param.19) | copy-start | bytes 147460
  4.3 37.7 %copy-start.3 = (f32[1,6144]{1,0:T(1,128)S(1)}, f32[1,6144]{1,0:T(1,128)}, u32[]{:S(2)}) copy-start(f32[1,6144]{1,0:T(1,128)} %param.14) | copy-start | bytes 73732
  4.3 37.7 %copy-start.4 = (f32[1,6144]{1,0:T(1,128)S(1)}, f32[1,6144]{1,0:T(1,128)}, u32[]{:S(2)}) copy-start(f32[1,6144]{1,0:T(1,128)} %param.15) | copy-start | bytes 73732
  4.3 37.7 %copy-start.5 = (f32[1,6144]{1,0:T(1,128)S(1)}, f32[1,6144]{1,0:T(1,128)}, u32[]{:S(2)}) copy-start(f32[1,6144]{1,0:T(1,128)} %param.16) | copy-start | bytes 73732
  4.3 1.7 %collective-permute-start.1 = (bf16[1152,128]{1,0:T(8,128)(2,1)S(1)}, bf16[1152,128]{1,0:T(8,128)(2,1)S(1)}, u32[]{:S(2)}, u32[]{:S(2)}) collective-permute-start(bf16[1152,128]{1,0:T(8,128)(2,1)S(1)} %get-tuple-element.26), channel_id=1, source_target_pairs={{0,1},{1,0},{2,3},{3,2},{4,5},{5,4},{6,7},{7,6},{8,9},{9,8},{10,11... | collective-permute-start | bytes 884744 | tf_op jit(solution)/shard_map/ppermute | solution.py:297
  6.1 8.5 %collective-permute-start.2 = (bf16[288,128]{1,0:T(8,128)(2,1)S(1)}, bf16[288,128]{1,0:T(8,128)(2,1)S(1)}, u32[]{:S(2)}, u32[]{:S(2)}) collective-permute-start(bf16[288,128]{1,0:T(8,128)(2,1)S(1)} %get-tuple-element.42), channel_id=1, source_target_pairs={{0,6},{1,7},{2,4},{3,5},{4,2},{5,3},{6,0},{7,1},{8,14},{9,15},{10,... | collective-permute-start | bytes 221192 | tf_op jit(solution)/shard_map/ppermute | solution.py:297
  10.0 4.6 %collective-permute-start.3 = (bf16[288,128]{1,0:T(8,128)(2,1)S(1)}, bf16[288,128]{1,0:T(8,128)(2,1)S(1)}, u32[]{:S(2)}, u32[]{:S(2)}) collective-permute-start(bf16[288,128]{1,0:T(8,128)(2,1)S(1)} %get-tuple-element.41), channel_id=1, source_target_pairs={{0,4},{1,5},{2,6},{3,7},{4,0},{5,1},{6,2},{7,3},{8,12},{9,13},{10,... | collective-permute-start | bytes 221192 | tf_op jit(solution)/shard_map/ppermute | solution.py:297
  10.5 4.4 %collective-permute-start.4 = (bf16[288,128]{1,0:T(8,128)(2,1)S(1)}, bf16[288,128]{1,0:T(8,128)(2,1)S(1)}, u32[]{:S(2)}, u32[]{:S(2)}) collective-permute-start(bf16[288,128]{1,0:T(8,128)(2,1)S(1)} %get-tuple-element.40), channel_id=1, source_target_pairs={{0,2},{1,3},{2,0},{3,1},{4,6},{5,7},{6,4},{7,5},{8,10},{9,11},{10,... | collective-permute-start | bytes 221192 | tf_op jit(solution)/shard_map/ppermute | solution.py:297
  10.7 4.0 %collective-permute-start = (bf16[144,128]{1,0:T(8,128)(2,1)S(1)}, bf16[144,128]{1,0:T(8,128)(2,1)S(1)}, u32[]{:S(2)}, u32[]{:S(2)}) collective-permute-start(bf16[144,128]{1,0:T(8,128)(2,1)S(1)} %get-tuple-element.24.refs_0_), channel_id=1, source_target_pairs={{0,8},{8,0},{16,24},{24,16},{1,9},{9,1},{17,25},{25,17},{2,10},{10... | collective-permute-start | bytes 110600 | tf_op jit(solution)/shard_map/ppermute | solution.py:297
  14.9 4.2 %collective-permute-start.5 = (bf16[208,128]{1,0:T(8,128)(2,1)S(1)}, bf16[208,128]{1,0:T(8,128)(2,1)S(1)}, u32[]{:S(2)}, u32[]{:S(2)}) collective-permute-start(bf16[208,128]{1,0:T(8,128)(2,1)S(1)} %get-tuple-element.27.refs_0_), channel_id=1, source_target_pairs={{0,8},{8,0},{16,24},{24,16},{1,9},{9,1},{17,25},{25,17},{2,10},{10... | collective-permute-start | bytes 159752 | tf_op jit(solution)/shard_map/ppermute | solution.py:297
  19.1 6.8 %collective-permute-start.6 = (bf16[208,128]{1,0:T(8,128)(2,1)S(1)}, bf16[208,128]{1,0:T(8,128)(2,1)S(1)}, u32[]{:S(2)}, u32[]{:S(2)}) collective-permute-start(bf16[208,128]{1,0:T(8,128)(2,1)S(1)} %shard_map.163.refs_0_), channel_id=1, source_target_pairs={{0,16},{8,24},{16,0},{24,8},{1,17},{9,25},{17,1},{25,9},{2,18},{10... | collective-permute-start | bytes 159752 | tf_op jit(solution)/shard_map/ppermute | solution.py:297
  22.0 8.3 %collective-permute-start.7 = (bf16[144,128]{1,0:T(8,128)(2,1)S(1)}, bf16[144,128]{1,0:T(8,128)(2,1)S(1)}, u32[]{:S(2)}, u32[]{:S(2)}) collective-permute-start(bf16[144,128]{1,0:T(8,128)(2,1)S(1)} %get-tuple-element.24.refs_0_), channel_id=1, source_target_pairs={{0,16},{8,24},{16,0},{24,8},{1,17},{9,25},{17,1},{25,9},{2,18},{10... | collective-permute-start | bytes 110600 | tf_op jit(solution)/shard_map/ppermute | solution.py:297
  22.1 8.1 %collective-permute-start.8 = (bf16[144,128]{1,0:T(8,128)(2,1)S(1)}, bf16[144,128]{1,0:T(8,128)(2,1)S(1)}, u32[]{:S(2)}, u32[]{:S(2)}) collective-permute-start(bf16[144,128]{1,0:T(8,128)(2,1)S(1)} %get-tuple-element.24.refs_0_), channel_id=1, source_target_pairs={{0,24},{8,16},{16,8},{24,0},{1,25},{9,17},{17,9},{25,1},{2,26},{10... | collective-permute-start | bytes 110600 | tf_op jit(solution)/shard_map/ppermute | solution.py:297
  26.5 8.6 %all-to-all-start = ((f32[8,8,128]{2,1,0:T(8,128)}), f32[8,8,128]{2,1,0:T(8,128)S(1)}, u32[]{:S(2)}, u32[]{:S(2)}) async-start(f32[8,8,128]{2,1,0:T(8,128)} %get-tuple-element.28), calls=%async_computation | async-start | bytes 65536 | tf_op jit(solution)/shard_map/all_to_all | solution.py:344
  35.4 5.8 %collective-permute-start.9 = (bf16[288,128]{1,0:T(8,128)(2,1)S(1)}, bf16[288,128]{1,0:T(8,128)(2,1)S(1)}, u32[]{:S(2)}, u32[]{:S(2)}) collective-permute-start(bf16[288,128]{1,0:T(8,128)(2,1)S(1)} %shard_map.166.refs_0_), channel_id=1, source_target_pairs={{0,6},{1,7},{2,4},{3,5},{4,2},{5,3},{6,0},{7,1},{8,14},{9,15},{10,... | collective-permute-start | bytes 221192 | tf_op jit(solution)/shard_map/ppermute | solution.py:297
  36.0 5.5 %collective-permute-start.10 = (bf16[288,128]{1,0:T(8,128)(2,1)S(1)}, bf16[288,128]{1,0:T(8,128)(2,1)S(1)}, u32[]{:S(2)}, u32[]{:S(2)}) collective-permute-start(bf16[288,128]{1,0:T(8,128)(2,1)S(1)} %shard_map.166.refs_0_), channel_id=1, source_target_pairs={{0,4},{1,5},{2,6},{3,7},{4,0},{5,1},{6,2},{7,3},{8,12},{9,13},{10,... | collective-permute-start | bytes 221192 | tf_op jit(solution)/shard_map/ppermute | solution.py:297
  37.5 4.4 %collective-permute-start.11 = (bf16[288,128]{1,0:T(8,128)(2,1)S(1)}, bf16[288,128]{1,0:T(8,128)(2,1)S(1)}, u32[]{:S(2)}, u32[]{:S(2)}) collective-permute-start(bf16[288,128]{1,0:T(8,128)(2,1)S(1)} %shard_map.166.refs_0_), channel_id=1, source_target_pairs={{0,2},{1,3},{2,0},{3,1},{4,6},{5,7},{6,4},{7,5},{8,10},{9,11},{10,... | collective-permute-start | bytes 221192 | tf_op jit(solution)/shard_map/ppermute | solution.py:297
  39.0 4.0 %collective-permute-start.12 = (bf16[288,128]{1,0:T(8,128)(2,1)S(1)}, bf16[288,128]{1,0:T(8,128)(2,1)S(1)}, u32[]{:S(2)}, u32[]{:S(2)}) collective-permute-start(bf16[288,128]{1,0:T(8,128)(2,1)S(1)} %shard_map.166.refs_0_), channel_id=1, source_target_pairs={{0,1},{1,0},{2,3},{3,2},{4,5},{5,4},{6,7},{7,6},{8,9},{9,8},{10,11... | collective-permute-start | bytes 221192 | tf_op jit(solution)/shard_map/ppermute | solution.py:297
  41.2 1.7 %collective-permute-start.13 = (bf16[288,128]{1,0:T(8,128)(2,1)S(1)}, bf16[288,128]{1,0:T(8,128)(2,1)S(1)}, u32[]{:S(2)}, u32[]{:S(2)}) collective-permute-start(bf16[288,128]{1,0:T(8,128)(2,1)S(1)} %collective-permute-done.9.refs_1_), channel_id=1, source_target_pairs={{0,1},{1,0},{2,3},{3,2},{4,5},{5,4},{6,7},{7,6},{8,9},{9,8},{10,11... | collective-permute-start | bytes 221192 | tf_op jit(solution)/shard_map/ppermute | solution.py:297
  41.5 1.4 %collective-permute-start.14 = (bf16[288,128]{1,0:T(8,128)(2,1)S(1)}, bf16[288,128]{1,0:T(8,128)(2,1)S(1)}, u32[]{:S(2)}, u32[]{:S(2)}) collective-permute-start(bf16[288,128]{1,0:T(8,128)(2,1)S(1)} %collective-permute-done.10.refs_2_), channel_id=1, source_target_pairs={{0,1},{1,0},{2,3},{3,2},{4,5},{5,4},{6,7},{7,6},{8,9},{9,8},{10,11... | collective-permute-start | bytes 221192 | tf_op jit(solution)/shard_map/ppermute | solution.py:297
  41.8 1.3 %collective-permute-start.15 = (bf16[288,128]{1,0:T(8,128)(2,1)S(1)}, bf16[288,128]{1,0:T(8,128)(2,1)S(1)}, u32[]{:S(2)}, u32[]{:S(2)}) collective-permute-start(bf16[288,128]{1,0:T(8,128)(2,1)S(1)} %collective-permute-done.11.refs_3_), channel_id=1, source_target_pairs={{0,1},{1,0},{2,3},{3,2},{4,5},{5,4},{6,7},{7,6},{8,9},{9,8},{10,11... | collective-permute-start | bytes 221192 | tf_op jit(solution)/shard_map/ppermute | solution.py:297

commit v11 on v10

--- a/solution.py
+++ b/solution.py
@@ -26,6 +26,10 @@
     update = moment_new / bias_first / (jnp.sqrt(second_new / bias_second) + adam_eps)
     weight_new = weight - learn_rate * (update + decay_rate * weight)
     return (weight_new, moment_new, second_new)
+
+
+def role_of(chip, core, expert):
+    return core ^ ((chip ^ expert ^ (expert // 2)) % 2)
 
 
 class Plan:
@@ -106,21 +110,27 @@
     for copy in small + big + extra:
         copy.start()
 
-    me = lax.axis_index("dp")
-
-    def pick(groups, per_owner, count):
+    me, me_ex = lax.axis_index("dp"), lax.axis_index("expert")
+    my_role = role_of(me // 2, me % 2, me_ex)
+
+    def pick(groups, per_owner, count, expert):
         shape = (groups * plan.n_dp, count)
         row = lax.broadcasted_iota(jnp.int32, shape, 0)
         col = lax.broadcasted_iota(jnp.int32, shape, 1)
         group, place = row // plan.n_dp, row % plan.n_dp
-        owner = (2 * (place % plan.chips) + place // plan.chips) ^ me
-        want = ((group // per_owner) * plan.n_dp + owner) * per_owner + group % per_owner
+        chip, role = (place % plan.chips) ^ (me // 2), (place // plan.chips) ^ my_role
+        if expert is None:
+            expert, base = group // per_owner, (group // per_owner) * plan.n_dp
+        else:
+            base = 0
+        owner = 2 * chip + role_of(chip, role, expert)
+        want = (base + owner) * per_owner + group % per_owner
         return (want == col).astype(bf16)
 
     for copy in small:
         copy.wait()
-    left_a = dot(pick(plan.n_expert * plan.rows_a, plan.rows_a, act_a.shape[0]), act_a_v[...]).astype(bf16)
-    left_e = dot(pick(plan.rows_e, plan.rows_e, act_e.shape[0]), act_e_v[...]).astype(bf16)
+    left_a = dot(pick(plan.n_expert * plan.rows_a, plan.rows_a, act_a.shape[0], None), act_a_v[...]).astype(bf16)
+    left_e = dot(pick(plan.rows_e, plan.rows_e, act_e.shape[0], me_ex), act_e_v[...]).astype(bf16)
     n_dp = plan.n_dp
     for t in range(STEPS):
         cols = pl.ds(t * tile, tile)
@@ -194,17 +204,20 @@
 def last_kernel(plan, mine, other, g_attn, square):
     attn, partial = pair_sum(plan, mine, other)
     g_attn[...] = attn
-    square[...] = jnp.broadcast_to((partial + by_eights(attn * attn))[None], square.shape)
-
-
-def clip_factor(limit, square):
-    norm = jnp.sqrt(jnp.sum(jnp.sum(square[...], axis=0), keepdims=True))
+    square[...] = partial + by_eights(attn * attn)
+
+
+def clip_factor(limit, squares):
+    values = [squares[-i % len(squares)][...] for i in range(len(squares))]
+    while len(values) > 1:
+        values = [values[i] + values[i + 1] for i in range(0, len(values), 2)]
+    norm = jnp.sqrt(jnp.sum(values[0], keepdims=True))
     return jnp.minimum(1.0, limit / (norm + 1e-06))
 
 
-def rows_kernel(plan, limit, square, g_attn, g_exp, we, me, ve, both, *refs):
-    far, mine = refs[:-1], refs[-1]
-    factor = clip_factor(limit, square)
+def rows_kernel(plan, limit, *refs):
+    factor = clip_factor(limit, refs[: plan.chips])
+    g_attn, g_exp, we, me, ve, both, *far, mine = refs[plan.chips :]
     size, place = plan.size_a, lax.axis_index("expert")
     for q, states in enumerate([both.at[0], both.at[1], *far]):
         rows = pl.ds(pl.multiple_of((place ^ q) * size, 16), size)
@@ -216,9 +229,9 @@
 
 
 def own_kernel(plan, limit, *refs):
-    square, g_attn, g_exp = refs[:3]
-    state, new = refs[3:9], refs[9:]
-    factor = clip_factor(limit, square)
+    factor = clip_factor(limit, refs[: plan.chips])
+    g_attn, g_exp = refs[plan.chips : plan.chips + 2]
+    state, new = refs[plan.chips + 2 : plan.chips + 8], refs[plan.chips + 8 :]
     rows = pl.ds(pl.multiple_of(lax.axis_index("expert") * plan.size_a, 16), plan.size_a)
     for b, grad in enumerate((g_attn[rows, :], g_exp[...])):
         values = adamw(grad, *[ref[...] for ref in state[3 * b : 3 * b + 3]], factor)
@@ -233,9 +246,15 @@
     n_dp = plan.n_dp
     parts, (attn, exp, rows, rows_a, rows_e, attn_v, exp_v, sems) = refs[:n_dp], refs[n_dp:]
     me = lax.axis_index("dp")
+    me_ex = lax.axis_index("expert")
+    my_role = role_of(me // 2, me % 2, me_ex)
     for i, part in enumerate(parts):
-        owner = (2 * (-i % plan.chips) + i // plan.chips) ^ me
-        rows[pl.ds(pl.multiple_of(owner * plan.chunk, 16), plan.chunk), :] = part[...].astype(f32)
+        chip, role = (-i % plan.chips) ^ (me // 2), (i // plan.chips) ^ my_role
+        blocks = [(e, e * plan.size_a, plan.size_a) for e in range(plan.n_expert)]
+        for expert, start, size in blocks + [(me_ex, plan.all_a, plan.size_e)]:
+            owner = 2 * chip + role_of(chip, role, expert)
+            to = pl.multiple_of(owner * plan.chunk + start, 16)
+            rows[pl.ds(to, size), :] = part[pl.ds(start, size), :].astype(f32)
     count_e = exp.shape[1]
 
     def lanes(b):
@@ -292,9 +311,19 @@
     )
 
 
-def swap(value, axis, distance):
-    size = lax.axis_size(axis)
-    return lax.ppermute(value, axis, [(i, i ^ distance) for i in range(size)])
+def swap(value, chips=0, experts=0):
+    n_expert, n_dp = lax.axis_size("expert"), lax.axis_size("dp")
+    pairs = []
+    for e in range(n_expert):
+        for j in range(n_dp):
+            role = role_of(j // 2, j % 2, e)
+            chip, expert = (j // 2) ^ chips, e ^ experts
+            pairs.append((e * n_dp + j, expert * n_dp + 2 * chip + role_of(chip, role, expert)))
+    return lax.ppermute(value, ("expert", "dp"), pairs)
+
+
+def swap_cores(value):
+    return lax.ppermute(value, "dp", [(i, i ^ 1) for i in range(lax.axis_size("dp"))])
 
 
 def to_blocks(value):
@@ -320,41 +349,42 @@
 
     held = [pltpu.with_memory_space_constraint(x, pltpu.HBM) for x in (act_attn.T, dy_attn, act_exp[0].T, dy_exp[0])]
     full, send, pack = make_terms(plan, *held, *[pltpu.with_memory_space_constraint(x, pltpu.HBM) for x in state_a])
-    got = swap(send, "dp", 1)
+    got = swap_cores(send)
     sums = [
         full[c * chunk : (c + 1) * chunk] + got[c * chunk : (c + 1) * chunk].astype(f32) for c in range(chips)
     ]
-    got = [swap(sums[c].astype(bf16), "dp", 2 * c) for c in reversed(range(1, chips))]
+    got = [swap(sums[c].astype(bf16), chips=c) for c in reversed(range(1, chips))]
     shared = ((plan.all_a + 16, LANES), bf16)
     payload, g_exp, both = call(
         lambda *refs: share_kernel(plan, *refs),
-        [pack, swap(pack, "expert", 1), sums[0]] + got,
+        [pack, swap(pack, experts=1), sums[0]] + got,
         [shared, ((plan.size_e, LANES), f32), ((2,) + pack.shape, bf16)],
     )
     distance = 1
     while 2 * distance < n_expert:
-        other = swap(payload, "expert", distance)
+        other = swap(payload, experts=distance)
         (payload,) = call(lambda *refs: again_kernel(plan, *refs), [payload, other], [shared])
         distance *= 2
-    other = swap(payload, "expert", distance)
-    far = [swap(pack, "expert", q) for q in range(2, n_expert)]
+    other = swap(payload, experts=distance)
+    far = [swap(pack, experts=q) for q in range(2, n_expert)]
     g_attn, square = call(
-        lambda *refs: last_kernel(plan, *refs), [payload, other], [((plan.all_a, LANES), f32), ((n_dp, 8, LANES), f32)]
-    )
-    square = lax.all_to_all(square, "dp", 0, 0, tiled=True)
+        lambda *refs: last_kernel(plan, *refs), [payload, other], [((plan.all_a, LANES), f32), ((8, LANES), f32)]
+    )
+    square = square + swap_cores(square)
+    squares = [square] + [swap(square, chips=c) for c in reversed(range(1, chips))]
     block_a, block_e = ((plan.size_a, LANES), f32), ((plan.size_e, LANES), f32)
     (mine,) = call(
         lambda *refs: rows_kernel(plan, limit, *refs),
-        [square, g_attn, g_exp, *state_e, both, *far],
+        [*squares, g_attn, g_exp, *state_e, both, *far],
         [((chunk, LANES), bf16)],
     )
     wa, ma, va, we, me, ve = call(
         lambda *refs: own_kernel(plan, limit, *refs),
-        [square, g_attn, g_exp, *state_a, *state_e],
+        [*squares, g_attn, g_exp, *state_a, *state_e],
         [block_a] * 3 + [block_e] * 3,
     )
-    near = [mine] + [swap(mine, "dp", 2 * c) for c in reversed(range(1, chips))]
-    far = [swap(piece, "dp", 1) for piece in near]
+    near = [mine] + [swap(mine, chips=c) for c in reversed(range(1, chips))]
+    far = [swap_cores(piece) for piece in near]
     attn_full, expert_full = put_in_order(plan, near + far)
     new_a = [from_blocks(value, rows_a) for value in (wa, ma, va)]
     new_e = [from_blocks(value, rows_e)[None] for value in (we, me, ve)]

time: 45 us -> 42.6 us (0.947)
  starting transfers between devices: 23.2 us -> 21.1 us
  Pallas kernels: 7.1 us -> 6.49 us
    ppermute x16 -> x20, waiting for transfers between devices: 8.78 us -> 14 us  [the longest x14 11.6 us: swap(): return lax.ppermute(value, ('expert', 'dp'), pairs)]
    all_to_all x1 -> x0, waiting for transfers between devices: 4.83 us -> none  [body(): square = lax.all_to_all(square, 'dp', 0, 0, tiled=True)]
    all_to_all x1 -> x0, starting transfers between devices: 3.72 us -> none  [body(): square = lax.all_to_all(square, 'dp', 0, 0, tiled=True)]
    ppermute x16 -> x20, starting transfers between devices: 19.5 us -> 21.1 us  [the longest x14 20 us: swap(): return lax.ppermute(value, ('expert', 'dp'), pairs)]
    pallas_call x7, Pallas kernels: 7.1 us -> 6.49 us  [call(): pl.pallas_call(kernel, in_specs=[pl.BlockSpec(memory_space=in_space)] * l...]
  transfers between devices with their start and end apart: 17 -> 20, of which waited for: 9 -> 10; matrix products, arithmetic and copies ran while one was open for 0% -> 0% of each run, Pallas kernels for 3% -> 2%
where the time goes in v11:
time: 42.6 us; the launch traced here: 42.4 us
  starting transfers between devices  21.1 us (50%)
  waiting for transfers between devices  14 us (33%)
  Pallas kernels  6.49 us (15%)
  between operations  0.75 us (2%)
    ppermute x14, starting transfers between devices, swap(): return lax.ppermute(value, ('expert', 'dp'), pairs)  20 us
    ppermute x14, waiting for transfers between devices, swap(): return lax.ppermute(value, ('expert', 'dp'), pairs)  11.6 us
    pallas_call x7, Pallas kernels, call(): pl.pallas_call(kernel, in_specs=[pl.BlockSpec(memory_space=in_space)] * l...  6.49 us
    ppermute x6, waiting for transfers between devices, swap_cores(): lax.ppermute(value, 'dp', [(i, i ^ 1) for i in range(lax.axis_size('dp'))])  2.41 us
    ppermute x6, starting transfers between devices, swap_cores(): lax.ppermute(value, 'dp', [(i, i ^ 1) for i in range(lax.axis_size('dp'))])  1.1 us
  transfers between devices with their start and end apart: 20, of which 10 were waited for; matrix products, arithmetic and copies ran while one was open for 0% of the time, Pallas kernels for 2%

profile of v11, /device:TPU:0, one launch (start us, length us, event | category | flops | bytes accessed | tf_op | source)
XLA Modules:
  0.0 42.4 jit_solution(15136489357350297320)
XLA Ops:
  0.6 3.6 %shard_map.161 = (f32[2304,128]{1,0:T(8,128)S(1)}, bf16[1152,128]{1,0:T(8,128)(2,1)S(1)}, bf16[144,128]{1,0:T(8,128)(2,1)S(1)}) custom-call(bf16[32,256]{1,0:T(8,128)(2,1)} %bitcast.54, bf16[256,6144]{1,0:T(8,128)(2,1)} %refs_1_.1, bf16[16,128]{1,0:T(8,128)(2,1)} %bitcast.55, bf16[128,6144]{1,0:T(8,128)(2,1)} %bitcast.53, f32[48,128]{1,0:T(8,128)} %bitcast.47, ...), custom_call_target="tpu_custom_call" | custom-call | tf_op jit(solution)/shard_map/pallas_call | solution.py:68
  4.3 0.5 %collective-permute-start.1 = (bf16[1152,128]{1,0:T(8,128)(2,1)S(1)}, bf16[1152,128]{1,0:T(8,128)(2,1)S(1)}, u32[]{:S(2)}, u32[]{:S(2)}) collective-permute-start(bf16[1152,128]{1,0:T(8,128)(2,1)S(1)} %get-tuple-element.26), channel_id=1, source_target_pairs={{0,1},{1,0},{2,3},{3,2},{4,5},{5,4},{6,7},{7,6},{8,9},{9,8},{10,11... | collective-permute-start | bytes 884744 | tf_op jit(solution)/shard_map/ppermute | solution.py:326
  4.9 1.2 %collective-permute-done.1 = bf16[1152,128]{1,0:T(8,128)(2,1)S(1)} collective-permute-done((bf16[1152,128]{1,0:T(8,128)(2,1)S(1)}, bf16[1152,128]{1,0:T(8,128)(2,1)S(1)}, u32[]{:S(2)}, u32[]{:S(2)}) %collective-permute-start.1) | collective-permute-done | bytes 294944 | tf_op jit(solution)/shard_map/ppermute | solution.py:326
  6.1 0.1 add_convert_fusion
  6.1 3.6 %collective-permute-start.2 = (bf16[288,128]{1,0:T(8,128)(2,1)S(1)}, bf16[288,128]{1,0:T(8,128)(2,1)S(1)}, u32[]{:S(2)}, u32[]{:S(2)}) collective-permute-start(bf16[288,128]{1,0:T(8,128)(2,1)S(1)} %get-tuple-element.42), channel_id=1, source_target_pairs={{0,7},{1,6},{2,5},{3,4},{4,3},{5,2},{6,1},{7,0},{8,15},{9,14},{10,... | collective-permute-start | bytes 221192 | tf_op jit(solution)/shard_map/ppermute | solution.py:322
  9.8 0.5 %collective-permute-start.3 = (bf16[288,128]{1,0:T(8,128)(2,1)S(1)}, bf16[288,128]{1,0:T(8,128)(2,1)S(1)}, u32[]{:S(2)}, u32[]{:S(2)}) collective-permute-start(bf16[288,128]{1,0:T(8,128)(2,1)S(1)} %get-tuple-element.41), channel_id=1, source_target_pairs={{0,4},{1,5},{2,6},{3,7},{4,0},{5,1},{6,2},{7,3},{8,12},{9,13},{10,... | collective-permute-start | bytes 221192 | tf_op jit(solution)/shard_map/ppermute | solution.py:322
  10.3 1.8 %collective-permute-start = (bf16[144,128]{1,0:T(8,128)(2,1)S(1)}, bf16[144,128]{1,0:T(8,128)(2,1)S(1)}, u32[]{:S(2)}, u32[]{:S(2)}) collective-permute-start(bf16[144,128]{1,0:T(8,128)(2,1)S(1)} %get-tuple-element.24.refs_0_), channel_id=1, source_target_pairs={{0,9},{1,8},{2,11},{3,10},{4,13},{5,12},{6,15},{7,14},{8,1},{9,0},... | collective-permute-start | bytes 110600 | tf_op jit(solution)/shard_map/ppermute | solution.py:322
  12.1 1.6 %collective-permute-done.refs_1_ = bf16[144,128]{1,0:T(8,128)(2,1)S(1)} collective-permute-done((bf16[144,128]{1,0:T(8,128)(2,1)S(1)}, bf16[144,128]{1,0:T(8,128)(2,1)S(1)}, u32[]{:S(2)}, u32[]{:S(2)}) %collective-permute-start) | collective-permute-done | bytes 36896 | tf_op jit(solution)/shard_map/ppermute | solution.py:322
  13.8 0.5 %collective-permute-done.3.refs_4_ = bf16[288,128]{1,0:T(8,128)(2,1)S(1)} collective-permute-done((bf16[288,128]{1,0:T(8,128)(2,1)S(1)}, bf16[288,128]{1,0:T(8,128)(2,1)S(1)}, u32[]{:S(2)}, u32[]{:S(2)}) %collective-permute-start.3) | collective-permute-done | bytes 73760 | tf_op jit(solution)/shard_map/ppermute | solution.py:322
  14.3 0.3 collective-permute-done.4.refs_5_
  14.6 1.4 %collective-permute-start.5 = (bf16[208,128]{1,0:T(8,128)(2,1)S(1)}, bf16[208,128]{1,0:T(8,128)(2,1)S(1)}, u32[]{:S(2)}, u32[]{:S(2)}) collective-permute-start(bf16[208,128]{1,0:T(8,128)(2,1)S(1)} %get-tuple-element.27.refs_0_), channel_id=1, source_target_pairs={{0,9},{1,8},{2,11},{3,10},{4,13},{5,12},{6,15},{7,14},{8,1},{9,0},... | collective-permute-start | bytes 159752 | tf_op jit(solution)/shard_map/ppermute | solution.py:322
  16.0 2.5 %collective-permute-done.5.refs_1_ = bf16[208,128]{1,0:T(8,128)(2,1)S(1)} collective-permute-done((bf16[208,128]{1,0:T(8,128)(2,1)S(1)}, bf16[208,128]{1,0:T(8,128)(2,1)S(1)}, u32[]{:S(2)}, u32[]{:S(2)}) %collective-permute-start.5) | collective-permute-done | bytes 53280 | tf_op jit(solution)/shard_map/ppermute | solution.py:322
  18.6 2.4 %collective-permute-start.6 = (bf16[208,128]{1,0:T(8,128)(2,1)S(1)}, bf16[208,128]{1,0:T(8,128)(2,1)S(1)}, u32[]{:S(2)}, u32[]{:S(2)}) collective-permute-start(bf16[208,128]{1,0:T(8,128)(2,1)S(1)} %shard_map.163.refs_0_), channel_id=1, source_target_pairs={{0,17},{1,16},{2,19},{3,18},{4,21},{5,20},{6,23},{7,22},{8,25},{9,... | collective-permute-start | bytes 159752 | tf_op jit(solution)/shard_map/ppermute | solution.py:322
  21.0 0.3 collective-permute-start.11
  21.3 3.7 %collective-permute-start.12 = (bf16[144,128]{1,0:T(8,128)(2,1)S(1)}, bf16[144,128]{1,0:T(8,128)(2,1)S(1)}, u32[]{:S(2)}, u32[]{:S(2)}) collective-permute-start(bf16[144,128]{1,0:T(8,128)(2,1)S(1)} %get-tuple-element.24.refs_0_), channel_id=1, source_target_pairs={{0,24},{1,25},{2,26},{3,27},{4,28},{5,29},{6,30},{7,31},{8,16},{9,... | collective-permute-start | bytes 110600 | tf_op jit(solution)/shard_map/ppermute | solution.py:322
  25.0 0.1 collective-permute-start.7
  25.1 1.2 %collective-permute-done.7 = f32[8,128]{1,0:T(8,128)S(1)} collective-permute-done((f32[8,128]{1,0:T(8,128)S(1)}, f32[8,128]{1,0:T(8,128)S(1)}, u32[]{:S(2)}, u32[]{:S(2)}) %collective-permute-start.7) | collective-permute-done | bytes 4128 | tf_op jit(solution)/shard_map/ppermute | solution.py:326
  26.2 1.3 %collective-permute-start.10 = (f32[8,128]{1,0:T(8,128)S(1)}, f32[8,128]{1,0:T(8,128)S(1)}, u32[]{:S(2)}, u32[]{:S(2)}) collective-permute-start(f32[8,128]{1,0:T(8,128)S(1)} %add.19.refs_0_), channel_id=1, source_target_pairs={{0,3},{1,2},{2,1},{3,0},{4,7},{5,6},{6,5},{7,4},{8,11},{9,10},{10,... | collective-permute-start | bytes 12296 | tf_op jit(solution)/shard_map/ppermute | solution.py:322
  27.5 1.4 %collective-permute-start.8 = (f32[8,128]{1,0:T(8,128)S(1)}, f32[8,128]{1,0:T(8,128)S(1)}, u32[]{:S(2)}, u32[]{:S(2)}) collective-permute-start(f32[8,128]{1,0:T(8,128)S(1)} %add.19.refs_0_), channel_id=1, source_target_pairs={{0,7},{1,6},{2,5},{3,4},{4,3},{5,2},{6,1},{7,0},{8,15},{9,14},{10,... | collective-permute-start | bytes 12296 | tf_op jit(solution)/shard_map/ppermute | solution.py:322
  28.9 0.5 %collective-permute-start.9 = (f32[8,128]{1,0:T(8,128)S(1)}, f32[8,128]{1,0:T(8,128)S(1)}, u32[]{:S(2)}, u32[]{:S(2)}) collective-permute-start(f32[8,128]{1,0:T(8,128)S(1)} %add.19.refs_0_), channel_id=1, source_target_pairs={{0,4},{1,5},{2,6},{3,7},{4,0},{5,1},{6,2},{7,3},{8,12},{9,13},{10,... | collective-permute-start | bytes 12296 | tf_op jit(solution)/shard_map/ppermute | solution.py:322
  29.4 2.0 %collective-permute-done.8.refs_1_ = f32[8,128]{1,0:T(8,128)S(1)} collective-permute-done((f32[8,128]{1,0:T(8,128)S(1)}, f32[8,128]{1,0:T(8,128)S(1)}, u32[]{:S(2)}, u32[]{:S(2)}) %collective-permute-start.8) | collective-permute-done | bytes 4128 | tf_op jit(solution)/shard_map/ppermute | solution.py:322
  31.4 1.1 %collective-permute-done.9.refs_2_ = f32[8,128]{1,0:T(8,128)S(1)} collective-permute-done((f32[8,128]{1,0:T(8,128)S(1)}, f32[8,128]{1,0:T(8,128)S(1)}, u32[]{:S(2)}, u32[]{:S(2)}) %collective-permute-start.9) | collective-permute-done | bytes 4128 | tf_op jit(solution)/shard_map/ppermute | solution.py:322
  32.5 0.3 shard_map.166.refs_0_
  32.8 0.4 collective-permute-start.13
  33.2 0.5 %collective-permute-start.14 = (bf16[288,128]{1,0:T(8,128)(2,1)S(1)}, bf16[288,128]{1,0:T(8,128)(2,1)S(1)}, u32[]{:S(2)}, u32[]{:S(2)}) collective-permute-start(bf16[288,128]{1,0:T(8,128)(2,1)S(1)} %shard_map.166.refs_0_), channel_id=1, source_target_pairs={{0,4},{1,5},{2,6},{3,7},{4,0},{5,1},{6,2},{7,3},{8,12},{9,13},{10,... | collective-permute-start | bytes 221192 | tf_op jit(solution)/shard_map/ppermute | solution.py:322
  33.7 2.0 %collective-permute-start.15 = (bf16[288,128]{1,0:T(8,128)(2,1)S(1)}, bf16[288,128]{1,0:T(8,128)(2,1)S(1)}, u32[]{:S(2)}, u32[]{:S(2)}) collective-permute-start(bf16[288,128]{1,0:T(8,128)(2,1)S(1)} %shard_map.166.refs_0_), channel_id=1, source_target_pairs={{0,3},{1,2},{2,1},{3,0},{4,7},{5,6},{6,5},{7,4},{8,11},{9,10},{10,... | collective-permute-start | bytes 221192 | tf_op jit(solution)/shard_map/ppermute | solution.py:322
  35.8 2.1 %collective-permute-done.13.refs_1_ = bf16[288,128]{1,0:T(8,128)(2,1)S(1)} collective-permute-done((bf16[288,128]{1,0:T(8,128)(2,1)S(1)}, bf16[288,128]{1,0:T(8,128)(2,1)S(1)}, u32[]{:S(2)}, u32[]{:S(2)}) %collective-permute-start.13) | collective-permute-done | bytes 73760 | tf_op jit(solution)/shard_map/ppermute | solution.py:322
  37.9 1.4 %collective-permute-done.14.refs_2_ = bf16[288,128]{1,0:T(8,128)(2,1)S(1)} collective-permute-done((bf16[288,128]{1,0:T(8,128)(2,1)S(1)}, bf16[288,128]{1,0:T(8,128)(2,1)S(1)}, u32[]{:S(2)}, u32[]{:S(2)}) %collective-permute-start.14) | collective-permute-done | bytes 73760 | tf_op jit(solution)/shard_map/ppermute | solution.py:322
  39.3 0.1 collective-permute-start.18
  39.4 0.4 collective-permute-start.19
  39.8 0.8 %shard_map.165 = (f32[48,128]{1,0:T(8,128)}, f32[48,128]{1,0:T(8,128)}, f32[48,128]{1,0:T(8,128)}, f32[96,128]{1,0:T(8,128)}, f32[96,128]{1,0:T(8,128)}, /*index=5*/f32[96,128]{1,0:T(8,128)}) custom-call(f32[8,128]{1,0:T(8,128)S(1)} %add.19.refs_0_, f32[8,128]{1,0:T(8,128)S(1)} %collective-permute-done.8.refs_1_, ...), custom_call_target="tpu_custom_call" | custom-call | tf_op jit(solution)/shard_map/pallas_call | solution.py:68
  40.7 1.6 %shard_map.167 = (bf16[32,6144]{1,0:T(8,128)(2,1)}, bf16[1,16,6144]{2,1,0:T(8,128)(2,1)}) custom-call(bf16[288,128]{1,0:T(8,128)(2,1)S(1)} %shard_map.166.refs_0_, bf16[288,128]{1,0:T(8,128)(2,1)S(1)} %collective-permute-done.13.refs_1_, bf16[288,128]{1,0:T(8,128)(2,1)S(1)} %collective-permute-done.14.refs_2_, ...), custom_call_target="tpu_custom_call" | custom-call | tf_op jit(solution)/shard_map/pallas_call | solution.py:68
  (29 shorter events, 0.2 us)
Async XLA Ops:
  4.3 28.2 %copy-start = (f32[1,2,6144]{2,1,0:T(2,128)S(1)}, f32[1,2,6144]{2,1,0:T(2,128)}, u32[]{:S(2)}) copy-start(f32[1,2,6144]{2,1,0:T(2,128)} %param.17) | copy-start | bytes 147460
  4.3 28.2 %copy-start.1 = (f32[1,2,6144]{2,1,0:T(2,128)S(1)}, f32[1,2,6144]{2,1,0:T(2,128)}, u32[]{:S(2)}) copy-start(f32[1,2,6144]{2,1,0:T(2,128)} %param.18) | copy-start | bytes 147460
  4.3 28.2 %copy-start.2 = (f32[1,2,6144]{2,1,0:T(2,128)S(1)}, f32[1,2,6144]{2,1,0:T(2,128)}, u32[]{:S(2)}) copy-start(f32[1,2,6144]{2,1,0:T(2,128)} %param.19) | copy-start | bytes 147460
  4.3 35.5 %copy-start.3 = (f32[1,6144]{1,0:T(1,128)S(1)}, f32[1,6144]{1,0:T(1,128)}, u32[]{:S(2)}) copy-start(f32[1,6144]{1,0:T(1,128)} %param.14) | copy-start | bytes 73732
  4.3 35.5 %copy-start.4 = (f32[1,6144]{1,0:T(1,128)S(1)}, f32[1,6144]{1,0:T(1,128)}, u32[]{:S(2)}) copy-start(f32[1,6144]{1,0:T(1,128)} %param.15) | copy-start | bytes 73732
  4.3 35.5 %copy-start.5 = (f32[1,6144]{1,0:T(1,128)S(1)}, f32[1,6144]{1,0:T(1,128)}, u32[]{:S(2)}) copy-start(f32[1,6144]{1,0:T(1,128)} %param.16) | copy-start | bytes 73732
  4.3 1.7 %collective-permute-start.1 = (bf16[1152,128]{1,0:T(8,128)(2,1)S(1)}, bf16[1152,128]{1,0:T(8,128)(2,1)S(1)}, u32[]{:S(2)}, u32[]{:S(2)}) collective-permute-start(bf16[1152,128]{1,0:T(8,128)(2,1)S(1)} %get-tuple-element.26), channel_id=1, source_target_pairs={{0,1},{1,0},{2,3},{3,2},{4,5},{5,4},{6,7},{7,6},{8,9},{9,8},{10,11... | collective-permute-start | bytes 884744 | tf_op jit(solution)/shard_map/ppermute | solution.py:326
  6.1 7.6 %collective-permute-start.2 = (bf16[288,128]{1,0:T(8,128)(2,1)S(1)}, bf16[288,128]{1,0:T(8,128)(2,1)S(1)}, u32[]{:S(2)}, u32[]{:S(2)}) collective-permute-start(bf16[288,128]{1,0:T(8,128)(2,1)S(1)} %get-tuple-element.42), channel_id=1, source_target_pairs={{0,7},{1,6},{2,5},{3,4},{4,3},{5,2},{6,1},{7,0},{8,15},{9,14},{10,... | collective-permute-start | bytes 221192 | tf_op jit(solution)/shard_map/ppermute | solution.py:322
  9.8 4.5 %collective-permute-start.3 = (bf16[288,128]{1,0:T(8,128)(2,1)S(1)}, bf16[288,128]{1,0:T(8,128)(2,1)S(1)}, u32[]{:S(2)}, u32[]{:S(2)}) collective-permute-start(bf16[288,128]{1,0:T(8,128)(2,1)S(1)} %get-tuple-element.41), channel_id=1, source_target_pairs={{0,4},{1,5},{2,6},{3,7},{4,0},{5,1},{6,2},{7,3},{8,12},{9,13},{10,... | collective-permute-start | bytes 221192 | tf_op jit(solution)/shard_map/ppermute | solution.py:322
  10.3 4.3 %collective-permute-start.4 = (bf16[288,128]{1,0:T(8,128)(2,1)S(1)}, bf16[288,128]{1,0:T(8,128)(2,1)S(1)}, u32[]{:S(2)}, u32[]{:S(2)}) collective-permute-start(bf16[288,128]{1,0:T(8,128)(2,1)S(1)} %get-tuple-element.40), channel_id=1, source_target_pairs={{0,3},{1,2},{2,1},{3,0},{4,7},{5,6},{6,5},{7,4},{8,11},{9,10},{10,... | collective-permute-start | bytes 221192 | tf_op jit(solution)/shard_map/ppermute | solution.py:322
  10.3 3.5 %collective-permute-start = (bf16[144,128]{1,0:T(8,128)(2,1)S(1)}, bf16[144,128]{1,0:T(8,128)(2,1)S(1)}, u32[]{:S(2)}, u32[]{:S(2)}) collective-permute-start(bf16[144,128]{1,0:T(8,128)(2,1)S(1)} %get-tuple-element.24.refs_0_), channel_id=1, source_target_pairs={{0,9},{1,8},{2,11},{3,10},{4,13},{5,12},{6,15},{7,14},{8,1},{9,0},... | collective-permute-start | bytes 110600 | tf_op jit(solution)/shard_map/ppermute | solution.py:322
  14.6 3.9 %collective-permute-start.5 = (bf16[208,128]{1,0:T(8,128)(2,1)S(1)}, bf16[208,128]{1,0:T(8,128)(2,1)S(1)}, u32[]{:S(2)}, u32[]{:S(2)}) collective-permute-start(bf16[208,128]{1,0:T(8,128)(2,1)S(1)} %get-tuple-element.27.refs_0_), channel_id=1, source_target_pairs={{0,9},{1,8},{2,11},{3,10},{4,13},{5,12},{6,15},{7,14},{8,1},{9,0},... | collective-permute-start | bytes 159752 | tf_op jit(solution)/shard_map/ppermute | solution.py:322
  18.6 6.4 %collective-permute-start.6 = (bf16[208,128]{1,0:T(8,128)(2,1)S(1)}, bf16[208,128]{1,0:T(8,128)(2,1)S(1)}, u32[]{:S(2)}, u32[]{:S(2)}) collective-permute-start(bf16[208,128]{1,0:T(8,128)(2,1)S(1)} %shard_map.163.refs_0_), channel_id=1, source_target_pairs={{0,17},{1,16},{2,19},{3,18},{4,21},{5,20},{6,23},{7,22},{8,25},{9,... | collective-permute-start | bytes 159752 | tf_op jit(solution)/shard_map/ppermute | solution.py:322
  21.0 8.5 %collective-permute-start.11 = (bf16[144,128]{1,0:T(8,128)(2,1)S(1)}, bf16[144,128]{1,0:T(8,128)(2,1)S(1)}, u32[]{:S(2)}, u32[]{:S(2)}) collective-permute-start(bf16[144,128]{1,0:T(8,128)(2,1)S(1)} %get-tuple-element.24.refs_0_), channel_id=1, source_target_pairs={{0,17},{1,16},{2,19},{3,18},{4,21},{5,20},{6,23},{7,22},{8,25},{9,... | collective-permute-start | bytes 110600 | tf_op jit(solution)/shard_map/ppermute | solution.py:322
  21.3 8.1 %collective-permute-start.12 = (bf16[144,128]{1,0:T(8,128)(2,1)S(1)}, bf16[144,128]{1,0:T(8,128)(2,1)S(1)}, u32[]{:S(2)}, u32[]{:S(2)}) collective-permute-start(bf16[144,128]{1,0:T(8,128)(2,1)S(1)} %get-tuple-element.24.refs_0_), channel_id=1, source_target_pairs={{0,24},{1,25},{2,26},{3,27},{4,28},{5,29},{6,30},{7,31},{8,16},{9,... | collective-permute-start | bytes 110600 | tf_op jit(solution)/shard_map/ppermute | solution.py:322
  25.0 1.2 %collective-permute-start.7 = (f32[8,128]{1,0:T(8,128)S(1)}, f32[8,128]{1,0:T(8,128)S(1)}, u32[]{:S(2)}, u32[]{:S(2)}) collective-permute-start(f32[8,128]{1,0:T(8,128)S(1)} %get-tuple-element.28), channel_id=1, source_target_pairs={{0,1},{1,0},{2,3},{3,2},{4,5},{5,4},{6,7},{7,6},{8,9},{9,8},{10,11... | collective-permute-start | bytes 12296 | tf_op jit(solution)/shard_map/ppermute | solution.py:326
  26.2 3.2 %collective-permute-start.10 = (f32[8,128]{1,0:T(8,128)S(1)}, f32[8,128]{1,0:T(8,128)S(1)}, u32[]{:S(2)}, u32[]{:S(2)}) collective-permute-start(f32[8,128]{1,0:T(8,128)S(1)} %add.19.refs_0_), channel_id=1, source_target_pairs={{0,3},{1,2},{2,1},{3,0},{4,7},{5,6},{6,5},{7,4},{8,11},{9,10},{10,... | collective-permute-start | bytes 12296 | tf_op jit(solution)/shard_map/ppermute | solution.py:322
  27.5 3.9 %collective-permute-start.8 = (f32[8,128]{1,0:T(8,128)S(1)}, f32[8,128]{1,0:T(8,128)S(1)}, u32[]{:S(2)}, u32[]{:S(2)}) collective-permute-start(f32[8,128]{1,0:T(8,128)S(1)} %add.19.refs_0_), channel_id=1, source_target_pairs={{0,7},{1,6},{2,5},{3,4},{4,3},{5,2},{6,1},{7,0},{8,15},{9,14},{10,... | collective-permute-start | bytes 12296 | tf_op jit(solution)/shard_map/ppermute | solution.py:322
  28.9 3.6 %collective-permute-start.9 = (f32[8,128]{1,0:T(8,128)S(1)}, f32[8,128]{1,0:T(8,128)S(1)}, u32[]{:S(2)}, u32[]{:S(2)}) collective-permute-start(f32[8,128]{1,0:T(8,128)S(1)} %add.19.refs_0_), channel_id=1, source_target_pairs={{0,4},{1,5},{2,6},{3,7},{4,0},{5,1},{6,2},{7,3},{8,12},{9,13},{10,... | collective-permute-start | bytes 12296 | tf_op jit(solution)/shard_map/ppermute | solution.py:322
  32.8 5.1 %collective-permute-start.13 = (bf16[288,128]{1,0:T(8,128)(2,1)S(1)}, bf16[288,128]{1,0:T(8,128)(2,1)S(1)}, u32[]{:S(2)}, u32[]{:S(2)}) collective-permute-start(bf16[288,128]{1,0:T(8,128)(2,1)S(1)} %shard_map.166.refs_0_), channel_id=1, source_target_pairs={{0,7},{1,6},{2,5},{3,4},{4,3},{5,2},{6,1},{7,0},{8,15},{9,14},{10,... | collective-permute-start | bytes 221192 | tf_op jit(solution)/shard_map/ppermute | solution.py:322
  33.2 6.1 %collective-permute-start.14 = (bf16[288,128]{1,0:T(8,128)(2,1)S(1)}, bf16[288,128]{1,0:T(8,128)(2,1)S(1)}, u32[]{:S(2)}, u32[]{:S(2)}) collective-permute-start(bf16[288,128]{1,0:T(8,128)(2,1)S(1)} %shard_map.166.refs_0_), channel_id=1, source_target_pairs={{0,4},{1,5},{2,6},{3,7},{4,0},{5,1},{6,2},{7,3},{8,12},{9,13},{10,... | collective-permute-start | bytes 221192 | tf_op jit(solution)/shard_map/ppermute | solution.py:322
  33.7 5.7 %collective-permute-start.15 = (bf16[288,128]{1,0:T(8,128)(2,1)S(1)}, bf16[288,128]{1,0:T(8,128)(2,1)S(1)}, u32[]{:S(2)}, u32[]{:S(2)}) collective-permute-start(bf16[288,128]{1,0:T(8,128)(2,1)S(1)} %shard_map.166.refs_0_), channel_id=1, source_target_pairs={{0,3},{1,2},{2,1},{3,0},{4,7},{5,6},{6,5},{7,4},{8,11},{9,10},{10,... | collective-permute-start | bytes 221192 | tf_op jit(solution)/shard_map/ppermute | solution.py:322
  35.8 4.9 %collective-permute-start.16 = (bf16[288,128]{1,0:T(8,128)(2,1)S(1)}, bf16[288,128]{1,0:T(8,128)(2,1)S(1)}, u32[]{:S(2)}, u32[]{:S(2)}) collective-permute-start(bf16[288,128]{1,0:T(8,128)(2,1)S(1)} %shard_map.166.refs_0_), channel_id=1, source_target_pairs={{0,1},{1,0},{2,3},{3,2},{4,5},{5,4},{6,7},{7,6},{8,9},{9,8},{10,11... | collective-permute-start | bytes 221192 | tf_op jit(solution)/shard_map/ppermute | solution.py:326
  37.9 2.8 %collective-permute-start.17 = (bf16[288,128]{1,0:T(8,128)(2,1)S(1)}, bf16[288,128]{1,0:T(8,128)(2,1)S(1)}, u32[]{:S(2)}, u32[]{:S(2)}) collective-permute-start(bf16[288,128]{1,0:T(8,128)(2,1)S(1)} %collective-permute-done.13.refs_1_), channel_id=1, source_target_pairs={{0,1},{1,0},{2,3},{3,2},{4,5},{5,4},{6,7},{7,6},{8,9},{9,8},{10,11... | collective-permute-start | bytes 221192 | tf_op jit(solution)/shard_map/ppermute | solution.py:326
  39.3 1.4 %collective-permute-start.18 = (bf16[288,128]{1,0:T(8,128)(2,1)S(1)}, bf16[288,128]{1,0:T(8,128)(2,1)S(1)}, u32[]{:S(2)}, u32[]{:S(2)}) collective-permute-start(bf16[288,128]{1,0:T(8,128)(2,1)S(1)} %collective-permute-done.14.refs_2_), channel_id=1, source_target_pairs={{0,1},{1,0},{2,3},{3,2},{4,5},{5,4},{6,7},{7,6},{8,9},{9,8},{10,11... | collective-permute-start | bytes 221192 | tf_op jit(solution)/shard_map/ppermute | solution.py:326
  39.4 1.3 %collective-permute-start.19 = (bf16[288,128]{1,0:T(8,128)(2,1)S(1)}, bf16[288,128]{1,0:T(8,128)(2,1)S(1)}, u32[]{:S(2)}, u32[]{:S(2)}) collective-permute-start(bf16[288,128]{1,0:T(8,128)(2,1)S(1)} %collective-permute-done.15.refs_3_), channel_id=1, source_target_pairs={{0,1},{1,0},{2,3},{3,2},{4,5},{5,4},{6,7},{7,6},{8,9},{9,8},{10,11... | collective-permute-start | bytes 221192 | tf_op jit(solution)/shard_map/ppermute | solution.py:326

commit v12 on v11

--- a/solution.py
+++ b/solution.py
@@ -42,6 +42,7 @@
         self.size_e = self.blocks * rows_e
         self.all_a = n_expert * self.size_a
         self.chunk = self.all_a + self.size_e
+        self.turned = n_dp == 8 and rows_a == 1
 
     def places(self, block):
         attn = [
@@ -207,8 +208,13 @@
     square[...] = partial + by_eights(attn * attn)
 
 
+def square_order(chips):
+    return [0, *reversed(range(1, chips - 1)), chips - 1]
+
+
 def clip_factor(limit, squares):
-    values = [squares[-i % len(squares)][...] for i in range(len(squares))]
+    order = square_order(len(squares))
+    values = [squares[order.index(c)][...] for c in range(len(squares))]
     while len(values) > 1:
         values = [values[i] + values[i + 1] for i in range(0, len(values), 2)]
     norm = jnp.sqrt(jnp.sum(values[0], keepdims=True))
@@ -260,6 +266,22 @@
     def lanes(b):
         return pl.ds(b * LANES if isinstance(b, int) else pl.multiple_of(b * LANES, LANES), LANES)
 
+    def turn(part):
+        for e in range(plan.n_expert):
+            first = e * plan.size_a + part * count
+            value = jnp.stack([rows[pl.ds(j * plan.chunk + first, count), :] for j in range(n_dp)])
+            value = value.transpose(1, 0, 2)
+            for b in range(count):
+                rows_a[pl.ds(e * n_dp, n_dp), lanes(b)] = value[b]
+        first = plan.all_a + part * count * plan.rows_e
+        value = jnp.stack([rows[pl.ds(j * plan.chunk + first, count * plan.rows_e), :] for j in range(n_dp)])
+        value = value.transpose(1, 0, 2)
+        for b in range(count):
+            for r in range(plan.rows_e):
+                start = (part * count + b) * count_e + r
+                rows_e[pl.ds(start, n_dp, stride=plan.rows_e), :] = value[b * plan.rows_e + r]
+        attn_v[:, pl.ds(part * count * LANES, count * LANES)] = rows_a[...].astype(bf16)
+
     def gather(b):
         places_a, places_e = plan.places(b)
         values = [rows[pl.ds(start, n_dp, stride=plan.chunk), :] for _, start in places_a]
@@ -281,7 +303,10 @@
     copies = []
     count = plan.blocks // PARTS
     for part in range(PARTS):
-        each(count, lambda b: gather(part * count + b), n_dp <= 8)
+        if plan.turned:
+            turn(part)
+        else:
+            each(count, lambda b: gather(part * count + b), n_dp <= 8)
         each(count, lambda b: finish(part * count + b), True)
         cols = pl.ds(part * count * LANES, count * LANES)
         copies.append(pltpu.make_async_copy(attn_v.at[:, cols], attn.at[:, cols], sems.at[2 * part]))
@@ -301,7 +326,7 @@
         [((count_a, plan.width), bf16), ((1, count_e, plan.width), bf16)],
         [
             ((plan.n_dp * plan.chunk, LANES), f32),
-            ((count_a, LANES), f32),
+            ((count_a, plan.width // PARTS if plan.turned else LANES), f32),
             ((plan.blocks * count_e, LANES), f32),
             ((count_a, plan.width), bf16),
             ((count_e, plan.width), bf16),
@@ -355,9 +380,10 @@
     ]
     got = [swap(sums[c].astype(bf16), chips=c) for c in reversed(range(1, chips))]
     shared = ((plan.all_a + 16, LANES), bf16)
+    packs = [pack, swap(pack, experts=1)]
     payload, g_exp, both = call(
         lambda *refs: share_kernel(plan, *refs),
-        [pack, swap(pack, experts=1), sums[0]] + got,
+        packs + [sums[0]] + got,
         [shared, ((plan.size_e, LANES), f32), ((2,) + pack.shape, bf16)],
     )
     distance = 1
@@ -366,12 +392,14 @@
         (payload,) = call(lambda *refs: again_kernel(plan, *refs), [payload, other], [shared])
         distance *= 2
     other = swap(payload, experts=distance)
-    far = [swap(pack, experts=q) for q in range(2, n_expert)]
+    far = []
+    for step in (2**i for i in range(1, n_expert.bit_length() - 1)):
+        far += [swap(value, experts=step) for value in packs + far]
     g_attn, square = call(
         lambda *refs: last_kernel(plan, *refs), [payload, other], [((plan.all_a, LANES), f32), ((8, LANES), f32)]
     )
     square = square + swap_cores(square)
-    squares = [square] + [swap(square, chips=c) for c in reversed(range(1, chips))]
+    squares = [square] + [swap(square, chips=c) for c in square_order(chips)[1:]]
     block_a, block_e = ((plan.size_a, LANES), f32), ((plan.size_e, LANES), f32)
     (mine,) = call(
         lambda *refs: rows_kernel(plan, limit, *refs),

time: 42.6 us -> 42.6 us (level)
  the two profiles are of different devices: /device:TPU:0 before, /device:TPU:25 now
where the time goes in v12:
time: 42.6 us; the launch traced here: 42.4 us
  waiting for transfers between devices  19.8 us (46%)
  starting transfers between devices  15.7 us (37%)
  Pallas kernels  6.03 us (14%)
  between operations  0.74 us (2%)
    ppermute x14, waiting for transfers between devices, swap(): return lax.ppermute(value, ('expert', 'dp'), pairs)  17.5 us
    ppermute x14, starting transfers between devices, swap(): return lax.ppermute(value, ('expert', 'dp'), pairs)  13.5 us
    pallas_call x7, Pallas kernels, call(): pl.pallas_call(kernel, in_specs=[pl.BlockSpec(memory_space=in_space)] * l...  6.03 us
    ppermute x6, waiting for transfers between devices, swap_cores(): lax.ppermute(value, 'dp', [(i, i ^ 1) for i in range(lax.axis_size('dp'))])  2.36 us
    ppermute x6, starting transfers between devices, swap_cores(): lax.ppermute(value, 'dp', [(i, i ^ 1) for i in range(lax.axis_size('dp'))])  2.19 us
  transfers between devices with their start and end apart: 20, of which 11 were waited for; matrix products, arithmetic and copies ran while one was open for 0% of the time, Pallas kernels for 2%

profile of v12, /device:TPU:25, one launch (start us, length us, event | category | flops | bytes accessed | tf_op | source)
XLA Modules:
  0.0 42.4 jit_solution(11796792093351632991)
XLA Ops:
  0.6 3.6 %shard_map.161 = (f32[2304,128]{1,0:T(8,128)S(1)}, bf16[1152,128]{1,0:T(8,128)(2,1)S(1)}, bf16[144,128]{1,0:T(8,128)(2,1)S(1)}) custom-call(bf16[32,256]{1,0:T(8,128)(2,1)} %bitcast.54, bf16[256,6144]{1,0:T(8,128)(2,1)} %refs_1_.1, bf16[16,128]{1,0:T(8,128)(2,1)} %bitcast.55, bf16[128,6144]{1,0:T(8,128)(2,1)} %bitcast.53, f32[48,128]{1,0:T(8,128)} %bitcast.47, ...), custom_call_target="tpu_custom_call" | custom-call | tf_op jit(solution)/shard_map/pallas_call | solution.py:69
  4.3 0.7 %collective-permute-start.1 = (bf16[1152,128]{1,0:T(8,128)(2,1)S(1)}, bf16[1152,128]{1,0:T(8,128)(2,1)S(1)}, u32[]{:S(2)}, u32[]{:S(2)}) collective-permute-start(bf16[1152,128]{1,0:T(8,128)(2,1)S(1)} %get-tuple-element.26), channel_id=1, source_target_pairs={{0,1},{1,0},{2,3},{3,2},{4,5},{5,4},{6,7},{7,6},{8,9},{9,8},{10,11... | collective-permute-start | bytes 884744 | tf_op jit(solution)/shard_map/ppermute | solution.py:351
  5.1 1.2 %collective-permute-done.1 = bf16[1152,128]{1,0:T(8,128)(2,1)S(1)} collective-permute-done((bf16[1152,128]{1,0:T(8,128)(2,1)S(1)}, bf16[1152,128]{1,0:T(8,128)(2,1)S(1)}, u32[]{:S(2)}, u32[]{:S(2)}) %collective-permute-start.1) | collective-permute-done | bytes 294944 | tf_op jit(solution)/shard_map/ppermute | solution.py:351
  6.4 2.5 %collective-permute-start.2 = (bf16[288,128]{1,0:T(8,128)(2,1)S(1)}, bf16[288,128]{1,0:T(8,128)(2,1)S(1)}, u32[]{:S(2)}, u32[]{:S(2)}) collective-permute-start(bf16[288,128]{1,0:T(8,128)(2,1)S(1)} %get-tuple-element.42), channel_id=1, source_target_pairs={{0,7},{1,6},{2,5},{3,4},{4,3},{5,2},{6,1},{7,0},{8,15},{9,14},{10,... | collective-permute-start | bytes 221192 | tf_op jit(solution)/shard_map/ppermute | solution.py:347
  8.9 0.2 collective-permute-start.3
  9.1 0.6 %collective-permute-start.4 = (bf16[288,128]{1,0:T(8,128)(2,1)S(1)}, bf16[288,128]{1,0:T(8,128)(2,1)S(1)}, u32[]{:S(2)}, u32[]{:S(2)}) collective-permute-start(bf16[288,128]{1,0:T(8,128)(2,1)S(1)} %get-tuple-element.40), channel_id=1, source_target_pairs={{0,3},{1,2},{2,1},{3,0},{4,7},{5,6},{6,5},{7,4},{8,11},{9,10},{10,... | collective-permute-start | bytes 221192 | tf_op jit(solution)/shard_map/ppermute | solution.py:347
  9.8 3.6 %collective-permute-done.refs_1_ = bf16[144,128]{1,0:T(8,128)(2,1)S(1)} collective-permute-done((bf16[144,128]{1,0:T(8,128)(2,1)S(1)}, bf16[144,128]{1,0:T(8,128)(2,1)S(1)}, u32[]{:S(2)}, u32[]{:S(2)}) %collective-permute-start) | collective-permute-done | bytes 36896 | tf_op jit(solution)/shard_map/ppermute | solution.py:347
  13.5 0.5 %collective-permute-start.5 = (bf16[208,128]{1,0:T(8,128)(2,1)S(1)}, bf16[208,128]{1,0:T(8,128)(2,1)S(1)}, u32[]{:S(2)}, u32[]{:S(2)}) collective-permute-start(bf16[208,128]{1,0:T(8,128)(2,1)S(1)} %get-tuple-element.27.refs_0_), channel_id=1, source_target_pairs={{0,9},{1,8},{2,11},{3,10},{4,13},{5,12},{6,15},{7,14},{8,1},{9,0},... | collective-permute-start | bytes 159752 | tf_op jit(solution)/shard_map/ppermute | solution.py:347
  14.0 3.4 %collective-permute-done.5.refs_1_ = bf16[208,128]{1,0:T(8,128)(2,1)S(1)} collective-permute-done((bf16[208,128]{1,0:T(8,128)(2,1)S(1)}, bf16[208,128]{1,0:T(8,128)(2,1)S(1)}, u32[]{:S(2)}, u32[]{:S(2)}) %collective-permute-start.5) | collective-permute-done | bytes 53280 | tf_op jit(solution)/shard_map/ppermute | solution.py:347
  17.4 0.4 collective-permute-start.6
  17.8 2.3 %collective-permute-start.11 = (bf16[144,128]{1,0:T(8,128)(2,1)S(1)}, bf16[144,128]{1,0:T(8,128)(2,1)S(1)}, u32[]{:S(2)}, u32[]{:S(2)}) collective-permute-start(bf16[144,128]{1,0:T(8,128)(2,1)S(1)} %get-tuple-element.24.refs_0_), channel_id=1, source_target_pairs={{0,17},{1,16},{2,19},{3,18},{4,21},{5,20},{6,23},{7,22},{8,25},{9,... | collective-permute-start | bytes 110600 | tf_op jit(solution)/shard_map/ppermute | solution.py:347
  20.1 0.3 collective-permute-start.12
  20.5 4.7 %collective-permute-done.6.refs_1_ = bf16[208,128]{1,0:T(8,128)(2,1)S(1)} collective-permute-done((bf16[208,128]{1,0:T(8,128)(2,1)S(1)}, bf16[208,128]{1,0:T(8,128)(2,1)S(1)}, u32[]{:S(2)}, u32[]{:S(2)}) %collective-permute-start.6) | collective-permute-done | bytes 53280 | tf_op jit(solution)/shard_map/ppermute | solution.py:347
  25.2 0.4 collective-permute-start.7
  25.6 0.8 %collective-permute-done.7 = f32[8,128]{1,0:T(8,128)S(1)} collective-permute-done((f32[8,128]{1,0:T(8,128)S(1)}, f32[8,128]{1,0:T(8,128)S(1)}, u32[]{:S(2)}, u32[]{:S(2)}) %collective-permute-start.7) | collective-permute-done | bytes 4128 | tf_op jit(solution)/shard_map/ppermute | solution.py:351
  26.4 1.4 %collective-permute-start.10 = (f32[8,128]{1,0:T(8,128)S(1)}, f32[8,128]{1,0:T(8,128)S(1)}, u32[]{:S(2)}, u32[]{:S(2)}) collective-permute-start(f32[8,128]{1,0:T(8,128)S(1)} %add.19.refs_0_), channel_id=1, source_target_pairs={{0,7},{1,6},{2,5},{3,4},{4,3},{5,2},{6,1},{7,0},{8,15},{9,14},{10,... | collective-permute-start | bytes 12296 | tf_op jit(solution)/shard_map/ppermute | solution.py:347
  27.8 1.2 %collective-permute-start.8 = (f32[8,128]{1,0:T(8,128)S(1)}, f32[8,128]{1,0:T(8,128)S(1)}, u32[]{:S(2)}, u32[]{:S(2)}) collective-permute-start(f32[8,128]{1,0:T(8,128)S(1)} %add.19.refs_0_), channel_id=1, source_target_pairs={{0,4},{1,5},{2,6},{3,7},{4,0},{5,1},{6,2},{7,3},{8,12},{9,13},{10,... | collective-permute-start | bytes 12296 | tf_op jit(solution)/shard_map/ppermute | solution.py:347
  29.1 0.6 %collective-permute-start.9 = (f32[8,128]{1,0:T(8,128)S(1)}, f32[8,128]{1,0:T(8,128)S(1)}, u32[]{:S(2)}, u32[]{:S(2)}) collective-permute-start(f32[8,128]{1,0:T(8,128)S(1)} %add.19.refs_0_), channel_id=1, source_target_pairs={{0,3},{1,2},{2,1},{3,0},{4,7},{5,6},{6,5},{7,4},{8,11},{9,10},{10,... | collective-permute-start | bytes 12296 | tf_op jit(solution)/shard_map/ppermute | solution.py:347
  29.6 0.7 %collective-permute-done.10.refs_3_ = f32[8,128]{1,0:T(8,128)S(1)} collective-permute-done((f32[8,128]{1,0:T(8,128)S(1)}, f32[8,128]{1,0:T(8,128)S(1)}, u32[]{:S(2)}, u32[]{:S(2)}) %collective-permute-start.10) | collective-permute-done | bytes 4128 | tf_op jit(solution)/shard_map/ppermute | solution.py:347
  30.4 1.8 %collective-permute-done.9.refs_2_ = f32[8,128]{1,0:T(8,128)S(1)} collective-permute-done((f32[8,128]{1,0:T(8,128)S(1)}, f32[8,128]{1,0:T(8,128)S(1)}, u32[]{:S(2)}, u32[]{:S(2)}) %collective-permute-start.9) | collective-permute-done | bytes 4128 | tf_op jit(solution)/shard_map/ppermute | solution.py:347
  32.1 0.3 shard_map.166.refs_0_
  32.4 1.6 %collective-permute-start.13 = (bf16[288,128]{1,0:T(8,128)(2,1)S(1)}, bf16[288,128]{1,0:T(8,128)(2,1)S(1)}, u32[]{:S(2)}, u32[]{:S(2)}) collective-permute-start(bf16[288,128]{1,0:T(8,128)(2,1)S(1)} %shard_map.166.refs_0_), channel_id=1, source_target_pairs={{0,7},{1,6},{2,5},{3,4},{4,3},{5,2},{6,1},{7,0},{8,15},{9,14},{10,... | collective-permute-start | bytes 221192 | tf_op jit(solution)/shard_map/ppermute | solution.py:347
  34.0 0.3 collective-permute-start.14
  34.3 1.4 %collective-permute-start.15 = (bf16[288,128]{1,0:T(8,128)(2,1)S(1)}, bf16[288,128]{1,0:T(8,128)(2,1)S(1)}, u32[]{:S(2)}, u32[]{:S(2)}) collective-permute-start(bf16[288,128]{1,0:T(8,128)(2,1)S(1)} %shard_map.166.refs_0_), channel_id=1, source_target_pairs={{0,3},{1,2},{2,1},{3,0},{4,7},{5,6},{6,5},{7,4},{8,11},{9,10},{10,... | collective-permute-start | bytes 221192 | tf_op jit(solution)/shard_map/ppermute | solution.py:347
  35.7 0.1 collective-permute-start.16
  35.8 1.9 %collective-permute-done.13.refs_1_ = bf16[288,128]{1,0:T(8,128)(2,1)S(1)} collective-permute-done((bf16[288,128]{1,0:T(8,128)(2,1)S(1)}, bf16[288,128]{1,0:T(8,128)(2,1)S(1)}, u32[]{:S(2)}, u32[]{:S(2)}) %collective-permute-start.13) | collective-permute-done | bytes 73760 | tf_op jit(solution)/shard_map/ppermute | solution.py:347
  37.8 0.4 collective-permute-start.17
  38.1 1.3 %collective-permute-done.14.refs_2_ = bf16[288,128]{1,0:T(8,128)(2,1)S(1)} collective-permute-done((bf16[288,128]{1,0:T(8,128)(2,1)S(1)}, bf16[288,128]{1,0:T(8,128)(2,1)S(1)}, u32[]{:S(2)}, u32[]{:S(2)}) %collective-permute-start.14) | collective-permute-done | bytes 73760 | tf_op jit(solution)/shard_map/ppermute | solution.py:347
  39.5 0.4 %collective-permute-start.18 = (bf16[288,128]{1,0:T(8,128)(2,1)S(1)}, bf16[288,128]{1,0:T(8,128)(2,1)S(1)}, u32[]{:S(2)}, u32[]{:S(2)}) collective-permute-start(bf16[288,128]{1,0:T(8,128)(2,1)S(1)} %collective-permute-done.14.refs_2_), channel_id=1, source_target_pairs={{0,1},{1,0},{2,3},{3,2},{4,5},{5,4},{6,7},{7,6},{8,9},{9,8},{10,11... | collective-permute-start | bytes 221192 | tf_op jit(solution)/shard_map/ppermute | solution.py:351
  40.0 0.8 %shard_map.165 = (f32[48,128]{1,0:T(8,128)}, f32[48,128]{1,0:T(8,128)}, f32[48,128]{1,0:T(8,128)}, f32[96,128]{1,0:T(8,128)}, f32[96,128]{1,0:T(8,128)}, /*index=5*/f32[96,128]{1,0:T(8,128)}) custom-call(f32[8,128]{1,0:T(8,128)S(1)} %add.19.refs_0_, f32[8,128]{1,0:T(8,128)S(1)} %collective-permute-done.8.refs_1_, ...), custom_call_target="tpu_custom_call" | custom-call | tf_op jit(solution)/shard_map/pallas_call | solution.py:69
  40.9 0.3 collective-permute-done.19.refs_7_
  41.2 1.2 %shard_map.167 = (bf16[32,6144]{1,0:T(8,128)(2,1)}, bf16[1,16,6144]{2,1,0:T(8,128)(2,1)}) custom-call(bf16[288,128]{1,0:T(8,128)(2,1)S(1)} %shard_map.166.refs_0_, bf16[288,128]{1,0:T(8,128)(2,1)S(1)} %collective-permute-done.13.refs_1_, bf16[288,128]{1,0:T(8,128)(2,1)S(1)} %collective-permute-done.14.refs_2_, ...), custom_call_target="tpu_custom_call" | custom-call | tf_op jit(solution)/shard_map/pallas_call | solution.py:69
  (29 shorter events, 0.5 us)
Async XLA Ops:
  4.3 27.9 %copy-start = (f32[1,2,6144]{2,1,0:T(2,128)S(1)}, f32[1,2,6144]{2,1,0:T(2,128)}, u32[]{:S(2)}) copy-start(f32[1,2,6144]{2,1,0:T(2,128)} %param.17) | copy-start | bytes 147460
  4.3 27.9 %copy-start.1 = (f32[1,2,6144]{2,1,0:T(2,128)S(1)}, f32[1,2,6144]{2,1,0:T(2,128)}, u32[]{:S(2)}) copy-start(f32[1,2,6144]{2,1,0:T(2,128)} %param.18) | copy-start | bytes 147460
  4.3 27.8 %copy-start.2 = (f32[1,2,6144]{2,1,0:T(2,128)S(1)}, f32[1,2,6144]{2,1,0:T(2,128)}, u32[]{:S(2)}) copy-start(f32[1,2,6144]{2,1,0:T(2,128)} %param.19) | copy-start | bytes 147460
  4.3 35.7 %copy-start.3 = (f32[1,6144]{1,0:T(1,128)S(1)}, f32[1,6144]{1,0:T(1,128)}, u32[]{:S(2)}) copy-start(f32[1,6144]{1,0:T(1,128)} %param.14) | copy-start | bytes 73732
  4.3 35.7 %copy-start.4 = (f32[1,6144]{1,0:T(1,128)S(1)}, f32[1,6144]{1,0:T(1,128)}, u32[]{:S(2)}) copy-start(f32[1,6144]{1,0:T(1,128)} %param.15) | copy-start | bytes 73732
  4.3 35.7 %copy-start.5 = (f32[1,6144]{1,0:T(1,128)S(1)}, f32[1,6144]{1,0:T(1,128)}, u32[]{:S(2)}) copy-start(f32[1,6144]{1,0:T(1,128)} %param.16) | copy-start | bytes 73732
  4.3 1.9 %collective-permute-start.1 = (bf16[1152,128]{1,0:T(8,128)(2,1)S(1)}, bf16[1152,128]{1,0:T(8,128)(2,1)S(1)}, u32[]{:S(2)}, u32[]{:S(2)}) collective-permute-start(bf16[1152,128]{1,0:T(8,128)(2,1)S(1)} %get-tuple-element.26), channel_id=1, source_target_pairs={{0,1},{1,0},{2,3},{3,2},{4,5},{5,4},{6,7},{7,6},{8,9},{9,8},{10,11... | collective-permute-start | bytes 884744 | tf_op jit(solution)/shard_map/ppermute | solution.py:351
  6.4 7.0 %collective-permute-start.2 = (bf16[288,128]{1,0:T(8,128)(2,1)S(1)}, bf16[288,128]{1,0:T(8,128)(2,1)S(1)}, u32[]{:S(2)}, u32[]{:S(2)}) collective-permute-start(bf16[288,128]{1,0:T(8,128)(2,1)S(1)} %get-tuple-element.42), channel_id=1, source_target_pairs={{0,7},{1,6},{2,5},{3,4},{4,3},{5,2},{6,1},{7,0},{8,15},{9,14},{10,... | collective-permute-start | bytes 221192 | tf_op jit(solution)/shard_map/ppermute | solution.py:347
  8.9 4.5 %collective-permute-start.3 = (bf16[288,128]{1,0:T(8,128)(2,1)S(1)}, bf16[288,128]{1,0:T(8,128)(2,1)S(1)}, u32[]{:S(2)}, u32[]{:S(2)}) collective-permute-start(bf16[288,128]{1,0:T(8,128)(2,1)S(1)} %get-tuple-element.41), channel_id=1, source_target_pairs={{0,4},{1,5},{2,6},{3,7},{4,0},{5,1},{6,2},{7,3},{8,12},{9,13},{10,... | collective-permute-start | bytes 221192 | tf_op jit(solution)/shard_map/ppermute | solution.py:347
  9.1 4.4 %collective-permute-start.4 = (bf16[288,128]{1,0:T(8,128)(2,1)S(1)}, bf16[288,128]{1,0:T(8,128)(2,1)S(1)}, u32[]{:S(2)}, u32[]{:S(2)}) collective-permute-start(bf16[288,128]{1,0:T(8,128)(2,1)S(1)} %get-tuple-element.40), channel_id=1, source_target_pairs={{0,3},{1,2},{2,1},{3,0},{4,7},{5,6},{6,5},{7,4},{8,11},{9,10},{10,... | collective-permute-start | bytes 221192 | tf_op jit(solution)/shard_map/ppermute | solution.py:347
  9.7 3.7 %collective-permute-start = (bf16[144,128]{1,0:T(8,128)(2,1)S(1)}, bf16[144,128]{1,0:T(8,128)(2,1)S(1)}, u32[]{:S(2)}, u32[]{:S(2)}) collective-permute-start(bf16[144,128]{1,0:T(8,128)(2,1)S(1)} %get-tuple-element.24.refs_0_), channel_id=1, source_target_pairs={{0,9},{1,8},{2,11},{3,10},{4,13},{5,12},{6,15},{7,14},{8,1},{9,0},... | collective-permute-start | bytes 110600 | tf_op jit(solution)/shard_map/ppermute | solution.py:347
  13.5 3.9 %collective-permute-start.5 = (bf16[208,128]{1,0:T(8,128)(2,1)S(1)}, bf16[208,128]{1,0:T(8,128)(2,1)S(1)}, u32[]{:S(2)}, u32[]{:S(2)}) collective-permute-start(bf16[208,128]{1,0:T(8,128)(2,1)S(1)} %get-tuple-element.27.refs_0_), channel_id=1, source_target_pairs={{0,9},{1,8},{2,11},{3,10},{4,13},{5,12},{6,15},{7,14},{8,1},{9,0},... | collective-permute-start | bytes 159752 | tf_op jit(solution)/shard_map/ppermute | solution.py:347
  17.4 7.7 %collective-permute-start.6 = (bf16[208,128]{1,0:T(8,128)(2,1)S(1)}, bf16[208,128]{1,0:T(8,128)(2,1)S(1)}, u32[]{:S(2)}, u32[]{:S(2)}) collective-permute-start(bf16[208,128]{1,0:T(8,128)(2,1)S(1)} %shard_map.163.refs_0_), channel_id=1, source_target_pairs={{0,17},{1,16},{2,19},{3,18},{4,21},{5,20},{6,23},{7,22},{8,25},{9,... | collective-permute-start | bytes 159752 | tf_op jit(solution)/shard_map/ppermute | solution.py:347
  17.8 11.8 %collective-permute-start.11 = (bf16[144,128]{1,0:T(8,128)(2,1)S(1)}, bf16[144,128]{1,0:T(8,128)(2,1)S(1)}, u32[]{:S(2)}, u32[]{:S(2)}) collective-permute-start(bf16[144,128]{1,0:T(8,128)(2,1)S(1)} %get-tuple-element.24.refs_0_), channel_id=1, source_target_pairs={{0,17},{1,16},{2,19},{3,18},{4,21},{5,20},{6,23},{7,22},{8,25},{9,... | collective-permute-start | bytes 110600 | tf_op jit(solution)/shard_map/ppermute | solution.py:347
  20.1 9.5 %collective-permute-start.12 = (bf16[144,128]{1,0:T(8,128)(2,1)S(1)}, bf16[144,128]{1,0:T(8,128)(2,1)S(1)}, u32[]{:S(2)}, u32[]{:S(2)}) collective-permute-start(bf16[144,128]{1,0:T(8,128)(2,1)S(1)} %collective-permute-done.refs_1_), channel_id=1, source_target_pairs={{0,17},{1,16},{2,19},{3,18},{4,21},{5,20},{6,23},{7,22},{8,25},{9,... | collective-permute-start | bytes 110600 | tf_op jit(solution)/shard_map/ppermute | solution.py:347
  25.2 1.2 %collective-permute-start.7 = (f32[8,128]{1,0:T(8,128)S(1)}, f32[8,128]{1,0:T(8,128)S(1)}, u32[]{:S(2)}, u32[]{:S(2)}) collective-permute-start(f32[8,128]{1,0:T(8,128)S(1)} %get-tuple-element.28), channel_id=1, source_target_pairs={{0,1},{1,0},{2,3},{3,2},{4,5},{5,4},{6,7},{7,6},{8,9},{9,8},{10,11... | collective-permute-start | bytes 12296 | tf_op jit(solution)/shard_map/ppermute | solution.py:351
  26.4 3.9 %collective-permute-start.10 = (f32[8,128]{1,0:T(8,128)S(1)}, f32[8,128]{1,0:T(8,128)S(1)}, u32[]{:S(2)}, u32[]{:S(2)}) collective-permute-start(f32[8,128]{1,0:T(8,128)S(1)} %add.19.refs_0_), channel_id=1, source_target_pairs={{0,7},{1,6},{2,5},{3,4},{4,3},{5,2},{6,1},{7,0},{8,15},{9,14},{10,... | collective-permute-start | bytes 12296 | tf_op jit(solution)/shard_map/ppermute | solution.py:347
  27.8 2.6 %collective-permute-start.8 = (f32[8,128]{1,0:T(8,128)S(1)}, f32[8,128]{1,0:T(8,128)S(1)}, u32[]{:S(2)}, u32[]{:S(2)}) collective-permute-start(f32[8,128]{1,0:T(8,128)S(1)} %add.19.refs_0_), channel_id=1, source_target_pairs={{0,4},{1,5},{2,6},{3,7},{4,0},{5,1},{6,2},{7,3},{8,12},{9,13},{10,... | collective-permute-start | bytes 12296 | tf_op jit(solution)/shard_map/ppermute | solution.py:347
  29.1 3.1 %collective-permute-start.9 = (f32[8,128]{1,0:T(8,128)S(1)}, f32[8,128]{1,0:T(8,128)S(1)}, u32[]{:S(2)}, u32[]{:S(2)}) collective-permute-start(f32[8,128]{1,0:T(8,128)S(1)} %add.19.refs_0_), channel_id=1, source_target_pairs={{0,3},{1,2},{2,1},{3,0},{4,7},{5,6},{6,5},{7,4},{8,11},{9,10},{10,... | collective-permute-start | bytes 12296 | tf_op jit(solution)/shard_map/ppermute | solution.py:347
  32.4 5.3 %collective-permute-start.13 = (bf16[288,128]{1,0:T(8,128)(2,1)S(1)}, bf16[288,128]{1,0:T(8,128)(2,1)S(1)}, u32[]{:S(2)}, u32[]{:S(2)}) collective-permute-start(bf16[288,128]{1,0:T(8,128)(2,1)S(1)} %shard_map.166.refs_0_), channel_id=1, source_target_pairs={{0,7},{1,6},{2,5},{3,4},{4,3},{5,2},{6,1},{7,0},{8,15},{9,14},{10,... | collective-permute-start | bytes 221192 | tf_op jit(solution)/shard_map/ppermute | solution.py:347
  34.0 5.5 %collective-permute-start.14 = (bf16[288,128]{1,0:T(8,128)(2,1)S(1)}, bf16[288,128]{1,0:T(8,128)(2,1)S(1)}, u32[]{:S(2)}, u32[]{:S(2)}) collective-permute-start(bf16[288,128]{1,0:T(8,128)(2,1)S(1)} %shard_map.166.refs_0_), channel_id=1, source_target_pairs={{0,4},{1,5},{2,6},{3,7},{4,0},{5,1},{6,2},{7,3},{8,12},{9,13},{10,... | collective-permute-start | bytes 221192 | tf_op jit(solution)/shard_map/ppermute | solution.py:347
  34.3 5.6 %collective-permute-start.15 = (bf16[288,128]{1,0:T(8,128)(2,1)S(1)}, bf16[288,128]{1,0:T(8,128)(2,1)S(1)}, u32[]{:S(2)}, u32[]{:S(2)}) collective-permute-start(bf16[288,128]{1,0:T(8,128)(2,1)S(1)} %shard_map.166.refs_0_), channel_id=1, source_target_pairs={{0,3},{1,2},{2,1},{3,0},{4,7},{5,6},{6,5},{7,4},{8,11},{9,10},{10,... | collective-permute-start | bytes 221192 | tf_op jit(solution)/shard_map/ppermute | solution.py:347
  35.7 5.2 %collective-permute-start.16 = (bf16[288,128]{1,0:T(8,128)(2,1)S(1)}, bf16[288,128]{1,0:T(8,128)(2,1)S(1)}, u32[]{:S(2)}, u32[]{:S(2)}) collective-permute-start(bf16[288,128]{1,0:T(8,128)(2,1)S(1)} %shard_map.166.refs_0_), channel_id=1, source_target_pairs={{0,1},{1,0},{2,3},{3,2},{4,5},{5,4},{6,7},{7,6},{8,9},{9,8},{10,11... | collective-permute-start | bytes 221192 | tf_op jit(solution)/shard_map/ppermute | solution.py:351
  37.8 3.1 %collective-permute-start.17 = (bf16[288,128]{1,0:T(8,128)(2,1)S(1)}, bf16[288,128]{1,0:T(8,128)(2,1)S(1)}, u32[]{:S(2)}, u32[]{:S(2)}) collective-permute-start(bf16[288,128]{1,0:T(8,128)(2,1)S(1)} %collective-permute-done.13.refs_1_), channel_id=1, source_target_pairs={{0,1},{1,0},{2,3},{3,2},{4,5},{5,4},{6,7},{7,6},{8,9},{9,8},{10,11... | collective-permute-start | bytes 221192 | tf_op jit(solution)/shard_map/ppermute | solution.py:351
  39.5 1.4 %collective-permute-start.18 = (bf16[288,128]{1,0:T(8,128)(2,1)S(1)}, bf16[288,128]{1,0:T(8,128)(2,1)S(1)}, u32[]{:S(2)}, u32[]{:S(2)}) collective-permute-start(bf16[288,128]{1,0:T(8,128)(2,1)S(1)} %collective-permute-done.14.refs_2_), channel_id=1, source_target_pairs={{0,1},{1,0},{2,3},{3,2},{4,5},{5,4},{6,7},{7,6},{8,9},{9,8},{10,11... | collective-permute-start | bytes 221192 | tf_op jit(solution)/shard_map/ppermute | solution.py:351
  39.9 1.3 %collective-permute-start.19 = (bf16[288,128]{1,0:T(8,128)(2,1)S(1)}, bf16[288,128]{1,0:T(8,128)(2,1)S(1)}, u32[]{:S(2)}, u32[]{:S(2)}) collective-permute-start(bf16[288,128]{1,0:T(8,128)(2,1)S(1)} %collective-permute-done.15.refs_3_), channel_id=1, source_target_pairs={{0,1},{1,0},{2,3},{3,2},{4,5},{5,4},{6,7},{7,6},{8,9},{9,8},{10,11... | collective-permute-start | bytes 221192 | tf_op jit(solution)/shard_map/ppermute | solution.py:351

commit v13 on v12

--- a/solution.py
+++ b/solution.py
@@ -29,7 +29,10 @@
 
 
 def role_of(chip, core, expert):
-    return core ^ ((chip ^ expert ^ (expert // 2)) % 2)
+    bits = chip ^ expert
+    for shift in (4, 2, 1):
+        bits = bits ^ (bits >> shift)
+    return core ^ (bits & 1)
 
 
 class Plan:
@@ -85,7 +88,7 @@
     return jnp.sum(value.reshape(-1, 8, LANES), axis=0)
 
 
-STEPS = 4
+STEPS = (4, 4, 4, 2, 2)
 
 
 def each(count, step, unrolled):
@@ -97,17 +100,18 @@
 
 
 def terms_kernel(plan, act_a, dy_a, act_e, dy_e, w, m, v, full, send, pack, act_a_v, dy_a_v, act_e_v, dy_e_v, state, sems):
-    tile = plan.width // STEPS
+    unit = plan.blocks // sum(STEPS)
+    tiles = [(sum(STEPS[:t]) * unit, STEPS[t] * unit) for t in range(len(STEPS))]
     small = [
         pltpu.make_async_copy(act_a, act_a_v, sems.at[0]),
         pltpu.make_async_copy(act_e, act_e_v, sems.at[1]),
     ]
     big = []
-    for t in range(STEPS):
-        cols = pl.ds(t * tile, tile)
+    for t, (first, count) in enumerate(tiles):
+        cols = pl.ds(first * LANES, count * LANES)
         big.append(pltpu.make_async_copy(dy_a.at[:, cols], dy_a_v.at[:, cols], sems.at[2 + 2 * t]))
         big.append(pltpu.make_async_copy(dy_e.at[:, cols], dy_e_v.at[:, cols], sems.at[3 + 2 * t]))
-    extra = [pltpu.make_async_copy(ref, state.at[i], sems.at[2 + 2 * STEPS + i]) for i, ref in enumerate((w, m, v))]
+    extra = [pltpu.make_async_copy(ref, state.at[i], sems.at[2 + 2 * len(STEPS) + i]) for i, ref in enumerate((w, m, v))]
     for copy in small + big + extra:
         copy.start()
 
@@ -133,14 +137,14 @@
     left_a = dot(pick(plan.n_expert * plan.rows_a, plan.rows_a, act_a.shape[0], None), act_a_v[...]).astype(bf16)
     left_e = dot(pick(plan.rows_e, plan.rows_e, act_e.shape[0], me_ex), act_e_v[...]).astype(bf16)
     n_dp = plan.n_dp
-    for t in range(STEPS):
-        cols = pl.ds(t * tile, tile)
+    for t, (first, count) in enumerate(tiles):
+        cols = pl.ds(first * LANES, count * LANES)
         big[2 * t].wait()
         terms_a = dot(left_a, dy_a_v[:, cols])
         big[2 * t + 1].wait()
         terms_e = dot(left_e, dy_e_v[:, cols])
-        for b in range(tile // LANES):
-            attn, exp = plan.places(t * (tile // LANES) + b)
+        for b in range(count):
+            attn, exp = plan.places(first + b)
             span = slice(b * LANES, (b + 1) * LANES)
             for terms, places in ((terms_a, attn), (terms_e, exp)):
                 for group, start in places:
@@ -176,8 +180,9 @@
 
 
 def share_kernel(plan, *refs):
-    held, far, own, got, (payload, g_exp, both) = *refs[:3], refs[3:-3], refs[-3:]
-    both[0], both[1] = held[...], far[...]
+    held, own, got, (payload, g_exp, both) = refs[:3], refs[3], refs[4:-3], refs[-3:]
+    for i, pack in enumerate(held):
+        both[i] = pack[...]
     total = own[...]
     for ref in got:
         total = total + ref[...].astype(f32)
@@ -209,7 +214,7 @@
 
 
 def square_order(chips):
-    return [0, *reversed(range(1, chips - 1)), chips - 1]
+    return [0, *range(1, chips - 2), chips - 1, chips - 2]
 
 
 def clip_factor(limit, squares):
@@ -223,9 +228,9 @@
 
 def rows_kernel(plan, limit, *refs):
     factor = clip_factor(limit, refs[: plan.chips])
-    g_attn, g_exp, we, me, ve, both, *far, mine = refs[plan.chips :]
+    g_attn, g_exp, we, me, ve, both, far, mine = refs[plan.chips :]
     size, place = plan.size_a, lax.axis_index("expert")
-    for q, states in enumerate([both.at[0], both.at[1], *far]):
+    for q, states in enumerate([both.at[0], both.at[1], both.at[2], far]):
         rows = pl.ds(pl.multiple_of((place ^ q) * size, 16), size)
         old = [states[pl.ds(i * size, size), :].astype(f32) for i in range(3)]
         weight, _, _ = adamw(g_attn[rows, :], *old, factor)
@@ -380,11 +385,11 @@
     ]
     got = [swap(sums[c].astype(bf16), chips=c) for c in reversed(range(1, chips))]
     shared = ((plan.all_a + 16, LANES), bf16)
-    packs = [pack, swap(pack, experts=1)]
+    packs = [pack, swap(pack, experts=1), swap(pack, experts=2)]
     payload, g_exp, both = call(
         lambda *refs: share_kernel(plan, *refs),
         packs + [sums[0]] + got,
-        [shared, ((plan.size_e, LANES), f32), ((2,) + pack.shape, bf16)],
+        [shared, ((plan.size_e, LANES), f32), ((3,) + pack.shape, bf16)],
     )
     distance = 1
     while 2 * distance < n_expert:
@@ -392,9 +397,7 @@
         (payload,) = call(lambda *refs: again_kernel(plan, *refs), [payload, other], [shared])
         distance *= 2
     other = swap(payload, experts=distance)
-    far = []
-    for step in (2**i for i in range(1, n_expert.bit_length() - 1)):
-        far += [swap(value, experts=step) for value in packs + far]
+    far = swap(packs[1], experts=2)
     g_attn, square = call(
         lambda *refs: last_kernel(plan, *refs), [payload, other], [((plan.all_a, LANES), f32), ((8, LANES), f32)]
     )
@@ -403,7 +406,7 @@
     block_a, block_e = ((plan.size_a, LANES), f32), ((plan.size_e, LANES), f32)
     (mine,) = call(
         lambda *refs: rows_kernel(plan, limit, *refs),
-        [*squares, g_attn, g_exp, *state_e, both, *far],
+        [*squares, g_attn, g_exp, *state_e, both, far],
         [((chunk, LANES), bf16)],
     )
     wa, ma, va, we, me, ve = call(

time: 42.6 us -> 45.4 us (1.066)
  the two profiles are of different devices: /device:TPU:25 before, /device:TPU:0 now
where the time goes in v13:
time: 45.4 us; the launch traced here: 45.2 us
  starting transfers between devices  24.1 us (53%)
  waiting for transfers between devices  13.9 us (31%)
  Pallas kernels  6.3 us (14%)
  between operations  0.75 us (2%)
    ppermute x14, starting transfers between devices, swap(): return lax.ppermute(value, ('expert', 'dp'), pairs)  19.1 us
    ppermute x14, waiting for transfers between devices, swap(): return lax.ppermute(value, ('expert', 'dp'), pairs)  11.9 us
    pallas_call x7, Pallas kernels, call(): pl.pallas_call(kernel, in_specs=[pl.BlockSpec(memory_space=in_space)] * l...  6.3 us
    ppermute x6, starting transfers between devices, swap_cores(): lax.ppermute(value, 'dp', [(i, i ^ 1) for i in range(lax.axis_size('dp'))])  5.03 us
    ppermute x6, waiting for transfers between devices, swap_cores(): lax.ppermute(value, 'dp', [(i, i ^ 1) for i in range(lax.axis_size('dp'))])  2.08 us
  transfers between devices with their start and end apart: 20, of which 10 were waited for; matrix products, arithmetic and copies ran while one was open for 0% of the time, Pallas kernels for 2%

profile of v13, /device:TPU:0, one launch (start us, length us, event | category | flops | bytes accessed | tf_op | source)
XLA Modules:
  0.0 45.2 jit_solution(15429023009764349854)
XLA Ops:
  0.6 3.9 %shard_map.161 = (f32[2304,128]{1,0:T(8,128)S(1)}, bf16[1152,128]{1,0:T(8,128)(2,1)S(1)}, bf16[144,128]{1,0:T(8,128)(2,1)S(1)}) custom-call(bf16[32,256]{1,0:T(8,128)(2,1)} %bitcast.54, bf16[256,6144]{1,0:T(8,128)(2,1)} %refs_1_.1, bf16[16,128]{1,0:T(8,128)(2,1)} %bitcast.55, bf16[128,6144]{1,0:T(8,128)(2,1)} %bitcast.53, f32[48,128]{1,0:T(8,128)} %bitcast.47, ...), custom_call_target="tpu_custom_call" | custom-call | tf_op jit(solution)/shard_map/pallas_call | solution.py:72
  4.6 0.5 %collective-permute-start.2 = (bf16[1152,128]{1,0:T(8,128)(2,1)S(1)}, bf16[1152,128]{1,0:T(8,128)(2,1)S(1)}, u32[]{:S(2)}, u32[]{:S(2)}) collective-permute-start(bf16[1152,128]{1,0:T(8,128)(2,1)S(1)} %get-tuple-element.26), channel_id=1, source_target_pairs={{0,1},{1,0},{2,3},{3,2},{4,5},{5,4},{6,7},{7,6},{8,9},{9,8},{10,11... | collective-permute-start | bytes 884744 | tf_op jit(solution)/shard_map/ppermute | solution.py:356
  5.1 1.2 %collective-permute-done.2 = bf16[1152,128]{1,0:T(8,128)(2,1)S(1)} collective-permute-done((bf16[1152,128]{1,0:T(8,128)(2,1)S(1)}, bf16[1152,128]{1,0:T(8,128)(2,1)S(1)}, u32[]{:S(2)}, u32[]{:S(2)}) %collective-permute-start.2) | collective-permute-done | bytes 294944 | tf_op jit(solution)/shard_map/ppermute | solution.py:356
  6.4 3.9 %collective-permute-start.3 = (bf16[288,128]{1,0:T(8,128)(2,1)S(1)}, bf16[288,128]{1,0:T(8,128)(2,1)S(1)}, u32[]{:S(2)}, u32[]{:S(2)}) collective-permute-start(bf16[288,128]{1,0:T(8,128)(2,1)S(1)} %get-tuple-element.42), channel_id=1, source_target_pairs={{0,6},{1,7},{2,4},{3,5},{4,2},{5,3},{6,0},{7,1},{8,14},{9,15},{10,... | collective-permute-start | bytes 221192 | tf_op jit(solution)/shard_map/ppermute | solution.py:352
  10.3 0.4 collective-permute-start.5
  10.7 1.5 %collective-permute-start = (bf16[144,128]{1,0:T(8,128)(2,1)S(1)}, bf16[144,128]{1,0:T(8,128)(2,1)S(1)}, u32[]{:S(2)}, u32[]{:S(2)}) collective-permute-start(bf16[144,128]{1,0:T(8,128)(2,1)S(1)} %get-tuple-element.24.refs_0_), channel_id=1, source_target_pairs={{0,9},{1,8},{2,11},{3,10},{4,13},{5,12},{6,15},{7,14},{8,1},{9,0},... | collective-permute-start | bytes 110600 | tf_op jit(solution)/shard_map/ppermute | solution.py:352
  12.1 2.8 %collective-permute-start.1 = (bf16[144,128]{1,0:T(8,128)(2,1)S(1)}, bf16[144,128]{1,0:T(8,128)(2,1)S(1)}, u32[]{:S(2)}, u32[]{:S(2)}) collective-permute-start(bf16[144,128]{1,0:T(8,128)(2,1)S(1)} %get-tuple-element.24.refs_0_), channel_id=1, source_target_pairs={{0,17},{1,16},{2,19},{3,18},{4,21},{5,20},{6,23},{7,22},{8,25},{9,... | collective-permute-start | bytes 110600 | tf_op jit(solution)/shard_map/ppermute | solution.py:352
  15.0 1.6 %collective-permute-done.1.refs_2_ = bf16[144,128]{1,0:T(8,128)(2,1)S(1)} collective-permute-done((bf16[144,128]{1,0:T(8,128)(2,1)S(1)}, bf16[144,128]{1,0:T(8,128)(2,1)S(1)}, u32[]{:S(2)}, u32[]{:S(2)}) %collective-permute-start.1) | collective-permute-done | bytes 36896 | tf_op jit(solution)/shard_map/ppermute | solution.py:352
  16.7 1.3 %collective-permute-start.6 = (bf16[208,128]{1,0:T(8,128)(2,1)S(1)}, bf16[208,128]{1,0:T(8,128)(2,1)S(1)}, u32[]{:S(2)}, u32[]{:S(2)}) collective-permute-start(bf16[208,128]{1,0:T(8,128)(2,1)S(1)} %get-tuple-element.27.refs_0_), channel_id=1, source_target_pairs={{0,9},{1,8},{2,11},{3,10},{4,13},{5,12},{6,15},{7,14},{8,1},{9,0},... | collective-permute-start | bytes 159752 | tf_op jit(solution)/shard_map/ppermute | solution.py:352
  18.0 2.3 %collective-permute-done.6.refs_1_ = bf16[208,128]{1,0:T(8,128)(2,1)S(1)} collective-permute-done((bf16[208,128]{1,0:T(8,128)(2,1)S(1)}, bf16[208,128]{1,0:T(8,128)(2,1)S(1)}, u32[]{:S(2)}, u32[]{:S(2)}) %collective-permute-start.6) | collective-permute-done | bytes 53280 | tf_op jit(solution)/shard_map/ppermute | solution.py:352
  20.3 2.7 %collective-permute-start.7 = (bf16[208,128]{1,0:T(8,128)(2,1)S(1)}, bf16[208,128]{1,0:T(8,128)(2,1)S(1)}, u32[]{:S(2)}, u32[]{:S(2)}) collective-permute-start(bf16[208,128]{1,0:T(8,128)(2,1)S(1)} %shard_map.163.refs_0_), channel_id=1, source_target_pairs={{0,17},{1,16},{2,19},{3,18},{4,21},{5,20},{6,23},{7,22},{8,25},{9,... | collective-permute-start | bytes 159752 | tf_op jit(solution)/shard_map/ppermute | solution.py:352
  23.0 0.1 collective-permute-start.12
  23.1 1.7 %collective-permute-done.7.refs_1_ = bf16[208,128]{1,0:T(8,128)(2,1)S(1)} collective-permute-done((bf16[208,128]{1,0:T(8,128)(2,1)S(1)}, bf16[208,128]{1,0:T(8,128)(2,1)S(1)}, u32[]{:S(2)}, u32[]{:S(2)}) %collective-permute-start.7) | collective-permute-done | bytes 53280 | tf_op jit(solution)/shard_map/ppermute | solution.py:352
  24.9 3.8 %collective-permute-start.8 = (f32[8,128]{1,0:T(8,128)S(1)}, f32[8,128]{1,0:T(8,128)S(1)}, u32[]{:S(2)}, u32[]{:S(2)}) collective-permute-start(f32[8,128]{1,0:T(8,128)S(1)} %get-tuple-element.28), channel_id=1, source_target_pairs={{0,1},{1,0},{2,3},{3,2},{4,5},{5,4},{6,7},{7,6},{8,9},{9,8},{10,11... | collective-permute-start | bytes 12296 | tf_op jit(solution)/shard_map/ppermute | solution.py:356
  28.7 0.8 %collective-permute-done.8 = f32[8,128]{1,0:T(8,128)S(1)} collective-permute-done((f32[8,128]{1,0:T(8,128)S(1)}, f32[8,128]{1,0:T(8,128)S(1)}, u32[]{:S(2)}, u32[]{:S(2)}) %collective-permute-start.8) | collective-permute-done | bytes 4128 | tf_op jit(solution)/shard_map/ppermute | solution.py:356
  29.5 2.4 %collective-permute-start.10 = (f32[8,128]{1,0:T(8,128)S(1)}, f32[8,128]{1,0:T(8,128)S(1)}, u32[]{:S(2)}, u32[]{:S(2)}) collective-permute-start(f32[8,128]{1,0:T(8,128)S(1)} %add.19.refs_0_), channel_id=1, source_target_pairs={{0,6},{1,7},{2,4},{3,5},{4,2},{5,3},{6,0},{7,1},{8,14},{9,15},{10,... | collective-permute-start | bytes 12296 | tf_op jit(solution)/shard_map/ppermute | solution.py:352
  32.0 0.2 collective-permute-start.11
  32.1 0.6 %collective-permute-start.9 = (f32[8,128]{1,0:T(8,128)S(1)}, f32[8,128]{1,0:T(8,128)S(1)}, u32[]{:S(2)}, u32[]{:S(2)}) collective-permute-start(f32[8,128]{1,0:T(8,128)S(1)} %add.19.refs_0_), channel_id=1, source_target_pairs={{0,3},{1,2},{2,1},{3,0},{4,7},{5,6},{6,5},{7,4},{8,11},{9,10},{10,... | collective-permute-start | bytes 12296 | tf_op jit(solution)/shard_map/ppermute | solution.py:352
  32.7 1.3 %collective-permute-done.10.refs_2_ = f32[8,128]{1,0:T(8,128)S(1)} collective-permute-done((f32[8,128]{1,0:T(8,128)S(1)}, f32[8,128]{1,0:T(8,128)S(1)}, u32[]{:S(2)}, u32[]{:S(2)}) %collective-permute-start.10) | collective-permute-done | bytes 4128 | tf_op jit(solution)/shard_map/ppermute | solution.py:352
  34.0 1.0 %collective-permute-done.11.refs_3_ = f32[8,128]{1,0:T(8,128)S(1)} collective-permute-done((f32[8,128]{1,0:T(8,128)S(1)}, f32[8,128]{1,0:T(8,128)S(1)}, u32[]{:S(2)}, u32[]{:S(2)}) %collective-permute-start.11) | collective-permute-done | bytes 4128 | tf_op jit(solution)/shard_map/ppermute | solution.py:352
  35.0 0.2 collective-permute-done.9.refs_1_
  35.2 0.3 shard_map.166.refs_0_
  35.5 1.6 %collective-permute-start.13 = (bf16[288,128]{1,0:T(8,128)(2,1)S(1)}, bf16[288,128]{1,0:T(8,128)(2,1)S(1)}, u32[]{:S(2)}, u32[]{:S(2)}) collective-permute-start(bf16[288,128]{1,0:T(8,128)(2,1)S(1)} %shard_map.166.refs_0_), channel_id=1, source_target_pairs={{0,6},{1,7},{2,4},{3,5},{4,2},{5,3},{6,0},{7,1},{8,14},{9,15},{10,... | collective-permute-start | bytes 221192 | tf_op jit(solution)/shard_map/ppermute | solution.py:352
  37.0 0.3 collective-permute-start.14
  37.3 1.4 %collective-permute-start.15 = (bf16[288,128]{1,0:T(8,128)(2,1)S(1)}, bf16[288,128]{1,0:T(8,128)(2,1)S(1)}, u32[]{:S(2)}, u32[]{:S(2)}) collective-permute-start(bf16[288,128]{1,0:T(8,128)(2,1)S(1)} %shard_map.166.refs_0_), channel_id=1, source_target_pairs={{0,3},{1,2},{2,1},{3,0},{4,7},{5,6},{6,5},{7,4},{8,11},{9,10},{10,... | collective-permute-start | bytes 221192 | tf_op jit(solution)/shard_map/ppermute | solution.py:352
  38.7 0.2 collective-permute-start.16
  38.9 2.2 %collective-permute-done.13.refs_1_ = bf16[288,128]{1,0:T(8,128)(2,1)S(1)} collective-permute-done((bf16[288,128]{1,0:T(8,128)(2,1)S(1)}, bf16[288,128]{1,0:T(8,128)(2,1)S(1)}, u32[]{:S(2)}, u32[]{:S(2)}) %collective-permute-start.13) | collective-permute-done | bytes 73760 | tf_op jit(solution)/shard_map/ppermute | solution.py:352
  41.2 1.4 %collective-permute-done.14.refs_2_ = bf16[288,128]{1,0:T(8,128)(2,1)S(1)} collective-permute-done((bf16[288,128]{1,0:T(8,128)(2,1)S(1)}, bf16[288,128]{1,0:T(8,128)(2,1)S(1)}, u32[]{:S(2)}, u32[]{:S(2)}) %collective-permute-start.14) | collective-permute-done | bytes 73760 | tf_op jit(solution)/shard_map/ppermute | solution.py:352
  42.6 0.1 collective-permute-start.18
  42.7 0.4 collective-permute-start.19
  43.1 0.8 %shard_map.165 = (f32[48,128]{1,0:T(8,128)}, f32[48,128]{1,0:T(8,128)}, f32[48,128]{1,0:T(8,128)}, f32[96,128]{1,0:T(8,128)}, f32[96,128]{1,0:T(8,128)}, /*index=5*/f32[96,128]{1,0:T(8,128)}) custom-call(f32[8,128]{1,0:T(8,128)S(1)} %add.19.refs_0_, f32[8,128]{1,0:T(8,128)S(1)} %collective-permute-done.9.refs_1_, ...), custom_call_target="tpu_custom_call" | custom-call | tf_op jit(solution)/shard_map/pallas_call | solution.py:72
  44.0 1.2 %shard_map.167 = (bf16[32,6144]{1,0:T(8,128)(2,1)}, bf16[1,16,6144]{2,1,0:T(8,128)(2,1)}) custom-call(bf16[288,128]{1,0:T(8,128)(2,1)S(1)} %shard_map.166.refs_0_, bf16[288,128]{1,0:T(8,128)(2,1)S(1)} %collective-permute-done.13.refs_1_, bf16[288,128]{1,0:T(8,128)(2,1)S(1)} %collective-permute-done.14.refs_2_, ...), custom_call_target="tpu_custom_call" | custom-call | tf_op jit(solution)/shard_map/pallas_call | solution.py:72
  (29 shorter events, 0.3 us)
Async XLA Ops:
  4.6 30.6 %copy-start = (f32[1,2,6144]{2,1,0:T(2,128)S(1)}, f32[1,2,6144]{2,1,0:T(2,128)}, u32[]{:S(2)}) copy-start(f32[1,2,6144]{2,1,0:T(2,128)} %param.17) | copy-start | bytes 147460
  4.6 30.6 %copy-start.1 = (f32[1,2,6144]{2,1,0:T(2,128)S(1)}, f32[1,2,6144]{2,1,0:T(2,128)}, u32[]{:S(2)}) copy-start(f32[1,2,6144]{2,1,0:T(2,128)} %param.18) | copy-start | bytes 147460
  4.6 30.6 %copy-start.2 = (f32[1,2,6144]{2,1,0:T(2,128)S(1)}, f32[1,2,6144]{2,1,0:T(2,128)}, u32[]{:S(2)}) copy-start(f32[1,2,6144]{2,1,0:T(2,128)} %param.19) | copy-start | bytes 147460
  4.6 38.5 %copy-start.3 = (f32[1,6144]{1,0:T(1,128)S(1)}, f32[1,6144]{1,0:T(1,128)}, u32[]{:S(2)}) copy-start(f32[1,6144]{1,0:T(1,128)} %param.14) | copy-start | bytes 73732
  4.6 38.5 %copy-start.4 = (f32[1,6144]{1,0:T(1,128)S(1)}, f32[1,6144]{1,0:T(1,128)}, u32[]{:S(2)}) copy-start(f32[1,6144]{1,0:T(1,128)} %param.15) | copy-start | bytes 73732
  4.6 38.5 %copy-start.5 = (f32[1,6144]{1,0:T(1,128)S(1)}, f32[1,6144]{1,0:T(1,128)}, u32[]{:S(2)}) copy-start(f32[1,6144]{1,0:T(1,128)} %param.16) | copy-start | bytes 73732
  4.6 1.7 %collective-permute-start.2 = (bf16[1152,128]{1,0:T(8,128)(2,1)S(1)}, bf16[1152,128]{1,0:T(8,128)(2,1)S(1)}, u32[]{:S(2)}, u32[]{:S(2)}) collective-permute-start(bf16[1152,128]{1,0:T(8,128)(2,1)S(1)} %get-tuple-element.26), channel_id=1, source_target_pairs={{0,1},{1,0},{2,3},{3,2},{4,5},{5,4},{6,7},{7,6},{8,9},{9,8},{10,11... | collective-permute-start | bytes 884744 | tf_op jit(solution)/shard_map/ppermute | solution.py:356
  6.4 10.2 %collective-permute-start.3 = (bf16[288,128]{1,0:T(8,128)(2,1)S(1)}, bf16[288,128]{1,0:T(8,128)(2,1)S(1)}, u32[]{:S(2)}, u32[]{:S(2)}) collective-permute-start(bf16[288,128]{1,0:T(8,128)(2,1)S(1)} %get-tuple-element.42), channel_id=1, source_target_pairs={{0,6},{1,7},{2,4},{3,5},{4,2},{5,3},{6,0},{7,1},{8,14},{9,15},{10,... | collective-permute-start | bytes 221192 | tf_op jit(solution)/shard_map/ppermute | solution.py:352
  10.3 6.3 %collective-permute-start.4 = (bf16[288,128]{1,0:T(8,128)(2,1)S(1)}, bf16[288,128]{1,0:T(8,128)(2,1)S(1)}, u32[]{:S(2)}, u32[]{:S(2)}) collective-permute-start(bf16[288,128]{1,0:T(8,128)(2,1)S(1)} %get-tuple-element.41), channel_id=1, source_target_pairs={{0,5},{1,4},{2,7},{3,6},{4,1},{5,0},{6,3},{7,2},{8,13},{9,12},{10,... | collective-permute-start | bytes 221192 | tf_op jit(solution)/shard_map/ppermute | solution.py:352
  10.3 6.3 %collective-permute-start.5 = (bf16[288,128]{1,0:T(8,128)(2,1)S(1)}, bf16[288,128]{1,0:T(8,128)(2,1)S(1)}, u32[]{:S(2)}, u32[]{:S(2)}) collective-permute-start(bf16[288,128]{1,0:T(8,128)(2,1)S(1)} %get-tuple-element.40), channel_id=1, source_target_pairs={{0,3},{1,2},{2,1},{3,0},{4,7},{5,6},{6,5},{7,4},{8,11},{9,10},{10,... | collective-permute-start | bytes 221192 | tf_op jit(solution)/shard_map/ppermute | solution.py:352
  10.7 4.3 %collective-permute-start = (bf16[144,128]{1,0:T(8,128)(2,1)S(1)}, bf16[144,128]{1,0:T(8,128)(2,1)S(1)}, u32[]{:S(2)}, u32[]{:S(2)}) collective-permute-start(bf16[144,128]{1,0:T(8,128)(2,1)S(1)} %get-tuple-element.24.refs_0_), channel_id=1, source_target_pairs={{0,9},{1,8},{2,11},{3,10},{4,13},{5,12},{6,15},{7,14},{8,1},{9,0},... | collective-permute-start | bytes 110600 | tf_op jit(solution)/shard_map/ppermute | solution.py:352
  12.1 4.5 %collective-permute-start.1 = (bf16[144,128]{1,0:T(8,128)(2,1)S(1)}, bf16[144,128]{1,0:T(8,128)(2,1)S(1)}, u32[]{:S(2)}, u32[]{:S(2)}) collective-permute-start(bf16[144,128]{1,0:T(8,128)(2,1)S(1)} %get-tuple-element.24.refs_0_), channel_id=1, source_target_pairs={{0,17},{1,16},{2,19},{3,18},{4,21},{5,20},{6,23},{7,22},{8,25},{9,... | collective-permute-start | bytes 110600 | tf_op jit(solution)/shard_map/ppermute | solution.py:352
  16.7 3.6 %collective-permute-start.6 = (bf16[208,128]{1,0:T(8,128)(2,1)S(1)}, bf16[208,128]{1,0:T(8,128)(2,1)S(1)}, u32[]{:S(2)}, u32[]{:S(2)}) collective-permute-start(bf16[208,128]{1,0:T(8,128)(2,1)S(1)} %get-tuple-element.27.refs_0_), channel_id=1, source_target_pairs={{0,9},{1,8},{2,11},{3,10},{4,13},{5,12},{6,15},{7,14},{8,1},{9,0},... | collective-permute-start | bytes 159752 | tf_op jit(solution)/shard_map/ppermute | solution.py:352
  20.3 4.5 %collective-permute-start.7 = (bf16[208,128]{1,0:T(8,128)(2,1)S(1)}, bf16[208,128]{1,0:T(8,128)(2,1)S(1)}, u32[]{:S(2)}, u32[]{:S(2)}) collective-permute-start(bf16[208,128]{1,0:T(8,128)(2,1)S(1)} %shard_map.163.refs_0_), channel_id=1, source_target_pairs={{0,17},{1,16},{2,19},{3,18},{4,21},{5,20},{6,23},{7,22},{8,25},{9,... | collective-permute-start | bytes 159752 | tf_op jit(solution)/shard_map/ppermute | solution.py:352
  23.0 9.7 %collective-permute-start.12 = (bf16[144,128]{1,0:T(8,128)(2,1)S(1)}, bf16[144,128]{1,0:T(8,128)(2,1)S(1)}, u32[]{:S(2)}, u32[]{:S(2)}) collective-permute-start(bf16[144,128]{1,0:T(8,128)(2,1)S(1)} %collective-permute-done.refs_1_), channel_id=1, source_target_pairs={{0,17},{1,16},{2,19},{3,18},{4,21},{5,20},{6,23},{7,22},{8,25},{9,... | collective-permute-start | bytes 110600 | tf_op jit(solution)/shard_map/ppermute | solution.py:352
  24.9 4.6 %collective-permute-start.8 = (f32[8,128]{1,0:T(8,128)S(1)}, f32[8,128]{1,0:T(8,128)S(1)}, u32[]{:S(2)}, u32[]{:S(2)}) collective-permute-start(f32[8,128]{1,0:T(8,128)S(1)} %get-tuple-element.28), channel_id=1, source_target_pairs={{0,1},{1,0},{2,3},{3,2},{4,5},{5,4},{6,7},{7,6},{8,9},{9,8},{10,11... | collective-permute-start | bytes 12296 | tf_op jit(solution)/shard_map/ppermute | solution.py:356
  29.5 4.5 %collective-permute-start.10 = (f32[8,128]{1,0:T(8,128)S(1)}, f32[8,128]{1,0:T(8,128)S(1)}, u32[]{:S(2)}, u32[]{:S(2)}) collective-permute-start(f32[8,128]{1,0:T(8,128)S(1)} %add.19.refs_0_), channel_id=1, source_target_pairs={{0,6},{1,7},{2,4},{3,5},{4,2},{5,3},{6,0},{7,1},{8,14},{9,15},{10,... | collective-permute-start | bytes 12296 | tf_op jit(solution)/shard_map/ppermute | solution.py:352
  32.0 3.0 %collective-permute-start.11 = (f32[8,128]{1,0:T(8,128)S(1)}, f32[8,128]{1,0:T(8,128)S(1)}, u32[]{:S(2)}, u32[]{:S(2)}) collective-permute-start(f32[8,128]{1,0:T(8,128)S(1)} %add.19.refs_0_), channel_id=1, source_target_pairs={{0,5},{1,4},{2,7},{3,6},{4,1},{5,0},{6,3},{7,2},{8,13},{9,12},{10,... | collective-permute-start | bytes 12296 | tf_op jit(solution)/shard_map/ppermute | solution.py:352
  32.1 3.0 %collective-permute-start.9 = (f32[8,128]{1,0:T(8,128)S(1)}, f32[8,128]{1,0:T(8,128)S(1)}, u32[]{:S(2)}, u32[]{:S(2)}) collective-permute-start(f32[8,128]{1,0:T(8,128)S(1)} %add.19.refs_0_), channel_id=1, source_target_pairs={{0,3},{1,2},{2,1},{3,0},{4,7},{5,6},{6,5},{7,4},{8,11},{9,10},{10,... | collective-permute-start | bytes 12296 | tf_op jit(solution)/shard_map/ppermute | solution.py:352
  35.5 5.7 %collective-permute-start.13 = (bf16[288,128]{1,0:T(8,128)(2,1)S(1)}, bf16[288,128]{1,0:T(8,128)(2,1)S(1)}, u32[]{:S(2)}, u32[]{:S(2)}) collective-permute-start(bf16[288,128]{1,0:T(8,128)(2,1)S(1)} %shard_map.166.refs_0_), channel_id=1, source_target_pairs={{0,6},{1,7},{2,4},{3,5},{4,2},{5,3},{6,0},{7,1},{8,14},{9,15},{10,... | collective-permute-start | bytes 221192 | tf_op jit(solution)/shard_map/ppermute | solution.py:352
  37.0 5.6 %collective-permute-start.14 = (bf16[288,128]{1,0:T(8,128)(2,1)S(1)}, bf16[288,128]{1,0:T(8,128)(2,1)S(1)}, u32[]{:S(2)}, u32[]{:S(2)}) collective-permute-start(bf16[288,128]{1,0:T(8,128)(2,1)S(1)} %shard_map.166.refs_0_), channel_id=1, source_target_pairs={{0,5},{1,4},{2,7},{3,6},{4,1},{5,0},{6,3},{7,2},{8,13},{9,12},{10,... | collective-permute-start | bytes 221192 | tf_op jit(solution)/shard_map/ppermute | solution.py:352
  37.3 5.4 %collective-permute-start.15 = (bf16[288,128]{1,0:T(8,128)(2,1)S(1)}, bf16[288,128]{1,0:T(8,128)(2,1)S(1)}, u32[]{:S(2)}, u32[]{:S(2)}) collective-permute-start(bf16[288,128]{1,0:T(8,128)(2,1)S(1)} %shard_map.166.refs_0_), channel_id=1, source_target_pairs={{0,3},{1,2},{2,1},{3,0},{4,7},{5,6},{6,5},{7,4},{8,11},{9,10},{10,... | collective-permute-start | bytes 221192 | tf_op jit(solution)/shard_map/ppermute | solution.py:352
  38.7 5.2 %collective-permute-start.16 = (bf16[288,128]{1,0:T(8,128)(2,1)S(1)}, bf16[288,128]{1,0:T(8,128)(2,1)S(1)}, u32[]{:S(2)}, u32[]{:S(2)}) collective-permute-start(bf16[288,128]{1,0:T(8,128)(2,1)S(1)} %shard_map.166.refs_0_), channel_id=1, source_target_pairs={{0,1},{1,0},{2,3},{3,2},{4,5},{5,4},{6,7},{7,6},{8,9},{9,8},{10,11... | collective-permute-start | bytes 221192 | tf_op jit(solution)/shard_map/ppermute | solution.py:356
  41.2 2.8 %collective-permute-start.17 = (bf16[288,128]{1,0:T(8,128)(2,1)S(1)}, bf16[288,128]{1,0:T(8,128)(2,1)S(1)}, u32[]{:S(2)}, u32[]{:S(2)}) collective-permute-start(bf16[288,128]{1,0:T(8,128)(2,1)S(1)} %collective-permute-done.13.refs_1_), channel_id=1, source_target_pairs={{0,1},{1,0},{2,3},{3,2},{4,5},{5,4},{6,7},{7,6},{8,9},{9,8},{10,11... | collective-permute-start | bytes 221192 | tf_op jit(solution)/shard_map/ppermute | solution.py:356
  42.6 1.4 %collective-permute-start.18 = (bf16[288,128]{1,0:T(8,128)(2,1)S(1)}, bf16[288,128]{1,0:T(8,128)(2,1)S(1)}, u32[]{:S(2)}, u32[]{:S(2)}) collective-permute-start(bf16[288,128]{1,0:T(8,128)(2,1)S(1)} %collective-permute-done.14.refs_2_), channel_id=1, source_target_pairs={{0,1},{1,0},{2,3},{3,2},{4,5},{5,4},{6,7},{7,6},{8,9},{9,8},{10,11... | collective-permute-start | bytes 221192 | tf_op jit(solution)/shard_map/ppermute | solution.py:356
  42.7 1.3 %collective-permute-start.19 = (bf16[288,128]{1,0:T(8,128)(2,1)S(1)}, bf16[288,128]{1,0:T(8,128)(2,1)S(1)}, u32[]{:S(2)}, u32[]{:S(2)}) collective-permute-start(bf16[288,128]{1,0:T(8,128)(2,1)S(1)} %collective-permute-done.15.refs_3_), channel_id=1, source_target_pairs={{0,1},{1,0},{2,3},{3,2},{4,5},{5,4},{6,7},{7,6},{8,9},{9,8},{10,11... | collective-permute-start | bytes 221192 | tf_op jit(solution)/shard_map/ppermute | solution.py:356

commit v14 on v12

--- a/solution.py
+++ b/solution.py
@@ -85,7 +85,7 @@
     return jnp.sum(value.reshape(-1, 8, LANES), axis=0)
 
 
-STEPS = 4
+STEPS = 3
 
 
 def each(count, step, unrolled):
@@ -133,19 +133,37 @@
     left_a = dot(pick(plan.n_expert * plan.rows_a, plan.rows_a, act_a.shape[0], None), act_a_v[...]).astype(bf16)
     left_e = dot(pick(plan.rows_e, plan.rows_e, act_e.shape[0], me_ex), act_e_v[...]).astype(bf16)
     n_dp = plan.n_dp
+
+    def turn(start, pieces):
+        value = jnp.stack(pieces).transpose(1, 0, 2)
+        for c in range(plan.chips):
+            rows = pl.ds(c * plan.chunk + start, len(pieces))
+            full[rows, :] = value[c]
+            send[rows, :] = value[plan.chips + c].astype(bf16)
+
     for t in range(STEPS):
         cols = pl.ds(t * tile, tile)
         big[2 * t].wait()
         terms_a = dot(left_a, dy_a_v[:, cols])
         big[2 * t + 1].wait()
         terms_e = dot(left_e, dy_e_v[:, cols])
-        for b in range(tile // LANES):
-            attn, exp = plan.places(t * (tile // LANES) + b)
+        count = tile // LANES
+        if plan.turned:
+            blocks = [slice(b * LANES, (b + 1) * LANES) for b in range(count)]
+            for e in range(plan.n_expert):
+                turn(e * plan.size_a + t * count, [terms_a[e * n_dp : (e + 1) * n_dp, span] for span in blocks])
+            pieces = [
+                terms_e[r * n_dp : (r + 1) * n_dp, span] for span in blocks for r in range(plan.rows_e)
+            ]
+            turn(plan.all_a + t * count * plan.rows_e, pieces)
+            continue
+        for b in range(count):
+            attn, exp = plan.places(t * count + b)
             span = slice(b * LANES, (b + 1) * LANES)
             for terms, places in ((terms_a, attn), (terms_e, exp)):
                 for group, start in places:
                     full[pl.ds(start, n_dp, stride=plan.chunk), :] = terms[group * n_dp : (group + 1) * n_dp, span]
-    for c in range(plan.chips):
+    for c in range(0 if plan.turned else plan.chips):
         send[pl.ds(c * plan.chunk, plan.chunk), :] = full[
             pl.ds((plan.chips + c) * plan.chunk, plan.chunk), :
         ].astype(bf16)
@@ -162,7 +180,7 @@
     return call(
         lambda *refs: terms_kernel(plan, *refs),
         args,
-        [((2 * half, LANES), f32), ((half, LANES), bf16), ((3 * plan.size_a, LANES), bf16)],
+        [((half if plan.turned else 2 * half, LANES), f32), ((half, LANES), bf16), ((3 * plan.size_a, LANES), bf16)],
         [
             (act_a.shape, bf16),
             (dy_a.shape, bf16),
@@ -255,7 +273,7 @@
     me_ex = lax.axis_index("expert")
     my_role = role_of(me // 2, me % 2, me_ex)
     for i, part in enumerate(parts):
-        chip, role = (-i % plan.chips) ^ (me // 2), (i // plan.chips) ^ my_role
+        chip, role = (i % plan.chips) ^ (me // 2), (i // plan.chips) ^ my_role
         blocks = [(e, e * plan.size_a, plan.size_a) for e in range(plan.n_expert)]
         for expert, start, size in blocks + [(me_ex, plan.all_a, plan.size_e)]:
             owner = 2 * chip + role_of(chip, role, expert)
@@ -392,9 +410,7 @@
         (payload,) = call(lambda *refs: again_kernel(plan, *refs), [payload, other], [shared])
         distance *= 2
     other = swap(payload, experts=distance)
-    far = []
-    for step in (2**i for i in range(1, n_expert.bit_length() - 1)):
-        far += [swap(value, experts=step) for value in packs + far]
+    far = [swap(pack, experts=q) for q in range(2, n_expert)]
     g_attn, square = call(
         lambda *refs: last_kernel(plan, *refs), [payload, other], [((plan.all_a, LANES), f32), ((8, LANES), f32)]
     )
@@ -411,7 +427,7 @@
         [*squares, g_attn, g_exp, *state_a, *state_e],
         [block_a] * 3 + [block_e] * 3,
     )
-    near = [mine] + [swap(mine, chips=c) for c in reversed(range(1, chips))]
+    near = [mine] + [swap(mine, chips=c) for c in range(1, chips)]
     far = [swap_cores(piece) for piece in near]
     attn_full, expert_full = put_in_order(plan, near + far)
     new_a = [from_blocks(value, rows_a) for value in (wa, ma, va)]

time: 42.6 us -> 41.2 us (0.967)
  the two profiles are of different devices: /device:TPU:25 before, /device:TPU:0 now
where the time goes in v14:
time: 41.2 us; the launch traced here: 41.1 us
  starting transfers between devices  21.2 us (51%)
  waiting for transfers between devices  13.5 us (33%)
  Pallas kernels  5.44 us (13%)
  between operations  0.75 us (2%)
    ppermute x14, starting transfers between devices, swap(): return lax.ppermute(value, ('expert', 'dp'), pairs)  19.7 us
    ppermute x14, waiting for transfers between devices, swap(): return lax.ppermute(value, ('expert', 'dp'), pairs)  10.9 us
    pallas_call x7, Pallas kernels, call(): pl.pallas_call(kernel, in_specs=[pl.BlockSpec(memory_space=in_space)] * l...  5.44 us
    ppermute x6, waiting for transfers between devices, swap_cores(): lax.ppermute(value, 'dp', [(i, i ^ 1) for i in range(lax.axis_size('dp'))])  2.61 us
    ppermute x6, starting transfers between devices, swap_cores(): lax.ppermute(value, 'dp', [(i, i ^ 1) for i in range(lax.axis_size('dp'))])  1.51 us
  transfers between devices with their start and end apart: 20, of which 13 were waited for; matrix products, arithmetic and copies ran while one was open for 0% of the time, Pallas kernels for 2%

profile of v14, /device:TPU:0, one launch (start us, length us, event | category | flops | bytes accessed | tf_op | source)
XLA Modules:
  0.0 41.1 jit_solution(5117596845790162859)
XLA Ops:
  0.7 3.0 %shard_map.161 = (f32[1152,128]{1,0:T(8,128)S(1)}, bf16[1152,128]{1,0:T(8,128)(2,1)S(1)}, bf16[144,128]{1,0:T(8,128)(2,1)S(1)}) custom-call(bf16[32,256]{1,0:T(8,128)(2,1)} %bitcast.54, bf16[256,6144]{1,0:T(8,128)(2,1)} %refs_1_.1, bf16[16,128]{1,0:T(8,128)(2,1)} %bitcast.55, bf16[128,6144]{1,0:T(8,128)(2,1)} %bitcast.53, f32[48,128]{1,0:T(8,128)} %bitcast.47, ...), custom_call_target="tpu_custom_call" | custom-call | tf_op jit(solution)/shard_map/pallas_call | solution.py:69
  3.8 0.5 %collective-permute-start.1 = (bf16[1152,128]{1,0:T(8,128)(2,1)S(1)}, bf16[1152,128]{1,0:T(8,128)(2,1)S(1)}, u32[]{:S(2)}, u32[]{:S(2)}) collective-permute-start(bf16[1152,128]{1,0:T(8,128)(2,1)S(1)} %get-tuple-element.26), channel_id=1, source_target_pairs={{0,1},{1,0},{2,3},{3,2},{4,5},{5,4},{6,7},{7,6},{8,9},{9,8},{10,11... | collective-permute-start | bytes 884744 | tf_op jit(solution)/shard_map/ppermute | solution.py:369
  4.3 1.2 %collective-permute-done.1 = bf16[1152,128]{1,0:T(8,128)(2,1)S(1)} collective-permute-done((bf16[1152,128]{1,0:T(8,128)(2,1)S(1)}, bf16[1152,128]{1,0:T(8,128)(2,1)S(1)}, u32[]{:S(2)}, u32[]{:S(2)}) %collective-permute-start.1) | collective-permute-done | bytes 294944 | tf_op jit(solution)/shard_map/ppermute | solution.py:369
  5.6 3.6 %collective-permute-start.2 = (bf16[288,128]{1,0:T(8,128)(2,1)S(1)}, bf16[288,128]{1,0:T(8,128)(2,1)S(1)}, u32[]{:S(2)}, u32[]{:S(2)}) collective-permute-start(bf16[288,128]{1,0:T(8,128)(2,1)S(1)} %get-tuple-element.42), channel_id=1, source_target_pairs={{0,7},{1,6},{2,5},{3,4},{4,3},{5,2},{6,1},{7,0},{8,15},{9,14},{10,... | collective-permute-start | bytes 221192 | tf_op jit(solution)/shard_map/ppermute | solution.py:365
  9.2 0.5 %collective-permute-start.3 = (bf16[288,128]{1,0:T(8,128)(2,1)S(1)}, bf16[288,128]{1,0:T(8,128)(2,1)S(1)}, u32[]{:S(2)}, u32[]{:S(2)}) collective-permute-start(bf16[288,128]{1,0:T(8,128)(2,1)S(1)} %get-tuple-element.41), channel_id=1, source_target_pairs={{0,4},{1,5},{2,6},{3,7},{4,0},{5,1},{6,2},{7,3},{8,12},{9,13},{10,... | collective-permute-start | bytes 221192 | tf_op jit(solution)/shard_map/ppermute | solution.py:365
  9.7 1.8 %collective-permute-start = (bf16[144,128]{1,0:T(8,128)(2,1)S(1)}, bf16[144,128]{1,0:T(8,128)(2,1)S(1)}, u32[]{:S(2)}, u32[]{:S(2)}) collective-permute-start(bf16[144,128]{1,0:T(8,128)(2,1)S(1)} %get-tuple-element.24.refs_0_), channel_id=1, source_target_pairs={{0,9},{1,8},{2,11},{3,10},{4,13},{5,12},{6,15},{7,14},{8,1},{9,0},... | collective-permute-start | bytes 110600 | tf_op jit(solution)/shard_map/ppermute | solution.py:365
  11.5 1.6 %collective-permute-done.refs_1_ = bf16[144,128]{1,0:T(8,128)(2,1)S(1)} collective-permute-done((bf16[144,128]{1,0:T(8,128)(2,1)S(1)}, bf16[144,128]{1,0:T(8,128)(2,1)S(1)}, u32[]{:S(2)}, u32[]{:S(2)}) %collective-permute-start) | collective-permute-done | bytes 36896 | tf_op jit(solution)/shard_map/ppermute | solution.py:365
  13.2 0.5 %collective-permute-done.3.refs_4_ = bf16[288,128]{1,0:T(8,128)(2,1)S(1)} collective-permute-done((bf16[288,128]{1,0:T(8,128)(2,1)S(1)}, bf16[288,128]{1,0:T(8,128)(2,1)S(1)}, u32[]{:S(2)}, u32[]{:S(2)}) %collective-permute-start.3) | collective-permute-done | bytes 73760 | tf_op jit(solution)/shard_map/ppermute | solution.py:365
  13.7 0.3 collective-permute-done.4.refs_5_
  14.1 1.4 %collective-permute-start.5 = (bf16[208,128]{1,0:T(8,128)(2,1)S(1)}, bf16[208,128]{1,0:T(8,128)(2,1)S(1)}, u32[]{:S(2)}, u32[]{:S(2)}) collective-permute-start(bf16[208,128]{1,0:T(8,128)(2,1)S(1)} %get-tuple-element.27.refs_0_), channel_id=1, source_target_pairs={{0,9},{1,8},{2,11},{3,10},{4,13},{5,12},{6,15},{7,14},{8,1},{9,0},... | collective-permute-start | bytes 159752 | tf_op jit(solution)/shard_map/ppermute | solution.py:365
  15.4 2.5 %collective-permute-done.5.refs_1_ = bf16[208,128]{1,0:T(8,128)(2,1)S(1)} collective-permute-done((bf16[208,128]{1,0:T(8,128)(2,1)S(1)}, bf16[208,128]{1,0:T(8,128)(2,1)S(1)}, u32[]{:S(2)}, u32[]{:S(2)}) %collective-permute-start.5) | collective-permute-done | bytes 53280 | tf_op jit(solution)/shard_map/ppermute | solution.py:365
  18.0 2.4 %collective-permute-start.6 = (bf16[208,128]{1,0:T(8,128)(2,1)S(1)}, bf16[208,128]{1,0:T(8,128)(2,1)S(1)}, u32[]{:S(2)}, u32[]{:S(2)}) collective-permute-start(bf16[208,128]{1,0:T(8,128)(2,1)S(1)} %shard_map.163.refs_0_), channel_id=1, source_target_pairs={{0,17},{1,16},{2,19},{3,18},{4,21},{5,20},{6,23},{7,22},{8,25},{9,... | collective-permute-start | bytes 159752 | tf_op jit(solution)/shard_map/ppermute | solution.py:365
  20.4 0.3 collective-permute-start.11
  20.7 3.7 %collective-permute-start.12 = (bf16[144,128]{1,0:T(8,128)(2,1)S(1)}, bf16[144,128]{1,0:T(8,128)(2,1)S(1)}, u32[]{:S(2)}, u32[]{:S(2)}) collective-permute-start(bf16[144,128]{1,0:T(8,128)(2,1)S(1)} %get-tuple-element.24.refs_0_), channel_id=1, source_target_pairs={{0,24},{1,25},{2,26},{3,27},{4,28},{5,29},{6,30},{7,31},{8,16},{9,... | collective-permute-start | bytes 110600 | tf_op jit(solution)/shard_map/ppermute | solution.py:365
  24.5 1.2 %collective-permute-done.7 = f32[8,128]{1,0:T(8,128)S(1)} collective-permute-done((f32[8,128]{1,0:T(8,128)S(1)}, f32[8,128]{1,0:T(8,128)S(1)}, u32[]{:S(2)}, u32[]{:S(2)}) %collective-permute-start.7) | collective-permute-done | bytes 4128 | tf_op jit(solution)/shard_map/ppermute | solution.py:369
  25.6 1.2 %collective-permute-start.10 = (f32[8,128]{1,0:T(8,128)S(1)}, f32[8,128]{1,0:T(8,128)S(1)}, u32[]{:S(2)}, u32[]{:S(2)}) collective-permute-start(f32[8,128]{1,0:T(8,128)S(1)} %add.19.refs_0_), channel_id=1, source_target_pairs={{0,7},{1,6},{2,5},{3,4},{4,3},{5,2},{6,1},{7,0},{8,15},{9,14},{10,... | collective-permute-start | bytes 12296 | tf_op jit(solution)/shard_map/ppermute | solution.py:365
  26.8 1.5 %collective-permute-start.8 = (f32[8,128]{1,0:T(8,128)S(1)}, f32[8,128]{1,0:T(8,128)S(1)}, u32[]{:S(2)}, u32[]{:S(2)}) collective-permute-start(f32[8,128]{1,0:T(8,128)S(1)} %add.19.refs_0_), channel_id=1, source_target_pairs={{0,4},{1,5},{2,6},{3,7},{4,0},{5,1},{6,2},{7,3},{8,12},{9,13},{10,... | collective-permute-start | bytes 12296 | tf_op jit(solution)/shard_map/ppermute | solution.py:365
  28.4 0.2 collective-permute-start.9
  28.6 1.0 %collective-permute-done.10.refs_3_ = f32[8,128]{1,0:T(8,128)S(1)} collective-permute-done((f32[8,128]{1,0:T(8,128)S(1)}, f32[8,128]{1,0:T(8,128)S(1)}, u32[]{:S(2)}, u32[]{:S(2)}) %collective-permute-start.10) | collective-permute-done | bytes 4128 | tf_op jit(solution)/shard_map/ppermute | solution.py:365
  29.6 0.9 %collective-permute-done.8.refs_1_ = f32[8,128]{1,0:T(8,128)S(1)} collective-permute-done((f32[8,128]{1,0:T(8,128)S(1)}, f32[8,128]{1,0:T(8,128)S(1)}, u32[]{:S(2)}, u32[]{:S(2)}) %collective-permute-start.8) | collective-permute-done | bytes 4128 | tf_op jit(solution)/shard_map/ppermute | solution.py:365
  30.4 0.9 %collective-permute-done.9.refs_2_ = f32[8,128]{1,0:T(8,128)S(1)} collective-permute-done((f32[8,128]{1,0:T(8,128)S(1)}, f32[8,128]{1,0:T(8,128)S(1)}, u32[]{:S(2)}, u32[]{:S(2)}) %collective-permute-start.9) | collective-permute-done | bytes 4128 | tf_op jit(solution)/shard_map/ppermute | solution.py:365
  31.4 0.3 shard_map.166.refs_0_
  31.7 0.3 collective-permute-start.13
  32.0 1.5 %collective-permute-start.14 = (bf16[288,128]{1,0:T(8,128)(2,1)S(1)}, bf16[288,128]{1,0:T(8,128)(2,1)S(1)}, u32[]{:S(2)}, u32[]{:S(2)}) collective-permute-start(bf16[288,128]{1,0:T(8,128)(2,1)S(1)} %shard_map.166.refs_0_), channel_id=1, source_target_pairs={{0,4},{1,5},{2,6},{3,7},{4,0},{5,1},{6,2},{7,3},{8,12},{9,13},{10,... | collective-permute-start | bytes 221192 | tf_op jit(solution)/shard_map/ppermute | solution.py:365
  33.5 1.2 %collective-permute-start.15 = (bf16[288,128]{1,0:T(8,128)(2,1)S(1)}, bf16[288,128]{1,0:T(8,128)(2,1)S(1)}, u32[]{:S(2)}, u32[]{:S(2)}) collective-permute-start(bf16[288,128]{1,0:T(8,128)(2,1)S(1)} %shard_map.166.refs_0_), channel_id=1, source_target_pairs={{0,7},{1,6},{2,5},{3,4},{4,3},{5,2},{6,1},{7,0},{8,15},{9,14},{10,... | collective-permute-start | bytes 221192 | tf_op jit(solution)/shard_map/ppermute | solution.py:365
  34.7 0.4 collective-permute-start.16
  35.1 0.9 %collective-permute-done.13.refs_1_ = bf16[288,128]{1,0:T(8,128)(2,1)S(1)} collective-permute-done((bf16[288,128]{1,0:T(8,128)(2,1)S(1)}, bf16[288,128]{1,0:T(8,128)(2,1)S(1)}, u32[]{:S(2)}, u32[]{:S(2)}) %collective-permute-start.13) | collective-permute-done | bytes 73760 | tf_op jit(solution)/shard_map/ppermute | solution.py:365
  36.0 0.4 %collective-permute-start.17 = (bf16[288,128]{1,0:T(8,128)(2,1)S(1)}, bf16[288,128]{1,0:T(8,128)(2,1)S(1)}, u32[]{:S(2)}, u32[]{:S(2)}) collective-permute-start(bf16[288,128]{1,0:T(8,128)(2,1)S(1)} %collective-permute-done.13.refs_1_), channel_id=1, source_target_pairs={{0,1},{1,0},{2,3},{3,2},{4,5},{5,4},{6,7},{7,6},{8,9},{9,8},{10,11... | collective-permute-start | bytes 221192 | tf_op jit(solution)/shard_map/ppermute | solution.py:369
  36.6 2.0 %collective-permute-done.15.refs_3_ = bf16[288,128]{1,0:T(8,128)(2,1)S(1)} collective-permute-done((bf16[288,128]{1,0:T(8,128)(2,1)S(1)}, bf16[288,128]{1,0:T(8,128)(2,1)S(1)}, u32[]{:S(2)}, u32[]{:S(2)}) %collective-permute-start.15) | collective-permute-done | bytes 73760 | tf_op jit(solution)/shard_map/ppermute | solution.py:365
  38.8 0.8 %shard_map.165 = (f32[48,128]{1,0:T(8,128)}, f32[48,128]{1,0:T(8,128)}, f32[48,128]{1,0:T(8,128)}, f32[96,128]{1,0:T(8,128)}, f32[96,128]{1,0:T(8,128)}, /*index=5*/f32[96,128]{1,0:T(8,128)}) custom-call(f32[8,128]{1,0:T(8,128)S(1)} %add.19.refs_0_, f32[8,128]{1,0:T(8,128)S(1)} %collective-permute-done.8.refs_1_, ...), custom_call_target="tpu_custom_call" | custom-call | tf_op jit(solution)/shard_map/pallas_call | solution.py:69
  39.6 0.2 collective-permute-done.19.refs_7_
  39.9 1.2 %shard_map.167 = (bf16[32,6144]{1,0:T(8,128)(2,1)}, bf16[1,16,6144]{2,1,0:T(8,128)(2,1)}) custom-call(bf16[288,128]{1,0:T(8,128)(2,1)S(1)} %shard_map.166.refs_0_, bf16[288,128]{1,0:T(8,128)(2,1)S(1)} %collective-permute-done.13.refs_1_, bf16[288,128]{1,0:T(8,128)(2,1)S(1)} %collective-permute-done.14.refs_2_, ...), custom_call_target="tpu_custom_call" | custom-call | tf_op jit(solution)/shard_map/pallas_call | solution.py:69
  (29 shorter events, 0.6 us)
Async XLA Ops:
  0.6 30.8 %copy-start = (f32[1,2,6144]{2,1,0:T(2,128)S(1)}, f32[1,2,6144]{2,1,0:T(2,128)}, u32[]{:S(2)}) copy-start(f32[1,2,6144]{2,1,0:T(2,128)} %param.17) | copy-start | bytes 147460
  0.6 30.7 %copy-start.1 = (f32[1,2,6144]{2,1,0:T(2,128)S(1)}, f32[1,2,6144]{2,1,0:T(2,128)}, u32[]{:S(2)}) copy-start(f32[1,2,6144]{2,1,0:T(2,128)} %param.18) | copy-start | bytes 147460
  0.7 30.7 %copy-start.2 = (f32[1,2,6144]{2,1,0:T(2,128)S(1)}, f32[1,2,6144]{2,1,0:T(2,128)}, u32[]{:S(2)}) copy-start(f32[1,2,6144]{2,1,0:T(2,128)} %param.19) | copy-start | bytes 147460
  0.7 38.1 %copy-start.3 = (f32[1,6144]{1,0:T(1,128)S(1)}, f32[1,6144]{1,0:T(1,128)}, u32[]{:S(2)}) copy-start(f32[1,6144]{1,0:T(1,128)} %param.14) | copy-start | bytes 73732
  0.7 38.1 %copy-start.4 = (f32[1,6144]{1,0:T(1,128)S(1)}, f32[1,6144]{1,0:T(1,128)}, u32[]{:S(2)}) copy-start(f32[1,6144]{1,0:T(1,128)} %param.15) | copy-start | bytes 73732
  0.7 38.1 %copy-start.5 = (f32[1,6144]{1,0:T(1,128)S(1)}, f32[1,6144]{1,0:T(1,128)}, u32[]{:S(2)}) copy-start(f32[1,6144]{1,0:T(1,128)} %param.16) | copy-start | bytes 73732
  3.8 1.7 %collective-permute-start.1 = (bf16[1152,128]{1,0:T(8,128)(2,1)S(1)}, bf16[1152,128]{1,0:T(8,128)(2,1)S(1)}, u32[]{:S(2)}, u32[]{:S(2)}) collective-permute-start(bf16[1152,128]{1,0:T(8,128)(2,1)S(1)} %get-tuple-element.26), channel_id=1, source_target_pairs={{0,1},{1,0},{2,3},{3,2},{4,5},{5,4},{6,7},{7,6},{8,9},{9,8},{10,11... | collective-permute-start | bytes 884744 | tf_op jit(solution)/shard_map/ppermute | solution.py:369
  5.6 7.6 %collective-permute-start.2 = (bf16[288,128]{1,0:T(8,128)(2,1)S(1)}, bf16[288,128]{1,0:T(8,128)(2,1)S(1)}, u32[]{:S(2)}, u32[]{:S(2)}) collective-permute-start(bf16[288,128]{1,0:T(8,128)(2,1)S(1)} %get-tuple-element.42), channel_id=1, source_target_pairs={{0,7},{1,6},{2,5},{3,4},{4,3},{5,2},{6,1},{7,0},{8,15},{9,14},{10,... | collective-permute-start | bytes 221192 | tf_op jit(solution)/shard_map/ppermute | solution.py:365
  9.2 4.5 %collective-permute-start.3 = (bf16[288,128]{1,0:T(8,128)(2,1)S(1)}, bf16[288,128]{1,0:T(8,128)(2,1)S(1)}, u32[]{:S(2)}, u32[]{:S(2)}) collective-permute-start(bf16[288,128]{1,0:T(8,128)(2,1)S(1)} %get-tuple-element.41), channel_id=1, source_target_pairs={{0,4},{1,5},{2,6},{3,7},{4,0},{5,1},{6,2},{7,3},{8,12},{9,13},{10,... | collective-permute-start | bytes 221192 | tf_op jit(solution)/shard_map/ppermute | solution.py:365
  9.7 4.3 %collective-permute-start.4 = (bf16[288,128]{1,0:T(8,128)(2,1)S(1)}, bf16[288,128]{1,0:T(8,128)(2,1)S(1)}, u32[]{:S(2)}, u32[]{:S(2)}) collective-permute-start(bf16[288,128]{1,0:T(8,128)(2,1)S(1)} %get-tuple-element.40), channel_id=1, source_target_pairs={{0,3},{1,2},{2,1},{3,0},{4,7},{5,6},{6,5},{7,4},{8,11},{9,10},{10,... | collective-permute-start | bytes 221192 | tf_op jit(solution)/shard_map/ppermute | solution.py:365
  9.7 3.5 %collective-permute-start = (bf16[144,128]{1,0:T(8,128)(2,1)S(1)}, bf16[144,128]{1,0:T(8,128)(2,1)S(1)}, u32[]{:S(2)}, u32[]{:S(2)}) collective-permute-start(bf16[144,128]{1,0:T(8,128)(2,1)S(1)} %get-tuple-element.24.refs_0_), channel_id=1, source_target_pairs={{0,9},{1,8},{2,11},{3,10},{4,13},{5,12},{6,15},{7,14},{8,1},{9,0},... | collective-permute-start | bytes 110600 | tf_op jit(solution)/shard_map/ppermute | solution.py:365
  14.1 3.9 %collective-permute-start.5 = (bf16[208,128]{1,0:T(8,128)(2,1)S(1)}, bf16[208,128]{1,0:T(8,128)(2,1)S(1)}, u32[]{:S(2)}, u32[]{:S(2)}) collective-permute-start(bf16[208,128]{1,0:T(8,128)(2,1)S(1)} %get-tuple-element.27.refs_0_), channel_id=1, source_target_pairs={{0,9},{1,8},{2,11},{3,10},{4,13},{5,12},{6,15},{7,14},{8,1},{9,0},... | collective-permute-start | bytes 159752 | tf_op jit(solution)/shard_map/ppermute | solution.py:365
  18.0 6.4 %collective-permute-start.6 = (bf16[208,128]{1,0:T(8,128)(2,1)S(1)}, bf16[208,128]{1,0:T(8,128)(2,1)S(1)}, u32[]{:S(2)}, u32[]{:S(2)}) collective-permute-start(bf16[208,128]{1,0:T(8,128)(2,1)S(1)} %shard_map.163.refs_0_), channel_id=1, source_target_pairs={{0,17},{1,16},{2,19},{3,18},{4,21},{5,20},{6,23},{7,22},{8,25},{9,... | collective-permute-start | bytes 159752 | tf_op jit(solution)/shard_map/ppermute | solution.py:365
  20.4 8.2 %collective-permute-start.11 = (bf16[144,128]{1,0:T(8,128)(2,1)S(1)}, bf16[144,128]{1,0:T(8,128)(2,1)S(1)}, u32[]{:S(2)}, u32[]{:S(2)}) collective-permute-start(bf16[144,128]{1,0:T(8,128)(2,1)S(1)} %get-tuple-element.24.refs_0_), channel_id=1, source_target_pairs={{0,17},{1,16},{2,19},{3,18},{4,21},{5,20},{6,23},{7,22},{8,25},{9,... | collective-permute-start | bytes 110600 | tf_op jit(solution)/shard_map/ppermute | solution.py:365
  20.7 7.9 %collective-permute-start.12 = (bf16[144,128]{1,0:T(8,128)(2,1)S(1)}, bf16[144,128]{1,0:T(8,128)(2,1)S(1)}, u32[]{:S(2)}, u32[]{:S(2)}) collective-permute-start(bf16[144,128]{1,0:T(8,128)(2,1)S(1)} %get-tuple-element.24.refs_0_), channel_id=1, source_target_pairs={{0,24},{1,25},{2,26},{3,27},{4,28},{5,29},{6,30},{7,31},{8,16},{9,... | collective-permute-start | bytes 110600 | tf_op jit(solution)/shard_map/ppermute | solution.py:365
  24.4 1.2 %collective-permute-start.7 = (f32[8,128]{1,0:T(8,128)S(1)}, f32[8,128]{1,0:T(8,128)S(1)}, u32[]{:S(2)}, u32[]{:S(2)}) collective-permute-start(f32[8,128]{1,0:T(8,128)S(1)} %get-tuple-element.28), channel_id=1, source_target_pairs={{0,1},{1,0},{2,3},{3,2},{4,5},{5,4},{6,7},{7,6},{8,9},{9,8},{10,11... | collective-permute-start | bytes 12296 | tf_op jit(solution)/shard_map/ppermute | solution.py:369
  25.6 3.9 %collective-permute-start.10 = (f32[8,128]{1,0:T(8,128)S(1)}, f32[8,128]{1,0:T(8,128)S(1)}, u32[]{:S(2)}, u32[]{:S(2)}) collective-permute-start(f32[8,128]{1,0:T(8,128)S(1)} %add.19.refs_0_), channel_id=1, source_target_pairs={{0,7},{1,6},{2,5},{3,4},{4,3},{5,2},{6,1},{7,0},{8,15},{9,14},{10,... | collective-permute-start | bytes 12296 | tf_op jit(solution)/shard_map/ppermute | solution.py:365
  26.8 3.6 %collective-permute-start.8 = (f32[8,128]{1,0:T(8,128)S(1)}, f32[8,128]{1,0:T(8,128)S(1)}, u32[]{:S(2)}, u32[]{:S(2)}) collective-permute-start(f32[8,128]{1,0:T(8,128)S(1)} %add.19.refs_0_), channel_id=1, source_target_pairs={{0,4},{1,5},{2,6},{3,7},{4,0},{5,1},{6,2},{7,3},{8,12},{9,13},{10,... | collective-permute-start | bytes 12296 | tf_op jit(solution)/shard_map/ppermute | solution.py:365
  28.4 3.0 %collective-permute-start.9 = (f32[8,128]{1,0:T(8,128)S(1)}, f32[8,128]{1,0:T(8,128)S(1)}, u32[]{:S(2)}, u32[]{:S(2)}) collective-permute-start(f32[8,128]{1,0:T(8,128)S(1)} %add.19.refs_0_), channel_id=1, source_target_pairs={{0,3},{1,2},{2,1},{3,0},{4,7},{5,6},{6,5},{7,4},{8,11},{9,10},{10,... | collective-permute-start | bytes 12296 | tf_op jit(solution)/shard_map/ppermute | solution.py:365
  31.7 4.3 %collective-permute-start.13 = (bf16[288,128]{1,0:T(8,128)(2,1)S(1)}, bf16[288,128]{1,0:T(8,128)(2,1)S(1)}, u32[]{:S(2)}, u32[]{:S(2)}) collective-permute-start(bf16[288,128]{1,0:T(8,128)(2,1)S(1)} %shard_map.166.refs_0_), channel_id=1, source_target_pairs={{0,3},{1,2},{2,1},{3,0},{4,7},{5,6},{6,5},{7,4},{8,11},{9,10},{10,... | collective-permute-start | bytes 221192 | tf_op jit(solution)/shard_map/ppermute | solution.py:365
  32.0 4.6 %collective-permute-start.14 = (bf16[288,128]{1,0:T(8,128)(2,1)S(1)}, bf16[288,128]{1,0:T(8,128)(2,1)S(1)}, u32[]{:S(2)}, u32[]{:S(2)}) collective-permute-start(bf16[288,128]{1,0:T(8,128)(2,1)S(1)} %shard_map.166.refs_0_), channel_id=1, source_target_pairs={{0,4},{1,5},{2,6},{3,7},{4,0},{5,1},{6,2},{7,3},{8,12},{9,13},{10,... | collective-permute-start | bytes 221192 | tf_op jit(solution)/shard_map/ppermute | solution.py:365
  33.5 5.1 %collective-permute-start.15 = (bf16[288,128]{1,0:T(8,128)(2,1)S(1)}, bf16[288,128]{1,0:T(8,128)(2,1)S(1)}, u32[]{:S(2)}, u32[]{:S(2)}) collective-permute-start(bf16[288,128]{1,0:T(8,128)(2,1)S(1)} %shard_map.166.refs_0_), channel_id=1, source_target_pairs={{0,7},{1,6},{2,5},{3,4},{4,3},{5,2},{6,1},{7,0},{8,15},{9,14},{10,... | collective-permute-start | bytes 221192 | tf_op jit(solution)/shard_map/ppermute | solution.py:365
  34.7 4.9 %collective-permute-start.16 = (bf16[288,128]{1,0:T(8,128)(2,1)S(1)}, bf16[288,128]{1,0:T(8,128)(2,1)S(1)}, u32[]{:S(2)}, u32[]{:S(2)}) collective-permute-start(bf16[288,128]{1,0:T(8,128)(2,1)S(1)} %shard_map.166.refs_0_), channel_id=1, source_target_pairs={{0,1},{1,0},{2,3},{3,2},{4,5},{5,4},{6,7},{7,6},{8,9},{9,8},{10,11... | collective-permute-start | bytes 221192 | tf_op jit(solution)/shard_map/ppermute | solution.py:369
  36.0 3.6 %collective-permute-start.17 = (bf16[288,128]{1,0:T(8,128)(2,1)S(1)}, bf16[288,128]{1,0:T(8,128)(2,1)S(1)}, u32[]{:S(2)}, u32[]{:S(2)}) collective-permute-start(bf16[288,128]{1,0:T(8,128)(2,1)S(1)} %collective-permute-done.13.refs_1_), channel_id=1, source_target_pairs={{0,1},{1,0},{2,3},{3,2},{4,5},{5,4},{6,7},{7,6},{8,9},{9,8},{10,11... | collective-permute-start | bytes 221192 | tf_op jit(solution)/shard_map/ppermute | solution.py:369
  36.6 3.0 %collective-permute-start.18 = (bf16[288,128]{1,0:T(8,128)(2,1)S(1)}, bf16[288,128]{1,0:T(8,128)(2,1)S(1)}, u32[]{:S(2)}, u32[]{:S(2)}) collective-permute-start(bf16[288,128]{1,0:T(8,128)(2,1)S(1)} %collective-permute-done.14.refs_2_), channel_id=1, source_target_pairs={{0,1},{1,0},{2,3},{3,2},{4,5},{5,4},{6,7},{7,6},{8,9},{9,8},{10,11... | collective-permute-start | bytes 221192 | tf_op jit(solution)/shard_map/ppermute | solution.py:369
  38.6 1.3 %collective-permute-start.19 = (bf16[288,128]{1,0:T(8,128)(2,1)S(1)}, bf16[288,128]{1,0:T(8,128)(2,1)S(1)}, u32[]{:S(2)}, u32[]{:S(2)}) collective-permute-start(bf16[288,128]{1,0:T(8,128)(2,1)S(1)} %collective-permute-done.15.refs_3_), channel_id=1, source_target_pairs={{0,1},{1,0},{2,3},{3,2},{4,5},{5,4},{6,7},{7,6},{8,9},{9,8},{10,11... | collective-permute-start | bytes 221192 | tf_op jit(solution)/shard_map/ppermute | solution.py:369

commit v15 on v14

--- a/solution.py
+++ b/solution.py
@@ -85,7 +85,7 @@
     return jnp.sum(value.reshape(-1, 8, LANES), axis=0)
 
 
-STEPS = 3
+STEPS = 2
 
 
 def each(count, step, unrolled):
@@ -194,8 +194,7 @@
 
 
 def share_kernel(plan, *refs):
-    held, far, own, got, (payload, g_exp, both) = *refs[:3], refs[3:-3], refs[-3:]
-    both[0], both[1] = held[...], far[...]
+    own, got, (payload, g_exp) = refs[0], refs[1:-2], refs[-2:]
     total = own[...]
     for ref in got:
         total = total + ref[...].astype(f32)
@@ -213,7 +212,8 @@
     return attn, (one[:8] + one[8:]) + (two[:8] + two[8:])
 
 
-def again_kernel(plan, mine, other, payload):
+def again_kernel(plan, mine, other, pack, payload, held):
+    held[...] = pack[...]
     attn, square = pair_sum(plan, mine, other)
     a = plan.all_a
     payload[:a, :] = attn.astype(bf16)
@@ -241,9 +241,11 @@
 
 def rows_kernel(plan, limit, *refs):
     factor = clip_factor(limit, refs[: plan.chips])
-    g_attn, g_exp, we, me, ve, both, *far, mine = refs[plan.chips :]
+    g_attn, g_exp, we, me, ve, *packs, mine = refs[plan.chips :]
     size, place = plan.size_a, lax.axis_index("expert")
-    for q, states in enumerate([both.at[0], both.at[1], *far]):
+    half = len(packs) // 2
+    for i, states in enumerate(packs):
+        q = 2 * (i % half) + i // half
         rows = pl.ds(pl.multiple_of((place ^ q) * size, 16), size)
         old = [states[pl.ds(i * size, size), :].astype(f32) for i in range(3)]
         weight, _, _ = adamw(g_attn[rows, :], *old, factor)
@@ -398,19 +400,19 @@
     ]
     got = [swap(sums[c].astype(bf16), chips=c) for c in reversed(range(1, chips))]
     shared = ((plan.all_a + 16, LANES), bf16)
-    packs = [pack, swap(pack, experts=1)]
-    payload, g_exp, both = call(
-        lambda *refs: share_kernel(plan, *refs),
-        packs + [sums[0]] + got,
-        [shared, ((plan.size_e, LANES), f32), ((2,) + pack.shape, bf16)],
-    )
-    distance = 1
-    while 2 * distance < n_expert:
-        other = swap(payload, experts=distance)
-        (payload,) = call(lambda *refs: again_kernel(plan, *refs), [payload, other], [shared])
-        distance *= 2
-    other = swap(payload, experts=distance)
-    far = [swap(pack, experts=q) for q in range(2, n_expert)]
+    payload, g_exp = call(
+        lambda *refs: share_kernel(plan, *refs), [sums[0]] + got, [shared, ((plan.size_e, LANES), f32)]
+    )
+    packs, distance = [pack], n_expert // 2
+    while distance > 1:
+        other, far = swap(payload, experts=distance), [swap(value, experts=distance) for value in packs]
+        payload, held = call(
+            lambda *refs: again_kernel(plan, *refs), [payload, other, far[0]], [shared, (pack.shape, bf16)]
+        )
+        packs += [held] + far[1:]
+        distance //= 2
+    other, far = swap(payload, experts=1), [swap(value, experts=1) for value in packs]
+    states = [*packs, *far]
     g_attn, square = call(
         lambda *refs: last_kernel(plan, *refs), [payload, other], [((plan.all_a, LANES), f32), ((8, LANES), f32)]
     )
@@ -419,7 +421,7 @@
     block_a, block_e = ((plan.size_a, LANES), f32), ((plan.size_e, LANES), f32)
     (mine,) = call(
         lambda *refs: rows_kernel(plan, limit, *refs),
-        [*squares, g_attn, g_exp, *state_e, both, *far],
+        [*squares, g_attn, g_exp, *state_e, *states],
         [((chunk, LANES), bf16)],
     )
     wa, ma, va, we, me, ve = call(

time: 41.2 us -> 42 us (1.019); the launches traced: 41.1 us -> 41.4 us
  waiting for transfers between devices: 13.5 us -> 17.2 us
  starting transfers between devices: 21.2 us -> 17.9 us
    ppermute x14, waiting for transfers between devices: 10.9 us -> 14.7 us  [swap(): return lax.ppermute(value, ('expert', 'dp'), pairs)]
    ppermute x14, starting transfers between devices: 19.7 us -> 16.3 us  [swap(): return lax.ppermute(value, ('expert', 'dp'), pairs)]
  transfers between devices with their start and end apart: 20 -> 20, of which waited for: 13 -> 14; matrix products, arithmetic and copies ran while one was open for 0% -> 0% of each run, Pallas kernels for 2% -> 2%
where the time goes in v15:
time: 42 us; the launch traced here: 41.4 us
  starting transfers between devices  17.9 us (43%)
  waiting for transfers between devices  17.2 us (41%)
  Pallas kernels  5.43 us (13%)
  between operations  0.75 us (2%)
    ppermute x14, starting transfers between devices, swap(): return lax.ppermute(value, ('expert', 'dp'), pairs)  16.3 us
    ppermute x14, waiting for transfers between devices, swap(): return lax.ppermute(value, ('expert', 'dp'), pairs)  14.7 us
    pallas_call x7, Pallas kernels, call(): pl.pallas_call(kernel, in_specs=[pl.BlockSpec(memory_space=in_space)] * l...  5.43 us
    ppermute x6, waiting for transfers between devices, swap_cores(): lax.ppermute(value, 'dp', [(i, i ^ 1) for i in range(lax.axis_size('dp'))])  2.45 us
    ppermute x6, starting transfers between devices, swap_cores(): lax.ppermute(value, 'dp', [(i, i ^ 1) for i in range(lax.axis_size('dp'))])  1.68 us
  transfers between devices with their start and end apart: 20, of which 14 were waited for; matrix products, arithmetic and copies ran while one was open for 0% of the time, Pallas kernels for 2%

profile of v15, /device:TPU:0, one launch (start us, length us, event | category | flops | bytes accessed | tf_op | source)
XLA Modules:
  0.0 41.4 jit_solution(17105684111114187326)
XLA Ops:
  0.7 3.0 %shard_map.161 = (f32[1152,128]{1,0:T(8,128)S(1)}, bf16[1152,128]{1,0:T(8,128)(2,1)S(1)}, bf16[144,128]{1,0:T(8,128)(2,1)S(1)}) custom-call(bf16[32,256]{1,0:T(8,128)(2,1)} %bitcast.54, bf16[256,6144]{1,0:T(8,128)(2,1)} %refs_1_.1, bf16[16,128]{1,0:T(8,128)(2,1)} %bitcast.55, bf16[128,6144]{1,0:T(8,128)(2,1)} %bitcast.53, f32[48,128]{1,0:T(8,128)} %bitcast.47, ...), custom_call_target="tpu_custom_call" | custom-call | tf_op jit(solution)/shard_map/pallas_call | solution.py:69
  3.7 0.5 %collective-permute-start = (bf16[1152,128]{1,0:T(8,128)(2,1)S(1)}, bf16[1152,128]{1,0:T(8,128)(2,1)S(1)}, u32[]{:S(2)}, u32[]{:S(2)}) collective-permute-start(bf16[1152,128]{1,0:T(8,128)(2,1)S(1)} %get-tuple-element.26), channel_id=1, source_target_pairs={{0,1},{1,0},{2,3},{3,2},{4,5},{5,4},{6,7},{7,6},{8,9},{9,8},{10,11... | collective-permute-start | bytes 884744 | tf_op jit(solution)/shard_map/ppermute | solution.py:371
  4.3 1.2 %collective-permute-done = bf16[1152,128]{1,0:T(8,128)(2,1)S(1)} collective-permute-done((bf16[1152,128]{1,0:T(8,128)(2,1)S(1)}, bf16[1152,128]{1,0:T(8,128)(2,1)S(1)}, u32[]{:S(2)}, u32[]{:S(2)}) %collective-permute-start) | collective-permute-done | bytes 294944 | tf_op jit(solution)/shard_map/ppermute | solution.py:371
  5.5 3.6 %collective-permute-start.1 = (bf16[288,128]{1,0:T(8,128)(2,1)S(1)}, bf16[288,128]{1,0:T(8,128)(2,1)S(1)}, u32[]{:S(2)}, u32[]{:S(2)}) collective-permute-start(bf16[288,128]{1,0:T(8,128)(2,1)S(1)} %get-tuple-element.44), channel_id=1, source_target_pairs={{0,7},{1,6},{2,5},{3,4},{4,3},{5,2},{6,1},{7,0},{8,15},{9,14},{10,... | collective-permute-start | bytes 221192 | tf_op jit(solution)/shard_map/ppermute | solution.py:367
  9.2 0.5 %collective-permute-start.2 = (bf16[288,128]{1,0:T(8,128)(2,1)S(1)}, bf16[288,128]{1,0:T(8,128)(2,1)S(1)}, u32[]{:S(2)}, u32[]{:S(2)}) collective-permute-start(bf16[288,128]{1,0:T(8,128)(2,1)S(1)} %get-tuple-element.43), channel_id=1, source_target_pairs={{0,4},{1,5},{2,6},{3,7},{4,0},{5,1},{6,2},{7,3},{8,12},{9,13},{10,... | collective-permute-start | bytes 221192 | tf_op jit(solution)/shard_map/ppermute | solution.py:367
  9.7 2.2 %collective-permute-done.1.refs_1_ = bf16[288,128]{1,0:T(8,128)(2,1)S(1)} collective-permute-done((bf16[288,128]{1,0:T(8,128)(2,1)S(1)}, bf16[288,128]{1,0:T(8,128)(2,1)S(1)}, u32[]{:S(2)}, u32[]{:S(2)}) %collective-permute-start.1) | collective-permute-done | bytes 73760 | tf_op jit(solution)/shard_map/ppermute | solution.py:367
  11.9 1.8 %collective-permute-done.2.refs_2_ = bf16[288,128]{1,0:T(8,128)(2,1)S(1)} collective-permute-done((bf16[288,128]{1,0:T(8,128)(2,1)S(1)}, bf16[288,128]{1,0:T(8,128)(2,1)S(1)}, u32[]{:S(2)}, u32[]{:S(2)}) %collective-permute-start.2) | collective-permute-done | bytes 73760 | tf_op jit(solution)/shard_map/ppermute | solution.py:367
  13.7 0.3 collective-permute-done.3.refs_3_
  14.0 2.4 %collective-permute-start.4 = (bf16[208,128]{1,0:T(8,128)(2,1)S(1)}, bf16[208,128]{1,0:T(8,128)(2,1)S(1)}, u32[]{:S(2)}, u32[]{:S(2)}) collective-permute-start(bf16[208,128]{1,0:T(8,128)(2,1)S(1)} %get-tuple-element.27.refs_0_), channel_id=1, source_target_pairs={{0,17},{1,16},{2,19},{3,18},{4,21},{5,20},{6,23},{7,22},{8,25},{9,... | collective-permute-start | bytes 159752 | tf_op jit(solution)/shard_map/ppermute | solution.py:367
  16.4 0.3 collective-permute-start.5
  16.8 4.0 %collective-permute-done.5.refs_2_ = bf16[144,128]{1,0:T(8,128)(2,1)S(1)} collective-permute-done((bf16[144,128]{1,0:T(8,128)(2,1)S(1)}, bf16[144,128]{1,0:T(8,128)(2,1)S(1)}, u32[]{:S(2)}, u32[]{:S(2)}) %collective-permute-start.5) | collective-permute-done | bytes 36896 | tf_op jit(solution)/shard_map/ppermute | solution.py:367
  20.8 1.7 %collective-permute-start.6 = (bf16[208,128]{1,0:T(8,128)(2,1)S(1)}, bf16[208,128]{1,0:T(8,128)(2,1)S(1)}, u32[]{:S(2)}, u32[]{:S(2)}) collective-permute-start(bf16[208,128]{1,0:T(8,128)(2,1)S(1)} %get-tuple-element.29.refs_0_), channel_id=1, source_target_pairs={{0,9},{1,8},{2,11},{3,10},{4,13},{5,12},{6,15},{7,14},{8,1},{9,0},... | collective-permute-start | bytes 159752 | tf_op jit(solution)/shard_map/ppermute | solution.py:367
  22.6 1.6 %collective-permute-start.12 = (bf16[144,128]{1,0:T(8,128)(2,1)S(1)}, bf16[144,128]{1,0:T(8,128)(2,1)S(1)}, u32[]{:S(2)}, u32[]{:S(2)}) collective-permute-start(bf16[144,128]{1,0:T(8,128)(2,1)S(1)} %get-tuple-element.39.refs_10_), channel_id=1, source_target_pairs={{0,9},{1,8},{2,11},{3,10},{4,13},{5,12},{6,15},{7,14},{8,1},{9,0},... | collective-permute-start | bytes 110600 | tf_op jit(solution)/shard_map/ppermute | solution.py:367
  24.2 0.5 %collective-permute-done.6.refs_1_ = bf16[208,128]{1,0:T(8,128)(2,1)S(1)} collective-permute-done((bf16[208,128]{1,0:T(8,128)(2,1)S(1)}, bf16[208,128]{1,0:T(8,128)(2,1)S(1)}, u32[]{:S(2)}, u32[]{:S(2)}) %collective-permute-start.6) | collective-permute-done | bytes 53280 | tf_op jit(solution)/shard_map/ppermute | solution.py:367
  24.9 1.0 %collective-permute-done.7 = f32[8,128]{1,0:T(8,128)S(1)} collective-permute-done((f32[8,128]{1,0:T(8,128)S(1)}, f32[8,128]{1,0:T(8,128)S(1)}, u32[]{:S(2)}, u32[]{:S(2)}) %collective-permute-start.7) | collective-permute-done | bytes 4128 | tf_op jit(solution)/shard_map/ppermute | solution.py:371
  25.9 1.5 %collective-permute-start.10 = (f32[8,128]{1,0:T(8,128)S(1)}, f32[8,128]{1,0:T(8,128)S(1)}, u32[]{:S(2)}, u32[]{:S(2)}) collective-permute-start(f32[8,128]{1,0:T(8,128)S(1)} %add.19.refs_0_), channel_id=1, source_target_pairs={{0,7},{1,6},{2,5},{3,4},{4,3},{5,2},{6,1},{7,0},{8,15},{9,14},{10,... | collective-permute-start | bytes 12296 | tf_op jit(solution)/shard_map/ppermute | solution.py:367
  27.4 1.2 %collective-permute-start.8 = (f32[8,128]{1,0:T(8,128)S(1)}, f32[8,128]{1,0:T(8,128)S(1)}, u32[]{:S(2)}, u32[]{:S(2)}) collective-permute-start(f32[8,128]{1,0:T(8,128)S(1)} %add.19.refs_0_), channel_id=1, source_target_pairs={{0,4},{1,5},{2,6},{3,7},{4,0},{5,1},{6,2},{7,3},{8,12},{9,13},{10,... | collective-permute-start | bytes 12296 | tf_op jit(solution)/shard_map/ppermute | solution.py:367
  28.9 1.0 %collective-permute-done.10.refs_3_ = f32[8,128]{1,0:T(8,128)S(1)} collective-permute-done((f32[8,128]{1,0:T(8,128)S(1)}, f32[8,128]{1,0:T(8,128)S(1)}, u32[]{:S(2)}, u32[]{:S(2)}) %collective-permute-start.10) | collective-permute-done | bytes 4128 | tf_op jit(solution)/shard_map/ppermute | solution.py:367
  29.8 1.2 %collective-permute-done.8.refs_1_ = f32[8,128]{1,0:T(8,128)S(1)} collective-permute-done((f32[8,128]{1,0:T(8,128)S(1)}, f32[8,128]{1,0:T(8,128)S(1)}, u32[]{:S(2)}, u32[]{:S(2)}) %collective-permute-start.8) | collective-permute-done | bytes 4128 | tf_op jit(solution)/shard_map/ppermute | solution.py:367
  31.0 0.7 %collective-permute-done.9.refs_2_ = f32[8,128]{1,0:T(8,128)S(1)} collective-permute-done((f32[8,128]{1,0:T(8,128)S(1)}, f32[8,128]{1,0:T(8,128)S(1)}, u32[]{:S(2)}, u32[]{:S(2)}) %collective-permute-start.9) | collective-permute-done | bytes 4128 | tf_op jit(solution)/shard_map/ppermute | solution.py:367
  31.7 0.3 shard_map.166.refs_0_
  32.0 0.4 collective-permute-start.13
  32.3 1.5 %collective-permute-start.14 = (bf16[288,128]{1,0:T(8,128)(2,1)S(1)}, bf16[288,128]{1,0:T(8,128)(2,1)S(1)}, u32[]{:S(2)}, u32[]{:S(2)}) collective-permute-start(bf16[288,128]{1,0:T(8,128)(2,1)S(1)} %shard_map.166.refs_0_), channel_id=1, source_target_pairs={{0,4},{1,5},{2,6},{3,7},{4,0},{5,1},{6,2},{7,3},{8,12},{9,13},{10,... | collective-permute-start | bytes 221192 | tf_op jit(solution)/shard_map/ppermute | solution.py:367
  33.8 1.2 %collective-permute-start.15 = (bf16[288,128]{1,0:T(8,128)(2,1)S(1)}, bf16[288,128]{1,0:T(8,128)(2,1)S(1)}, u32[]{:S(2)}, u32[]{:S(2)}) collective-permute-start(bf16[288,128]{1,0:T(8,128)(2,1)S(1)} %shard_map.166.refs_0_), channel_id=1, source_target_pairs={{0,7},{1,6},{2,5},{3,4},{4,3},{5,2},{6,1},{7,0},{8,15},{9,14},{10,... | collective-permute-start | bytes 221192 | tf_op jit(solution)/shard_map/ppermute | solution.py:367
  35.0 0.4 collective-permute-start.16
  35.3 0.9 %collective-permute-done.13.refs_1_ = bf16[288,128]{1,0:T(8,128)(2,1)S(1)} collective-permute-done((bf16[288,128]{1,0:T(8,128)(2,1)S(1)}, bf16[288,128]{1,0:T(8,128)(2,1)S(1)}, u32[]{:S(2)}, u32[]{:S(2)}) %collective-permute-start.13) | collective-permute-done | bytes 73760 | tf_op jit(solution)/shard_map/ppermute | solution.py:367
  36.3 0.4 collective-permute-start.17
  36.7 0.2 collective-permute-done.14.refs_2_
  37.0 2.0 %collective-permute-done.15.refs_3_ = bf16[288,128]{1,0:T(8,128)(2,1)S(1)} collective-permute-done((bf16[288,128]{1,0:T(8,128)(2,1)S(1)}, bf16[288,128]{1,0:T(8,128)(2,1)S(1)}, u32[]{:S(2)}, u32[]{:S(2)}) %collective-permute-start.15) | collective-permute-done | bytes 73760 | tf_op jit(solution)/shard_map/ppermute | solution.py:367
  39.1 0.8 %shard_map.165 = (f32[48,128]{1,0:T(8,128)}, f32[48,128]{1,0:T(8,128)}, f32[48,128]{1,0:T(8,128)}, f32[96,128]{1,0:T(8,128)}, f32[96,128]{1,0:T(8,128)}, /*index=5*/f32[96,128]{1,0:T(8,128)}) custom-call(f32[8,128]{1,0:T(8,128)S(1)} %add.19.refs_0_, f32[8,128]{1,0:T(8,128)S(1)} %collective-permute-done.8.refs_1_, ...), custom_call_target="tpu_custom_call" | custom-call | tf_op jit(solution)/shard_map/pallas_call | solution.py:69
  40.0 0.2 collective-permute-done.19.refs_7_
  40.2 1.2 %shard_map.167 = (bf16[32,6144]{1,0:T(8,128)(2,1)}, bf16[1,16,6144]{2,1,0:T(8,128)(2,1)}) custom-call(bf16[288,128]{1,0:T(8,128)(2,1)S(1)} %shard_map.166.refs_0_, bf16[288,128]{1,0:T(8,128)(2,1)S(1)} %collective-permute-done.13.refs_1_, bf16[288,128]{1,0:T(8,128)(2,1)S(1)} %collective-permute-done.14.refs_2_, ...), custom_call_target="tpu_custom_call" | custom-call | tf_op jit(solution)/shard_map/pallas_call | solution.py:69
  (29 shorter events, 0.9 us)
Async XLA Ops:
  0.6 31.0 %copy-start = (f32[1,2,6144]{2,1,0:T(2,128)S(1)}, f32[1,2,6144]{2,1,0:T(2,128)}, u32[]{:S(2)}) copy-start(f32[1,2,6144]{2,1,0:T(2,128)} %param.17) | copy-start | bytes 147460
  0.6 31.0 %copy-start.1 = (f32[1,2,6144]{2,1,0:T(2,128)S(1)}, f32[1,2,6144]{2,1,0:T(2,128)}, u32[]{:S(2)}) copy-start(f32[1,2,6144]{2,1,0:T(2,128)} %param.18) | copy-start | bytes 147460
  0.7 31.0 %copy-start.2 = (f32[1,2,6144]{2,1,0:T(2,128)S(1)}, f32[1,2,6144]{2,1,0:T(2,128)}, u32[]{:S(2)}) copy-start(f32[1,2,6144]{2,1,0:T(2,128)} %param.19) | copy-start | bytes 147460
  0.7 38.4 %copy-start.3 = (f32[1,6144]{1,0:T(1,128)S(1)}, f32[1,6144]{1,0:T(1,128)}, u32[]{:S(2)}) copy-start(f32[1,6144]{1,0:T(1,128)} %param.14) | copy-start | bytes 73732
  0.7 38.4 %copy-start.4 = (f32[1,6144]{1,0:T(1,128)S(1)}, f32[1,6144]{1,0:T(1,128)}, u32[]{:S(2)}) copy-start(f32[1,6144]{1,0:T(1,128)} %param.15) | copy-start | bytes 73732
  0.7 38.4 %copy-start.5 = (f32[1,6144]{1,0:T(1,128)S(1)}, f32[1,6144]{1,0:T(1,128)}, u32[]{:S(2)}) copy-start(f32[1,6144]{1,0:T(1,128)} %param.16) | copy-start | bytes 73732
  3.7 1.7 %collective-permute-start = (bf16[1152,128]{1,0:T(8,128)(2,1)S(1)}, bf16[1152,128]{1,0:T(8,128)(2,1)S(1)}, u32[]{:S(2)}, u32[]{:S(2)}) collective-permute-start(bf16[1152,128]{1,0:T(8,128)(2,1)S(1)} %get-tuple-element.26), channel_id=1, source_target_pairs={{0,1},{1,0},{2,3},{3,2},{4,5},{5,4},{6,7},{7,6},{8,9},{9,8},{10,11... | collective-permute-start | bytes 884744 | tf_op jit(solution)/shard_map/ppermute | solution.py:371
  5.5 6.3 %collective-permute-start.1 = (bf16[288,128]{1,0:T(8,128)(2,1)S(1)}, bf16[288,128]{1,0:T(8,128)(2,1)S(1)}, u32[]{:S(2)}, u32[]{:S(2)}) collective-permute-start(bf16[288,128]{1,0:T(8,128)(2,1)S(1)} %get-tuple-element.44), channel_id=1, source_target_pairs={{0,7},{1,6},{2,5},{3,4},{4,3},{5,2},{6,1},{7,0},{8,15},{9,14},{10,... | collective-permute-start | bytes 221192 | tf_op jit(solution)/shard_map/ppermute | solution.py:367
  9.2 4.5 %collective-permute-start.2 = (bf16[288,128]{1,0:T(8,128)(2,1)S(1)}, bf16[288,128]{1,0:T(8,128)(2,1)S(1)}, u32[]{:S(2)}, u32[]{:S(2)}) collective-permute-start(bf16[288,128]{1,0:T(8,128)(2,1)S(1)} %get-tuple-element.43), channel_id=1, source_target_pairs={{0,4},{1,5},{2,6},{3,7},{4,0},{5,1},{6,2},{7,3},{8,12},{9,13},{10,... | collective-permute-start | bytes 221192 | tf_op jit(solution)/shard_map/ppermute | solution.py:367
  9.7 4.3 %collective-permute-start.3 = (bf16[288,128]{1,0:T(8,128)(2,1)S(1)}, bf16[288,128]{1,0:T(8,128)(2,1)S(1)}, u32[]{:S(2)}, u32[]{:S(2)}) collective-permute-start(bf16[288,128]{1,0:T(8,128)(2,1)S(1)} %get-tuple-element.42), channel_id=1, source_target_pairs={{0,3},{1,2},{2,1},{3,0},{4,7},{5,6},{6,5},{7,4},{8,11},{9,10},{10,... | collective-permute-start | bytes 221192 | tf_op jit(solution)/shard_map/ppermute | solution.py:367
  14.0 6.7 %collective-permute-start.4 = (bf16[208,128]{1,0:T(8,128)(2,1)S(1)}, bf16[208,128]{1,0:T(8,128)(2,1)S(1)}, u32[]{:S(2)}, u32[]{:S(2)}) collective-permute-start(bf16[208,128]{1,0:T(8,128)(2,1)S(1)} %get-tuple-element.27.refs_0_), channel_id=1, source_target_pairs={{0,17},{1,16},{2,19},{3,18},{4,21},{5,20},{6,23},{7,22},{8,25},{9,... | collective-permute-start | bytes 159752 | tf_op jit(solution)/shard_map/ppermute | solution.py:367
  16.4 4.3 %collective-permute-start.5 = (bf16[144,128]{1,0:T(8,128)(2,1)S(1)}, bf16[144,128]{1,0:T(8,128)(2,1)S(1)}, u32[]{:S(2)}, u32[]{:S(2)}) collective-permute-start(bf16[144,128]{1,0:T(8,128)(2,1)S(1)} %get-tuple-element.28.refs_9_), channel_id=1, source_target_pairs={{0,17},{1,16},{2,19},{3,18},{4,21},{5,20},{6,23},{7,22},{8,25},{9,... | collective-permute-start | bytes 110600 | tf_op jit(solution)/shard_map/ppermute | solution.py:367
  20.8 3.9 %collective-permute-start.6 = (bf16[208,128]{1,0:T(8,128)(2,1)S(1)}, bf16[208,128]{1,0:T(8,128)(2,1)S(1)}, u32[]{:S(2)}, u32[]{:S(2)}) collective-permute-start(bf16[208,128]{1,0:T(8,128)(2,1)S(1)} %get-tuple-element.29.refs_0_), channel_id=1, source_target_pairs={{0,9},{1,8},{2,11},{3,10},{4,13},{5,12},{6,15},{7,14},{8,1},{9,0},... | collective-permute-start | bytes 159752 | tf_op jit(solution)/shard_map/ppermute | solution.py:367
  22.4 6.4 %collective-permute-start.11 = (bf16[144,128]{1,0:T(8,128)(2,1)S(1)}, bf16[144,128]{1,0:T(8,128)(2,1)S(1)}, u32[]{:S(2)}, u32[]{:S(2)}) collective-permute-start(bf16[144,128]{1,0:T(8,128)(2,1)S(1)} %get-tuple-element.28.refs_9_), channel_id=1, source_target_pairs={{0,9},{1,8},{2,11},{3,10},{4,13},{5,12},{6,15},{7,14},{8,1},{9,0},... | collective-permute-start | bytes 110600 | tf_op jit(solution)/shard_map/ppermute | solution.py:367
  22.6 6.3 %collective-permute-start.12 = (bf16[144,128]{1,0:T(8,128)(2,1)S(1)}, bf16[144,128]{1,0:T(8,128)(2,1)S(1)}, u32[]{:S(2)}, u32[]{:S(2)}) collective-permute-start(bf16[144,128]{1,0:T(8,128)(2,1)S(1)} %get-tuple-element.39.refs_10_), channel_id=1, source_target_pairs={{0,9},{1,8},{2,11},{3,10},{4,13},{5,12},{6,15},{7,14},{8,1},{9,0},... | collective-permute-start | bytes 110600 | tf_op jit(solution)/shard_map/ppermute | solution.py:367
  24.7 1.2 %collective-permute-start.7 = (f32[8,128]{1,0:T(8,128)S(1)}, f32[8,128]{1,0:T(8,128)S(1)}, u32[]{:S(2)}, u32[]{:S(2)}) collective-permute-start(f32[8,128]{1,0:T(8,128)S(1)} %get-tuple-element.30), channel_id=1, source_target_pairs={{0,1},{1,0},{2,3},{3,2},{4,5},{5,4},{6,7},{7,6},{8,9},{9,8},{10,11... | collective-permute-start | bytes 12296 | tf_op jit(solution)/shard_map/ppermute | solution.py:371
  25.9 3.9 %collective-permute-start.10 = (f32[8,128]{1,0:T(8,128)S(1)}, f32[8,128]{1,0:T(8,128)S(1)}, u32[]{:S(2)}, u32[]{:S(2)}) collective-permute-start(f32[8,128]{1,0:T(8,128)S(1)} %add.19.refs_0_), channel_id=1, source_target_pairs={{0,7},{1,6},{2,5},{3,4},{4,3},{5,2},{6,1},{7,0},{8,15},{9,14},{10,... | collective-permute-start | bytes 12296 | tf_op jit(solution)/shard_map/ppermute | solution.py:367
  27.4 3.6 %collective-permute-start.8 = (f32[8,128]{1,0:T(8,128)S(1)}, f32[8,128]{1,0:T(8,128)S(1)}, u32[]{:S(2)}, u32[]{:S(2)}) collective-permute-start(f32[8,128]{1,0:T(8,128)S(1)} %add.19.refs_0_), channel_id=1, source_target_pairs={{0,4},{1,5},{2,6},{3,7},{4,0},{5,1},{6,2},{7,3},{8,12},{9,13},{10,... | collective-permute-start | bytes 12296 | tf_op jit(solution)/shard_map/ppermute | solution.py:367
  28.6 3.0 %collective-permute-start.9 = (f32[8,128]{1,0:T(8,128)S(1)}, f32[8,128]{1,0:T(8,128)S(1)}, u32[]{:S(2)}, u32[]{:S(2)}) collective-permute-start(f32[8,128]{1,0:T(8,128)S(1)} %add.19.refs_0_), channel_id=1, source_target_pairs={{0,3},{1,2},{2,1},{3,0},{4,7},{5,6},{6,5},{7,4},{8,11},{9,10},{10,... | collective-permute-start | bytes 12296 | tf_op jit(solution)/shard_map/ppermute | solution.py:367
  32.0 4.3 %collective-permute-start.13 = (bf16[288,128]{1,0:T(8,128)(2,1)S(1)}, bf16[288,128]{1,0:T(8,128)(2,1)S(1)}, u32[]{:S(2)}, u32[]{:S(2)}) collective-permute-start(bf16[288,128]{1,0:T(8,128)(2,1)S(1)} %shard_map.166.refs_0_), channel_id=1, source_target_pairs={{0,3},{1,2},{2,1},{3,0},{4,7},{5,6},{6,5},{7,4},{8,11},{9,10},{10,... | collective-permute-start | bytes 221192 | tf_op jit(solution)/shard_map/ppermute | solution.py:367
  32.3 4.6 %collective-permute-start.14 = (bf16[288,128]{1,0:T(8,128)(2,1)S(1)}, bf16[288,128]{1,0:T(8,128)(2,1)S(1)}, u32[]{:S(2)}, u32[]{:S(2)}) collective-permute-start(bf16[288,128]{1,0:T(8,128)(2,1)S(1)} %shard_map.166.refs_0_), channel_id=1, source_target_pairs={{0,4},{1,5},{2,6},{3,7},{4,0},{5,1},{6,2},{7,3},{8,12},{9,13},{10,... | collective-permute-start | bytes 221192 | tf_op jit(solution)/shard_map/ppermute | solution.py:367
  33.8 5.1 %collective-permute-start.15 = (bf16[288,128]{1,0:T(8,128)(2,1)S(1)}, bf16[288,128]{1,0:T(8,128)(2,1)S(1)}, u32[]{:S(2)}, u32[]{:S(2)}) collective-permute-start(bf16[288,128]{1,0:T(8,128)(2,1)S(1)} %shard_map.166.refs_0_), channel_id=1, source_target_pairs={{0,7},{1,6},{2,5},{3,4},{4,3},{5,2},{6,1},{7,0},{8,15},{9,14},{10,... | collective-permute-start | bytes 221192 | tf_op jit(solution)/shard_map/ppermute | solution.py:367
  35.0 5.0 %collective-permute-start.16 = (bf16[288,128]{1,0:T(8,128)(2,1)S(1)}, bf16[288,128]{1,0:T(8,128)(2,1)S(1)}, u32[]{:S(2)}, u32[]{:S(2)}) collective-permute-start(bf16[288,128]{1,0:T(8,128)(2,1)S(1)} %shard_map.166.refs_0_), channel_id=1, source_target_pairs={{0,1},{1,0},{2,3},{3,2},{4,5},{5,4},{6,7},{7,6},{8,9},{9,8},{10,11... | collective-permute-start | bytes 221192 | tf_op jit(solution)/shard_map/ppermute | solution.py:371
  36.3 3.7 %collective-permute-start.17 = (bf16[288,128]{1,0:T(8,128)(2,1)S(1)}, bf16[288,128]{1,0:T(8,128)(2,1)S(1)}, u32[]{:S(2)}, u32[]{:S(2)}) collective-permute-start(bf16[288,128]{1,0:T(8,128)(2,1)S(1)} %collective-permute-done.13.refs_1_), channel_id=1, source_target_pairs={{0,1},{1,0},{2,3},{3,2},{4,5},{5,4},{6,7},{7,6},{8,9},{9,8},{10,11... | collective-permute-start | bytes 221192 | tf_op jit(solution)/shard_map/ppermute | solution.py:371
  36.9 3.0 %collective-permute-start.18 = (bf16[288,128]{1,0:T(8,128)(2,1)S(1)}, bf16[288,128]{1,0:T(8,128)(2,1)S(1)}, u32[]{:S(2)}, u32[]{:S(2)}) collective-permute-start(bf16[288,128]{1,0:T(8,128)(2,1)S(1)} %collective-permute-done.14.refs_2_), channel_id=1, source_target_pairs={{0,1},{1,0},{2,3},{3,2},{4,5},{5,4},{6,7},{7,6},{8,9},{9,8},{10,11... | collective-permute-start | bytes 221192 | tf_op jit(solution)/shard_map/ppermute | solution.py:371
  38.9 1.3 %collective-permute-start.19 = (bf16[288,128]{1,0:T(8,128)(2,1)S(1)}, bf16[288,128]{1,0:T(8,128)(2,1)S(1)}, u32[]{:S(2)}, u32[]{:S(2)}) collective-permute-start(bf16[288,128]{1,0:T(8,128)(2,1)S(1)} %collective-permute-done.15.refs_3_), channel_id=1, source_target_pairs={{0,1},{1,0},{2,3},{3,2},{4,5},{5,4},{6,7},{7,6},{8,9},{9,8},{10,11... | collective-permute-start | bytes 221192 | tf_op jit(solution)/shard_map/ppermute | solution.py:371

commit v16 on v14

--- a/solution.py
+++ b/solution.py
@@ -85,7 +85,7 @@
     return jnp.sum(value.reshape(-1, 8, LANES), axis=0)
 
 
-STEPS = 3
+STEPS = (2, 1)
 
 
 def each(count, step, unrolled):
@@ -97,17 +97,18 @@
 
 
 def terms_kernel(plan, act_a, dy_a, act_e, dy_e, w, m, v, full, send, pack, act_a_v, dy_a_v, act_e_v, dy_e_v, state, sems):
-    tile = plan.width // STEPS
+    unit = plan.blocks // sum(STEPS)
+    tiles = [(sum(STEPS[:t]) * unit, STEPS[t] * unit) for t in range(len(STEPS))]
     small = [
         pltpu.make_async_copy(act_a, act_a_v, sems.at[0]),
         pltpu.make_async_copy(act_e, act_e_v, sems.at[1]),
     ]
     big = []
-    for t in range(STEPS):
-        cols = pl.ds(t * tile, tile)
+    for t, (first, count) in enumerate(tiles):
+        cols = pl.ds(first * LANES, count * LANES)
         big.append(pltpu.make_async_copy(dy_a.at[:, cols], dy_a_v.at[:, cols], sems.at[2 + 2 * t]))
         big.append(pltpu.make_async_copy(dy_e.at[:, cols], dy_e_v.at[:, cols], sems.at[3 + 2 * t]))
-    extra = [pltpu.make_async_copy(ref, state.at[i], sems.at[2 + 2 * STEPS + i]) for i, ref in enumerate((w, m, v))]
+    extra = [pltpu.make_async_copy(ref, state.at[i], sems.at[2 + 2 * len(STEPS) + i]) for i, ref in enumerate((w, m, v))]
     for copy in small + big + extra:
         copy.start()
 
@@ -141,24 +142,23 @@
             full[rows, :] = value[c]
             send[rows, :] = value[plan.chips + c].astype(bf16)
 
-    for t in range(STEPS):
-        cols = pl.ds(t * tile, tile)
+    for t, (first, count) in enumerate(tiles):
+        cols = pl.ds(first * LANES, count * LANES)
         big[2 * t].wait()
         terms_a = dot(left_a, dy_a_v[:, cols])
         big[2 * t + 1].wait()
         terms_e = dot(left_e, dy_e_v[:, cols])
-        count = tile // LANES
         if plan.turned:
             blocks = [slice(b * LANES, (b + 1) * LANES) for b in range(count)]
             for e in range(plan.n_expert):
-                turn(e * plan.size_a + t * count, [terms_a[e * n_dp : (e + 1) * n_dp, span] for span in blocks])
+                turn(e * plan.size_a + first, [terms_a[e * n_dp : (e + 1) * n_dp, span] for span in blocks])
             pieces = [
                 terms_e[r * n_dp : (r + 1) * n_dp, span] for span in blocks for r in range(plan.rows_e)
             ]
-            turn(plan.all_a + t * count * plan.rows_e, pieces)
+            turn(plan.all_a + first * plan.rows_e, pieces)
             continue
         for b in range(count):
-            attn, exp = plan.places(t * count + b)
+            attn, exp = plan.places(first + b)
             span = slice(b * LANES, (b + 1) * LANES)
             for terms, places in ((terms_a, attn), (terms_e, exp)):
                 for group, start in places:
@@ -226,22 +226,14 @@
     square[...] = partial + by_eights(attn * attn)
 
 
-def square_order(chips):
-    return [0, *reversed(range(1, chips - 1)), chips - 1]
-
-
 def clip_factor(limit, squares):
-    order = square_order(len(squares))
-    values = [squares[order.index(c)][...] for c in range(len(squares))]
-    while len(values) > 1:
-        values = [values[i] + values[i + 1] for i in range(0, len(values), 2)]
-    norm = jnp.sqrt(jnp.sum(values[0], keepdims=True))
+    norm = jnp.sqrt(jnp.sum(jnp.sum(squares[...], axis=0), keepdims=True))
     return jnp.minimum(1.0, limit / (norm + 1e-06))
 
 
 def rows_kernel(plan, limit, *refs):
-    factor = clip_factor(limit, refs[: plan.chips])
-    g_attn, g_exp, we, me, ve, both, *far, mine = refs[plan.chips :]
+    factor = clip_factor(limit, refs[0])
+    g_attn, g_exp, we, me, ve, both, *far, mine = refs[1:]
     size, place = plan.size_a, lax.axis_index("expert")
     for q, states in enumerate([both.at[0], both.at[1], *far]):
         rows = pl.ds(pl.multiple_of((place ^ q) * size, 16), size)
@@ -253,9 +245,9 @@
 
 
 def own_kernel(plan, limit, *refs):
-    factor = clip_factor(limit, refs[: plan.chips])
-    g_attn, g_exp = refs[plan.chips : plan.chips + 2]
-    state, new = refs[plan.chips + 2 : plan.chips + 8], refs[plan.chips + 8 :]
+    factor = clip_factor(limit, refs[0])
+    g_attn, g_exp = refs[1:3]
+    state, new = refs[3:9], refs[9:]
     rows = pl.ds(pl.multiple_of(lax.axis_index("expert") * plan.size_a, 16), plan.size_a)
     for b, grad in enumerate((g_attn[rows, :], g_exp[...])):
         values = adamw(grad, *[ref[...] for ref in state[3 * b : 3 * b + 3]], factor)
@@ -414,17 +406,16 @@
     g_attn, square = call(
         lambda *refs: last_kernel(plan, *refs), [payload, other], [((plan.all_a, LANES), f32), ((8, LANES), f32)]
     )
-    square = square + swap_cores(square)
-    squares = [square] + [swap(square, chips=c) for c in square_order(chips)[1:]]
+    squares = lax.all_gather(square, "dp")
     block_a, block_e = ((plan.size_a, LANES), f32), ((plan.size_e, LANES), f32)
     (mine,) = call(
         lambda *refs: rows_kernel(plan, limit, *refs),
-        [*squares, g_attn, g_exp, *state_e, both, *far],
+        [squares, g_attn, g_exp, *state_e, both, *far],
         [((chunk, LANES), bf16)],
     )
     wa, ma, va, we, me, ve = call(
         lambda *refs: own_kernel(plan, limit, *refs),
-        [*squares, g_attn, g_exp, *state_a, *state_e],
+        [squares, g_attn, g_exp, *state_a, *state_e],
         [block_a] * 3 + [block_e] * 3,
     )
     near = [mine] + [swap(mine, chips=c) for c in range(1, chips)]

time: 41.2 us -> 43.9 us (1.066)
  blocking collectives: 0 us -> 9.05 us
  waiting for transfers between devices: 13.5 us -> 9.7 us
  starting transfers between devices: 21.2 us -> 18.6 us
    all_gather x0 -> x1, blocking collectives: none -> 9.05 us  [body(): squares = lax.all_gather(square, 'dp')]
    ppermute x14 -> x11, starting transfers between devices: 19.7 us -> 16.8 us  [swap(): return lax.ppermute(value, ('expert', 'dp'), pairs)]
    ppermute x14 -> x11, waiting for transfers between devices: 10.9 us -> 8.22 us  [swap(): return lax.ppermute(value, ('expert', 'dp'), pairs)]
    ppermute x6 -> x5, waiting for transfers between devices: 2.61 us -> 1.49 us  [swap_cores(): lax.ppermute(value, 'dp', [(i, i ^ 1) for i in range(lax.axis_size('dp'))])]
    ppermute x6 -> x5, starting transfers between devices: 1.51 us -> 1.79 us  [swap_cores(): lax.ppermute(value, 'dp', [(i, i ^ 1) for i in range(lax.axis_size('dp'))])]
  transfers between devices with their start and end apart: 20 -> 16, of which waited for: 13 -> 9; matrix products, arithmetic and copies ran while one was open for 0% -> 0% of each run, Pallas kernels for 2% -> 2%
where the time goes in v16:
time: 43.9 us; the launch traced here: 43.7 us
  starting transfers between devices  18.6 us (42%)
  waiting for transfers between devices  9.7 us (22%)
  blocking collectives  9.05 us (21%)
  Pallas kernels  5.59 us (13%)
  between operations  0.76 us (2%)
    ppermute x11, starting transfers between devices, swap(): return lax.ppermute(value, ('expert', 'dp'), pairs)  16.8 us
    all_gather x1, blocking collectives, body(): squares = lax.all_gather(square, 'dp')  9.05 us
    ppermute x11, waiting for transfers between devices, swap(): return lax.ppermute(value, ('expert', 'dp'), pairs)  8.22 us
    pallas_call x7, Pallas kernels, call(): pl.pallas_call(kernel, in_specs=[pl.BlockSpec(memory_space=in_space)] * l...  5.59 us
    ppermute x5, starting transfers between devices, swap_cores(): lax.ppermute(value, 'dp', [(i, i ^ 1) for i in range(lax.axis_size('dp'))])  1.79 us
    ppermute x5, waiting for transfers between devices, swap_cores(): lax.ppermute(value, 'dp', [(i, i ^ 1) for i in range(lax.axis_size('dp'))])  1.49 us
  transfers between devices with their start and end apart: 16, of which 9 were waited for; matrix products, arithmetic and copies ran while one was open for 0% of the time, Pallas kernels for 2%

profile of v16, /device:TPU:0, one launch (start us, length us, event | category | flops | bytes accessed | tf_op | source)
XLA Modules:
  0.0 43.7 jit_solution(1246115386757454582)
XLA Ops:
  0.7 3.2 %shard_map.161 = (f32[1152,128]{1,0:T(8,128)S(1)}, bf16[1152,128]{1,0:T(8,128)(2,1)S(1)}, bf16[144,128]{1,0:T(8,128)(2,1)S(1)}) custom-call(bf16[32,256]{1,0:T(8,128)(2,1)} %bitcast.57, bf16[256,6144]{1,0:T(8,128)(2,1)} %refs_1_.1, bf16[16,128]{1,0:T(8,128)(2,1)} %bitcast.58, bf16[128,6144]{1,0:T(8,128)(2,1)} %bitcast.56, f32[48,128]{1,0:T(8,128)} %bitcast.50, ...), custom_call_target="tpu_custom_call" | custom-call | tf_op jit(solution)/shard_map/pallas_call | solution.py:69
  3.9 0.5 %collective-permute-start.1 = (bf16[1152,128]{1,0:T(8,128)(2,1)S(1)}, bf16[1152,128]{1,0:T(8,128)(2,1)S(1)}, u32[]{:S(2)}, u32[]{:S(2)}) collective-permute-start(bf16[1152,128]{1,0:T(8,128)(2,1)S(1)} %get-tuple-element.26), channel_id=1, source_target_pairs={{0,1},{1,0},{2,3},{3,2},{4,5},{5,4},{6,7},{7,6},{8,9},{9,8},{10,11... | collective-permute-start | bytes 884744 | tf_op jit(solution)/shard_map/ppermute | solution.py:361
  4.4 1.2 %collective-permute-done.1 = bf16[1152,128]{1,0:T(8,128)(2,1)S(1)} collective-permute-done((bf16[1152,128]{1,0:T(8,128)(2,1)S(1)}, bf16[1152,128]{1,0:T(8,128)(2,1)S(1)}, u32[]{:S(2)}, u32[]{:S(2)}) %collective-permute-start.1) | collective-permute-done | bytes 294944 | tf_op jit(solution)/shard_map/ppermute | solution.py:361
  5.6 0.1 add_convert_fusion
  5.7 3.6 %collective-permute-start.2 = (bf16[288,128]{1,0:T(8,128)(2,1)S(1)}, bf16[288,128]{1,0:T(8,128)(2,1)S(1)}, u32[]{:S(2)}, u32[]{:S(2)}) collective-permute-start(bf16[288,128]{1,0:T(8,128)(2,1)S(1)} %get-tuple-element.42), channel_id=1, source_target_pairs={{0,7},{1,6},{2,5},{3,4},{4,3},{5,2},{6,1},{7,0},{8,15},{9,14},{10,... | collective-permute-start | bytes 221192 | tf_op jit(solution)/shard_map/ppermute | solution.py:357
  9.3 0.5 %collective-permute-start.3 = (bf16[288,128]{1,0:T(8,128)(2,1)S(1)}, bf16[288,128]{1,0:T(8,128)(2,1)S(1)}, u32[]{:S(2)}, u32[]{:S(2)}) collective-permute-start(bf16[288,128]{1,0:T(8,128)(2,1)S(1)} %get-tuple-element.41), channel_id=1, source_target_pairs={{0,4},{1,5},{2,6},{3,7},{4,0},{5,1},{6,2},{7,3},{8,12},{9,13},{10,... | collective-permute-start | bytes 221192 | tf_op jit(solution)/shard_map/ppermute | solution.py:357
  9.8 0.0 collective-permute-start.4
  9.8 1.8 %collective-permute-start = (bf16[144,128]{1,0:T(8,128)(2,1)S(1)}, bf16[144,128]{1,0:T(8,128)(2,1)S(1)}, u32[]{:S(2)}, u32[]{:S(2)}) collective-permute-start(bf16[144,128]{1,0:T(8,128)(2,1)S(1)} %get-tuple-element.24.refs_0_), channel_id=1, source_target_pairs={{0,9},{1,8},{2,11},{3,10},{4,13},{5,12},{6,15},{7,14},{8,1},{9,0},... | collective-permute-start | bytes 110600 | tf_op jit(solution)/shard_map/ppermute | solution.py:357
  11.7 1.6 %collective-permute-done.refs_1_ = bf16[144,128]{1,0:T(8,128)(2,1)S(1)} collective-permute-done((bf16[144,128]{1,0:T(8,128)(2,1)S(1)}, bf16[144,128]{1,0:T(8,128)(2,1)S(1)}, u32[]{:S(2)}, u32[]{:S(2)}) %collective-permute-start) | collective-permute-done | bytes 36896 | tf_op jit(solution)/shard_map/ppermute | solution.py:357
  13.3 0.5 %collective-permute-done.3.refs_4_ = bf16[288,128]{1,0:T(8,128)(2,1)S(1)} collective-permute-done((bf16[288,128]{1,0:T(8,128)(2,1)S(1)}, bf16[288,128]{1,0:T(8,128)(2,1)S(1)}, u32[]{:S(2)}, u32[]{:S(2)}) %collective-permute-start.3) | collective-permute-done | bytes 73760 | tf_op jit(solution)/shard_map/ppermute | solution.py:357
  13.9 0.3 collective-permute-done.4.refs_5_
  14.2 1.4 %collective-permute-start.5 = (bf16[208,128]{1,0:T(8,128)(2,1)S(1)}, bf16[208,128]{1,0:T(8,128)(2,1)S(1)}, u32[]{:S(2)}, u32[]{:S(2)}) collective-permute-start(bf16[208,128]{1,0:T(8,128)(2,1)S(1)} %get-tuple-element.27.refs_0_), channel_id=1, source_target_pairs={{0,9},{1,8},{2,11},{3,10},{4,13},{5,12},{6,15},{7,14},{8,1},{9,0},... | collective-permute-start | bytes 159752 | tf_op jit(solution)/shard_map/ppermute | solution.py:357
  15.6 2.5 %collective-permute-done.5.refs_1_ = bf16[208,128]{1,0:T(8,128)(2,1)S(1)} collective-permute-done((bf16[208,128]{1,0:T(8,128)(2,1)S(1)}, bf16[208,128]{1,0:T(8,128)(2,1)S(1)}, u32[]{:S(2)}, u32[]{:S(2)}) %collective-permute-start.5) | collective-permute-done | bytes 53280 | tf_op jit(solution)/shard_map/ppermute | solution.py:357
  18.1 2.4 %collective-permute-start.6 = (bf16[208,128]{1,0:T(8,128)(2,1)S(1)}, bf16[208,128]{1,0:T(8,128)(2,1)S(1)}, u32[]{:S(2)}, u32[]{:S(2)}) collective-permute-start(bf16[208,128]{1,0:T(8,128)(2,1)S(1)} %shard_map.163.refs_0_), channel_id=1, source_target_pairs={{0,17},{1,16},{2,19},{3,18},{4,21},{5,20},{6,23},{7,22},{8,25},{9,... | collective-permute-start | bytes 159752 | tf_op jit(solution)/shard_map/ppermute | solution.py:357
  20.5 0.3 collective-permute-start.7
  20.8 3.7 %collective-permute-start.8 = (bf16[144,128]{1,0:T(8,128)(2,1)S(1)}, bf16[144,128]{1,0:T(8,128)(2,1)S(1)}, u32[]{:S(2)}, u32[]{:S(2)}) collective-permute-start(bf16[144,128]{1,0:T(8,128)(2,1)S(1)} %get-tuple-element.24.refs_0_), channel_id=1, source_target_pairs={{0,24},{1,25},{2,26},{3,27},{4,28},{5,29},{6,30},{7,31},{8,16},{9,... | collective-permute-start | bytes 110600 | tf_op jit(solution)/shard_map/ppermute | solution.py:357
  24.5 0.0 collective-permute-done.6.refs_1_
  24.5 9.0 %all-gather = f32[64,128]{1,0:T(8,128)S(1)} all-gather(f32[8,128]{1,0:T(8,128)S(1)} %get-tuple-element.28), channel_id=2, replica_groups=mesh['expert'=4,'dp'=8] {'dp'}, dimensions={0}, use_global_device_ids=true | all-gather | bytes 36864 | tf_op jit(solution)/shard_map/all_gather | solution.py:409
  33.6 0.0 collective-permute-done.7.refs_7_
  33.6 0.3 shard_map.166.refs_0_
  33.9 0.5 %collective-permute-start.9 = (bf16[288,128]{1,0:T(8,128)(2,1)S(1)}, bf16[288,128]{1,0:T(8,128)(2,1)S(1)}, u32[]{:S(2)}, u32[]{:S(2)}) collective-permute-start(bf16[288,128]{1,0:T(8,128)(2,1)S(1)} %shard_map.166.refs_0_), channel_id=1, source_target_pairs={{0,3},{1,2},{2,1},{3,0},{4,7},{5,6},{6,5},{7,4},{8,11},{9,10},{10,... | collective-permute-start | bytes 221192 | tf_op jit(solution)/shard_map/ppermute | solution.py:357
  34.4 1.5 %collective-permute-start.10 = (bf16[288,128]{1,0:T(8,128)(2,1)S(1)}, bf16[288,128]{1,0:T(8,128)(2,1)S(1)}, u32[]{:S(2)}, u32[]{:S(2)}) collective-permute-start(bf16[288,128]{1,0:T(8,128)(2,1)S(1)} %shard_map.166.refs_0_), channel_id=1, source_target_pairs={{0,4},{1,5},{2,6},{3,7},{4,0},{5,1},{6,2},{7,3},{8,12},{9,13},{10,... | collective-permute-start | bytes 221192 | tf_op jit(solution)/shard_map/ppermute | solution.py:357
  35.9 1.0 %collective-permute-start.11 = (bf16[288,128]{1,0:T(8,128)(2,1)S(1)}, bf16[288,128]{1,0:T(8,128)(2,1)S(1)}, u32[]{:S(2)}, u32[]{:S(2)}) collective-permute-start(bf16[288,128]{1,0:T(8,128)(2,1)S(1)} %shard_map.166.refs_0_), channel_id=1, source_target_pairs={{0,7},{1,6},{2,5},{3,4},{4,3},{5,2},{6,1},{7,0},{8,15},{9,14},{10,... | collective-permute-start | bytes 221192 | tf_op jit(solution)/shard_map/ppermute | solution.py:357
  36.9 0.6 %collective-permute-start.12 = (bf16[288,128]{1,0:T(8,128)(2,1)S(1)}, bf16[288,128]{1,0:T(8,128)(2,1)S(1)}, u32[]{:S(2)}, u32[]{:S(2)}) collective-permute-start(bf16[288,128]{1,0:T(8,128)(2,1)S(1)} %shard_map.166.refs_0_), channel_id=1, source_target_pairs={{0,1},{1,0},{2,3},{3,2},{4,5},{5,4},{6,7},{7,6},{8,9},{9,8},{10,11... | collective-permute-start | bytes 221192 | tf_op jit(solution)/shard_map/ppermute | solution.py:361
  37.5 0.6 %collective-permute-done.9.refs_1_ = bf16[288,128]{1,0:T(8,128)(2,1)S(1)} collective-permute-done((bf16[288,128]{1,0:T(8,128)(2,1)S(1)}, bf16[288,128]{1,0:T(8,128)(2,1)S(1)}, u32[]{:S(2)}, u32[]{:S(2)}) %collective-permute-start.9) | collective-permute-done | bytes 73760 | tf_op jit(solution)/shard_map/ppermute | solution.py:357
  38.1 0.6 %collective-permute-start.13 = (bf16[288,128]{1,0:T(8,128)(2,1)S(1)}, bf16[288,128]{1,0:T(8,128)(2,1)S(1)}, u32[]{:S(2)}, u32[]{:S(2)}) collective-permute-start(bf16[288,128]{1,0:T(8,128)(2,1)S(1)} %collective-permute-done.9.refs_1_), channel_id=1, source_target_pairs={{0,1},{1,0},{2,3},{3,2},{4,5},{5,4},{6,7},{7,6},{8,9},{9,8},{10,11... | collective-permute-start | bytes 221192 | tf_op jit(solution)/shard_map/ppermute | solution.py:361
  38.6 0.1 collective-permute-done.10.refs_2_
  38.8 2.5 %collective-permute-done.11.refs_3_ = bf16[288,128]{1,0:T(8,128)(2,1)S(1)} collective-permute-done((bf16[288,128]{1,0:T(8,128)(2,1)S(1)}, bf16[288,128]{1,0:T(8,128)(2,1)S(1)}, u32[]{:S(2)}, u32[]{:S(2)}) %collective-permute-start.11) | collective-permute-done | bytes 73760 | tf_op jit(solution)/shard_map/ppermute | solution.py:357
  41.3 0.1 collective-permute-start.15
  41.4 0.9 %shard_map.165 = (f32[48,128]{1,0:T(8,128)}, f32[48,128]{1,0:T(8,128)}, f32[48,128]{1,0:T(8,128)}, f32[96,128]{1,0:T(8,128)}, f32[96,128]{1,0:T(8,128)}, /*index=5*/f32[96,128]{1,0:T(8,128)}) custom-call(f32[8,8,128]{2,1,0:T(8,128)S(1)} %bitcast.43, f32[192,128]{1,0:T(8,128)S(1)} %get-tuple-element.29.refs_1_, f32[96,128]{1,0:T(8,128)S(1)} %get-tuple-element.30.refs_2_, ...), custom_call_target="tpu_custom_call" | custom-call | tf_op jit(solution)/shard_map/pallas_call | solution.py:69
  42.3 0.3 collective-permute-done.15.refs_7_
  42.6 1.2 %shard_map.167 = (bf16[32,6144]{1,0:T(8,128)(2,1)}, bf16[1,16,6144]{2,1,0:T(8,128)(2,1)}) custom-call(bf16[288,128]{1,0:T(8,128)(2,1)S(1)} %shard_map.166.refs_0_, bf16[288,128]{1,0:T(8,128)(2,1)S(1)} %collective-permute-done.9.refs_1_, bf16[288,128]{1,0:T(8,128)(2,1)S(1)} %collective-permute-done.10.refs_2_, ...), custom_call_target="tpu_custom_call" | custom-call | tf_op jit(solution)/shard_map/pallas_call | solution.py:69
  (21 shorter events, 0.1 us)
Async XLA Ops:
  0.6 33.0 %copy-start = (f32[1,2,6144]{2,1,0:T(2,128)S(1)}, f32[1,2,6144]{2,1,0:T(2,128)}, u32[]{:S(2)}) copy-start(f32[1,2,6144]{2,1,0:T(2,128)} %param.17) | copy-start | bytes 147460
  0.6 32.9 %copy-start.1 = (f32[1,2,6144]{2,1,0:T(2,128)S(1)}, f32[1,2,6144]{2,1,0:T(2,128)}, u32[]{:S(2)}) copy-start(f32[1,2,6144]{2,1,0:T(2,128)} %param.18) | copy-start | bytes 147460
  0.7 32.9 %copy-start.2 = (f32[1,2,6144]{2,1,0:T(2,128)S(1)}, f32[1,2,6144]{2,1,0:T(2,128)}, u32[]{:S(2)}) copy-start(f32[1,2,6144]{2,1,0:T(2,128)} %param.19) | copy-start | bytes 147460
  0.7 40.7 %copy-start.3 = (f32[1,6144]{1,0:T(1,128)S(1)}, f32[1,6144]{1,0:T(1,128)}, u32[]{:S(2)}) copy-start(f32[1,6144]{1,0:T(1,128)} %param.14) | copy-start | bytes 73732
  0.7 40.7 %copy-start.4 = (f32[1,6144]{1,0:T(1,128)S(1)}, f32[1,6144]{1,0:T(1,128)}, u32[]{:S(2)}) copy-start(f32[1,6144]{1,0:T(1,128)} %param.15) | copy-start | bytes 73732
  0.7 40.7 %copy-start.5 = (f32[1,6144]{1,0:T(1,128)S(1)}, f32[1,6144]{1,0:T(1,128)}, u32[]{:S(2)}) copy-start(f32[1,6144]{1,0:T(1,128)} %param.16) | copy-start | bytes 73732
  3.9 1.7 %collective-permute-start.1 = (bf16[1152,128]{1,0:T(8,128)(2,1)S(1)}, bf16[1152,128]{1,0:T(8,128)(2,1)S(1)}, u32[]{:S(2)}, u32[]{:S(2)}) collective-permute-start(bf16[1152,128]{1,0:T(8,128)(2,1)S(1)} %get-tuple-element.26), channel_id=1, source_target_pairs={{0,1},{1,0},{2,3},{3,2},{4,5},{5,4},{6,7},{7,6},{8,9},{9,8},{10,11... | collective-permute-start | bytes 884744 | tf_op jit(solution)/shard_map/ppermute | solution.py:361
  5.7 7.6 %collective-permute-start.2 = (bf16[288,128]{1,0:T(8,128)(2,1)S(1)}, bf16[288,128]{1,0:T(8,128)(2,1)S(1)}, u32[]{:S(2)}, u32[]{:S(2)}) collective-permute-start(bf16[288,128]{1,0:T(8,128)(2,1)S(1)} %get-tuple-element.42), channel_id=1, source_target_pairs={{0,7},{1,6},{2,5},{3,4},{4,3},{5,2},{6,1},{7,0},{8,15},{9,14},{10,... | collective-permute-start | bytes 221192 | tf_op jit(solution)/shard_map/ppermute | solution.py:357
  9.3 4.5 %collective-permute-start.3 = (bf16[288,128]{1,0:T(8,128)(2,1)S(1)}, bf16[288,128]{1,0:T(8,128)(2,1)S(1)}, u32[]{:S(2)}, u32[]{:S(2)}) collective-permute-start(bf16[288,128]{1,0:T(8,128)(2,1)S(1)} %get-tuple-element.41), channel_id=1, source_target_pairs={{0,4},{1,5},{2,6},{3,7},{4,0},{5,1},{6,2},{7,3},{8,12},{9,13},{10,... | collective-permute-start | bytes 221192 | tf_op jit(solution)/shard_map/ppermute | solution.py:357
  9.8 4.3 %collective-permute-start.4 = (bf16[288,128]{1,0:T(8,128)(2,1)S(1)}, bf16[288,128]{1,0:T(8,128)(2,1)S(1)}, u32[]{:S(2)}, u32[]{:S(2)}) collective-permute-start(bf16[288,128]{1,0:T(8,128)(2,1)S(1)} %get-tuple-element.40), channel_id=1, source_target_pairs={{0,3},{1,2},{2,1},{3,0},{4,7},{5,6},{6,5},{7,4},{8,11},{9,10},{10,... | collective-permute-start | bytes 221192 | tf_op jit(solution)/shard_map/ppermute | solution.py:357
  9.8 3.5 %collective-permute-start = (bf16[144,128]{1,0:T(8,128)(2,1)S(1)}, bf16[144,128]{1,0:T(8,128)(2,1)S(1)}, u32[]{:S(2)}, u32[]{:S(2)}) collective-permute-start(bf16[144,128]{1,0:T(8,128)(2,1)S(1)} %get-tuple-element.24.refs_0_), channel_id=1, source_target_pairs={{0,9},{1,8},{2,11},{3,10},{4,13},{5,12},{6,15},{7,14},{8,1},{9,0},... | collective-permute-start | bytes 110600 | tf_op jit(solution)/shard_map/ppermute | solution.py:357
  14.2 3.9 %collective-permute-start.5 = (bf16[208,128]{1,0:T(8,128)(2,1)S(1)}, bf16[208,128]{1,0:T(8,128)(2,1)S(1)}, u32[]{:S(2)}, u32[]{:S(2)}) collective-permute-start(bf16[208,128]{1,0:T(8,128)(2,1)S(1)} %get-tuple-element.27.refs_0_), channel_id=1, source_target_pairs={{0,9},{1,8},{2,11},{3,10},{4,13},{5,12},{6,15},{7,14},{8,1},{9,0},... | collective-permute-start | bytes 159752 | tf_op jit(solution)/shard_map/ppermute | solution.py:357
  18.1 6.4 %collective-permute-start.6 = (bf16[208,128]{1,0:T(8,128)(2,1)S(1)}, bf16[208,128]{1,0:T(8,128)(2,1)S(1)}, u32[]{:S(2)}, u32[]{:S(2)}) collective-permute-start(bf16[208,128]{1,0:T(8,128)(2,1)S(1)} %shard_map.163.refs_0_), channel_id=1, source_target_pairs={{0,17},{1,16},{2,19},{3,18},{4,21},{5,20},{6,23},{7,22},{8,25},{9,... | collective-permute-start | bytes 159752 | tf_op jit(solution)/shard_map/ppermute | solution.py:357
  20.5 13.1 %collective-permute-start.7 = (bf16[144,128]{1,0:T(8,128)(2,1)S(1)}, bf16[144,128]{1,0:T(8,128)(2,1)S(1)}, u32[]{:S(2)}, u32[]{:S(2)}) collective-permute-start(bf16[144,128]{1,0:T(8,128)(2,1)S(1)} %get-tuple-element.24.refs_0_), channel_id=1, source_target_pairs={{0,17},{1,16},{2,19},{3,18},{4,21},{5,20},{6,23},{7,22},{8,25},{9,... | collective-permute-start | bytes 110600 | tf_op jit(solution)/shard_map/ppermute | solution.py:357
  20.8 12.7 %collective-permute-start.8 = (bf16[144,128]{1,0:T(8,128)(2,1)S(1)}, bf16[144,128]{1,0:T(8,128)(2,1)S(1)}, u32[]{:S(2)}, u32[]{:S(2)}) collective-permute-start(bf16[144,128]{1,0:T(8,128)(2,1)S(1)} %get-tuple-element.24.refs_0_), channel_id=1, source_target_pairs={{0,24},{1,25},{2,26},{3,27},{4,28},{5,29},{6,30},{7,31},{8,16},{9,... | collective-permute-start | bytes 110600 | tf_op jit(solution)/shard_map/ppermute | solution.py:357
  33.9 4.2 %collective-permute-start.9 = (bf16[288,128]{1,0:T(8,128)(2,1)S(1)}, bf16[288,128]{1,0:T(8,128)(2,1)S(1)}, u32[]{:S(2)}, u32[]{:S(2)}) collective-permute-start(bf16[288,128]{1,0:T(8,128)(2,1)S(1)} %shard_map.166.refs_0_), channel_id=1, source_target_pairs={{0,3},{1,2},{2,1},{3,0},{4,7},{5,6},{6,5},{7,4},{8,11},{9,10},{10,... | collective-permute-start | bytes 221192 | tf_op jit(solution)/shard_map/ppermute | solution.py:357
  34.4 4.4 %collective-permute-start.10 = (bf16[288,128]{1,0:T(8,128)(2,1)S(1)}, bf16[288,128]{1,0:T(8,128)(2,1)S(1)}, u32[]{:S(2)}, u32[]{:S(2)}) collective-permute-start(bf16[288,128]{1,0:T(8,128)(2,1)S(1)} %shard_map.166.refs_0_), channel_id=1, source_target_pairs={{0,4},{1,5},{2,6},{3,7},{4,0},{5,1},{6,2},{7,3},{8,12},{9,13},{10,... | collective-permute-start | bytes 221192 | tf_op jit(solution)/shard_map/ppermute | solution.py:357
  35.9 5.4 %collective-permute-start.11 = (bf16[288,128]{1,0:T(8,128)(2,1)S(1)}, bf16[288,128]{1,0:T(8,128)(2,1)S(1)}, u32[]{:S(2)}, u32[]{:S(2)}) collective-permute-start(bf16[288,128]{1,0:T(8,128)(2,1)S(1)} %shard_map.166.refs_0_), channel_id=1, source_target_pairs={{0,7},{1,6},{2,5},{3,4},{4,3},{5,2},{6,1},{7,0},{8,15},{9,14},{10,... | collective-permute-start | bytes 221192 | tf_op jit(solution)/shard_map/ppermute | solution.py:357
  36.9 5.4 %collective-permute-start.12 = (bf16[288,128]{1,0:T(8,128)(2,1)S(1)}, bf16[288,128]{1,0:T(8,128)(2,1)S(1)}, u32[]{:S(2)}, u32[]{:S(2)}) collective-permute-start(bf16[288,128]{1,0:T(8,128)(2,1)S(1)} %shard_map.166.refs_0_), channel_id=1, source_target_pairs={{0,1},{1,0},{2,3},{3,2},{4,5},{5,4},{6,7},{7,6},{8,9},{9,8},{10,11... | collective-permute-start | bytes 221192 | tf_op jit(solution)/shard_map/ppermute | solution.py:361
  38.1 4.2 %collective-permute-start.13 = (bf16[288,128]{1,0:T(8,128)(2,1)S(1)}, bf16[288,128]{1,0:T(8,128)(2,1)S(1)}, u32[]{:S(2)}, u32[]{:S(2)}) collective-permute-start(bf16[288,128]{1,0:T(8,128)(2,1)S(1)} %collective-permute-done.9.refs_1_), channel_id=1, source_target_pairs={{0,1},{1,0},{2,3},{3,2},{4,5},{5,4},{6,7},{7,6},{8,9},{9,8},{10,11... | collective-permute-start | bytes 221192 | tf_op jit(solution)/shard_map/ppermute | solution.py:361
  38.8 3.5 %collective-permute-start.14 = (bf16[288,128]{1,0:T(8,128)(2,1)S(1)}, bf16[288,128]{1,0:T(8,128)(2,1)S(1)}, u32[]{:S(2)}, u32[]{:S(2)}) collective-permute-start(bf16[288,128]{1,0:T(8,128)(2,1)S(1)} %collective-permute-done.10.refs_2_), channel_id=1, source_target_pairs={{0,1},{1,0},{2,3},{3,2},{4,5},{5,4},{6,7},{7,6},{8,9},{9,8},{10,11... | collective-permute-start | bytes 221192 | tf_op jit(solution)/shard_map/ppermute | solution.py:361
  41.3 1.3 %collective-permute-start.15 = (bf16[288,128]{1,0:T(8,128)(2,1)S(1)}, bf16[288,128]{1,0:T(8,128)(2,1)S(1)}, u32[]{:S(2)}, u32[]{:S(2)}) collective-permute-start(bf16[288,128]{1,0:T(8,128)(2,1)S(1)} %collective-permute-done.11.refs_3_), channel_id=1, source_target_pairs={{0,1},{1,0},{2,3},{3,2},{4,5},{5,4},{6,7},{7,6},{8,9},{9,8},{10,11... | collective-permute-start | bytes 221192 | tf_op jit(solution)/shard_map/ppermute | solution.py:361

commit v17 on v14

--- a/solution.py
+++ b/solution.py
@@ -85,7 +85,7 @@
     return jnp.sum(value.reshape(-1, 8, LANES), axis=0)
 
 
-STEPS = 3
+STEPS = 2
 
 
 def each(count, step, unrolled):
@@ -220,6 +220,12 @@
     payload[a:, :] = jnp.concatenate(two_pieces(square), axis=0).astype(bf16)
 
 
+def hold_kernel(*refs):
+    count = len(refs) // 2
+    for ref, out in zip(refs[:count], refs[count:]):
+        out[...] = ref[...]
+
+
 def last_kernel(plan, mine, other, g_attn, square):
     attn, partial = pair_sum(plan, mine, other)
     g_attn[...] = attn
@@ -410,7 +416,12 @@
         (payload,) = call(lambda *refs: again_kernel(plan, *refs), [payload, other], [shared])
         distance *= 2
     other = swap(payload, experts=distance)
-    far = [swap(pack, experts=q) for q in range(2, n_expert)]
+    early = [q for q in range(2, n_expert) if q != distance]
+    held = [pack] + [swap(pack, experts=q) for q in early]
+    held = call(hold_kernel, held, [(pack.shape, bf16)] * len(held))
+    far = dict(zip(early, held[1:]))
+    far[distance] = swap(held[0], experts=distance)
+    far = [far[q] for q in range(2, n_expert)]
     g_attn, square = call(
         lambda *refs: last_kernel(plan, *refs), [payload, other], [((plan.all_a, LANES), f32), ((8, LANES), f32)]
     )

time: 41.2 us -> 40.8 us (level)
    ppermute x14, starting transfers between devices: 19.7 us -> 19.2 us  [swap(): return lax.ppermute(value, ('expert', 'dp'), pairs)]
    pallas_call x7 -> x8, Pallas kernels: 5.44 us -> 5.44 us  [call(): pl.pallas_call(kernel, in_specs=[pl.BlockSpec(memory_space=in_space)] * l...]
  transfers between devices with their start and end apart: 20 -> 20, of which waited for: 13 -> 14; matrix products, arithmetic and copies ran while one was open for 0% -> 0% of each run, Pallas kernels for 2% -> 2%
where the time goes in v17:
time: 40.8 us; the launch traced here: 40.6 us
  starting transfers between devices  20.9 us (51%)
  waiting for transfers between devices  13.5 us (33%)
  Pallas kernels  5.44 us (13%)
  between operations  0.75 us (2%)
    ppermute x14, starting transfers between devices, swap(): return lax.ppermute(value, ('expert', 'dp'), pairs)  19.2 us
    ppermute x14, waiting for transfers between devices, swap(): return lax.ppermute(value, ('expert', 'dp'), pairs)  11 us
    pallas_call x8, Pallas kernels, call(): pl.pallas_call(kernel, in_specs=[pl.BlockSpec(memory_space=in_space)] * l...  5.44 us
    ppermute x6, waiting for transfers between devices, swap_cores(): lax.ppermute(value, 'dp', [(i, i ^ 1) for i in range(lax.axis_size('dp'))])  2.48 us
    ppermute x6, starting transfers between devices, swap_cores(): lax.ppermute(value, 'dp', [(i, i ^ 1) for i in range(lax.axis_size('dp'))])  1.64 us
  transfers between devices with their start and end apart: 20, of which 14 were waited for; matrix products, arithmetic and copies ran while one was open for 0% of the time, Pallas kernels for 2%

profile of v17, /device:TPU:0, one launch (start us, length us, event | category | flops | bytes accessed | tf_op | source)
XLA Modules:
  0.0 40.6 jit_solution(1322356611382103716)
XLA Ops:
  0.7 3.0 %shard_map.161 = (f32[1152,128]{1,0:T(8,128)S(1)}, bf16[1152,128]{1,0:T(8,128)(2,1)S(1)}, bf16[144,128]{1,0:T(8,128)(2,1)S(1)}) custom-call(bf16[32,256]{1,0:T(8,128)(2,1)} %bitcast.54, bf16[256,6144]{1,0:T(8,128)(2,1)} %refs_1_.1, bf16[16,128]{1,0:T(8,128)(2,1)} %bitcast.55, bf16[128,6144]{1,0:T(8,128)(2,1)} %bitcast.53, f32[48,128]{1,0:T(8,128)} %bitcast.47, ...), custom_call_target="tpu_custom_call" | custom-call | tf_op jit(solution)/shard_map/pallas_call | solution.py:69
  3.7 0.5 %collective-permute-start.1 = (bf16[1152,128]{1,0:T(8,128)(2,1)S(1)}, bf16[1152,128]{1,0:T(8,128)(2,1)S(1)}, u32[]{:S(2)}, u32[]{:S(2)}) collective-permute-start(bf16[1152,128]{1,0:T(8,128)(2,1)S(1)} %get-tuple-element.28), channel_id=1, source_target_pairs={{0,1},{1,0},{2,3},{3,2},{4,5},{5,4},{6,7},{7,6},{8,9},{9,8},{10,11... | collective-permute-start | bytes 884744 | tf_op jit(solution)/shard_map/ppermute | solution.py:375
  4.3 1.2 %collective-permute-done.1 = bf16[1152,128]{1,0:T(8,128)(2,1)S(1)} collective-permute-done((bf16[1152,128]{1,0:T(8,128)(2,1)S(1)}, bf16[1152,128]{1,0:T(8,128)(2,1)S(1)}, u32[]{:S(2)}, u32[]{:S(2)}) %collective-permute-start.1) | collective-permute-done | bytes 294944 | tf_op jit(solution)/shard_map/ppermute | solution.py:375
  5.5 3.6 %collective-permute-start.2 = (bf16[288,128]{1,0:T(8,128)(2,1)S(1)}, bf16[288,128]{1,0:T(8,128)(2,1)S(1)}, u32[]{:S(2)}, u32[]{:S(2)}) collective-permute-start(bf16[288,128]{1,0:T(8,128)(2,1)S(1)} %get-tuple-element.46), channel_id=1, source_target_pairs={{0,7},{1,6},{2,5},{3,4},{4,3},{5,2},{6,1},{7,0},{8,15},{9,14},{10,... | collective-permute-start | bytes 221192 | tf_op jit(solution)/shard_map/ppermute | solution.py:371
  9.2 0.5 %collective-permute-start.3 = (bf16[288,128]{1,0:T(8,128)(2,1)S(1)}, bf16[288,128]{1,0:T(8,128)(2,1)S(1)}, u32[]{:S(2)}, u32[]{:S(2)}) collective-permute-start(bf16[288,128]{1,0:T(8,128)(2,1)S(1)} %get-tuple-element.45), channel_id=1, source_target_pairs={{0,4},{1,5},{2,6},{3,7},{4,0},{5,1},{6,2},{7,3},{8,12},{9,13},{10,... | collective-permute-start | bytes 221192 | tf_op jit(solution)/shard_map/ppermute | solution.py:371
  9.7 1.8 %collective-permute-start = (bf16[144,128]{1,0:T(8,128)(2,1)S(1)}, bf16[144,128]{1,0:T(8,128)(2,1)S(1)}, u32[]{:S(2)}, u32[]{:S(2)}) collective-permute-start(bf16[144,128]{1,0:T(8,128)(2,1)S(1)} %get-tuple-element.26.refs_0_), channel_id=1, source_target_pairs={{0,9},{1,8},{2,11},{3,10},{4,13},{5,12},{6,15},{7,14},{8,1},{9,0},... | collective-permute-start | bytes 110600 | tf_op jit(solution)/shard_map/ppermute | solution.py:371
  11.5 1.6 %collective-permute-done.refs_1_ = bf16[144,128]{1,0:T(8,128)(2,1)S(1)} collective-permute-done((bf16[144,128]{1,0:T(8,128)(2,1)S(1)}, bf16[144,128]{1,0:T(8,128)(2,1)S(1)}, u32[]{:S(2)}, u32[]{:S(2)}) %collective-permute-start) | collective-permute-done | bytes 36896 | tf_op jit(solution)/shard_map/ppermute | solution.py:371
  13.2 0.5 %collective-permute-done.3.refs_4_ = bf16[288,128]{1,0:T(8,128)(2,1)S(1)} collective-permute-done((bf16[288,128]{1,0:T(8,128)(2,1)S(1)}, bf16[288,128]{1,0:T(8,128)(2,1)S(1)}, u32[]{:S(2)}, u32[]{:S(2)}) %collective-permute-start.3) | collective-permute-done | bytes 73760 | tf_op jit(solution)/shard_map/ppermute | solution.py:371
  13.7 0.3 collective-permute-done.4.refs_5_
  14.0 1.4 %collective-permute-start.5 = (bf16[208,128]{1,0:T(8,128)(2,1)S(1)}, bf16[208,128]{1,0:T(8,128)(2,1)S(1)}, u32[]{:S(2)}, u32[]{:S(2)}) collective-permute-start(bf16[208,128]{1,0:T(8,128)(2,1)S(1)} %get-tuple-element.29.refs_0_), channel_id=1, source_target_pairs={{0,9},{1,8},{2,11},{3,10},{4,13},{5,12},{6,15},{7,14},{8,1},{9,0},... | collective-permute-start | bytes 159752 | tf_op jit(solution)/shard_map/ppermute | solution.py:371
  15.4 2.5 %collective-permute-start.11 = (bf16[144,128]{1,0:T(8,128)(2,1)S(1)}, bf16[144,128]{1,0:T(8,128)(2,1)S(1)}, u32[]{:S(2)}, u32[]{:S(2)}) collective-permute-start(bf16[144,128]{1,0:T(8,128)(2,1)S(1)} %get-tuple-element.26.refs_0_), channel_id=1, source_target_pairs={{0,24},{1,25},{2,26},{3,27},{4,28},{5,29},{6,30},{7,31},{8,16},{9,... | collective-permute-start | bytes 110600 | tf_op jit(solution)/shard_map/ppermute | solution.py:371
  18.0 2.5 %collective-permute-start.6 = (bf16[208,128]{1,0:T(8,128)(2,1)S(1)}, bf16[208,128]{1,0:T(8,128)(2,1)S(1)}, u32[]{:S(2)}, u32[]{:S(2)}) collective-permute-start(bf16[208,128]{1,0:T(8,128)(2,1)S(1)} %shard_map.163.refs_0_), channel_id=1, source_target_pairs={{0,17},{1,16},{2,19},{3,18},{4,21},{5,20},{6,23},{7,22},{8,25},{9,... | collective-permute-start | bytes 159752 | tf_op jit(solution)/shard_map/ppermute | solution.py:371
  20.4 0.8 %collective-permute-done.11.refs_1_ = bf16[144,128]{1,0:T(8,128)(2,1)S(1)} collective-permute-done((bf16[144,128]{1,0:T(8,128)(2,1)S(1)}, bf16[144,128]{1,0:T(8,128)(2,1)S(1)}, u32[]{:S(2)}, u32[]{:S(2)}) %collective-permute-start.11) | collective-permute-done | bytes 36896 | tf_op jit(solution)/shard_map/ppermute | solution.py:371
  21.2 1.5 %collective-permute-done.6.refs_1_ = bf16[208,128]{1,0:T(8,128)(2,1)S(1)} collective-permute-done((bf16[208,128]{1,0:T(8,128)(2,1)S(1)}, bf16[208,128]{1,0:T(8,128)(2,1)S(1)}, u32[]{:S(2)}, u32[]{:S(2)}) %collective-permute-start.6) | collective-permute-done | bytes 53280 | tf_op jit(solution)/shard_map/ppermute | solution.py:371
  22.8 0.2 collective-permute-start.7
  23.0 1.0 %collective-permute-done.7 = f32[8,128]{1,0:T(8,128)S(1)} collective-permute-done((f32[8,128]{1,0:T(8,128)S(1)}, f32[8,128]{1,0:T(8,128)S(1)}, u32[]{:S(2)}, u32[]{:S(2)}) %collective-permute-start.7) | collective-permute-done | bytes 4128 | tf_op jit(solution)/shard_map/ppermute | solution.py:375
  24.0 3.2 %collective-permute-start.10 = (f32[8,128]{1,0:T(8,128)S(1)}, f32[8,128]{1,0:T(8,128)S(1)}, u32[]{:S(2)}, u32[]{:S(2)}) collective-permute-start(f32[8,128]{1,0:T(8,128)S(1)} %add.19.refs_0_), channel_id=1, source_target_pairs={{0,7},{1,6},{2,5},{3,4},{4,3},{5,2},{6,1},{7,0},{8,15},{9,14},{10,... | collective-permute-start | bytes 12296 | tf_op jit(solution)/shard_map/ppermute | solution.py:371
  27.2 0.7 %collective-permute-start.8 = (f32[8,128]{1,0:T(8,128)S(1)}, f32[8,128]{1,0:T(8,128)S(1)}, u32[]{:S(2)}, u32[]{:S(2)}) collective-permute-start(f32[8,128]{1,0:T(8,128)S(1)} %add.19.refs_0_), channel_id=1, source_target_pairs={{0,4},{1,5},{2,6},{3,7},{4,0},{5,1},{6,2},{7,3},{8,12},{9,13},{10,... | collective-permute-start | bytes 12296 | tf_op jit(solution)/shard_map/ppermute | solution.py:371
  27.9 0.7 %collective-permute-done.10.refs_3_ = f32[8,128]{1,0:T(8,128)S(1)} collective-permute-done((f32[8,128]{1,0:T(8,128)S(1)}, f32[8,128]{1,0:T(8,128)S(1)}, u32[]{:S(2)}, u32[]{:S(2)}) %collective-permute-start.10) | collective-permute-done | bytes 4128 | tf_op jit(solution)/shard_map/ppermute | solution.py:371
  28.5 2.3 %collective-permute-done.8.refs_1_ = f32[8,128]{1,0:T(8,128)S(1)} collective-permute-done((f32[8,128]{1,0:T(8,128)S(1)}, f32[8,128]{1,0:T(8,128)S(1)}, u32[]{:S(2)}, u32[]{:S(2)}) %collective-permute-start.8) | collective-permute-done | bytes 4128 | tf_op jit(solution)/shard_map/ppermute | solution.py:371
  30.9 0.3 shard_map.167.refs_0_
  31.2 0.4 collective-permute-start.13
  31.6 1.5 %collective-permute-start.14 = (bf16[288,128]{1,0:T(8,128)(2,1)S(1)}, bf16[288,128]{1,0:T(8,128)(2,1)S(1)}, u32[]{:S(2)}, u32[]{:S(2)}) collective-permute-start(bf16[288,128]{1,0:T(8,128)(2,1)S(1)} %shard_map.167.refs_0_), channel_id=1, source_target_pairs={{0,4},{1,5},{2,6},{3,7},{4,0},{5,1},{6,2},{7,3},{8,12},{9,13},{10,... | collective-permute-start | bytes 221192 | tf_op jit(solution)/shard_map/ppermute | solution.py:371
  33.0 1.2 %collective-permute-start.15 = (bf16[288,128]{1,0:T(8,128)(2,1)S(1)}, bf16[288,128]{1,0:T(8,128)(2,1)S(1)}, u32[]{:S(2)}, u32[]{:S(2)}) collective-permute-start(bf16[288,128]{1,0:T(8,128)(2,1)S(1)} %shard_map.167.refs_0_), channel_id=1, source_target_pairs={{0,7},{1,6},{2,5},{3,4},{4,3},{5,2},{6,1},{7,0},{8,15},{9,14},{10,... | collective-permute-start | bytes 221192 | tf_op jit(solution)/shard_map/ppermute | solution.py:371
  34.2 0.4 collective-permute-start.16
  34.6 0.9 %collective-permute-done.13.refs_1_ = bf16[288,128]{1,0:T(8,128)(2,1)S(1)} collective-permute-done((bf16[288,128]{1,0:T(8,128)(2,1)S(1)}, bf16[288,128]{1,0:T(8,128)(2,1)S(1)}, u32[]{:S(2)}, u32[]{:S(2)}) %collective-permute-start.13) | collective-permute-done | bytes 73760 | tf_op jit(solution)/shard_map/ppermute | solution.py:371
  35.5 0.4 %collective-permute-start.17 = (bf16[288,128]{1,0:T(8,128)(2,1)S(1)}, bf16[288,128]{1,0:T(8,128)(2,1)S(1)}, u32[]{:S(2)}, u32[]{:S(2)}) collective-permute-start(bf16[288,128]{1,0:T(8,128)(2,1)S(1)} %collective-permute-done.13.refs_1_), channel_id=1, source_target_pairs={{0,1},{1,0},{2,3},{3,2},{4,5},{5,4},{6,7},{7,6},{8,9},{9,8},{10,11... | collective-permute-start | bytes 221192 | tf_op jit(solution)/shard_map/ppermute | solution.py:375
  35.9 0.2 collective-permute-done.14.refs_2_
  36.2 2.0 %collective-permute-done.15.refs_3_ = bf16[288,128]{1,0:T(8,128)(2,1)S(1)} collective-permute-done((bf16[288,128]{1,0:T(8,128)(2,1)S(1)}, bf16[288,128]{1,0:T(8,128)(2,1)S(1)}, u32[]{:S(2)}, u32[]{:S(2)}) %collective-permute-start.15) | collective-permute-done | bytes 73760 | tf_op jit(solution)/shard_map/ppermute | solution.py:371
  38.3 0.8 %shard_map.165 = (f32[48,128]{1,0:T(8,128)}, f32[48,128]{1,0:T(8,128)}, f32[48,128]{1,0:T(8,128)}, f32[96,128]{1,0:T(8,128)}, f32[96,128]{1,0:T(8,128)}, /*index=5*/f32[96,128]{1,0:T(8,128)}) custom-call(f32[8,128]{1,0:T(8,128)S(1)} %add.19.refs_0_, f32[8,128]{1,0:T(8,128)S(1)} %collective-permute-done.8.refs_1_, ...), custom_call_target="tpu_custom_call" | custom-call | tf_op jit(solution)/shard_map/pallas_call | solution.py:69
  39.2 0.2 collective-permute-done.19.refs_7_
  39.4 1.2 %shard_map.168 = (bf16[32,6144]{1,0:T(8,128)(2,1)}, bf16[1,16,6144]{2,1,0:T(8,128)(2,1)}) custom-call(bf16[288,128]{1,0:T(8,128)(2,1)S(1)} %shard_map.167.refs_0_, bf16[288,128]{1,0:T(8,128)(2,1)S(1)} %collective-permute-done.13.refs_1_, bf16[288,128]{1,0:T(8,128)(2,1)S(1)} %collective-permute-done.14.refs_2_, ...), custom_call_target="tpu_custom_call" | custom-call | tf_op jit(solution)/shard_map/pallas_call | solution.py:69
  (30 shorter events, 0.5 us)
Async XLA Ops:
  0.6 30.3 %copy-start = (f32[1,2,6144]{2,1,0:T(2,128)S(1)}, f32[1,2,6144]{2,1,0:T(2,128)}, u32[]{:S(2)}) copy-start(f32[1,2,6144]{2,1,0:T(2,128)} %param.17) | copy-start | bytes 147460
  0.6 30.3 %copy-start.1 = (f32[1,2,6144]{2,1,0:T(2,128)S(1)}, f32[1,2,6144]{2,1,0:T(2,128)}, u32[]{:S(2)}) copy-start(f32[1,2,6144]{2,1,0:T(2,128)} %param.18) | copy-start | bytes 147460
  0.7 30.3 %copy-start.2 = (f32[1,2,6144]{2,1,0:T(2,128)S(1)}, f32[1,2,6144]{2,1,0:T(2,128)}, u32[]{:S(2)}) copy-start(f32[1,2,6144]{2,1,0:T(2,128)} %param.19) | copy-start | bytes 147460
  0.7 37.7 %copy-start.3 = (f32[1,6144]{1,0:T(1,128)S(1)}, f32[1,6144]{1,0:T(1,128)}, u32[]{:S(2)}) copy-start(f32[1,6144]{1,0:T(1,128)} %param.14) | copy-start | bytes 73732
  0.7 37.6 %copy-start.4 = (f32[1,6144]{1,0:T(1,128)S(1)}, f32[1,6144]{1,0:T(1,128)}, u32[]{:S(2)}) copy-start(f32[1,6144]{1,0:T(1,128)} %param.15) | copy-start | bytes 73732
  0.7 37.6 %copy-start.5 = (f32[1,6144]{1,0:T(1,128)S(1)}, f32[1,6144]{1,0:T(1,128)}, u32[]{:S(2)}) copy-start(f32[1,6144]{1,0:T(1,128)} %param.16) | copy-start | bytes 73732
  3.7 1.7 %collective-permute-start.1 = (bf16[1152,128]{1,0:T(8,128)(2,1)S(1)}, bf16[1152,128]{1,0:T(8,128)(2,1)S(1)}, u32[]{:S(2)}, u32[]{:S(2)}) collective-permute-start(bf16[1152,128]{1,0:T(8,128)(2,1)S(1)} %get-tuple-element.28), channel_id=1, source_target_pairs={{0,1},{1,0},{2,3},{3,2},{4,5},{5,4},{6,7},{7,6},{8,9},{9,8},{10,11... | collective-permute-start | bytes 884744 | tf_op jit(solution)/shard_map/ppermute | solution.py:375
  5.5 7.6 %collective-permute-start.2 = (bf16[288,128]{1,0:T(8,128)(2,1)S(1)}, bf16[288,128]{1,0:T(8,128)(2,1)S(1)}, u32[]{:S(2)}, u32[]{:S(2)}) collective-permute-start(bf16[288,128]{1,0:T(8,128)(2,1)S(1)} %get-tuple-element.46), channel_id=1, source_target_pairs={{0,7},{1,6},{2,5},{3,4},{4,3},{5,2},{6,1},{7,0},{8,15},{9,14},{10,... | collective-permute-start | bytes 221192 | tf_op jit(solution)/shard_map/ppermute | solution.py:371
  9.2 4.5 %collective-permute-start.3 = (bf16[288,128]{1,0:T(8,128)(2,1)S(1)}, bf16[288,128]{1,0:T(8,128)(2,1)S(1)}, u32[]{:S(2)}, u32[]{:S(2)}) collective-permute-start(bf16[288,128]{1,0:T(8,128)(2,1)S(1)} %get-tuple-element.45), channel_id=1, source_target_pairs={{0,4},{1,5},{2,6},{3,7},{4,0},{5,1},{6,2},{7,3},{8,12},{9,13},{10,... | collective-permute-start | bytes 221192 | tf_op jit(solution)/shard_map/ppermute | solution.py:371
  9.7 4.3 %collective-permute-start.4 = (bf16[288,128]{1,0:T(8,128)(2,1)S(1)}, bf16[288,128]{1,0:T(8,128)(2,1)S(1)}, u32[]{:S(2)}, u32[]{:S(2)}) collective-permute-start(bf16[288,128]{1,0:T(8,128)(2,1)S(1)} %get-tuple-element.44), channel_id=1, source_target_pairs={{0,3},{1,2},{2,1},{3,0},{4,7},{5,6},{6,5},{7,4},{8,11},{9,10},{10,... | collective-permute-start | bytes 221192 | tf_op jit(solution)/shard_map/ppermute | solution.py:371
  9.7 3.5 %collective-permute-start = (bf16[144,128]{1,0:T(8,128)(2,1)S(1)}, bf16[144,128]{1,0:T(8,128)(2,1)S(1)}, u32[]{:S(2)}, u32[]{:S(2)}) collective-permute-start(bf16[144,128]{1,0:T(8,128)(2,1)S(1)} %get-tuple-element.26.refs_0_), channel_id=1, source_target_pairs={{0,9},{1,8},{2,11},{3,10},{4,13},{5,12},{6,15},{7,14},{8,1},{9,0},... | collective-permute-start | bytes 110600 | tf_op jit(solution)/shard_map/ppermute | solution.py:371
  14.0 3.9 %collective-permute-start.5 = (bf16[208,128]{1,0:T(8,128)(2,1)S(1)}, bf16[208,128]{1,0:T(8,128)(2,1)S(1)}, u32[]{:S(2)}, u32[]{:S(2)}) collective-permute-start(bf16[208,128]{1,0:T(8,128)(2,1)S(1)} %get-tuple-element.29.refs_0_), channel_id=1, source_target_pairs={{0,9},{1,8},{2,11},{3,10},{4,13},{5,12},{6,15},{7,14},{8,1},{9,0},... | collective-permute-start | bytes 159752 | tf_op jit(solution)/shard_map/ppermute | solution.py:371
  15.4 5.8 %collective-permute-start.11 = (bf16[144,128]{1,0:T(8,128)(2,1)S(1)}, bf16[144,128]{1,0:T(8,128)(2,1)S(1)}, u32[]{:S(2)}, u32[]{:S(2)}) collective-permute-start(bf16[144,128]{1,0:T(8,128)(2,1)S(1)} %get-tuple-element.26.refs_0_), channel_id=1, source_target_pairs={{0,24},{1,25},{2,26},{3,27},{4,28},{5,29},{6,30},{7,31},{8,16},{9,... | collective-permute-start | bytes 110600 | tf_op jit(solution)/shard_map/ppermute | solution.py:371
  18.0 4.8 %collective-permute-start.6 = (bf16[208,128]{1,0:T(8,128)(2,1)S(1)}, bf16[208,128]{1,0:T(8,128)(2,1)S(1)}, u32[]{:S(2)}, u32[]{:S(2)}) collective-permute-start(bf16[208,128]{1,0:T(8,128)(2,1)S(1)} %shard_map.163.refs_0_), channel_id=1, source_target_pairs={{0,17},{1,16},{2,19},{3,18},{4,21},{5,20},{6,23},{7,22},{8,25},{9,... | collective-permute-start | bytes 159752 | tf_op jit(solution)/shard_map/ppermute | solution.py:371
  21.2 6.7 %collective-permute-start.12 = (bf16[144,128]{1,0:T(8,128)(2,1)S(1)}, bf16[144,128]{1,0:T(8,128)(2,1)S(1)}, u32[]{:S(2)}, u32[]{:S(2)}) collective-permute-start(bf16[144,128]{1,0:T(8,128)(2,1)S(1)} %get-tuple-element.40), channel_id=1, source_target_pairs={{0,17},{1,16},{2,19},{3,18},{4,21},{5,20},{6,23},{7,22},{8,25},{9,... | collective-permute-start | bytes 110600 | tf_op jit(solution)/shard_map/ppermute | solution.py:371
  22.8 1.2 %collective-permute-start.7 = (f32[8,128]{1,0:T(8,128)S(1)}, f32[8,128]{1,0:T(8,128)S(1)}, u32[]{:S(2)}, u32[]{:S(2)}) collective-permute-start(f32[8,128]{1,0:T(8,128)S(1)} %get-tuple-element.30), channel_id=1, source_target_pairs={{0,1},{1,0},{2,3},{3,2},{4,5},{5,4},{6,7},{7,6},{8,9},{9,8},{10,11... | collective-permute-start | bytes 12296 | tf_op jit(solution)/shard_map/ppermute | solution.py:375
  24.0 4.5 %collective-permute-start.10 = (f32[8,128]{1,0:T(8,128)S(1)}, f32[8,128]{1,0:T(8,128)S(1)}, u32[]{:S(2)}, u32[]{:S(2)}) collective-permute-start(f32[8,128]{1,0:T(8,128)S(1)} %add.19.refs_0_), channel_id=1, source_target_pairs={{0,7},{1,6},{2,5},{3,4},{4,3},{5,2},{6,1},{7,0},{8,15},{9,14},{10,... | collective-permute-start | bytes 12296 | tf_op jit(solution)/shard_map/ppermute | solution.py:371
  27.2 3.6 %collective-permute-start.8 = (f32[8,128]{1,0:T(8,128)S(1)}, f32[8,128]{1,0:T(8,128)S(1)}, u32[]{:S(2)}, u32[]{:S(2)}) collective-permute-start(f32[8,128]{1,0:T(8,128)S(1)} %add.19.refs_0_), channel_id=1, source_target_pairs={{0,4},{1,5},{2,6},{3,7},{4,0},{5,1},{6,2},{7,3},{8,12},{9,13},{10,... | collective-permute-start | bytes 12296 | tf_op jit(solution)/shard_map/ppermute | solution.py:371
  27.9 3.0 %collective-permute-start.9 = (f32[8,128]{1,0:T(8,128)S(1)}, f32[8,128]{1,0:T(8,128)S(1)}, u32[]{:S(2)}, u32[]{:S(2)}) collective-permute-start(f32[8,128]{1,0:T(8,128)S(1)} %add.19.refs_0_), channel_id=1, source_target_pairs={{0,3},{1,2},{2,1},{3,0},{4,7},{5,6},{6,5},{7,4},{8,11},{9,10},{10,... | collective-permute-start | bytes 12296 | tf_op jit(solution)/shard_map/ppermute | solution.py:371
  31.2 4.3 %collective-permute-start.13 = (bf16[288,128]{1,0:T(8,128)(2,1)S(1)}, bf16[288,128]{1,0:T(8,128)(2,1)S(1)}, u32[]{:S(2)}, u32[]{:S(2)}) collective-permute-start(bf16[288,128]{1,0:T(8,128)(2,1)S(1)} %shard_map.167.refs_0_), channel_id=1, source_target_pairs={{0,3},{1,2},{2,1},{3,0},{4,7},{5,6},{6,5},{7,4},{8,11},{9,10},{10,... | collective-permute-start | bytes 221192 | tf_op jit(solution)/shard_map/ppermute | solution.py:371
  31.6 4.6 %collective-permute-start.14 = (bf16[288,128]{1,0:T(8,128)(2,1)S(1)}, bf16[288,128]{1,0:T(8,128)(2,1)S(1)}, u32[]{:S(2)}, u32[]{:S(2)}) collective-permute-start(bf16[288,128]{1,0:T(8,128)(2,1)S(1)} %shard_map.167.refs_0_), channel_id=1, source_target_pairs={{0,4},{1,5},{2,6},{3,7},{4,0},{5,1},{6,2},{7,3},{8,12},{9,13},{10,... | collective-permute-start | bytes 221192 | tf_op jit(solution)/shard_map/ppermute | solution.py:371
  33.0 5.1 %collective-permute-start.15 = (bf16[288,128]{1,0:T(8,128)(2,1)S(1)}, bf16[288,128]{1,0:T(8,128)(2,1)S(1)}, u32[]{:S(2)}, u32[]{:S(2)}) collective-permute-start(bf16[288,128]{1,0:T(8,128)(2,1)S(1)} %shard_map.167.refs_0_), channel_id=1, source_target_pairs={{0,7},{1,6},{2,5},{3,4},{4,3},{5,2},{6,1},{7,0},{8,15},{9,14},{10,... | collective-permute-start | bytes 221192 | tf_op jit(solution)/shard_map/ppermute | solution.py:371
  34.2 5.0 %collective-permute-start.16 = (bf16[288,128]{1,0:T(8,128)(2,1)S(1)}, bf16[288,128]{1,0:T(8,128)(2,1)S(1)}, u32[]{:S(2)}, u32[]{:S(2)}) collective-permute-start(bf16[288,128]{1,0:T(8,128)(2,1)S(1)} %shard_map.167.refs_0_), channel_id=1, source_target_pairs={{0,1},{1,0},{2,3},{3,2},{4,5},{5,4},{6,7},{7,6},{8,9},{9,8},{10,11... | collective-permute-start | bytes 221192 | tf_op jit(solution)/shard_map/ppermute | solution.py:375
  35.5 3.6 %collective-permute-start.17 = (bf16[288,128]{1,0:T(8,128)(2,1)S(1)}, bf16[288,128]{1,0:T(8,128)(2,1)S(1)}, u32[]{:S(2)}, u32[]{:S(2)}) collective-permute-start(bf16[288,128]{1,0:T(8,128)(2,1)S(1)} %collective-permute-done.13.refs_1_), channel_id=1, source_target_pairs={{0,1},{1,0},{2,3},{3,2},{4,5},{5,4},{6,7},{7,6},{8,9},{9,8},{10,11... | collective-permute-start | bytes 221192 | tf_op jit(solution)/shard_map/ppermute | solution.py:375
  36.2 3.0 %collective-permute-start.18 = (bf16[288,128]{1,0:T(8,128)(2,1)S(1)}, bf16[288,128]{1,0:T(8,128)(2,1)S(1)}, u32[]{:S(2)}, u32[]{:S(2)}) collective-permute-start(bf16[288,128]{1,0:T(8,128)(2,1)S(1)} %collective-permute-done.14.refs_2_), channel_id=1, source_target_pairs={{0,1},{1,0},{2,3},{3,2},{4,5},{5,4},{6,7},{7,6},{8,9},{9,8},{10,11... | collective-permute-start | bytes 221192 | tf_op jit(solution)/shard_map/ppermute | solution.py:375
  38.2 1.3 %collective-permute-start.19 = (bf16[288,128]{1,0:T(8,128)(2,1)S(1)}, bf16[288,128]{1,0:T(8,128)(2,1)S(1)}, u32[]{:S(2)}, u32[]{:S(2)}) collective-permute-start(bf16[288,128]{1,0:T(8,128)(2,1)S(1)} %collective-permute-done.15.refs_3_), channel_id=1, source_target_pairs={{0,1},{1,0},{2,3},{3,2},{4,5},{5,4},{6,7},{7,6},{8,9},{9,8},{10,11... | collective-permute-start | bytes 221192 | tf_op jit(solution)/shard_map/ppermute | solution.py:375

commit v18 on v17

--- a/solution.py
+++ b/solution.py
@@ -194,8 +194,7 @@
 
 
 def share_kernel(plan, *refs):
-    held, far, own, got, (payload, g_exp, both) = *refs[:3], refs[3:-3], refs[-3:]
-    both[0], both[1] = held[...], far[...]
+    own, got, (payload, g_exp) = refs[0], refs[1:-2], refs[-2:]
     total = own[...]
     for ref in got:
         total = total + ref[...].astype(f32)
@@ -233,7 +232,7 @@
 
 
 def square_order(chips):
-    return [0, *reversed(range(1, chips - 1)), chips - 1]
+    return [0, *reversed(range(1, chips))]
 
 
 def clip_factor(limit, squares):
@@ -247,9 +246,9 @@
 
 def rows_kernel(plan, limit, *refs):
     factor = clip_factor(limit, refs[: plan.chips])
-    g_attn, g_exp, we, me, ve, both, *far, mine = refs[plan.chips :]
+    g_attn, g_exp, we, me, ve, *packs, mine = refs[plan.chips :]
     size, place = plan.size_a, lax.axis_index("expert")
-    for q, states in enumerate([both.at[0], both.at[1], *far]):
+    for q, states in enumerate(packs):
         rows = pl.ds(pl.multiple_of((place ^ q) * size, 16), size)
         old = [states[pl.ds(i * size, size), :].astype(f32) for i in range(3)]
         weight, _, _ = adamw(g_attn[rows, :], *old, factor)
@@ -404,11 +403,8 @@
     ]
     got = [swap(sums[c].astype(bf16), chips=c) for c in reversed(range(1, chips))]
     shared = ((plan.all_a + 16, LANES), bf16)
-    packs = [pack, swap(pack, experts=1)]
-    payload, g_exp, both = call(
-        lambda *refs: share_kernel(plan, *refs),
-        packs + [sums[0]] + got,
-        [shared, ((plan.size_e, LANES), f32), ((2,) + pack.shape, bf16)],
+    payload, g_exp = call(
+        lambda *refs: share_kernel(plan, *refs), [sums[0]] + got, [shared, ((plan.size_e, LANES), f32)]
     )
     distance = 1
     while 2 * distance < n_expert:
@@ -416,12 +412,10 @@
         (payload,) = call(lambda *refs: again_kernel(plan, *refs), [payload, other], [shared])
         distance *= 2
     other = swap(payload, experts=distance)
-    early = [q for q in range(2, n_expert) if q != distance]
-    held = [pack] + [swap(pack, experts=q) for q in early]
-    held = call(hold_kernel, held, [(pack.shape, bf16)] * len(held))
-    far = dict(zip(early, held[1:]))
-    far[distance] = swap(held[0], experts=distance)
-    far = [far[q] for q in range(2, n_expert)]
+    states = [pack] + [swap(pack, experts=q) for q in range(2, n_expert, 2)]
+    states = call(hold_kernel, states, [(pack.shape, bf16)] * len(states))
+    pairs = [(state, swap(state, experts=1)) for state in states]
+    states = [state for pair in pairs for state in pair]
     g_attn, square = call(
         lambda *refs: last_kernel(plan, *refs), [payload, other], [((plan.all_a, LANES), f32), ((8, LANES), f32)]
     )
@@ -430,7 +424,7 @@
     block_a, block_e = ((plan.size_a, LANES), f32), ((plan.size_e, LANES), f32)
     (mine,) = call(
         lambda *refs: rows_kernel(plan, limit, *refs),
-        [*squares, g_attn, g_exp, *state_e, both, *far],
+        [*squares, g_attn, g_exp, *state_e, *states],
         [((chunk, LANES), bf16)],
     )
     wa, ma, va, we, me, ve = call(

time: 40.8 us -> 41 us (level)
  starting transfers between devices: 20.9 us -> 21.4 us
    ppermute x6, starting transfers between devices: 1.64 us -> 2.84 us  [swap_cores(): lax.ppermute(value, 'dp', [(i, i ^ 1) for i in range(lax.axis_size('dp'))])]
    ppermute x14, starting transfers between devices: 19.2 us -> 18.5 us  [swap(): return lax.ppermute(value, ('expert', 'dp'), pairs)]
  transfers between devices with their start and end apart: 20 -> 20, of which waited for: 14 -> 13; matrix products, arithmetic and copies ran while one was open for 0% -> 0% of each run, Pallas kernels for 2% -> 2%
where the time goes in v18:
time: 41 us; the launch traced here: 40.8 us
  starting transfers between devices  21.4 us (52%)
  waiting for transfers between devices  13.1 us (32%)
  Pallas kernels  5.43 us (13%)
  between operations  0.75 us (2%)
    ppermute x14, starting transfers between devices, swap(): return lax.ppermute(value, ('expert', 'dp'), pairs)  18.5 us
    ppermute x14, waiting for transfers between devices, swap(): return lax.ppermute(value, ('expert', 'dp'), pairs)  10.9 us
    pallas_call x8, Pallas kernels, call(): pl.pallas_call(kernel, in_specs=[pl.BlockSpec(memory_space=in_space)] * l...  5.43 us
    ppermute x6, starting transfers between devices, swap_cores(): lax.ppermute(value, 'dp', [(i, i ^ 1) for i in range(lax.axis_size('dp'))])  2.84 us
    ppermute x6, waiting for transfers between devices, swap_cores(): lax.ppermute(value, 'dp', [(i, i ^ 1) for i in range(lax.axis_size('dp'))])  2.28 us
  transfers between devices with their start and end apart: 20, of which 13 were waited for; matrix products, arithmetic and copies ran while one was open for 0% of the time, Pallas kernels for 2%

profile of v18, /device:TPU:0, one launch (start us, length us, event | category | flops | bytes accessed | tf_op | source)
XLA Modules:
  0.0 40.8 jit_solution(13380627075119395203)
XLA Ops:
  0.7 3.0 %shard_map.161 = (f32[1152,128]{1,0:T(8,128)S(1)}, bf16[1152,128]{1,0:T(8,128)(2,1)S(1)}, bf16[144,128]{1,0:T(8,128)(2,1)S(1)}) custom-call(bf16[32,256]{1,0:T(8,128)(2,1)} %bitcast.54, bf16[256,6144]{1,0:T(8,128)(2,1)} %refs_1_.1, bf16[16,128]{1,0:T(8,128)(2,1)} %bitcast.55, bf16[128,6144]{1,0:T(8,128)(2,1)} %bitcast.53, f32[48,128]{1,0:T(8,128)} %bitcast.47, ...), custom_call_target="tpu_custom_call" | custom-call | tf_op jit(solution)/shard_map/pallas_call | solution.py:69
  3.7 0.5 %collective-permute-start = (bf16[1152,128]{1,0:T(8,128)(2,1)S(1)}, bf16[1152,128]{1,0:T(8,128)(2,1)S(1)}, u32[]{:S(2)}, u32[]{:S(2)}) collective-permute-start(bf16[1152,128]{1,0:T(8,128)(2,1)S(1)} %get-tuple-element.26), channel_id=1, source_target_pairs={{0,1},{1,0},{2,3},{3,2},{4,5},{5,4},{6,7},{7,6},{8,9},{9,8},{10,11... | collective-permute-start | bytes 884744 | tf_op jit(solution)/shard_map/ppermute | solution.py:374
  4.3 1.2 %collective-permute-done = bf16[1152,128]{1,0:T(8,128)(2,1)S(1)} collective-permute-done((bf16[1152,128]{1,0:T(8,128)(2,1)S(1)}, bf16[1152,128]{1,0:T(8,128)(2,1)S(1)}, u32[]{:S(2)}, u32[]{:S(2)}) %collective-permute-start) | collective-permute-done | bytes 294944 | tf_op jit(solution)/shard_map/ppermute | solution.py:374
  5.5 3.6 %collective-permute-start.1 = (bf16[288,128]{1,0:T(8,128)(2,1)S(1)}, bf16[288,128]{1,0:T(8,128)(2,1)S(1)}, u32[]{:S(2)}, u32[]{:S(2)}) collective-permute-start(bf16[288,128]{1,0:T(8,128)(2,1)S(1)} %get-tuple-element.44), channel_id=1, source_target_pairs={{0,7},{1,6},{2,5},{3,4},{4,3},{5,2},{6,1},{7,0},{8,15},{9,14},{10,... | collective-permute-start | bytes 221192 | tf_op jit(solution)/shard_map/ppermute | solution.py:370
  9.2 0.5 %collective-permute-start.2 = (bf16[288,128]{1,0:T(8,128)(2,1)S(1)}, bf16[288,128]{1,0:T(8,128)(2,1)S(1)}, u32[]{:S(2)}, u32[]{:S(2)}) collective-permute-start(bf16[288,128]{1,0:T(8,128)(2,1)S(1)} %get-tuple-element.43), channel_id=1, source_target_pairs={{0,4},{1,5},{2,6},{3,7},{4,0},{5,1},{6,2},{7,3},{8,12},{9,13},{10,... | collective-permute-start | bytes 221192 | tf_op jit(solution)/shard_map/ppermute | solution.py:370
  9.7 2.2 %collective-permute-done.1.refs_1_ = bf16[288,128]{1,0:T(8,128)(2,1)S(1)} collective-permute-done((bf16[288,128]{1,0:T(8,128)(2,1)S(1)}, bf16[288,128]{1,0:T(8,128)(2,1)S(1)}, u32[]{:S(2)}, u32[]{:S(2)}) %collective-permute-start.1) | collective-permute-done | bytes 73760 | tf_op jit(solution)/shard_map/ppermute | solution.py:370
  11.9 1.8 %collective-permute-done.2.refs_2_ = bf16[288,128]{1,0:T(8,128)(2,1)S(1)} collective-permute-done((bf16[288,128]{1,0:T(8,128)(2,1)S(1)}, bf16[288,128]{1,0:T(8,128)(2,1)S(1)}, u32[]{:S(2)}, u32[]{:S(2)}) %collective-permute-start.2) | collective-permute-done | bytes 73760 | tf_op jit(solution)/shard_map/ppermute | solution.py:370
  13.7 0.3 collective-permute-done.3.refs_3_
  14.0 1.4 %collective-permute-start.4 = (bf16[208,128]{1,0:T(8,128)(2,1)S(1)}, bf16[208,128]{1,0:T(8,128)(2,1)S(1)}, u32[]{:S(2)}, u32[]{:S(2)}) collective-permute-start(bf16[208,128]{1,0:T(8,128)(2,1)S(1)} %get-tuple-element.27.refs_0_), channel_id=1, source_target_pairs={{0,9},{1,8},{2,11},{3,10},{4,13},{5,12},{6,15},{7,14},{8,1},{9,0},... | collective-permute-start | bytes 159752 | tf_op jit(solution)/shard_map/ppermute | solution.py:370
  15.4 2.6 %collective-permute-start.10 = (bf16[144,128]{1,0:T(8,128)(2,1)S(1)}, bf16[144,128]{1,0:T(8,128)(2,1)S(1)}, u32[]{:S(2)}, u32[]{:S(2)}) collective-permute-start(bf16[144,128]{1,0:T(8,128)(2,1)S(1)} %get-tuple-element.37.refs_0_), channel_id=1, source_target_pairs={{0,17},{1,16},{2,19},{3,18},{4,21},{5,20},{6,23},{7,22},{8,25},{9,... | collective-permute-start | bytes 110600 | tf_op jit(solution)/shard_map/ppermute | solution.py:370
  18.1 2.6 %collective-permute-start.5 = (bf16[208,128]{1,0:T(8,128)(2,1)S(1)}, bf16[208,128]{1,0:T(8,128)(2,1)S(1)}, u32[]{:S(2)}, u32[]{:S(2)}) collective-permute-start(bf16[208,128]{1,0:T(8,128)(2,1)S(1)} %shard_map.163.refs_0_), channel_id=1, source_target_pairs={{0,17},{1,16},{2,19},{3,18},{4,21},{5,20},{6,23},{7,22},{8,25},{9,... | collective-permute-start | bytes 159752 | tf_op jit(solution)/shard_map/ppermute | solution.py:370
  20.7 1.3 %collective-permute-start.11 = (bf16[144,128]{1,0:T(8,128)(2,1)S(1)}, bf16[144,128]{1,0:T(8,128)(2,1)S(1)}, u32[]{:S(2)}, u32[]{:S(2)}) collective-permute-start(bf16[144,128]{1,0:T(8,128)(2,1)S(1)} %get-tuple-element.38.refs_9_), channel_id=1, source_target_pairs={{0,9},{1,8},{2,11},{3,10},{4,13},{5,12},{6,15},{7,14},{8,1},{9,0},... | collective-permute-start | bytes 110600 | tf_op jit(solution)/shard_map/ppermute | solution.py:370
  22.0 0.5 %collective-permute-start.12 = (bf16[144,128]{1,0:T(8,128)(2,1)S(1)}, bf16[144,128]{1,0:T(8,128)(2,1)S(1)}, u32[]{:S(2)}, u32[]{:S(2)}) collective-permute-start(bf16[144,128]{1,0:T(8,128)(2,1)S(1)} %get-tuple-element.39.refs_11_), channel_id=1, source_target_pairs={{0,9},{1,8},{2,11},{3,10},{4,13},{5,12},{6,15},{7,14},{8,1},{9,0},... | collective-permute-start | bytes 110600 | tf_op jit(solution)/shard_map/ppermute | solution.py:370
  22.5 0.4 collective-permute-done.5.refs_1_
  22.9 1.4 %collective-permute-start.6 = (f32[8,128]{1,0:T(8,128)S(1)}, f32[8,128]{1,0:T(8,128)S(1)}, u32[]{:S(2)}, u32[]{:S(2)}) collective-permute-start(f32[8,128]{1,0:T(8,128)S(1)} %get-tuple-element.28), channel_id=1, source_target_pairs={{0,1},{1,0},{2,3},{3,2},{4,5},{5,4},{6,7},{7,6},{8,9},{9,8},{10,11... | collective-permute-start | bytes 12296 | tf_op jit(solution)/shard_map/ppermute | solution.py:374
  24.3 0.8 %collective-permute-done.6 = f32[8,128]{1,0:T(8,128)S(1)} collective-permute-done((f32[8,128]{1,0:T(8,128)S(1)}, f32[8,128]{1,0:T(8,128)S(1)}, u32[]{:S(2)}, u32[]{:S(2)}) %collective-permute-start.6) | collective-permute-done | bytes 4128 | tf_op jit(solution)/shard_map/ppermute | solution.py:374
  25.2 1.7 %collective-permute-start.7 = (f32[8,128]{1,0:T(8,128)S(1)}, f32[8,128]{1,0:T(8,128)S(1)}, u32[]{:S(2)}, u32[]{:S(2)}) collective-permute-start(f32[8,128]{1,0:T(8,128)S(1)} %add.19.refs_0_), channel_id=1, source_target_pairs={{0,7},{1,6},{2,5},{3,4},{4,3},{5,2},{6,1},{7,0},{8,15},{9,14},{10,... | collective-permute-start | bytes 12296 | tf_op jit(solution)/shard_map/ppermute | solution.py:370
  26.8 1.2 %collective-permute-start.8 = (f32[8,128]{1,0:T(8,128)S(1)}, f32[8,128]{1,0:T(8,128)S(1)}, u32[]{:S(2)}, u32[]{:S(2)}) collective-permute-start(f32[8,128]{1,0:T(8,128)S(1)} %add.19.refs_0_), channel_id=1, source_target_pairs={{0,4},{1,5},{2,6},{3,7},{4,0},{5,1},{6,2},{7,3},{8,12},{9,13},{10,... | collective-permute-start | bytes 12296 | tf_op jit(solution)/shard_map/ppermute | solution.py:370
  28.1 1.0 %collective-permute-done.7.refs_1_ = f32[8,128]{1,0:T(8,128)S(1)} collective-permute-done((f32[8,128]{1,0:T(8,128)S(1)}, f32[8,128]{1,0:T(8,128)S(1)}, u32[]{:S(2)}, u32[]{:S(2)}) %collective-permute-start.7) | collective-permute-done | bytes 4128 | tf_op jit(solution)/shard_map/ppermute | solution.py:370
  29.1 1.4 %collective-permute-done.8.refs_2_ = f32[8,128]{1,0:T(8,128)S(1)} collective-permute-done((f32[8,128]{1,0:T(8,128)S(1)}, f32[8,128]{1,0:T(8,128)S(1)}, u32[]{:S(2)}, u32[]{:S(2)}) %collective-permute-start.8) | collective-permute-done | bytes 4128 | tf_op jit(solution)/shard_map/ppermute | solution.py:370
  30.4 0.6 %collective-permute-done.9.refs_3_ = f32[8,128]{1,0:T(8,128)S(1)} collective-permute-done((f32[8,128]{1,0:T(8,128)S(1)}, f32[8,128]{1,0:T(8,128)S(1)}, u32[]{:S(2)}, u32[]{:S(2)}) %collective-permute-start.9) | collective-permute-done | bytes 4128 | tf_op jit(solution)/shard_map/ppermute | solution.py:370
  31.1 0.3 shard_map.167.refs_0_
  31.4 0.4 collective-permute-start.13
  31.8 1.5 %collective-permute-start.14 = (bf16[288,128]{1,0:T(8,128)(2,1)S(1)}, bf16[288,128]{1,0:T(8,128)(2,1)S(1)}, u32[]{:S(2)}, u32[]{:S(2)}) collective-permute-start(bf16[288,128]{1,0:T(8,128)(2,1)S(1)} %shard_map.167.refs_0_), channel_id=1, source_target_pairs={{0,4},{1,5},{2,6},{3,7},{4,0},{5,1},{6,2},{7,3},{8,12},{9,13},{10,... | collective-permute-start | bytes 221192 | tf_op jit(solution)/shard_map/ppermute | solution.py:370
  33.2 1.2 %collective-permute-start.15 = (bf16[288,128]{1,0:T(8,128)(2,1)S(1)}, bf16[288,128]{1,0:T(8,128)(2,1)S(1)}, u32[]{:S(2)}, u32[]{:S(2)}) collective-permute-start(bf16[288,128]{1,0:T(8,128)(2,1)S(1)} %shard_map.167.refs_0_), channel_id=1, source_target_pairs={{0,7},{1,6},{2,5},{3,4},{4,3},{5,2},{6,1},{7,0},{8,15},{9,14},{10,... | collective-permute-start | bytes 221192 | tf_op jit(solution)/shard_map/ppermute | solution.py:370
  34.4 0.4 collective-permute-start.16
  34.8 0.9 %collective-permute-done.13.refs_1_ = bf16[288,128]{1,0:T(8,128)(2,1)S(1)} collective-permute-done((bf16[288,128]{1,0:T(8,128)(2,1)S(1)}, bf16[288,128]{1,0:T(8,128)(2,1)S(1)}, u32[]{:S(2)}, u32[]{:S(2)}) %collective-permute-start.13) | collective-permute-done | bytes 73760 | tf_op jit(solution)/shard_map/ppermute | solution.py:370
  35.7 0.4 %collective-permute-start.17 = (bf16[288,128]{1,0:T(8,128)(2,1)S(1)}, bf16[288,128]{1,0:T(8,128)(2,1)S(1)}, u32[]{:S(2)}, u32[]{:S(2)}) collective-permute-start(bf16[288,128]{1,0:T(8,128)(2,1)S(1)} %collective-permute-done.13.refs_1_), channel_id=1, source_target_pairs={{0,1},{1,0},{2,3},{3,2},{4,5},{5,4},{6,7},{7,6},{8,9},{9,8},{10,11... | collective-permute-start | bytes 221192 | tf_op jit(solution)/shard_map/ppermute | solution.py:374
  36.1 0.2 collective-permute-done.14.refs_2_
  36.4 2.0 %collective-permute-done.15.refs_3_ = bf16[288,128]{1,0:T(8,128)(2,1)S(1)} collective-permute-done((bf16[288,128]{1,0:T(8,128)(2,1)S(1)}, bf16[288,128]{1,0:T(8,128)(2,1)S(1)}, u32[]{:S(2)}, u32[]{:S(2)}) %collective-permute-start.15) | collective-permute-done | bytes 73760 | tf_op jit(solution)/shard_map/ppermute | solution.py:370
  38.5 0.8 %shard_map.165 = (f32[48,128]{1,0:T(8,128)}, f32[48,128]{1,0:T(8,128)}, f32[48,128]{1,0:T(8,128)}, f32[96,128]{1,0:T(8,128)}, f32[96,128]{1,0:T(8,128)}, /*index=5*/f32[96,128]{1,0:T(8,128)}) custom-call(f32[8,128]{1,0:T(8,128)S(1)} %add.19.refs_0_, f32[8,128]{1,0:T(8,128)S(1)} %collective-permute-done.7.refs_1_, ...), custom_call_target="tpu_custom_call" | custom-call | tf_op jit(solution)/shard_map/pallas_call | solution.py:69
  39.6 1.2 %shard_map.168 = (bf16[32,6144]{1,0:T(8,128)(2,1)}, bf16[1,16,6144]{2,1,0:T(8,128)(2,1)}) custom-call(bf16[288,128]{1,0:T(8,128)(2,1)S(1)} %shard_map.167.refs_0_, bf16[288,128]{1,0:T(8,128)(2,1)S(1)} %collective-permute-done.13.refs_1_, bf16[288,128]{1,0:T(8,128)(2,1)S(1)} %collective-permute-done.14.refs_2_, ...), custom_call_target="tpu_custom_call" | custom-call | tf_op jit(solution)/shard_map/pallas_call | solution.py:69
  (30 shorter events, 0.6 us)
Async XLA Ops:
  0.6 30.5 %copy-start = (f32[1,2,6144]{2,1,0:T(2,128)S(1)}, f32[1,2,6144]{2,1,0:T(2,128)}, u32[]{:S(2)}) copy-start(f32[1,2,6144]{2,1,0:T(2,128)} %param.17) | copy-start | bytes 147460
  0.6 30.5 %copy-start.1 = (f32[1,2,6144]{2,1,0:T(2,128)S(1)}, f32[1,2,6144]{2,1,0:T(2,128)}, u32[]{:S(2)}) copy-start(f32[1,2,6144]{2,1,0:T(2,128)} %param.18) | copy-start | bytes 147460
  0.7 30.4 %copy-start.2 = (f32[1,2,6144]{2,1,0:T(2,128)S(1)}, f32[1,2,6144]{2,1,0:T(2,128)}, u32[]{:S(2)}) copy-start(f32[1,2,6144]{2,1,0:T(2,128)} %param.19) | copy-start | bytes 147460
  0.7 37.8 %copy-start.3 = (f32[1,6144]{1,0:T(1,128)S(1)}, f32[1,6144]{1,0:T(1,128)}, u32[]{:S(2)}) copy-start(f32[1,6144]{1,0:T(1,128)} %param.14) | copy-start | bytes 73732
  0.7 37.8 %copy-start.4 = (f32[1,6144]{1,0:T(1,128)S(1)}, f32[1,6144]{1,0:T(1,128)}, u32[]{:S(2)}) copy-start(f32[1,6144]{1,0:T(1,128)} %param.15) | copy-start | bytes 73732
  0.7 37.8 %copy-start.5 = (f32[1,6144]{1,0:T(1,128)S(1)}, f32[1,6144]{1,0:T(1,128)}, u32[]{:S(2)}) copy-start(f32[1,6144]{1,0:T(1,128)} %param.16) | copy-start | bytes 73732
  3.7 1.7 %collective-permute-start = (bf16[1152,128]{1,0:T(8,128)(2,1)S(1)}, bf16[1152,128]{1,0:T(8,128)(2,1)S(1)}, u32[]{:S(2)}, u32[]{:S(2)}) collective-permute-start(bf16[1152,128]{1,0:T(8,128)(2,1)S(1)} %get-tuple-element.26), channel_id=1, source_target_pairs={{0,1},{1,0},{2,3},{3,2},{4,5},{5,4},{6,7},{7,6},{8,9},{9,8},{10,11... | collective-permute-start | bytes 884744 | tf_op jit(solution)/shard_map/ppermute | solution.py:374
  5.5 6.3 %collective-permute-start.1 = (bf16[288,128]{1,0:T(8,128)(2,1)S(1)}, bf16[288,128]{1,0:T(8,128)(2,1)S(1)}, u32[]{:S(2)}, u32[]{:S(2)}) collective-permute-start(bf16[288,128]{1,0:T(8,128)(2,1)S(1)} %get-tuple-element.44), channel_id=1, source_target_pairs={{0,7},{1,6},{2,5},{3,4},{4,3},{5,2},{6,1},{7,0},{8,15},{9,14},{10,... | collective-permute-start | bytes 221192 | tf_op jit(solution)/shard_map/ppermute | solution.py:370
  9.2 4.5 %collective-permute-start.2 = (bf16[288,128]{1,0:T(8,128)(2,1)S(1)}, bf16[288,128]{1,0:T(8,128)(2,1)S(1)}, u32[]{:S(2)}, u32[]{:S(2)}) collective-permute-start(bf16[288,128]{1,0:T(8,128)(2,1)S(1)} %get-tuple-element.43), channel_id=1, source_target_pairs={{0,4},{1,5},{2,6},{3,7},{4,0},{5,1},{6,2},{7,3},{8,12},{9,13},{10,... | collective-permute-start | bytes 221192 | tf_op jit(solution)/shard_map/ppermute | solution.py:370
  9.7 4.3 %collective-permute-start.3 = (bf16[288,128]{1,0:T(8,128)(2,1)S(1)}, bf16[288,128]{1,0:T(8,128)(2,1)S(1)}, u32[]{:S(2)}, u32[]{:S(2)}) collective-permute-start(bf16[288,128]{1,0:T(8,128)(2,1)S(1)} %get-tuple-element.42), channel_id=1, source_target_pairs={{0,3},{1,2},{2,1},{3,0},{4,7},{5,6},{6,5},{7,4},{8,11},{9,10},{10,... | collective-permute-start | bytes 221192 | tf_op jit(solution)/shard_map/ppermute | solution.py:370
  14.0 4.0 %collective-permute-start.4 = (bf16[208,128]{1,0:T(8,128)(2,1)S(1)}, bf16[208,128]{1,0:T(8,128)(2,1)S(1)}, u32[]{:S(2)}, u32[]{:S(2)}) collective-permute-start(bf16[208,128]{1,0:T(8,128)(2,1)S(1)} %get-tuple-element.27.refs_0_), channel_id=1, source_target_pairs={{0,9},{1,8},{2,11},{3,10},{4,13},{5,12},{6,15},{7,14},{8,1},{9,0},... | collective-permute-start | bytes 159752 | tf_op jit(solution)/shard_map/ppermute | solution.py:370
  15.4 5.3 %collective-permute-start.10 = (bf16[144,128]{1,0:T(8,128)(2,1)S(1)}, bf16[144,128]{1,0:T(8,128)(2,1)S(1)}, u32[]{:S(2)}, u32[]{:S(2)}) collective-permute-start(bf16[144,128]{1,0:T(8,128)(2,1)S(1)} %get-tuple-element.37.refs_0_), channel_id=1, source_target_pairs={{0,17},{1,16},{2,19},{3,18},{4,21},{5,20},{6,23},{7,22},{8,25},{9,... | collective-permute-start | bytes 110600 | tf_op jit(solution)/shard_map/ppermute | solution.py:370
  18.1 4.8 %collective-permute-start.5 = (bf16[208,128]{1,0:T(8,128)(2,1)S(1)}, bf16[208,128]{1,0:T(8,128)(2,1)S(1)}, u32[]{:S(2)}, u32[]{:S(2)}) collective-permute-start(bf16[208,128]{1,0:T(8,128)(2,1)S(1)} %shard_map.163.refs_0_), channel_id=1, source_target_pairs={{0,17},{1,16},{2,19},{3,18},{4,21},{5,20},{6,23},{7,22},{8,25},{9,... | collective-permute-start | bytes 159752 | tf_op jit(solution)/shard_map/ppermute | solution.py:370
  20.7 7.4 %collective-permute-start.11 = (bf16[144,128]{1,0:T(8,128)(2,1)S(1)}, bf16[144,128]{1,0:T(8,128)(2,1)S(1)}, u32[]{:S(2)}, u32[]{:S(2)}) collective-permute-start(bf16[144,128]{1,0:T(8,128)(2,1)S(1)} %get-tuple-element.38.refs_9_), channel_id=1, source_target_pairs={{0,9},{1,8},{2,11},{3,10},{4,13},{5,12},{6,15},{7,14},{8,1},{9,0},... | collective-permute-start | bytes 110600 | tf_op jit(solution)/shard_map/ppermute | solution.py:370
  22.0 6.1 %collective-permute-start.12 = (bf16[144,128]{1,0:T(8,128)(2,1)S(1)}, bf16[144,128]{1,0:T(8,128)(2,1)S(1)}, u32[]{:S(2)}, u32[]{:S(2)}) collective-permute-start(bf16[144,128]{1,0:T(8,128)(2,1)S(1)} %get-tuple-element.39.refs_11_), channel_id=1, source_target_pairs={{0,9},{1,8},{2,11},{3,10},{4,13},{5,12},{6,15},{7,14},{8,1},{9,0},... | collective-permute-start | bytes 110600 | tf_op jit(solution)/shard_map/ppermute | solution.py:370
  22.9 2.2 %collective-permute-start.6 = (f32[8,128]{1,0:T(8,128)S(1)}, f32[8,128]{1,0:T(8,128)S(1)}, u32[]{:S(2)}, u32[]{:S(2)}) collective-permute-start(f32[8,128]{1,0:T(8,128)S(1)} %get-tuple-element.28), channel_id=1, source_target_pairs={{0,1},{1,0},{2,3},{3,2},{4,5},{5,4},{6,7},{7,6},{8,9},{9,8},{10,11... | collective-permute-start | bytes 12296 | tf_op jit(solution)/shard_map/ppermute | solution.py:374
  25.2 3.9 %collective-permute-start.7 = (f32[8,128]{1,0:T(8,128)S(1)}, f32[8,128]{1,0:T(8,128)S(1)}, u32[]{:S(2)}, u32[]{:S(2)}) collective-permute-start(f32[8,128]{1,0:T(8,128)S(1)} %add.19.refs_0_), channel_id=1, source_target_pairs={{0,7},{1,6},{2,5},{3,4},{4,3},{5,2},{6,1},{7,0},{8,15},{9,14},{10,... | collective-permute-start | bytes 12296 | tf_op jit(solution)/shard_map/ppermute | solution.py:370
  26.8 3.6 %collective-permute-start.8 = (f32[8,128]{1,0:T(8,128)S(1)}, f32[8,128]{1,0:T(8,128)S(1)}, u32[]{:S(2)}, u32[]{:S(2)}) collective-permute-start(f32[8,128]{1,0:T(8,128)S(1)} %add.19.refs_0_), channel_id=1, source_target_pairs={{0,4},{1,5},{2,6},{3,7},{4,0},{5,1},{6,2},{7,3},{8,12},{9,13},{10,... | collective-permute-start | bytes 12296 | tf_op jit(solution)/shard_map/ppermute | solution.py:370
  28.1 3.0 %collective-permute-start.9 = (f32[8,128]{1,0:T(8,128)S(1)}, f32[8,128]{1,0:T(8,128)S(1)}, u32[]{:S(2)}, u32[]{:S(2)}) collective-permute-start(f32[8,128]{1,0:T(8,128)S(1)} %add.19.refs_0_), channel_id=1, source_target_pairs={{0,3},{1,2},{2,1},{3,0},{4,7},{5,6},{6,5},{7,4},{8,11},{9,10},{10,... | collective-permute-start | bytes 12296 | tf_op jit(solution)/shard_map/ppermute | solution.py:370
  31.4 4.3 %collective-permute-start.13 = (bf16[288,128]{1,0:T(8,128)(2,1)S(1)}, bf16[288,128]{1,0:T(8,128)(2,1)S(1)}, u32[]{:S(2)}, u32[]{:S(2)}) collective-permute-start(bf16[288,128]{1,0:T(8,128)(2,1)S(1)} %shard_map.167.refs_0_), channel_id=1, source_target_pairs={{0,3},{1,2},{2,1},{3,0},{4,7},{5,6},{6,5},{7,4},{8,11},{9,10},{10,... | collective-permute-start | bytes 221192 | tf_op jit(solution)/shard_map/ppermute | solution.py:370
  31.8 4.6 %collective-permute-start.14 = (bf16[288,128]{1,0:T(8,128)(2,1)S(1)}, bf16[288,128]{1,0:T(8,128)(2,1)S(1)}, u32[]{:S(2)}, u32[]{:S(2)}) collective-permute-start(bf16[288,128]{1,0:T(8,128)(2,1)S(1)} %shard_map.167.refs_0_), channel_id=1, source_target_pairs={{0,4},{1,5},{2,6},{3,7},{4,0},{5,1},{6,2},{7,3},{8,12},{9,13},{10,... | collective-permute-start | bytes 221192 | tf_op jit(solution)/shard_map/ppermute | solution.py:370
  33.2 5.1 %collective-permute-start.15 = (bf16[288,128]{1,0:T(8,128)(2,1)S(1)}, bf16[288,128]{1,0:T(8,128)(2,1)S(1)}, u32[]{:S(2)}, u32[]{:S(2)}) collective-permute-start(bf16[288,128]{1,0:T(8,128)(2,1)S(1)} %shard_map.167.refs_0_), channel_id=1, source_target_pairs={{0,7},{1,6},{2,5},{3,4},{4,3},{5,2},{6,1},{7,0},{8,15},{9,14},{10,... | collective-permute-start | bytes 221192 | tf_op jit(solution)/shard_map/ppermute | solution.py:370
  34.4 5.0 %collective-permute-start.16 = (bf16[288,128]{1,0:T(8,128)(2,1)S(1)}, bf16[288,128]{1,0:T(8,128)(2,1)S(1)}, u32[]{:S(2)}, u32[]{:S(2)}) collective-permute-start(bf16[288,128]{1,0:T(8,128)(2,1)S(1)} %shard_map.167.refs_0_), channel_id=1, source_target_pairs={{0,1},{1,0},{2,3},{3,2},{4,5},{5,4},{6,7},{7,6},{8,9},{9,8},{10,11... | collective-permute-start | bytes 221192 | tf_op jit(solution)/shard_map/ppermute | solution.py:374
  35.7 3.7 %collective-permute-start.17 = (bf16[288,128]{1,0:T(8,128)(2,1)S(1)}, bf16[288,128]{1,0:T(8,128)(2,1)S(1)}, u32[]{:S(2)}, u32[]{:S(2)}) collective-permute-start(bf16[288,128]{1,0:T(8,128)(2,1)S(1)} %collective-permute-done.13.refs_1_), channel_id=1, source_target_pairs={{0,1},{1,0},{2,3},{3,2},{4,5},{5,4},{6,7},{7,6},{8,9},{9,8},{10,11... | collective-permute-start | bytes 221192 | tf_op jit(solution)/shard_map/ppermute | solution.py:374
  36.4 3.0 %collective-permute-start.18 = (bf16[288,128]{1,0:T(8,128)(2,1)S(1)}, bf16[288,128]{1,0:T(8,128)(2,1)S(1)}, u32[]{:S(2)}, u32[]{:S(2)}) collective-permute-start(bf16[288,128]{1,0:T(8,128)(2,1)S(1)} %collective-permute-done.14.refs_2_), channel_id=1, source_target_pairs={{0,1},{1,0},{2,3},{3,2},{4,5},{5,4},{6,7},{7,6},{8,9},{9,8},{10,11... | collective-permute-start | bytes 221192 | tf_op jit(solution)/shard_map/ppermute | solution.py:374
  38.4 1.3 %collective-permute-start.19 = (bf16[288,128]{1,0:T(8,128)(2,1)S(1)}, bf16[288,128]{1,0:T(8,128)(2,1)S(1)}, u32[]{:S(2)}, u32[]{:S(2)}) collective-permute-start(bf16[288,128]{1,0:T(8,128)(2,1)S(1)} %collective-permute-done.15.refs_3_), channel_id=1, source_target_pairs={{0,1},{1,0},{2,3},{3,2},{4,5},{5,4},{6,7},{7,6},{8,9},{9,8},{10,11... | collective-permute-start | bytes 221192 | tf_op jit(solution)/shard_map/ppermute | solution.py:374

commit v19 on v17

--- a/solution.py
+++ b/solution.py
@@ -272,6 +272,10 @@
 PARTS = 2
 
 
+def gather_order(chips):
+    return [0, 1, chips - 1, *range(2, chips - 1)] if chips > 2 else list(range(chips))
+
+
 def order_kernel(plan, *refs):
     n_dp = plan.n_dp
     parts, (attn, exp, rows, rows_a, rows_e, attn_v, exp_v, sems) = refs[:n_dp], refs[n_dp:]
@@ -279,7 +283,7 @@
     me_ex = lax.axis_index("expert")
     my_role = role_of(me // 2, me % 2, me_ex)
     for i, part in enumerate(parts):
-        chip, role = (i % plan.chips) ^ (me // 2), (i // plan.chips) ^ my_role
+        chip, role = gather_order(plan.chips)[i % plan.chips] ^ (me // 2), (i // plan.chips) ^ my_role
         blocks = [(e, e * plan.size_a, plan.size_a) for e in range(plan.n_expert)]
         for expert, start, size in blocks + [(me_ex, plan.all_a, plan.size_e)]:
             owner = 2 * chip + role_of(chip, role, expert)
@@ -438,7 +442,7 @@
         [*squares, g_attn, g_exp, *state_a, *state_e],
         [block_a] * 3 + [block_e] * 3,
     )
-    near = [mine] + [swap(mine, chips=c) for c in range(1, chips)]
+    near = [mine] + [swap(mine, chips=c) for c in gather_order(chips)[1:]]
     far = [swap_cores(piece) for piece in near]
     attn_full, expert_full = put_in_order(plan, near + far)
     new_a = [from_blocks(value, rows_a) for value in (wa, ma, va)]

time: 40.8 us -> 42.2 us (1.034)
  waiting for transfers between devices: 13.5 us -> 15 us
    ppermute x14, waiting for transfers between devices: 11 us -> 12.3 us  [swap(): return lax.ppermute(value, ('expert', 'dp'), pairs)]
where the time goes in v19:
time: 42.2 us; the launch traced here: 42 us
  starting transfers between devices  20.8 us (49%)
  waiting for transfers between devices  15 us (36%)
  Pallas kernels  5.44 us (13%)
  between operations  0.76 us (2%)
    ppermute x14, starting transfers between devices, swap(): return lax.ppermute(value, ('expert', 'dp'), pairs)  19.5 us
    ppermute x14, waiting for transfers between devices, swap(): return lax.ppermute(value, ('expert', 'dp'), pairs)  12.3 us
    pallas_call x8, Pallas kernels, call(): pl.pallas_call(kernel, in_specs=[pl.BlockSpec(memory_space=in_space)] * l...  5.44 us
    ppermute x6, waiting for transfers between devices, swap_cores(): lax.ppermute(value, 'dp', [(i, i ^ 1) for i in range(lax.axis_size('dp'))])  2.62 us
    ppermute x6, starting transfers between devices, swap_cores(): lax.ppermute(value, 'dp', [(i, i ^ 1) for i in range(lax.axis_size('dp'))])  1.25 us
  transfers between devices with their start and end apart: 20, of which 14 were waited for; matrix products, arithmetic and copies ran while one was open for 0% of the time, Pallas kernels for 2%

profile of v19, /device:TPU:0, one launch (start us, length us, event | category | flops | bytes accessed | tf_op | source)
XLA Modules:
  0.0 42.0 jit_solution(4257048731196988371)
XLA Ops:
  0.7 3.0 %shard_map.161 = (f32[1152,128]{1,0:T(8,128)S(1)}, bf16[1152,128]{1,0:T(8,128)(2,1)S(1)}, bf16[144,128]{1,0:T(8,128)(2,1)S(1)}) custom-call(bf16[32,256]{1,0:T(8,128)(2,1)} %bitcast.54, bf16[256,6144]{1,0:T(8,128)(2,1)} %refs_1_.1, bf16[16,128]{1,0:T(8,128)(2,1)} %bitcast.55, bf16[128,6144]{1,0:T(8,128)(2,1)} %bitcast.53, f32[48,128]{1,0:T(8,128)} %bitcast.47, ...), custom_call_target="tpu_custom_call" | custom-call | tf_op jit(solution)/shard_map/pallas_call | solution.py:69
  3.7 0.5 %collective-permute-start.1 = (bf16[1152,128]{1,0:T(8,128)(2,1)S(1)}, bf16[1152,128]{1,0:T(8,128)(2,1)S(1)}, u32[]{:S(2)}, u32[]{:S(2)}) collective-permute-start(bf16[1152,128]{1,0:T(8,128)(2,1)S(1)} %get-tuple-element.28), channel_id=1, source_target_pairs={{0,1},{1,0},{2,3},{3,2},{4,5},{5,4},{6,7},{7,6},{8,9},{9,8},{10,11... | collective-permute-start | bytes 884744 | tf_op jit(solution)/shard_map/ppermute | solution.py:379
  4.3 1.2 %collective-permute-done.1 = bf16[1152,128]{1,0:T(8,128)(2,1)S(1)} collective-permute-done((bf16[1152,128]{1,0:T(8,128)(2,1)S(1)}, bf16[1152,128]{1,0:T(8,128)(2,1)S(1)}, u32[]{:S(2)}, u32[]{:S(2)}) %collective-permute-start.1) | collective-permute-done | bytes 294944 | tf_op jit(solution)/shard_map/ppermute | solution.py:379
  5.5 3.6 %collective-permute-start.2 = (bf16[288,128]{1,0:T(8,128)(2,1)S(1)}, bf16[288,128]{1,0:T(8,128)(2,1)S(1)}, u32[]{:S(2)}, u32[]{:S(2)}) collective-permute-start(bf16[288,128]{1,0:T(8,128)(2,1)S(1)} %get-tuple-element.46), channel_id=1, source_target_pairs={{0,7},{1,6},{2,5},{3,4},{4,3},{5,2},{6,1},{7,0},{8,15},{9,14},{10,... | collective-permute-start | bytes 221192 | tf_op jit(solution)/shard_map/ppermute | solution.py:375
  9.2 0.5 %collective-permute-start.3 = (bf16[288,128]{1,0:T(8,128)(2,1)S(1)}, bf16[288,128]{1,0:T(8,128)(2,1)S(1)}, u32[]{:S(2)}, u32[]{:S(2)}) collective-permute-start(bf16[288,128]{1,0:T(8,128)(2,1)S(1)} %get-tuple-element.45), channel_id=1, source_target_pairs={{0,4},{1,5},{2,6},{3,7},{4,0},{5,1},{6,2},{7,3},{8,12},{9,13},{10,... | collective-permute-start | bytes 221192 | tf_op jit(solution)/shard_map/ppermute | solution.py:375
  9.7 1.8 %collective-permute-start = (bf16[144,128]{1,0:T(8,128)(2,1)S(1)}, bf16[144,128]{1,0:T(8,128)(2,1)S(1)}, u32[]{:S(2)}, u32[]{:S(2)}) collective-permute-start(bf16[144,128]{1,0:T(8,128)(2,1)S(1)} %get-tuple-element.26.refs_0_), channel_id=1, source_target_pairs={{0,9},{1,8},{2,11},{3,10},{4,13},{5,12},{6,15},{7,14},{8,1},{9,0},... | collective-permute-start | bytes 110600 | tf_op jit(solution)/shard_map/ppermute | solution.py:375
  11.5 1.6 %collective-permute-done.refs_1_ = bf16[144,128]{1,0:T(8,128)(2,1)S(1)} collective-permute-done((bf16[144,128]{1,0:T(8,128)(2,1)S(1)}, bf16[144,128]{1,0:T(8,128)(2,1)S(1)}, u32[]{:S(2)}, u32[]{:S(2)}) %collective-permute-start) | collective-permute-done | bytes 36896 | tf_op jit(solution)/shard_map/ppermute | solution.py:375
  13.2 0.5 %collective-permute-done.3.refs_4_ = bf16[288,128]{1,0:T(8,128)(2,1)S(1)} collective-permute-done((bf16[288,128]{1,0:T(8,128)(2,1)S(1)}, bf16[288,128]{1,0:T(8,128)(2,1)S(1)}, u32[]{:S(2)}, u32[]{:S(2)}) %collective-permute-start.3) | collective-permute-done | bytes 73760 | tf_op jit(solution)/shard_map/ppermute | solution.py:375
  13.7 0.3 collective-permute-done.4.refs_5_
  14.0 1.4 %collective-permute-start.5 = (bf16[208,128]{1,0:T(8,128)(2,1)S(1)}, bf16[208,128]{1,0:T(8,128)(2,1)S(1)}, u32[]{:S(2)}, u32[]{:S(2)}) collective-permute-start(bf16[208,128]{1,0:T(8,128)(2,1)S(1)} %get-tuple-element.29.refs_0_), channel_id=1, source_target_pairs={{0,9},{1,8},{2,11},{3,10},{4,13},{5,12},{6,15},{7,14},{8,1},{9,0},... | collective-permute-start | bytes 159752 | tf_op jit(solution)/shard_map/ppermute | solution.py:375
  15.4 2.5 %collective-permute-start.11 = (bf16[144,128]{1,0:T(8,128)(2,1)S(1)}, bf16[144,128]{1,0:T(8,128)(2,1)S(1)}, u32[]{:S(2)}, u32[]{:S(2)}) collective-permute-start(bf16[144,128]{1,0:T(8,128)(2,1)S(1)} %get-tuple-element.26.refs_0_), channel_id=1, source_target_pairs={{0,24},{1,25},{2,26},{3,27},{4,28},{5,29},{6,30},{7,31},{8,16},{9,... | collective-permute-start | bytes 110600 | tf_op jit(solution)/shard_map/ppermute | solution.py:375
  18.0 2.5 %collective-permute-start.6 = (bf16[208,128]{1,0:T(8,128)(2,1)S(1)}, bf16[208,128]{1,0:T(8,128)(2,1)S(1)}, u32[]{:S(2)}, u32[]{:S(2)}) collective-permute-start(bf16[208,128]{1,0:T(8,128)(2,1)S(1)} %shard_map.163.refs_0_), channel_id=1, source_target_pairs={{0,17},{1,16},{2,19},{3,18},{4,21},{5,20},{6,23},{7,22},{8,25},{9,... | collective-permute-start | bytes 159752 | tf_op jit(solution)/shard_map/ppermute | solution.py:375
  20.4 0.8 %collective-permute-done.11.refs_1_ = bf16[144,128]{1,0:T(8,128)(2,1)S(1)} collective-permute-done((bf16[144,128]{1,0:T(8,128)(2,1)S(1)}, bf16[144,128]{1,0:T(8,128)(2,1)S(1)}, u32[]{:S(2)}, u32[]{:S(2)}) %collective-permute-start.11) | collective-permute-done | bytes 36896 | tf_op jit(solution)/shard_map/ppermute | solution.py:375
  21.2 1.5 %collective-permute-done.6.refs_1_ = bf16[208,128]{1,0:T(8,128)(2,1)S(1)} collective-permute-done((bf16[208,128]{1,0:T(8,128)(2,1)S(1)}, bf16[208,128]{1,0:T(8,128)(2,1)S(1)}, u32[]{:S(2)}, u32[]{:S(2)}) %collective-permute-start.6) | collective-permute-done | bytes 53280 | tf_op jit(solution)/shard_map/ppermute | solution.py:375
  22.8 0.2 collective-permute-start.7
  23.0 1.0 %collective-permute-done.7 = f32[8,128]{1,0:T(8,128)S(1)} collective-permute-done((f32[8,128]{1,0:T(8,128)S(1)}, f32[8,128]{1,0:T(8,128)S(1)}, u32[]{:S(2)}, u32[]{:S(2)}) %collective-permute-start.7) | collective-permute-done | bytes 4128 | tf_op jit(solution)/shard_map/ppermute | solution.py:379
  24.0 3.2 %collective-permute-start.10 = (f32[8,128]{1,0:T(8,128)S(1)}, f32[8,128]{1,0:T(8,128)S(1)}, u32[]{:S(2)}, u32[]{:S(2)}) collective-permute-start(f32[8,128]{1,0:T(8,128)S(1)} %add.19.refs_0_), channel_id=1, source_target_pairs={{0,7},{1,6},{2,5},{3,4},{4,3},{5,2},{6,1},{7,0},{8,15},{9,14},{10,... | collective-permute-start | bytes 12296 | tf_op jit(solution)/shard_map/ppermute | solution.py:375
  27.2 0.7 %collective-permute-start.8 = (f32[8,128]{1,0:T(8,128)S(1)}, f32[8,128]{1,0:T(8,128)S(1)}, u32[]{:S(2)}, u32[]{:S(2)}) collective-permute-start(f32[8,128]{1,0:T(8,128)S(1)} %add.19.refs_0_), channel_id=1, source_target_pairs={{0,4},{1,5},{2,6},{3,7},{4,0},{5,1},{6,2},{7,3},{8,12},{9,13},{10,... | collective-permute-start | bytes 12296 | tf_op jit(solution)/shard_map/ppermute | solution.py:375
  27.9 0.7 %collective-permute-done.10.refs_3_ = f32[8,128]{1,0:T(8,128)S(1)} collective-permute-done((f32[8,128]{1,0:T(8,128)S(1)}, f32[8,128]{1,0:T(8,128)S(1)}, u32[]{:S(2)}, u32[]{:S(2)}) %collective-permute-start.10) | collective-permute-done | bytes 4128 | tf_op jit(solution)/shard_map/ppermute | solution.py:375
  28.5 2.3 %collective-permute-done.8.refs_1_ = f32[8,128]{1,0:T(8,128)S(1)} collective-permute-done((f32[8,128]{1,0:T(8,128)S(1)}, f32[8,128]{1,0:T(8,128)S(1)}, u32[]{:S(2)}, u32[]{:S(2)}) %collective-permute-start.8) | collective-permute-done | bytes 4128 | tf_op jit(solution)/shard_map/ppermute | solution.py:375
  30.9 0.3 shard_map.167.refs_0_
  31.2 0.4 collective-permute-start.13
  31.6 2.3 %collective-permute-start.14 = (bf16[288,128]{1,0:T(8,128)(2,1)S(1)}, bf16[288,128]{1,0:T(8,128)(2,1)S(1)}, u32[]{:S(2)}, u32[]{:S(2)}) collective-permute-start(bf16[288,128]{1,0:T(8,128)(2,1)S(1)} %shard_map.167.refs_0_), channel_id=1, source_target_pairs={{0,7},{1,6},{2,5},{3,4},{4,3},{5,2},{6,1},{7,0},{8,15},{9,14},{10,... | collective-permute-start | bytes 221192 | tf_op jit(solution)/shard_map/ppermute | solution.py:375
  33.8 0.7 %collective-permute-start.15 = (bf16[288,128]{1,0:T(8,128)(2,1)S(1)}, bf16[288,128]{1,0:T(8,128)(2,1)S(1)}, u32[]{:S(2)}, u32[]{:S(2)}) collective-permute-start(bf16[288,128]{1,0:T(8,128)(2,1)S(1)} %shard_map.167.refs_0_), channel_id=1, source_target_pairs={{0,4},{1,5},{2,6},{3,7},{4,0},{5,1},{6,2},{7,3},{8,12},{9,13},{10,... | collective-permute-start | bytes 221192 | tf_op jit(solution)/shard_map/ppermute | solution.py:375
  34.5 1.0 %collective-permute-done.13.refs_1_ = bf16[288,128]{1,0:T(8,128)(2,1)S(1)} collective-permute-done((bf16[288,128]{1,0:T(8,128)(2,1)S(1)}, bf16[288,128]{1,0:T(8,128)(2,1)S(1)}, u32[]{:S(2)}, u32[]{:S(2)}) %collective-permute-start.13) | collective-permute-done | bytes 73760 | tf_op jit(solution)/shard_map/ppermute | solution.py:375
  35.5 0.4 collective-permute-start.17
  35.9 2.1 %collective-permute-done.14.refs_2_ = bf16[288,128]{1,0:T(8,128)(2,1)S(1)} collective-permute-done((bf16[288,128]{1,0:T(8,128)(2,1)S(1)}, bf16[288,128]{1,0:T(8,128)(2,1)S(1)}, u32[]{:S(2)}, u32[]{:S(2)}) %collective-permute-start.14) | collective-permute-done | bytes 73760 | tf_op jit(solution)/shard_map/ppermute | solution.py:375
  38.0 0.1 collective-permute-start.18
  38.1 1.5 %collective-permute-done.15.refs_3_ = bf16[288,128]{1,0:T(8,128)(2,1)S(1)} collective-permute-done((bf16[288,128]{1,0:T(8,128)(2,1)S(1)}, bf16[288,128]{1,0:T(8,128)(2,1)S(1)}, u32[]{:S(2)}, u32[]{:S(2)}) %collective-permute-start.15) | collective-permute-done | bytes 73760 | tf_op jit(solution)/shard_map/ppermute | solution.py:375
  39.6 0.9 %shard_map.165 = (f32[48,128]{1,0:T(8,128)}, f32[48,128]{1,0:T(8,128)}, f32[48,128]{1,0:T(8,128)}, f32[96,128]{1,0:T(8,128)}, f32[96,128]{1,0:T(8,128)}, /*index=5*/f32[96,128]{1,0:T(8,128)}) custom-call(f32[8,128]{1,0:T(8,128)S(1)} %add.19.refs_0_, f32[8,128]{1,0:T(8,128)S(1)} %collective-permute-done.8.refs_1_, ...), custom_call_target="tpu_custom_call" | custom-call | tf_op jit(solution)/shard_map/pallas_call | solution.py:69
  40.5 0.4 collective-permute-done.19.refs_7_
  40.8 1.2 %shard_map.168 = (bf16[32,6144]{1,0:T(8,128)(2,1)}, bf16[1,16,6144]{2,1,0:T(8,128)(2,1)}) custom-call(bf16[288,128]{1,0:T(8,128)(2,1)S(1)} %shard_map.167.refs_0_, bf16[288,128]{1,0:T(8,128)(2,1)S(1)} %collective-permute-done.13.refs_1_, bf16[288,128]{1,0:T(8,128)(2,1)S(1)} %collective-permute-done.14.refs_2_, ...), custom_call_target="tpu_custom_call" | custom-call | tf_op jit(solution)/shard_map/pallas_call | solution.py:69
  (30 shorter events, 0.4 us)
Async XLA Ops:
  0.6 30.3 %copy-start = (f32[1,2,6144]{2,1,0:T(2,128)S(1)}, f32[1,2,6144]{2,1,0:T(2,128)}, u32[]{:S(2)}) copy-start(f32[1,2,6144]{2,1,0:T(2,128)} %param.17) | copy-start | bytes 147460
  0.6 30.3 %copy-start.1 = (f32[1,2,6144]{2,1,0:T(2,128)S(1)}, f32[1,2,6144]{2,1,0:T(2,128)}, u32[]{:S(2)}) copy-start(f32[1,2,6144]{2,1,0:T(2,128)} %param.18) | copy-start | bytes 147460
  0.7 30.3 %copy-start.2 = (f32[1,2,6144]{2,1,0:T(2,128)S(1)}, f32[1,2,6144]{2,1,0:T(2,128)}, u32[]{:S(2)}) copy-start(f32[1,2,6144]{2,1,0:T(2,128)} %param.19) | copy-start | bytes 147460
  0.7 38.9 %copy-start.3 = (f32[1,6144]{1,0:T(1,128)S(1)}, f32[1,6144]{1,0:T(1,128)}, u32[]{:S(2)}) copy-start(f32[1,6144]{1,0:T(1,128)} %param.14) | copy-start | bytes 73732
  0.7 38.9 %copy-start.4 = (f32[1,6144]{1,0:T(1,128)S(1)}, f32[1,6144]{1,0:T(1,128)}, u32[]{:S(2)}) copy-start(f32[1,6144]{1,0:T(1,128)} %param.15) | copy-start | bytes 73732
  0.7 38.9 %copy-start.5 = (f32[1,6144]{1,0:T(1,128)S(1)}, f32[1,6144]{1,0:T(1,128)}, u32[]{:S(2)}) copy-start(f32[1,6144]{1,0:T(1,128)} %param.16) | copy-start | bytes 73732
  3.7 1.7 %collective-permute-start.1 = (bf16[1152,128]{1,0:T(8,128)(2,1)S(1)}, bf16[1152,128]{1,0:T(8,128)(2,1)S(1)}, u32[]{:S(2)}, u32[]{:S(2)}) collective-permute-start(bf16[1152,128]{1,0:T(8,128)(2,1)S(1)} %get-tuple-element.28), channel_id=1, source_target_pairs={{0,1},{1,0},{2,3},{3,2},{4,5},{5,4},{6,7},{7,6},{8,9},{9,8},{10,11... | collective-permute-start | bytes 884744 | tf_op jit(solution)/shard_map/ppermute | solution.py:379
  5.5 7.6 %collective-permute-start.2 = (bf16[288,128]{1,0:T(8,128)(2,1)S(1)}, bf16[288,128]{1,0:T(8,128)(2,1)S(1)}, u32[]{:S(2)}, u32[]{:S(2)}) collective-permute-start(bf16[288,128]{1,0:T(8,128)(2,1)S(1)} %get-tuple-element.46), channel_id=1, source_target_pairs={{0,7},{1,6},{2,5},{3,4},{4,3},{5,2},{6,1},{7,0},{8,15},{9,14},{10,... | collective-permute-start | bytes 221192 | tf_op jit(solution)/shard_map/ppermute | solution.py:375
  9.2 4.5 %collective-permute-start.3 = (bf16[288,128]{1,0:T(8,128)(2,1)S(1)}, bf16[288,128]{1,0:T(8,128)(2,1)S(1)}, u32[]{:S(2)}, u32[]{:S(2)}) collective-permute-start(bf16[288,128]{1,0:T(8,128)(2,1)S(1)} %get-tuple-element.45), channel_id=1, source_target_pairs={{0,4},{1,5},{2,6},{3,7},{4,0},{5,1},{6,2},{7,3},{8,12},{9,13},{10,... | collective-permute-start | bytes 221192 | tf_op jit(solution)/shard_map/ppermute | solution.py:375
  9.7 4.3 %collective-permute-start.4 = (bf16[288,128]{1,0:T(8,128)(2,1)S(1)}, bf16[288,128]{1,0:T(8,128)(2,1)S(1)}, u32[]{:S(2)}, u32[]{:S(2)}) collective-permute-start(bf16[288,128]{1,0:T(8,128)(2,1)S(1)} %get-tuple-element.44), channel_id=1, source_target_pairs={{0,3},{1,2},{2,1},{3,0},{4,7},{5,6},{6,5},{7,4},{8,11},{9,10},{10,... | collective-permute-start | bytes 221192 | tf_op jit(solution)/shard_map/ppermute | solution.py:375
  9.7 3.5 %collective-permute-start = (bf16[144,128]{1,0:T(8,128)(2,1)S(1)}, bf16[144,128]{1,0:T(8,128)(2,1)S(1)}, u32[]{:S(2)}, u32[]{:S(2)}) collective-permute-start(bf16[144,128]{1,0:T(8,128)(2,1)S(1)} %get-tuple-element.26.refs_0_), channel_id=1, source_target_pairs={{0,9},{1,8},{2,11},{3,10},{4,13},{5,12},{6,15},{7,14},{8,1},{9,0},... | collective-permute-start | bytes 110600 | tf_op jit(solution)/shard_map/ppermute | solution.py:375
  14.0 3.9 %collective-permute-start.5 = (bf16[208,128]{1,0:T(8,128)(2,1)S(1)}, bf16[208,128]{1,0:T(8,128)(2,1)S(1)}, u32[]{:S(2)}, u32[]{:S(2)}) collective-permute-start(bf16[208,128]{1,0:T(8,128)(2,1)S(1)} %get-tuple-element.29.refs_0_), channel_id=1, source_target_pairs={{0,9},{1,8},{2,11},{3,10},{4,13},{5,12},{6,15},{7,14},{8,1},{9,0},... | collective-permute-start | bytes 159752 | tf_op jit(solution)/shard_map/ppermute | solution.py:375
  15.4 5.8 %collective-permute-start.11 = (bf16[144,128]{1,0:T(8,128)(2,1)S(1)}, bf16[144,128]{1,0:T(8,128)(2,1)S(1)}, u32[]{:S(2)}, u32[]{:S(2)}) collective-permute-start(bf16[144,128]{1,0:T(8,128)(2,1)S(1)} %get-tuple-element.26.refs_0_), channel_id=1, source_target_pairs={{0,24},{1,25},{2,26},{3,27},{4,28},{5,29},{6,30},{7,31},{8,16},{9,... | collective-permute-start | bytes 110600 | tf_op jit(solution)/shard_map/ppermute | solution.py:375
  18.0 4.8 %collective-permute-start.6 = (bf16[208,128]{1,0:T(8,128)(2,1)S(1)}, bf16[208,128]{1,0:T(8,128)(2,1)S(1)}, u32[]{:S(2)}, u32[]{:S(2)}) collective-permute-start(bf16[208,128]{1,0:T(8,128)(2,1)S(1)} %shard_map.163.refs_0_), channel_id=1, source_target_pairs={{0,17},{1,16},{2,19},{3,18},{4,21},{5,20},{6,23},{7,22},{8,25},{9,... | collective-permute-start | bytes 159752 | tf_op jit(solution)/shard_map/ppermute | solution.py:375
  21.2 6.7 %collective-permute-start.12 = (bf16[144,128]{1,0:T(8,128)(2,1)S(1)}, bf16[144,128]{1,0:T(8,128)(2,1)S(1)}, u32[]{:S(2)}, u32[]{:S(2)}) collective-permute-start(bf16[144,128]{1,0:T(8,128)(2,1)S(1)} %get-tuple-element.40), channel_id=1, source_target_pairs={{0,17},{1,16},{2,19},{3,18},{4,21},{5,20},{6,23},{7,22},{8,25},{9,... | collective-permute-start | bytes 110600 | tf_op jit(solution)/shard_map/ppermute | solution.py:375
  22.8 1.2 %collective-permute-start.7 = (f32[8,128]{1,0:T(8,128)S(1)}, f32[8,128]{1,0:T(8,128)S(1)}, u32[]{:S(2)}, u32[]{:S(2)}) collective-permute-start(f32[8,128]{1,0:T(8,128)S(1)} %get-tuple-element.30), channel_id=1, source_target_pairs={{0,1},{1,0},{2,3},{3,2},{4,5},{5,4},{6,7},{7,6},{8,9},{9,8},{10,11... | collective-permute-start | bytes 12296 | tf_op jit(solution)/shard_map/ppermute | solution.py:379
  24.0 4.5 %collective-permute-start.10 = (f32[8,128]{1,0:T(8,128)S(1)}, f32[8,128]{1,0:T(8,128)S(1)}, u32[]{:S(2)}, u32[]{:S(2)}) collective-permute-start(f32[8,128]{1,0:T(8,128)S(1)} %add.19.refs_0_), channel_id=1, source_target_pairs={{0,7},{1,6},{2,5},{3,4},{4,3},{5,2},{6,1},{7,0},{8,15},{9,14},{10,... | collective-permute-start | bytes 12296 | tf_op jit(solution)/shard_map/ppermute | solution.py:375
  27.2 3.6 %collective-permute-start.8 = (f32[8,128]{1,0:T(8,128)S(1)}, f32[8,128]{1,0:T(8,128)S(1)}, u32[]{:S(2)}, u32[]{:S(2)}) collective-permute-start(f32[8,128]{1,0:T(8,128)S(1)} %add.19.refs_0_), channel_id=1, source_target_pairs={{0,4},{1,5},{2,6},{3,7},{4,0},{5,1},{6,2},{7,3},{8,12},{9,13},{10,... | collective-permute-start | bytes 12296 | tf_op jit(solution)/shard_map/ppermute | solution.py:375
  27.9 3.0 %collective-permute-start.9 = (f32[8,128]{1,0:T(8,128)S(1)}, f32[8,128]{1,0:T(8,128)S(1)}, u32[]{:S(2)}, u32[]{:S(2)}) collective-permute-start(f32[8,128]{1,0:T(8,128)S(1)} %add.19.refs_0_), channel_id=1, source_target_pairs={{0,3},{1,2},{2,1},{3,0},{4,7},{5,6},{6,5},{7,4},{8,11},{9,10},{10,... | collective-permute-start | bytes 12296 | tf_op jit(solution)/shard_map/ppermute | solution.py:375
  31.2 4.3 %collective-permute-start.13 = (bf16[288,128]{1,0:T(8,128)(2,1)S(1)}, bf16[288,128]{1,0:T(8,128)(2,1)S(1)}, u32[]{:S(2)}, u32[]{:S(2)}) collective-permute-start(bf16[288,128]{1,0:T(8,128)(2,1)S(1)} %shard_map.167.refs_0_), channel_id=1, source_target_pairs={{0,3},{1,2},{2,1},{3,0},{4,7},{5,6},{6,5},{7,4},{8,11},{9,10},{10,... | collective-permute-start | bytes 221192 | tf_op jit(solution)/shard_map/ppermute | solution.py:375
  31.6 6.4 %collective-permute-start.14 = (bf16[288,128]{1,0:T(8,128)(2,1)S(1)}, bf16[288,128]{1,0:T(8,128)(2,1)S(1)}, u32[]{:S(2)}, u32[]{:S(2)}) collective-permute-start(bf16[288,128]{1,0:T(8,128)(2,1)S(1)} %shard_map.167.refs_0_), channel_id=1, source_target_pairs={{0,7},{1,6},{2,5},{3,4},{4,3},{5,2},{6,1},{7,0},{8,15},{9,14},{10,... | collective-permute-start | bytes 221192 | tf_op jit(solution)/shard_map/ppermute | solution.py:375
  33.8 5.7 %collective-permute-start.15 = (bf16[288,128]{1,0:T(8,128)(2,1)S(1)}, bf16[288,128]{1,0:T(8,128)(2,1)S(1)}, u32[]{:S(2)}, u32[]{:S(2)}) collective-permute-start(bf16[288,128]{1,0:T(8,128)(2,1)S(1)} %shard_map.167.refs_0_), channel_id=1, source_target_pairs={{0,4},{1,5},{2,6},{3,7},{4,0},{5,1},{6,2},{7,3},{8,12},{9,13},{10,... | collective-permute-start | bytes 221192 | tf_op jit(solution)/shard_map/ppermute | solution.py:375
  34.5 6.0 %collective-permute-start.16 = (bf16[288,128]{1,0:T(8,128)(2,1)S(1)}, bf16[288,128]{1,0:T(8,128)(2,1)S(1)}, u32[]{:S(2)}, u32[]{:S(2)}) collective-permute-start(bf16[288,128]{1,0:T(8,128)(2,1)S(1)} %shard_map.167.refs_0_), channel_id=1, source_target_pairs={{0,1},{1,0},{2,3},{3,2},{4,5},{5,4},{6,7},{7,6},{8,9},{9,8},{10,11... | collective-permute-start | bytes 221192 | tf_op jit(solution)/shard_map/ppermute | solution.py:379
  35.5 4.9 %collective-permute-start.17 = (bf16[288,128]{1,0:T(8,128)(2,1)S(1)}, bf16[288,128]{1,0:T(8,128)(2,1)S(1)}, u32[]{:S(2)}, u32[]{:S(2)}) collective-permute-start(bf16[288,128]{1,0:T(8,128)(2,1)S(1)} %collective-permute-done.13.refs_1_), channel_id=1, source_target_pairs={{0,1},{1,0},{2,3},{3,2},{4,5},{5,4},{6,7},{7,6},{8,9},{9,8},{10,11... | collective-permute-start | bytes 221192 | tf_op jit(solution)/shard_map/ppermute | solution.py:379
  38.0 2.5 %collective-permute-start.18 = (bf16[288,128]{1,0:T(8,128)(2,1)S(1)}, bf16[288,128]{1,0:T(8,128)(2,1)S(1)}, u32[]{:S(2)}, u32[]{:S(2)}) collective-permute-start(bf16[288,128]{1,0:T(8,128)(2,1)S(1)} %collective-permute-done.14.refs_2_), channel_id=1, source_target_pairs={{0,1},{1,0},{2,3},{3,2},{4,5},{5,4},{6,7},{7,6},{8,9},{9,8},{10,11... | collective-permute-start | bytes 221192 | tf_op jit(solution)/shard_map/ppermute | solution.py:379
  39.6 1.3 %collective-permute-start.19 = (bf16[288,128]{1,0:T(8,128)(2,1)S(1)}, bf16[288,128]{1,0:T(8,128)(2,1)S(1)}, u32[]{:S(2)}, u32[]{:S(2)}) collective-permute-start(bf16[288,128]{1,0:T(8,128)(2,1)S(1)} %collective-permute-done.15.refs_3_), channel_id=1, source_target_pairs={{0,1},{1,0},{2,3},{3,2},{4,5},{5,4},{6,7},{7,6},{8,9},{9,8},{10,11... | collective-permute-start | bytes 221192 | tf_op jit(solution)/shard_map/ppermute | solution.py:379

commit v20 on v17

--- a/solution.py
+++ b/solution.py
@@ -402,7 +402,7 @@
     sums = [
         full[c * chunk : (c + 1) * chunk] + got[c * chunk : (c + 1) * chunk].astype(f32) for c in range(chips)
     ]
-    got = [swap(sums[c].astype(bf16), chips=c) for c in reversed(range(1, chips))]
+    got = [swap(sums[c].astype(bf16), chips=c) for c in range(1, chips)]
     shared = ((plan.all_a + 16, LANES), bf16)
     packs = [pack, swap(pack, experts=1)]
     payload, g_exp, both = call(

time: 40.8 us -> 41.4 us (1.015)
    ppermute x6, starting transfers between devices: 1.64 us -> 2.83 us  [swap_cores(): lax.ppermute(value, 'dp', [(i, i ^ 1) for i in range(lax.axis_size('dp'))])]
    ppermute x14, starting transfers between devices: 19.2 us -> 18.2 us  [swap(): return lax.ppermute(value, ('expert', 'dp'), pairs)]
    ppermute x14, waiting for transfers between devices: 11 us -> 11.8 us  [swap(): return lax.ppermute(value, ('expert', 'dp'), pairs)]
  transfers between devices with their start and end apart: 20 -> 20, of which waited for: 14 -> 12; matrix products, arithmetic and copies ran while one was open for 0% -> 0% of each run, Pallas kernels for 2% -> 2%
where the time goes in v20:
time: 41.4 us; the launch traced here: 41.2 us
  starting transfers between devices  21 us (51%)
  waiting for transfers between devices  13.9 us (34%)
  Pallas kernels  5.43 us (13%)
  between operations  0.75 us (2%)
    ppermute x14, starting transfers between devices, swap(): return lax.ppermute(value, ('expert', 'dp'), pairs)  18.2 us
    ppermute x14, waiting for transfers between devices, swap(): return lax.ppermute(value, ('expert', 'dp'), pairs)  11.8 us
    pallas_call x8, Pallas kernels, call(): pl.pallas_call(kernel, in_specs=[pl.BlockSpec(memory_space=in_space)] * l...  5.43 us
    ppermute x6, starting transfers between devices, swap_cores(): lax.ppermute(value, 'dp', [(i, i ^ 1) for i in range(lax.axis_size('dp'))])  2.83 us
    ppermute x6, waiting for transfers between devices, swap_cores(): lax.ppermute(value, 'dp', [(i, i ^ 1) for i in range(lax.axis_size('dp'))])  2.08 us
  transfers between devices with their start and end apart: 20, of which 12 were waited for; matrix products, arithmetic and copies ran while one was open for 0% of the time, Pallas kernels for 2%

profile of v20, /device:TPU:0, one launch (start us, length us, event | category | flops | bytes accessed | tf_op | source)
XLA Modules:
  0.0 41.2 jit_solution(4471072635509870085)
XLA Ops:
  0.7 3.0 %shard_map.161 = (f32[1152,128]{1,0:T(8,128)S(1)}, bf16[1152,128]{1,0:T(8,128)(2,1)S(1)}, bf16[144,128]{1,0:T(8,128)(2,1)S(1)}) custom-call(bf16[32,256]{1,0:T(8,128)(2,1)} %bitcast.54, bf16[256,6144]{1,0:T(8,128)(2,1)} %refs_1_.1, bf16[16,128]{1,0:T(8,128)(2,1)} %bitcast.55, bf16[128,6144]{1,0:T(8,128)(2,1)} %bitcast.53, f32[48,128]{1,0:T(8,128)} %bitcast.47, ...), custom_call_target="tpu_custom_call" | custom-call | tf_op jit(solution)/shard_map/pallas_call | solution.py:69
  3.7 0.5 %collective-permute-start.1 = (bf16[1152,128]{1,0:T(8,128)(2,1)S(1)}, bf16[1152,128]{1,0:T(8,128)(2,1)S(1)}, u32[]{:S(2)}, u32[]{:S(2)}) collective-permute-start(bf16[1152,128]{1,0:T(8,128)(2,1)S(1)} %get-tuple-element.28), channel_id=1, source_target_pairs={{0,1},{1,0},{2,3},{3,2},{4,5},{5,4},{6,7},{7,6},{8,9},{9,8},{10,11... | collective-permute-start | bytes 884744 | tf_op jit(solution)/shard_map/ppermute | solution.py:375
  4.3 1.2 %collective-permute-done.1 = bf16[1152,128]{1,0:T(8,128)(2,1)S(1)} collective-permute-done((bf16[1152,128]{1,0:T(8,128)(2,1)S(1)}, bf16[1152,128]{1,0:T(8,128)(2,1)S(1)}, u32[]{:S(2)}, u32[]{:S(2)}) %collective-permute-start.1) | collective-permute-done | bytes 294944 | tf_op jit(solution)/shard_map/ppermute | solution.py:375
  5.5 2.7 %collective-permute-start.2 = (bf16[288,128]{1,0:T(8,128)(2,1)S(1)}, bf16[288,128]{1,0:T(8,128)(2,1)S(1)}, u32[]{:S(2)}, u32[]{:S(2)}) collective-permute-start(bf16[288,128]{1,0:T(8,128)(2,1)S(1)} %get-tuple-element.46), channel_id=1, source_target_pairs={{0,3},{1,2},{2,1},{3,0},{4,7},{5,6},{6,5},{7,4},{8,11},{9,10},{10,... | collective-permute-start | bytes 221192 | tf_op jit(solution)/shard_map/ppermute | solution.py:371
  8.2 1.5 %collective-permute-start.3 = (bf16[288,128]{1,0:T(8,128)(2,1)S(1)}, bf16[288,128]{1,0:T(8,128)(2,1)S(1)}, u32[]{:S(2)}, u32[]{:S(2)}) collective-permute-start(bf16[288,128]{1,0:T(8,128)(2,1)S(1)} %get-tuple-element.45), channel_id=1, source_target_pairs={{0,4},{1,5},{2,6},{3,7},{4,0},{5,1},{6,2},{7,3},{8,12},{9,13},{10,... | collective-permute-start | bytes 221192 | tf_op jit(solution)/shard_map/ppermute | solution.py:371
  9.7 1.8 %collective-permute-start = (bf16[144,128]{1,0:T(8,128)(2,1)S(1)}, bf16[144,128]{1,0:T(8,128)(2,1)S(1)}, u32[]{:S(2)}, u32[]{:S(2)}) collective-permute-start(bf16[144,128]{1,0:T(8,128)(2,1)S(1)} %get-tuple-element.26.refs_0_), channel_id=1, source_target_pairs={{0,9},{1,8},{2,11},{3,10},{4,13},{5,12},{6,15},{7,14},{8,1},{9,0},... | collective-permute-start | bytes 110600 | tf_op jit(solution)/shard_map/ppermute | solution.py:371
  11.5 1.6 %collective-permute-done.refs_1_ = bf16[144,128]{1,0:T(8,128)(2,1)S(1)} collective-permute-done((bf16[144,128]{1,0:T(8,128)(2,1)S(1)}, bf16[144,128]{1,0:T(8,128)(2,1)S(1)}, u32[]{:S(2)}, u32[]{:S(2)}) %collective-permute-start) | collective-permute-done | bytes 36896 | tf_op jit(solution)/shard_map/ppermute | solution.py:371
  13.2 1.8 %collective-permute-done.4.refs_5_ = bf16[288,128]{1,0:T(8,128)(2,1)S(1)} collective-permute-done((bf16[288,128]{1,0:T(8,128)(2,1)S(1)}, bf16[288,128]{1,0:T(8,128)(2,1)S(1)}, u32[]{:S(2)}, u32[]{:S(2)}) %collective-permute-start.4) | collective-permute-done | bytes 73760 | tf_op jit(solution)/shard_map/ppermute | solution.py:371
  15.0 1.4 %collective-permute-start.5 = (bf16[208,128]{1,0:T(8,128)(2,1)S(1)}, bf16[208,128]{1,0:T(8,128)(2,1)S(1)}, u32[]{:S(2)}, u32[]{:S(2)}) collective-permute-start(bf16[208,128]{1,0:T(8,128)(2,1)S(1)} %get-tuple-element.29.refs_0_), channel_id=1, source_target_pairs={{0,9},{1,8},{2,11},{3,10},{4,13},{5,12},{6,15},{7,14},{8,1},{9,0},... | collective-permute-start | bytes 159752 | tf_op jit(solution)/shard_map/ppermute | solution.py:371
  16.4 2.5 %collective-permute-start.11 = (bf16[144,128]{1,0:T(8,128)(2,1)S(1)}, bf16[144,128]{1,0:T(8,128)(2,1)S(1)}, u32[]{:S(2)}, u32[]{:S(2)}) collective-permute-start(bf16[144,128]{1,0:T(8,128)(2,1)S(1)} %get-tuple-element.26.refs_0_), channel_id=1, source_target_pairs={{0,24},{1,25},{2,26},{3,27},{4,28},{5,29},{6,30},{7,31},{8,16},{9,... | collective-permute-start | bytes 110600 | tf_op jit(solution)/shard_map/ppermute | solution.py:371
  18.9 2.4 %collective-permute-start.6 = (bf16[208,128]{1,0:T(8,128)(2,1)S(1)}, bf16[208,128]{1,0:T(8,128)(2,1)S(1)}, u32[]{:S(2)}, u32[]{:S(2)}) collective-permute-start(bf16[208,128]{1,0:T(8,128)(2,1)S(1)} %shard_map.163.refs_0_), channel_id=1, source_target_pairs={{0,17},{1,16},{2,19},{3,18},{4,21},{5,20},{6,23},{7,22},{8,25},{9,... | collective-permute-start | bytes 159752 | tf_op jit(solution)/shard_map/ppermute | solution.py:371
  21.4 0.8 %collective-permute-done.11.refs_1_ = bf16[144,128]{1,0:T(8,128)(2,1)S(1)} collective-permute-done((bf16[144,128]{1,0:T(8,128)(2,1)S(1)}, bf16[144,128]{1,0:T(8,128)(2,1)S(1)}, u32[]{:S(2)}, u32[]{:S(2)}) %collective-permute-start.11) | collective-permute-done | bytes 36896 | tf_op jit(solution)/shard_map/ppermute | solution.py:371
  22.1 1.6 %collective-permute-done.6.refs_1_ = bf16[208,128]{1,0:T(8,128)(2,1)S(1)} collective-permute-done((bf16[208,128]{1,0:T(8,128)(2,1)S(1)}, bf16[208,128]{1,0:T(8,128)(2,1)S(1)}, u32[]{:S(2)}, u32[]{:S(2)}) %collective-permute-start.6) | collective-permute-done | bytes 53280 | tf_op jit(solution)/shard_map/ppermute | solution.py:371
  23.7 1.3 %collective-permute-start.7 = (f32[8,128]{1,0:T(8,128)S(1)}, f32[8,128]{1,0:T(8,128)S(1)}, u32[]{:S(2)}, u32[]{:S(2)}) collective-permute-start(f32[8,128]{1,0:T(8,128)S(1)} %get-tuple-element.30), channel_id=1, source_target_pairs={{0,1},{1,0},{2,3},{3,2},{4,5},{5,4},{6,7},{7,6},{8,9},{9,8},{10,11... | collective-permute-start | bytes 12296 | tf_op jit(solution)/shard_map/ppermute | solution.py:375
  25.1 0.8 %collective-permute-done.7 = f32[8,128]{1,0:T(8,128)S(1)} collective-permute-done((f32[8,128]{1,0:T(8,128)S(1)}, f32[8,128]{1,0:T(8,128)S(1)}, u32[]{:S(2)}, u32[]{:S(2)}) %collective-permute-start.7) | collective-permute-done | bytes 4128 | tf_op jit(solution)/shard_map/ppermute | solution.py:375
  25.9 1.2 %collective-permute-start.10 = (f32[8,128]{1,0:T(8,128)S(1)}, f32[8,128]{1,0:T(8,128)S(1)}, u32[]{:S(2)}, u32[]{:S(2)}) collective-permute-start(f32[8,128]{1,0:T(8,128)S(1)} %add.19.refs_0_), channel_id=1, source_target_pairs={{0,7},{1,6},{2,5},{3,4},{4,3},{5,2},{6,1},{7,0},{8,15},{9,14},{10,... | collective-permute-start | bytes 12296 | tf_op jit(solution)/shard_map/ppermute | solution.py:371
  27.1 0.7 %collective-permute-start.8 = (f32[8,128]{1,0:T(8,128)S(1)}, f32[8,128]{1,0:T(8,128)S(1)}, u32[]{:S(2)}, u32[]{:S(2)}) collective-permute-start(f32[8,128]{1,0:T(8,128)S(1)} %add.19.refs_0_), channel_id=1, source_target_pairs={{0,4},{1,5},{2,6},{3,7},{4,0},{5,1},{6,2},{7,3},{8,12},{9,13},{10,... | collective-permute-start | bytes 12296 | tf_op jit(solution)/shard_map/ppermute | solution.py:371
  27.8 1.0 %collective-permute-start.9 = (f32[8,128]{1,0:T(8,128)S(1)}, f32[8,128]{1,0:T(8,128)S(1)}, u32[]{:S(2)}, u32[]{:S(2)}) collective-permute-start(f32[8,128]{1,0:T(8,128)S(1)} %add.19.refs_0_), channel_id=1, source_target_pairs={{0,3},{1,2},{2,1},{3,0},{4,7},{5,6},{6,5},{7,4},{8,11},{9,10},{10,... | collective-permute-start | bytes 12296 | tf_op jit(solution)/shard_map/ppermute | solution.py:371
  28.8 1.0 %collective-permute-done.10.refs_3_ = f32[8,128]{1,0:T(8,128)S(1)} collective-permute-done((f32[8,128]{1,0:T(8,128)S(1)}, f32[8,128]{1,0:T(8,128)S(1)}, u32[]{:S(2)}, u32[]{:S(2)}) %collective-permute-start.10) | collective-permute-done | bytes 4128 | tf_op jit(solution)/shard_map/ppermute | solution.py:371
  29.8 0.9 %collective-permute-done.8.refs_1_ = f32[8,128]{1,0:T(8,128)S(1)} collective-permute-done((f32[8,128]{1,0:T(8,128)S(1)}, f32[8,128]{1,0:T(8,128)S(1)}, u32[]{:S(2)}, u32[]{:S(2)}) %collective-permute-start.8) | collective-permute-done | bytes 4128 | tf_op jit(solution)/shard_map/ppermute | solution.py:371
  30.8 0.1 collective-permute-done.9.refs_2_
  30.9 0.3 shard_map.167.refs_0_
  31.2 1.3 %collective-permute-start.13 = (bf16[288,128]{1,0:T(8,128)(2,1)S(1)}, bf16[288,128]{1,0:T(8,128)(2,1)S(1)}, u32[]{:S(2)}, u32[]{:S(2)}) collective-permute-start(bf16[288,128]{1,0:T(8,128)(2,1)S(1)} %shard_map.167.refs_0_), channel_id=1, source_target_pairs={{0,3},{1,2},{2,1},{3,0},{4,7},{5,6},{6,5},{7,4},{8,11},{9,10},{10,... | collective-permute-start | bytes 221192 | tf_op jit(solution)/shard_map/ppermute | solution.py:371
  32.4 0.2 collective-permute-start.14
  32.6 1.6 %collective-permute-start.15 = (bf16[288,128]{1,0:T(8,128)(2,1)S(1)}, bf16[288,128]{1,0:T(8,128)(2,1)S(1)}, u32[]{:S(2)}, u32[]{:S(2)}) collective-permute-start(bf16[288,128]{1,0:T(8,128)(2,1)S(1)} %shard_map.167.refs_0_), channel_id=1, source_target_pairs={{0,7},{1,6},{2,5},{3,4},{4,3},{5,2},{6,1},{7,0},{8,15},{9,14},{10,... | collective-permute-start | bytes 221192 | tf_op jit(solution)/shard_map/ppermute | solution.py:371
  34.2 0.4 collective-permute-start.16
  34.5 0.9 %collective-permute-done.13.refs_1_ = bf16[288,128]{1,0:T(8,128)(2,1)S(1)} collective-permute-done((bf16[288,128]{1,0:T(8,128)(2,1)S(1)}, bf16[288,128]{1,0:T(8,128)(2,1)S(1)}, u32[]{:S(2)}, u32[]{:S(2)}) %collective-permute-start.13) | collective-permute-done | bytes 73760 | tf_op jit(solution)/shard_map/ppermute | solution.py:371
  35.5 0.1 collective-permute-start.17
  35.6 3.0 %collective-permute-done.14.refs_2_ = bf16[288,128]{1,0:T(8,128)(2,1)S(1)} collective-permute-done((bf16[288,128]{1,0:T(8,128)(2,1)S(1)}, bf16[288,128]{1,0:T(8,128)(2,1)S(1)}, u32[]{:S(2)}, u32[]{:S(2)}) %collective-permute-start.14) | collective-permute-done | bytes 73760 | tf_op jit(solution)/shard_map/ppermute | solution.py:371
  38.6 0.5 %collective-permute-start.19 = (bf16[288,128]{1,0:T(8,128)(2,1)S(1)}, bf16[288,128]{1,0:T(8,128)(2,1)S(1)}, u32[]{:S(2)}, u32[]{:S(2)}) collective-permute-start(bf16[288,128]{1,0:T(8,128)(2,1)S(1)} %collective-permute-done.15.refs_3_), channel_id=1, source_target_pairs={{0,1},{1,0},{2,3},{3,2},{4,5},{5,4},{6,7},{7,6},{8,9},{9,8},{10,11... | collective-permute-start | bytes 221192 | tf_op jit(solution)/shard_map/ppermute | solution.py:375
  39.1 0.8 %shard_map.165 = (f32[48,128]{1,0:T(8,128)}, f32[48,128]{1,0:T(8,128)}, f32[48,128]{1,0:T(8,128)}, f32[96,128]{1,0:T(8,128)}, f32[96,128]{1,0:T(8,128)}, /*index=5*/f32[96,128]{1,0:T(8,128)}) custom-call(f32[8,128]{1,0:T(8,128)S(1)} %add.19.refs_0_, f32[8,128]{1,0:T(8,128)S(1)} %collective-permute-done.8.refs_1_, ...), custom_call_target="tpu_custom_call" | custom-call | tf_op jit(solution)/shard_map/pallas_call | solution.py:69
  40.0 1.2 %shard_map.168 = (bf16[32,6144]{1,0:T(8,128)(2,1)}, bf16[1,16,6144]{2,1,0:T(8,128)(2,1)}) custom-call(bf16[288,128]{1,0:T(8,128)(2,1)S(1)} %shard_map.167.refs_0_, bf16[288,128]{1,0:T(8,128)(2,1)S(1)} %collective-permute-done.13.refs_1_, bf16[288,128]{1,0:T(8,128)(2,1)S(1)} %collective-permute-done.14.refs_2_, ...), custom_call_target="tpu_custom_call" | custom-call | tf_op jit(solution)/shard_map/pallas_call | solution.py:69
  (30 shorter events, 0.3 us)
Async XLA Ops:
  0.6 30.2 %copy-start = (f32[1,2,6144]{2,1,0:T(2,128)S(1)}, f32[1,2,6144]{2,1,0:T(2,128)}, u32[]{:S(2)}) copy-start(f32[1,2,6144]{2,1,0:T(2,128)} %param.17) | copy-start | bytes 147460
  0.6 30.2 %copy-start.1 = (f32[1,2,6144]{2,1,0:T(2,128)S(1)}, f32[1,2,6144]{2,1,0:T(2,128)}, u32[]{:S(2)}) copy-start(f32[1,2,6144]{2,1,0:T(2,128)} %param.18) | copy-start | bytes 147460
  0.7 30.2 %copy-start.2 = (f32[1,2,6144]{2,1,0:T(2,128)S(1)}, f32[1,2,6144]{2,1,0:T(2,128)}, u32[]{:S(2)}) copy-start(f32[1,2,6144]{2,1,0:T(2,128)} %param.19) | copy-start | bytes 147460
  0.7 38.5 %copy-start.3 = (f32[1,6144]{1,0:T(1,128)S(1)}, f32[1,6144]{1,0:T(1,128)}, u32[]{:S(2)}) copy-start(f32[1,6144]{1,0:T(1,128)} %param.14) | copy-start | bytes 73732
  0.7 38.5 %copy-start.4 = (f32[1,6144]{1,0:T(1,128)S(1)}, f32[1,6144]{1,0:T(1,128)}, u32[]{:S(2)}) copy-start(f32[1,6144]{1,0:T(1,128)} %param.15) | copy-start | bytes 73732
  0.7 38.4 %copy-start.5 = (f32[1,6144]{1,0:T(1,128)S(1)}, f32[1,6144]{1,0:T(1,128)}, u32[]{:S(2)}) copy-start(f32[1,6144]{1,0:T(1,128)} %param.16) | copy-start | bytes 73732
  3.7 1.7 %collective-permute-start.1 = (bf16[1152,128]{1,0:T(8,128)(2,1)S(1)}, bf16[1152,128]{1,0:T(8,128)(2,1)S(1)}, u32[]{:S(2)}, u32[]{:S(2)}) collective-permute-start(bf16[1152,128]{1,0:T(8,128)(2,1)S(1)} %get-tuple-element.28), channel_id=1, source_target_pairs={{0,1},{1,0},{2,3},{3,2},{4,5},{5,4},{6,7},{7,6},{8,9},{9,8},{10,11... | collective-permute-start | bytes 884744 | tf_op jit(solution)/shard_map/ppermute | solution.py:375
  5.5 7.6 %collective-permute-start.2 = (bf16[288,128]{1,0:T(8,128)(2,1)S(1)}, bf16[288,128]{1,0:T(8,128)(2,1)S(1)}, u32[]{:S(2)}, u32[]{:S(2)}) collective-permute-start(bf16[288,128]{1,0:T(8,128)(2,1)S(1)} %get-tuple-element.46), channel_id=1, source_target_pairs={{0,3},{1,2},{2,1},{3,0},{4,7},{5,6},{6,5},{7,4},{8,11},{9,10},{10,... | collective-permute-start | bytes 221192 | tf_op jit(solution)/shard_map/ppermute | solution.py:371
  8.2 5.0 %collective-permute-start.3 = (bf16[288,128]{1,0:T(8,128)(2,1)S(1)}, bf16[288,128]{1,0:T(8,128)(2,1)S(1)}, u32[]{:S(2)}, u32[]{:S(2)}) collective-permute-start(bf16[288,128]{1,0:T(8,128)(2,1)S(1)} %get-tuple-element.45), channel_id=1, source_target_pairs={{0,4},{1,5},{2,6},{3,7},{4,0},{5,1},{6,2},{7,3},{8,12},{9,13},{10,... | collective-permute-start | bytes 221192 | tf_op jit(solution)/shard_map/ppermute | solution.py:371
  9.7 5.2 %collective-permute-start.4 = (bf16[288,128]{1,0:T(8,128)(2,1)S(1)}, bf16[288,128]{1,0:T(8,128)(2,1)S(1)}, u32[]{:S(2)}, u32[]{:S(2)}) collective-permute-start(bf16[288,128]{1,0:T(8,128)(2,1)S(1)} %get-tuple-element.44), channel_id=1, source_target_pairs={{0,7},{1,6},{2,5},{3,4},{4,3},{5,2},{6,1},{7,0},{8,15},{9,14},{10,... | collective-permute-start | bytes 221192 | tf_op jit(solution)/shard_map/ppermute | solution.py:371
  9.7 3.4 %collective-permute-start = (bf16[144,128]{1,0:T(8,128)(2,1)S(1)}, bf16[144,128]{1,0:T(8,128)(2,1)S(1)}, u32[]{:S(2)}, u32[]{:S(2)}) collective-permute-start(bf16[144,128]{1,0:T(8,128)(2,1)S(1)} %get-tuple-element.26.refs_0_), channel_id=1, source_target_pairs={{0,9},{1,8},{2,11},{3,10},{4,13},{5,12},{6,15},{7,14},{8,1},{9,0},... | collective-permute-start | bytes 110600 | tf_op jit(solution)/shard_map/ppermute | solution.py:371
  15.0 3.9 %collective-permute-start.5 = (bf16[208,128]{1,0:T(8,128)(2,1)S(1)}, bf16[208,128]{1,0:T(8,128)(2,1)S(1)}, u32[]{:S(2)}, u32[]{:S(2)}) collective-permute-start(bf16[208,128]{1,0:T(8,128)(2,1)S(1)} %get-tuple-element.29.refs_0_), channel_id=1, source_target_pairs={{0,9},{1,8},{2,11},{3,10},{4,13},{5,12},{6,15},{7,14},{8,1},{9,0},... | collective-permute-start | bytes 159752 | tf_op jit(solution)/shard_map/ppermute | solution.py:371
  16.4 5.8 %collective-permute-start.11 = (bf16[144,128]{1,0:T(8,128)(2,1)S(1)}, bf16[144,128]{1,0:T(8,128)(2,1)S(1)}, u32[]{:S(2)}, u32[]{:S(2)}) collective-permute-start(bf16[144,128]{1,0:T(8,128)(2,1)S(1)} %get-tuple-element.26.refs_0_), channel_id=1, source_target_pairs={{0,24},{1,25},{2,26},{3,27},{4,28},{5,29},{6,30},{7,31},{8,16},{9,... | collective-permute-start | bytes 110600 | tf_op jit(solution)/shard_map/ppermute | solution.py:371
  18.9 4.8 %collective-permute-start.6 = (bf16[208,128]{1,0:T(8,128)(2,1)S(1)}, bf16[208,128]{1,0:T(8,128)(2,1)S(1)}, u32[]{:S(2)}, u32[]{:S(2)}) collective-permute-start(bf16[208,128]{1,0:T(8,128)(2,1)S(1)} %shard_map.163.refs_0_), channel_id=1, source_target_pairs={{0,17},{1,16},{2,19},{3,18},{4,21},{5,20},{6,23},{7,22},{8,25},{9,... | collective-permute-start | bytes 159752 | tf_op jit(solution)/shard_map/ppermute | solution.py:371
  22.1 6.7 %collective-permute-start.12 = (bf16[144,128]{1,0:T(8,128)(2,1)S(1)}, bf16[144,128]{1,0:T(8,128)(2,1)S(1)}, u32[]{:S(2)}, u32[]{:S(2)}) collective-permute-start(bf16[144,128]{1,0:T(8,128)(2,1)S(1)} %get-tuple-element.40), channel_id=1, source_target_pairs={{0,17},{1,16},{2,19},{3,18},{4,21},{5,20},{6,23},{7,22},{8,25},{9,... | collective-permute-start | bytes 110600 | tf_op jit(solution)/shard_map/ppermute | solution.py:371
  23.7 2.1 %collective-permute-start.7 = (f32[8,128]{1,0:T(8,128)S(1)}, f32[8,128]{1,0:T(8,128)S(1)}, u32[]{:S(2)}, u32[]{:S(2)}) collective-permute-start(f32[8,128]{1,0:T(8,128)S(1)} %get-tuple-element.30), channel_id=1, source_target_pairs={{0,1},{1,0},{2,3},{3,2},{4,5},{5,4},{6,7},{7,6},{8,9},{9,8},{10,11... | collective-permute-start | bytes 12296 | tf_op jit(solution)/shard_map/ppermute | solution.py:375
  25.9 3.9 %collective-permute-start.10 = (f32[8,128]{1,0:T(8,128)S(1)}, f32[8,128]{1,0:T(8,128)S(1)}, u32[]{:S(2)}, u32[]{:S(2)}) collective-permute-start(f32[8,128]{1,0:T(8,128)S(1)} %add.19.refs_0_), channel_id=1, source_target_pairs={{0,7},{1,6},{2,5},{3,4},{4,3},{5,2},{6,1},{7,0},{8,15},{9,14},{10,... | collective-permute-start | bytes 12296 | tf_op jit(solution)/shard_map/ppermute | solution.py:371
  27.1 3.6 %collective-permute-start.8 = (f32[8,128]{1,0:T(8,128)S(1)}, f32[8,128]{1,0:T(8,128)S(1)}, u32[]{:S(2)}, u32[]{:S(2)}) collective-permute-start(f32[8,128]{1,0:T(8,128)S(1)} %add.19.refs_0_), channel_id=1, source_target_pairs={{0,4},{1,5},{2,6},{3,7},{4,0},{5,1},{6,2},{7,3},{8,12},{9,13},{10,... | collective-permute-start | bytes 12296 | tf_op jit(solution)/shard_map/ppermute | solution.py:371
  27.8 3.0 %collective-permute-start.9 = (f32[8,128]{1,0:T(8,128)S(1)}, f32[8,128]{1,0:T(8,128)S(1)}, u32[]{:S(2)}, u32[]{:S(2)}) collective-permute-start(f32[8,128]{1,0:T(8,128)S(1)} %add.19.refs_0_), channel_id=1, source_target_pairs={{0,3},{1,2},{2,1},{3,0},{4,7},{5,6},{6,5},{7,4},{8,11},{9,10},{10,... | collective-permute-start | bytes 12296 | tf_op jit(solution)/shard_map/ppermute | solution.py:371
  31.2 4.3 %collective-permute-start.13 = (bf16[288,128]{1,0:T(8,128)(2,1)S(1)}, bf16[288,128]{1,0:T(8,128)(2,1)S(1)}, u32[]{:S(2)}, u32[]{:S(2)}) collective-permute-start(bf16[288,128]{1,0:T(8,128)(2,1)S(1)} %shard_map.167.refs_0_), channel_id=1, source_target_pairs={{0,3},{1,2},{2,1},{3,0},{4,7},{5,6},{6,5},{7,4},{8,11},{9,10},{10,... | collective-permute-start | bytes 221192 | tf_op jit(solution)/shard_map/ppermute | solution.py:371
  32.4 6.2 %collective-permute-start.14 = (bf16[288,128]{1,0:T(8,128)(2,1)S(1)}, bf16[288,128]{1,0:T(8,128)(2,1)S(1)}, u32[]{:S(2)}, u32[]{:S(2)}) collective-permute-start(bf16[288,128]{1,0:T(8,128)(2,1)S(1)} %shard_map.167.refs_0_), channel_id=1, source_target_pairs={{0,4},{1,5},{2,6},{3,7},{4,0},{5,1},{6,2},{7,3},{8,12},{9,13},{10,... | collective-permute-start | bytes 221192 | tf_op jit(solution)/shard_map/ppermute | solution.py:371
  32.6 6.0 %collective-permute-start.15 = (bf16[288,128]{1,0:T(8,128)(2,1)S(1)}, bf16[288,128]{1,0:T(8,128)(2,1)S(1)}, u32[]{:S(2)}, u32[]{:S(2)}) collective-permute-start(bf16[288,128]{1,0:T(8,128)(2,1)S(1)} %shard_map.167.refs_0_), channel_id=1, source_target_pairs={{0,7},{1,6},{2,5},{3,4},{4,3},{5,2},{6,1},{7,0},{8,15},{9,14},{10,... | collective-permute-start | bytes 221192 | tf_op jit(solution)/shard_map/ppermute | solution.py:371
  34.2 5.8 %collective-permute-start.16 = (bf16[288,128]{1,0:T(8,128)(2,1)S(1)}, bf16[288,128]{1,0:T(8,128)(2,1)S(1)}, u32[]{:S(2)}, u32[]{:S(2)}) collective-permute-start(bf16[288,128]{1,0:T(8,128)(2,1)S(1)} %shard_map.167.refs_0_), channel_id=1, source_target_pairs={{0,1},{1,0},{2,3},{3,2},{4,5},{5,4},{6,7},{7,6},{8,9},{9,8},{10,11... | collective-permute-start | bytes 221192 | tf_op jit(solution)/shard_map/ppermute | solution.py:375
  35.5 4.5 %collective-permute-start.17 = (bf16[288,128]{1,0:T(8,128)(2,1)S(1)}, bf16[288,128]{1,0:T(8,128)(2,1)S(1)}, u32[]{:S(2)}, u32[]{:S(2)}) collective-permute-start(bf16[288,128]{1,0:T(8,128)(2,1)S(1)} %collective-permute-done.13.refs_1_), channel_id=1, source_target_pairs={{0,1},{1,0},{2,3},{3,2},{4,5},{5,4},{6,7},{7,6},{8,9},{9,8},{10,11... | collective-permute-start | bytes 221192 | tf_op jit(solution)/shard_map/ppermute | solution.py:375
  38.6 1.4 %collective-permute-start.18 = (bf16[288,128]{1,0:T(8,128)(2,1)S(1)}, bf16[288,128]{1,0:T(8,128)(2,1)S(1)}, u32[]{:S(2)}, u32[]{:S(2)}) collective-permute-start(bf16[288,128]{1,0:T(8,128)(2,1)S(1)} %collective-permute-done.14.refs_2_), channel_id=1, source_target_pairs={{0,1},{1,0},{2,3},{3,2},{4,5},{5,4},{6,7},{7,6},{8,9},{9,8},{10,11... | collective-permute-start | bytes 221192 | tf_op jit(solution)/shard_map/ppermute | solution.py:375
  38.6 1.4 %collective-permute-start.19 = (bf16[288,128]{1,0:T(8,128)(2,1)S(1)}, bf16[288,128]{1,0:T(8,128)(2,1)S(1)}, u32[]{:S(2)}, u32[]{:S(2)}) collective-permute-start(bf16[288,128]{1,0:T(8,128)(2,1)S(1)} %collective-permute-done.15.refs_3_), channel_id=1, source_target_pairs={{0,1},{1,0},{2,3},{3,2},{4,5},{5,4},{6,7},{7,6},{8,9},{9,8},{10,11... | collective-permute-start | bytes 221192 | tf_op jit(solution)/shard_map/ppermute | solution.py:375
